TPU v7x, 32 devices: a whole 2x2x4 slice. The times are simulated.
32 devices in a mesh: dp: 8 (over y, x, core), tensor: 4 (over z).
Axes of the slice: x: 2, y: 2, z: 4, core: 2. Of those that a mesh axis runs over, the one named last changes fastest.
Arguments:
- image_in: bfloat16 [16384, 1536], P(('dp', 'tensor')), may hold values from -6 to 6
- text_in: bfloat16 [2464, 1536], P(('dp', 'tensor')), may hold values from -6 to 6
- condition: bfloat16 [16, 1536], P('dp'), may hold values from -6 to 6
- live_slots: int32 [16], P('dp'), may hold values from 0 to 1, as said below
- ada_weight: bfloat16 [2, 1536, 6, 1536], P(None, 'dp', None, 'tensor'), may hold values from -0.15625 to 0.15625
- ada_bias: bfloat16 [2, 6, 1536], replicated, may hold values from -3 to 3
- qkv_weight: bfloat16 [2, 3, 1536, 1536], P(None, None, 'dp', 'tensor'), may hold values from -0.21875 to 0.21875
- qv_bias: bfloat16 [2, 2, 1536], replicated, may hold values from -3 to 3
- proj_weight: bfloat16 [2, 1536, 1536], P(None, 'tensor', 'dp'), may hold values from -0.875 to 0.875
- proj_bias: bfloat16 [2, 1536], replicated, may hold values from -3 to 3
- up_weight: bfloat16 [2, 1536, 6144], P(None, 'dp', 'tensor'), may hold values from -0.15625 to 0.15625
- up_bias: bfloat16 [2, 6144], replicated, may hold values from -3 to 3
- down_weight: bfloat16 [2, 6144, 1536], P(None, 'tensor', 'dp'), may hold values from -0.078125 to 0.078125
- down_bias: bfloat16 [2, 1536], replicated, may hold values from -3 to 3
- image_grad: bfloat16 [16384, 1536], P(('dp', 'tensor')), may hold values from -6 to 6
- text_grad: bfloat16 [2464, 1536], P(('dp', 'tensor')), may hold values from -6 to 6
Outputs:
- image_out: bfloat16 [16384, 1536], P(('dp', 'tensor'))
- text_out: bfloat16 [2464, 1536], P(('dp', 'tensor'))
- image_in_grad: float32 [16384, 1536], P(('dp', 'tensor'))
- text_in_grad: float32 [2464, 1536], P(('dp', 'tensor'))
- condition_grad: float32 [16, 1536], P('dp', 'tensor')
- ada_weight_grad: float32 [2, 1536, 6, 1536], P(None, 'dp', None, 'tensor')
- ada_bias_grad: float32 [2, 6, 1536], replicated
- qkv_weight_grad: float32 [2, 3, 1536, 1536], P(None, None, 'dp', 'tensor')
- qv_bias_grad: float32 [2, 2, 1536], replicated
- proj_weight_grad: float32 [2, 1536, 1536], P(None, 'tensor', 'dp')
- proj_bias_grad: float32 [2, 1536], replicated
- up_weight_grad: float32 [2, 1536, 6144], P(None, 'dp', 'tensor')
- up_bias_grad: float32 [2, 6144], replicated
- down_weight_grad: float32 [2, 6144, 1536], P(None, 'tensor', 'dp')
- down_bias_grad: float32 [2, 1536], replicated
Inputs may be any that keep to these rules, and one draw needn't show every extreme that they name: `live_slots`: entry 2 * g + j is 1 when slot j of group g holds a sequence; the live slots of a group come first, every group has one or more, and some group has all 2.
All inputs are finite; a program needn't handle non-finite values.
Results may differ from a plain program's by a relative error of at most 0.015.
The roundings to bfloat16 on the way count: a program that leaves them out, or rounds other values in their place, can miss the bound.
Values may be sent and summed in bfloat16 or wider, within the bound.
A program may use at most 384 MiB of HBM per device.

v0:
```python
import jax
import jax.numpy as jnp
from jax import lax
from jax.sharding import PartitionSpec as P

D = 1536
FF = 6144
IMG = 1024
TXT = 154
HEAD_DIM = 64


def norm_parts(values):
    average = jnp.mean(values, axis=-1, keepdims=True)
    centred = values - average
    variance = jnp.mean(centred * centred, axis=-1, keepdims=True)
    inverse = lax.rsqrt(variance + 1e-06)
    return (centred * inverse, inverse)


def norm_back(normed, inverse, grad_in):
    first_mean = jnp.mean(grad_in, axis=-1, keepdims=True)
    cross_mean = jnp.mean(grad_in * normed, axis=-1, keepdims=True)
    return inverse * (grad_in - first_mean - normed * cross_mean)


def slot_table(row_count, length, slot_count):
    offset = lax.axis_index("tensor") * row_count
    owners = (offset + jnp.arange(row_count, dtype=jnp.int32)) // length
    return (owners[:, None] == jnp.arange(slot_count, dtype=jnp.int32)[None, :]).astype(jnp.float32)


def spread_rows(slot_rows, per_slot):
    return jnp.dot(slot_rows, per_slot, precision=lax.Precision.HIGHEST)


def gather_rows(first_rows, second_rows):
    return (
        lax.all_gather(first_rows, "tensor", axis=0, tiled=True),
        lax.all_gather(second_rows, "tensor", axis=0, tiled=True),
    )


def sum_rows(first_rows, second_rows):
    return (
        lax.psum_scatter(first_rows, "tensor", scatter_dimension=0, tiled=True),
        lax.psum_scatter(second_rows, "tensor", scatter_dimension=0, tiled=True),
    )


def split_heads(values):
    return values.reshape(values.shape[0], -1, HEAD_DIM)


def join_streams(image_part, text_part, slot_count):
    return jnp.concatenate(
        (image_part.reshape(slot_count, IMG, -1), text_part.reshape(slot_count, TXT, -1)), axis=1
    )


def split_streams(values, slot_count):
    columns = values.shape[2]
    return (
        values[:, :IMG].reshape(slot_count * IMG, columns),
        values[:, IMG:].reshape(slot_count * TXT, columns),
    )


def attend(query_rows, key_rows, value_rows):
    scaling = HEAD_DIM ** (-0.5)
    raw_scores = (
        jnp.einsum(
            "qhd,khd->hqk",
            split_heads(query_rows),
            split_heads(key_rows),
            preferred_element_type=jnp.float32,
        )
        * scaling
    )
    highest = jnp.max(raw_scores, axis=-1, keepdims=True)
    powers = jnp.exp(raw_scores - highest)
    totals = jnp.sum(powers, axis=-1, keepdims=True)
    weights = (powers / totals).astype(jnp.bfloat16)
    combined = jnp.einsum(
        "hqk,khd->qhd", weights, split_heads(value_rows), preferred_element_type=jnp.float32
    )
    return (
        combined.reshape(query_rows.shape[0], -1).astype(jnp.bfloat16),
        (highest + jnp.log(totals))[..., 0],
    )


def attend_back(query_rows, key_rows, value_rows, grad_combined, log_total):
    scaling = HEAD_DIM ** (-0.5)
    length = query_rows.shape[0]
    query_heads = split_heads(query_rows)
    key_heads = split_heads(key_rows)
    value_heads = split_heads(value_rows)
    grad_heads_in = split_heads(grad_combined)
    raw_scores = (
        jnp.einsum("qhd,khd->hqk", query_heads, key_heads, preferred_element_type=jnp.float32)
        * scaling
    )
    probability = jnp.exp(raw_scores - log_total[..., None])
    grad_probs = jnp.einsum(
        "qhd,khd->hqk", grad_heads_in, value_heads, preferred_element_type=jnp.float32
    )
    grad_value = jnp.einsum(
        "hqk,qhd->khd",
        probability.astype(jnp.bfloat16),
        grad_heads_in,
        preferred_element_type=jnp.float32,
    )
    inner_sum = jnp.sum(grad_probs * probability, axis=-1, keepdims=True)
    grad_scores = (probability * (grad_probs - inner_sum)).astype(jnp.bfloat16)
    grad_query = (
        jnp.einsum("hqk,khd->qhd", grad_scores, key_heads, preferred_element_type=jnp.float32)
        * scaling
    )
    grad_key = (
        jnp.einsum("hqk,qhd->khd", grad_scores, query_heads, preferred_element_type=jnp.float32)
        * scaling
    )
    return (
        grad_query.reshape(length, -1).astype(jnp.bfloat16),
        grad_key.reshape(length, -1).astype(jnp.bfloat16),
        grad_value.reshape(length, -1).astype(jnp.bfloat16),
    )


def forward_slot(slot_items):
    return attend(slot_items[0], slot_items[1], slot_items[2])


def backward_slot(slot_items):
    return attend_back(slot_items[0], slot_items[1], slot_items[2], slot_items[3], slot_items[4])


def body(
    image_in,
    text_in,
    condition,
    live_slots,
    ada_weight,
    ada_bias,
    qkv_weight,
    qv_bias,
    proj_weight,
    proj_bias,
    up_weight,
    up_bias,
    down_weight,
    down_bias,
    image_grad,
    text_grad,
):
    slot_count = condition.shape[0]
    tensor_size = lax.axis_size("tensor")
    tensor_index = lax.axis_index("tensor")
    width_part = D // tensor_size
    hidden_part = FF // tensor_size
    image_rows = image_in.shape[0]
    text_rows = text_in.shape[0]
    gathered = (
        lax.all_gather(ada_weight, "dp", axis=1, tiled=True),
        lax.all_gather(qkv_weight, "dp", axis=2, tiled=True),
        lax.all_gather(proj_weight, "dp", axis=2, tiled=True),
        lax.all_gather(up_weight, "dp", axis=1, tiled=True),
        lax.all_gather(down_weight, "dp", axis=2, tiled=True),
    )
    ada_full, qkv_full, proj_part, up_full, down_part = gathered
    cond_float = condition.astype(jnp.float32)
    silu_cond = jax.nn.silu(cond_float).astype(jnp.bfloat16)
    mod_part = jnp.einsum("sd,tdkc->tskc", silu_cond, ada_full, preferred_element_type=jnp.float32)
    modulation = (
        lax.all_gather(mod_part, "tensor", axis=3, tiled=True)
        + ada_bias.astype(jnp.float32)[:, None]
    )
    tables = (slot_table(image_rows, IMG, slot_count), slot_table(text_rows, TXT, slot_count))
    live_float = live_slots.astype(jnp.float32)
    row_mods = [
        spread_rows(tables[stream], modulation[stream].reshape(slot_count, 6 * D)).reshape(-1, 6, D)
        for stream in range(2)
    ]
    row_live = [spread_rows(tables[stream], live_float[:, None]) for stream in range(2)]
    inputs = (image_in.astype(jnp.float32), text_in.astype(jnp.float32))
    first_norm = [norm_parts(inputs[stream]) for stream in range(2)]
    first_hidden = [
        (first_norm[stream][0] * (1.0 + row_mods[stream][:, 1]) + row_mods[stream][:, 0]).astype(
            jnp.bfloat16
        )
        for stream in range(2)
    ]
    first_full = gather_rows(first_hidden[0], first_hidden[1])
    bias_slice = lax.dynamic_slice_in_dim(
        qv_bias.astype(jnp.float32), tensor_index * width_part, width_part, 2
    )
    projected = [
        jnp.einsum(
            "rd,kdc->rkc", first_full[stream], qkv_full[stream], preferred_element_type=jnp.float32
        )
        for stream in range(2)
    ]
    queries = [
        (projected[stream][:, 0] + bias_slice[stream, 0]).astype(jnp.bfloat16)
        for stream in range(2)
    ]
    keys_rows = [projected[stream][:, 1].astype(jnp.bfloat16) for stream in range(2)]
    values_rows = [
        (projected[stream][:, 2] + bias_slice[stream, 1]).astype(jnp.bfloat16)
        for stream in range(2)
    ]
    query_all = join_streams(queries[0], queries[1], slot_count)
    key_all = join_streams(keys_rows[0], keys_rows[1], slot_count)
    value_all = join_streams(values_rows[0], values_rows[1], slot_count)
    attended, log_totals = lax.map(forward_slot, (query_all, key_all, value_all))
    heads_out = split_streams(attended, slot_count)
    proj_bias_float = proj_bias.astype(jnp.float32)
    proj_terms = [
        jnp.dot(heads_out[stream], proj_part[stream], preferred_element_type=jnp.float32)
        for stream in range(2)
    ]
    branch_sums = sum_rows(proj_terms[0], proj_terms[1])
    branch_one = [branch_sums[stream] + proj_bias_float[stream] for stream in range(2)]
    middle = [inputs[stream] + row_mods[stream][:, 2] * branch_one[stream] for stream in range(2)]
    second_norm = [norm_parts(middle[stream]) for stream in range(2)]
    second_hidden = [
        (second_norm[stream][0] * (1.0 + row_mods[stream][:, 4]) + row_mods[stream][:, 3]).astype(
            jnp.bfloat16
        )
        for stream in range(2)
    ]
    second_full = gather_rows(second_hidden[0], second_hidden[1])
    up_slice = lax.dynamic_slice_in_dim(
        up_bias.astype(jnp.float32), tensor_index * hidden_part, hidden_part, 1
    )
    inner_rows = [
        jnp.dot(second_full[stream], up_full[stream], preferred_element_type=jnp.float32)
        + up_slice[stream]
        for stream in range(2)
    ]
    activated = [
        jax.nn.gelu(inner_rows[stream], approximate=True).astype(jnp.bfloat16)
        for stream in range(2)
    ]
    down_terms = [
        jnp.dot(activated[stream], down_part[stream], preferred_element_type=jnp.float32)
        for stream in range(2)
    ]
    down_sums = sum_rows(down_terms[0], down_terms[1])
    down_bias_float = down_bias.astype(jnp.float32)
    branch_two = [down_sums[stream] + down_bias_float[stream] for stream in range(2)]
    outputs = [
        row_live[stream] * (middle[stream] + row_mods[stream][:, 5] * branch_two[stream])
        for stream in range(2)
    ]
    gathered = (
        lax.all_gather(ada_weight, "dp", axis=1, tiled=True),
        lax.all_gather(qkv_weight, "dp", axis=2, tiled=True),
        lax.all_gather(proj_weight, "dp", axis=2, tiled=True),
        lax.all_gather(up_weight, "dp", axis=1, tiled=True),
        lax.all_gather(down_weight, "dp", axis=2, tiled=True),
    )
    ada_full, qkv_full, proj_part, up_full, down_part = gathered
    cotangent = (image_grad, text_grad)
    grad_out = [row_live[stream] * cotangent[stream].astype(jnp.float32) for stream in range(2)]
    grad_two = [
        (row_mods[stream][:, 5] * grad_out[stream]).astype(jnp.bfloat16) for stream in range(2)
    ]
    grad_gate_two = [branch_two[stream] * grad_out[stream] for stream in range(2)]
    grad_two_full = gather_rows(grad_two[0], grad_two[1])
    grad_act = [
        jnp.einsum(
            "rc,hc->rh",
            grad_two_full[stream],
            down_part[stream],
            preferred_element_type=jnp.float32,
        )
        for stream in range(2)
    ]
    grad_inner = []
    for stream in range(2):
        unused, gelu_pull = jax.vjp(
            lambda values: jax.nn.gelu(values, approximate=True), inner_rows[stream]
        )
        grad_inner.append(gelu_pull(grad_act[stream])[0].astype(jnp.bfloat16))
    down_grads = jnp.stack(
        [
            jnp.einsum(
                "rh,rc->hc",
                activated[stream],
                grad_two_full[stream],
                preferred_element_type=jnp.float32,
            )
            for stream in range(2)
        ]
    )
    up_grads = jnp.stack(
        [
            jnp.einsum(
                "rd,rh->dh",
                second_full[stream],
                grad_inner[stream],
                preferred_element_type=jnp.float32,
            )
            for stream in range(2)
        ]
    )
    up_bias_part = jnp.stack(
        [jnp.sum(grad_inner[stream].astype(jnp.float32), axis=0) for stream in range(2)]
    )
    hidden_terms = [
        jnp.einsum(
            "rh,dh->rd", grad_inner[stream], up_full[stream], preferred_element_type=jnp.float32
        )
        for stream in range(2)
    ]
    grad_hidden_two = sum_rows(hidden_terms[0], hidden_terms[1])
    grad_middle = [
        grad_out[stream]
        + norm_back(
            second_norm[stream][0],
            second_norm[stream][1],
            grad_hidden_two[stream] * (1.0 + row_mods[stream][:, 4]),
        )
        for stream in range(2)
    ]
    grad_one = [
        (row_mods[stream][:, 2] * grad_middle[stream]).astype(jnp.bfloat16) for stream in range(2)
    ]
    grad_gate_one = [branch_one[stream] * grad_middle[stream] for stream in range(2)]
    grad_one_full = gather_rows(grad_one[0], grad_one[1])
    grad_heads = [
        jnp.einsum(
            "rc,hc->rh",
            grad_one_full[stream],
            proj_part[stream],
            preferred_element_type=jnp.float32,
        ).astype(jnp.bfloat16)
        for stream in range(2)
    ]
    proj_grads = jnp.stack(
        [
            jnp.einsum(
                "rh,rc->hc",
                heads_out[stream],
                grad_one_full[stream],
                preferred_element_type=jnp.float32,
            )
            for stream in range(2)
        ]
    )
    grad_all = join_streams(grad_heads[0], grad_heads[1], slot_count)
    grad_query_all, grad_key_all, grad_value_all = lax.map(
        backward_slot, (query_all, key_all, value_all, grad_all, log_totals)
    )
    grad_query_rows = split_streams(grad_query_all, slot_count)
    grad_key_rows = split_streams(grad_key_all, slot_count)
    grad_value_rows = split_streams(grad_value_all, slot_count)
    grad_qkv = [
        jnp.stack((grad_query_rows[stream], grad_key_rows[stream], grad_value_rows[stream]), axis=1)
        for stream in range(2)
    ]
    qkv_grads = jnp.stack(
        [
            jnp.einsum(
                "rd,rkc->kdc",
                first_full[stream],
                grad_qkv[stream],
                preferred_element_type=jnp.float32,
            )
            for stream in range(2)
        ]
    )
    qv_part = jnp.stack(
        [jnp.sum(grad_qkv[stream][:, 0::2].astype(jnp.float32), axis=0) for stream in range(2)]
    )
    first_terms = [
        jnp.einsum(
            "rkc,kdc->rd", grad_qkv[stream], qkv_full[stream], preferred_element_type=jnp.float32
        )
        for stream in range(2)
    ]
    grad_hidden_one = sum_rows(first_terms[0], first_terms[1])
    input_grads = [
        grad_middle[stream]
        + norm_back(
            first_norm[stream][0],
            first_norm[stream][1],
            grad_hidden_one[stream] * (1.0 + row_mods[stream][:, 1]),
        )
        for stream in range(2)
    ]
    mod_rows = [
        jnp.stack(
            (
                grad_hidden_one[stream],
                grad_hidden_one[stream] * first_norm[stream][0],
                grad_gate_one[stream],
                grad_hidden_two[stream],
                grad_hidden_two[stream] * second_norm[stream][0],
                grad_gate_two[stream],
            ),
            axis=1,
        )
        for stream in range(2)
    ]
    mod_slots = jnp.stack(
        [
            jnp.einsum(
                "rs,rkd->skd", tables[stream], mod_rows[stream], precision=lax.Precision.HIGHEST
            )
            for stream in range(2)
        ]
    )
    ada_bias_part = jnp.sum(mod_slots, axis=1)
    mod_share = lax.psum_scatter(mod_slots, "tensor", scatter_dimension=3, tiled=True)
    ada_grads = jnp.einsum(
        "sd,tskc->tdkc", silu_cond.astype(jnp.float32), mod_share, precision=lax.Precision.HIGHEST
    )
    cond_terms = jnp.einsum(
        "tskc,tdkc->sd", mod_share, ada_full.astype(jnp.float32), precision=lax.Precision.HIGHEST
    )
    cond_share = lax.psum_scatter(cond_terms, "tensor", scatter_dimension=1, tiled=True)
    cond_slice = lax.dynamic_slice_in_dim(cond_float, tensor_index * width_part, width_part, 1)
    unused_cond, silu_pull = jax.vjp(jax.nn.silu, cond_slice)
    condition_grad = silu_pull(cond_share)[0]
    first_sums = (
        lax.psum_scatter(ada_grads, "dp", scatter_dimension=1, tiled=True),
        lax.psum_scatter(up_grads, "dp", scatter_dimension=1, tiled=True),
    )
    rest_sums = (
        lax.psum_scatter(qkv_grads, "dp", scatter_dimension=2, tiled=True),
        lax.psum_scatter(proj_grads, "dp", scatter_dimension=2, tiled=True),
        lax.psum_scatter(down_grads, "dp", scatter_dimension=2, tiled=True),
    )
    qv_whole = lax.dynamic_update_slice_in_dim(
        jnp.zeros((2, 2, D), jnp.float32), qv_part, tensor_index * width_part, 2
    )
    up_whole = lax.dynamic_update_slice_in_dim(
        jnp.zeros((2, FF), jnp.float32), up_bias_part, tensor_index * hidden_part, 1
    )
    proj_bias_part = jnp.stack(
        [jnp.sum(grad_one[stream].astype(jnp.float32), axis=0) for stream in range(2)]
    )
    down_bias_part = jnp.stack(
        [jnp.sum(grad_two[stream].astype(jnp.float32), axis=0) for stream in range(2)]
    )
    bias_sums = lax.psum(
        (ada_bias_part, qv_whole, proj_bias_part, up_whole, down_bias_part), ("dp", "tensor")
    )
    return (
        outputs[0].astype(jnp.bfloat16),
        outputs[1].astype(jnp.bfloat16),
        input_grads[0],
        input_grads[1],
        condition_grad,
        first_sums[0],
        bias_sums[0],
        rest_sums[0],
        bias_sums[1],
        rest_sums[1],
        bias_sums[2],
        first_sums[1],
        bias_sums[3],
        rest_sums[2],
        bias_sums[4],
    )


def solution(mesh):
    in_specs = (
        P(("dp", "tensor"), None),
        P(("dp", "tensor"), None),
        P("dp", None),
        P("dp"),
        P(None, "dp", None, "tensor"),
        P(),
        P(None, None, "dp", "tensor"),
        P(),
        P(None, "tensor", "dp"),
        P(),
        P(None, "dp", "tensor"),
        P(),
        P(None, "tensor", "dp"),
        P(),
        P(("dp", "tensor"), None),
        P(("dp", "tensor"), None),
    )
    out_specs = (
        P(("dp", "tensor"), None),
        P(("dp", "tensor"), None),
        P(("dp", "tensor"), None),
        P(("dp", "tensor"), None),
        P("dp", "tensor"),
        P(None, "dp", None, "tensor"),
        P(),
        P(None, None, "dp", "tensor"),
        P(),
        P(None, "tensor", "dp"),
        P(),
        P(None, "dp", "tensor"),
        P(),
        P(None, "tensor", "dp"),
        P(),
    )
    return jax.shard_map(body, mesh=mesh, in_specs=in_specs, out_specs=out_specs, check_vma=False)
```

profile of v0, /device:TPU:0, one launch (start us, length us, event | category | flops | bytes accessed | tf_op | source)
XLA Modules:
  0.0 3593.3 jit_solution(5848283492013139764)
XLA Ops:
  10.4 81.0 %all-gather.14.cloned.1.call-done = bf16[2,1536,6,384]{3,1,2,0:T(8,128)(2,1)} async-done(((bf16[2,192,6,384]{3,1,2,0:T(8,128)(2,1)}), bf16[2,1536,6,384]{3,1,2,0:T(8,128)(2,1)}) %all-gather.14.cloned.1.call-update) | async-done | bytes 14155792 | tf_op jit(solution)/shard_map/all_gather | solution.py:165
  98.4 13.6 all_gather.48
  133.2 21.7 all-gather
  161.4 98.4 %all-gather.16.cloned.1.call-done = bf16[2048,1536]{1,0:T(8,128)(2,1)} async-done(((bf16[512,1536]{1,0:T(8,128)(2,1)}), bf16[2048,1536]{1,0:T(8,128)(2,1)}) %all-gather.16.cloned.1.call-update) | async-done | bytes 6291472 | tf_op jit(solution)/shard_map/all_gather | solution.py:39
  259.8 11.4 fusion.27
  292.7 95.2 %while.26 = (s32[]{:T(128)}, bf16[2,1178,384]{1,2,0:T(8,128)(2,1)}, f32[2,6,1178]{2,1,0:T(8,128)}, bf16[2,1178,384]{1,2,0:T(8,128)(2,1)}, bf16[2,1178,384]{1,2,0...) while((s32[]{:T(128)}, bf16[2,1178,384]{1,2,0:T(8,128)(2,1)}, f32[2,6,1178]{2,1,0:T(8,128)}, ...), condition=%wide.region_7.8_spmd, body=%wide.region_4.7_spmd.sunk | while | flops 2190210560 | bytes 111086992 | solution.py:216
  295.5 14.2 fusion.200
  309.8 14.5 fusion.201
  324.3 14.5 fusion.202
  343.0 14.2 fusion.200
  357.3 14.5 fusion.201
  371.8 14.5 fusion.202
  402.8 209.2 %reduce-scatter.20.cloned.1.call-done = f32[512,1536]{1,0:T(8,128)} async-done(((f32[2048,1536]{1,0:T(8,128)}), f32[512,1536]{1,0:T(8,128)}) %reduce-scatter.20.cloned.1.call-update) | async-done | bytes 3145744 | tf_op jit(solution)/shard_map/reduce_scatter | solution.py:46
  628.2 45.5 %all-gather.24.cloned.1.call-done = bf16[2,1536,1536]{2,1,0:T(8,128)(2,1)} async-done(((bf16[2,192,1536]{2,1,0:T(8,128)(2,1)}), bf16[2,1536,1536]{2,1,0:T(8,128)(2,1)}) %all-gather.24.cloned.1.call-update) | async-done | bytes 9437200 | tf_op jit(solution)/shard_map/all_gather | solution.py:168
  673.7 117.5 %all-gather.22.cloned.1.call-done = bf16[2048,1536]{1,0:T(8,128)(2,1)} async-done(((bf16[512,1536]{1,0:T(8,128)(2,1)}), bf16[2048,1536]{1,0:T(8,128)(2,1)}) %all-gather.22.cloned.1.call-update) | async-done | bytes 6291472 | tf_op jit(solution)/shard_map/all_gather | solution.py:39
  791.3 16.3 fusion.33
  807.6 42.7 %all-gather.26.cloned.1.call-done = bf16[2,1536,1536]{1,2,0:T(8,128)(2,1)} async-done(((bf16[2,1536,192]{1,2,0:T(8,128)(2,1)}), bf16[2,1536,1536]{1,2,0:T(8,128)(2,1)}) %all-gather.26.cloned.1.call-update) | async-done | bytes 9437200 | tf_op jit(solution)/shard_map/all_gather | solution.py:169
  850.2 117.5 %all-gather.28.cloned.1.call-done = bf16[2048,1536]{1,0:T(8,128)(2,1)} async-done(((bf16[512,1536]{1,0:T(8,128)(2,1)}), bf16[2048,1536]{1,0:T(8,128)(2,1)}) %all-gather.28.cloned.1.call-update) | async-done | bytes 6291472 | tf_op jit(solution)/shard_map/all_gather | solution.py:39
  967.8 25.5 convert_reduce_fusion
  993.3 14.8 fusion.32
  1008.2 18.2 fusion.35
  1031.3 187.1 %reduce-scatter.24.cloned.1.call-done = f32[512,1536]{1,0:T(8,128)} async-done(((f32[2048,1536]{1,0:T(8,128)}), f32[512,1536]{1,0:T(8,128)}) %reduce-scatter.24.cloned.1.call-update) | async-done | bytes 3145744 | tf_op jit(solution)/shard_map/reduce_scatter | solution.py:46
  1222.1 211.6 %reduce-scatter.22.cloned.1.call-done = f32[512,1536]{1,0:T(8,128)} async-done(((f32[2048,1536]{1,0:T(8,128)}), f32[512,1536]{1,0:T(8,128)}) %reduce-scatter.22.cloned.1.call-update) | async-done | bytes 3145744 | tf_op jit(solution)/shard_map/reduce_scatter | solution.py:46
  1433.7 10.2 convert_reduce_fusion.4
  1447.5 73.2 %fusion = f32[80,1536]{1,0:T(8,128)S(1)} fusion(f32[308,1536]{1,0:T(8,128)} %fusion.78), kind=kCustom, calls=%all-reduce-scatter | all-reduce-scatter fusion | flops 491521 | bytes 2384384
  1521.3 10.5 collective-permute-start
  1543.4 38.8 %all-gather.2 = bf16[4,77,1536]{2,1,0:T(8,128)(2,1)} all-gather(bf16[1,77,1536]{2,1,0:T(8,128)(2,1)S(1)} %bitcast.436), channel_id=1, replica_groups=mesh['dp'=8,'tensor'=4] {'tensor'}, dimensions={0}, use_global_device_ids=true | all-gather | bytes 1182720 | tf_op jit(solution)/shard_map/all_gather | solution.py:40
  1584.6 36.8 %all-gather.1 = bf16[4,77,1536]{2,1,0:T(8,128)(2,1)} all-gather(bf16[1,77,1536]{2,1,0:T(8,128)(2,1)} %get-tuple-element.234), channel_id=1, replica_groups=mesh['dp'=8,'tensor'=4] {'tensor'}, dimensions={0}, use_global_device_ids=true | all-gather | bytes 1182720 | tf_op jit(solution)/shard_map/all_gather | solution.py:40
  1638.6 29.8 fusion.2
  1681.3 16.7 all-gather.3
  1715.6 227.7 %while.27 = (s32[]{:T(128)}, bf16[2,1178,384]{1,2,0:T(8,128)(2,1)}, bf16[2,1178,384]{1,2,0:T(8,128)(2,1)}, bf16[2,1178,384]{1,2,0:T(8,128)(2,1)}, bf16[2,1178,38...) while((s32[]{:T(128)}, bf16[2,1178,384]{1,2,0:T(8,128)(2,1)}, ...), condition=%wide.region_24.25_spmd, body=%wide.region_22.24_spmd.sunk | while | flops 5397570048 | bytes 333627648 | solution.py:354
  1719.8 14.3 fusion.213
  1734.2 15.2 fusion.215
  1749.4 26.6 multiply_reduce_fusion.6
  1776.0 29.6 multiply_convert_fusion.18
  1805.6 11.6 fusion.216
  1833.4 14.3 fusion.213
  1847.7 15.2 fusion.215
  1863.0 26.6 multiply_reduce_fusion.6
  1889.6 29.6 multiply_convert_fusion.18
  1919.2 11.6 fusion.216
  1930.8 9.6 fusion.214
  1955.5 13.9 convolution_bitcast_fusion.5
  1997.7 129.8 %fusion.130 = (f32[80,1536]{1,0:T(8,128)S(1)}, f32[80,1536]{1,0:T(8,128)S(1)}) fusion(f32[308,1536]{1,0:T(8,128)} %fusion.39, f32[308,1536]{1,0:T(8,128)} %fusion.61), kind=kCustom, calls=%all-reduce-scatter.4 | all-reduce-scatter fusion | flops 983041 | bytes 4768256
  2128.3 22.9 collective-permute-start.3
  2155.6 18.9 convolution_bitcast_fusion.1
  2185.2 62.7 %reduce-scatter.26.cloned.1.call-done = f32[512,1536]{1,0:T(8,128)} async-done(((f32[2048,1536]{1,0:T(8,128)}), f32[512,1536]{1,0:T(8,128)}) %reduce-scatter.26.cloned.1.call-update) | async-done | bytes 3145744 | tf_op jit(solution)/shard_map/reduce_scatter | solution.py:46
  2266.9 10.2 convolution_bitcast_fusion.10
  2295.2 14.6 pad_maximum_fusion.1
  2309.8 28.4 copy.112
  2361.9 11.9 fusion.29
  2373.8 13.6 pad_maximum_fusion.2
  2387.4 22.1 copy.110
  2412.6 15.5 fusion.65
  2428.2 14.7 convolution_bitcast_fusion
  2442.9 42.0 %copy.108 = f32[2,1536,6,384]{3,0,2,1:T(2,128)} copy(f32[2,1536,6,384]{1,3,2,0:T(8,128)} %convolution_bitcast_fusion) | data formatting | bytes 56623104 | tf_op jit(solution)/shard_map/sd,tskc->tdkc/transpose | solution.py:418
  2489.1 14.3 convolution_bitcast_fusion.2
  2512.9 67.0 %all-reduce.25.cloned.1.call-done = f32[2,1536,1536]{1,0,2:T(2,128)} async-done(((f32[2,1536,1536]{1,0,2:T(2,128)}), f32[2,1536,1536]{1,0,2:T(2,128)}) %all-reduce.25.cloned.1.call-update) | async-done | bytes 18874384
  2591.2 233.1 %all-reduce.29.cloned.1.call-done = (f32[2,3,1536,384]{3,0,1,2:T(2,128)}, f32[2,384,1536]{1,0,2:T(2,128)}) async-done(((f32[2,3,1536,384]{3,0,1,2:T(2,128)}, f32[2,384,1536]{1,0,2:T(2,128)}), (f32[2,3,1536,384]{3,0,1,2:T(2,128)}, f32[2,384,1536]{1,0,2:T(2,128)})) %all-reduce.29.cloned.1.call-update) | async-done | bytes 18874384
  2837.7 112.7 %all-reduce.21.cloned.1.call-done = f32[2,6,1536]{2,1,0:T(8,128)} async-done(((f32[2,6,1536]{2,1,0:T(8,128)}), f32[2,6,1536]{2,1,0:T(8,128)}) %all-reduce.21.cloned.1.call-update) | async-done | bytes 73744 | tf_op jit(solution)/shard_map/psum | solution.py:449
  2952.0 25.3 reduce-scatter.32.cloned.1.call-done
  2978.9 342.6 %all-reduce.23.cloned.1.call-done = f32[2,1536,6,384]{3,0,2,1:T(2,128)} async-done(((f32[2,1536,6,384]{3,0,2,1:T(2,128)}), f32[2,1536,6,384]{3,0,2,1:T(2,128)}) %all-reduce.23.cloned.1.call-update) | async-done | bytes 28311568
  3326.8 125.0 %reduce-scatter.28.cloned.1.call-done = f32[2,192,1536]{2,1,0:T(8,128)} async-done(((f32[2,1536,1536]{2,1,0:T(8,128)}), f32[2,192,1536]{2,1,0:T(8,128)}) %reduce-scatter.28.cloned.1.call-update) | async-done | bytes 2359312 | tf_op jit(solution)/shard_map/reduce_scatter | solution.py:430
  3451.8 128.8 %all-reduce.27.cloned.1.call-done = (f32[2,2,1536]{2,1,0:T(2,128)}, f32[2,1536]{1,0:T(2,128)}, f32[2,6144]{1,0:T(2,128)}, f32[2,1536]{1,0:T(2,128)}) async-done(((f32[2,2,1536]{2,1,0:T(2,128)}, f32[2,1536]{1,0:T(2,128)}, f32[2,6144]{1,0:T(2,128)}, f32[2,1536]{1,0:T(2,128)}), (f32[2,2,1536]{2,1,0:T(2,128)}, f32[2,1536]{1,0:T(2,128)}, f32[2,6144]{1,0:T(2,128)}, ...) | async-done | bytes 98320 | tf_op jit(solution)/shard_map/psum | solution.py:449
  (538 shorter events, 365.6 us)
Async XLA Ops:
  7.2 84.3 %copy-start.84 = (bf16[2,1536]{1,0:T(2,128)(2,1)S(1)}, bf16[2,1536]{1,0:T(2,128)(2,1)}, u32[]{:S(2)}) copy-start(bf16[2,1536]{1,0:T(2,128)(2,1)} %param.22) | copy-start | bytes 18436
  7.2 84.2 %all-gather.14.cloned.1.call-start = ((), (), s32[]{:S(2)}) async-start(), calls=%async_computation.7 | async-start | bytes 15925248 | tf_op jit(solution)/shard_map/all_gather | solution.py:165
  7.9 147.2 %all-gather.18.cloned.1.call-start = ((), (), s32[]{:S(2)}) async-start(), calls=%async_computation.9 | async-start | bytes 7962624 | tf_op jit(solution)/shard_map/all_gather | solution.py:166
  8.7 251.1 %all-gather.16.cloned.1.call-start = ((), (), s32[]{:S(2)}) async-start(), calls=%async_computation.8 | async-start | bytes 7864320 | tf_op jit(solution)/shard_map/all_gather | solution.py:39
  9.5 102.5 %copy-start.99 = (s32[512]{0:T(512)}, s32[512]{0:T(512)S(1)}, u32[]{:S(2)}) copy-start(s32[512]{0:T(512)S(1)} %add_select_fusion) | copy-start | bytes 6148
  9.8 109.8 %copy-start.76 = (f32[512]{0:T(512)}, f32[512]{0:T(512)S(1)}, u32[]{:S(2)}) copy-start(f32[512]{0:T(512)S(1)} %broadcast_multiply_fusion.5) | copy-start | bytes 6148
  10.4 109.2 %copy-start.86 = (f32[512]{0:T(512)}, f32[512]{0:T(512)S(1)}, u32[]{:S(2)}) copy-start(f32[512]{0:T(512)S(1)} %add_rsqrt_fusion.1) | copy-start | bytes 6148
  128.0 265.8 %all-gather.20.cloned.1.call-start = ((), (), s32[]{:S(2)}) async-start(), calls=%async_computation.10 | async-start | bytes 2654208 | tf_op jit(solution)/shard_map/all_gather | solution.py:167
  128.6 483.5 %reduce-scatter.20.cloned.1.call-start = ((), (), s32[]{:S(2)}) async-start(), calls=%async_computation.11 | async-start | bytes 15728640 | tf_op jit(solution)/shard_map/reduce_scatter | solution.py:46
  401.9 271.8 %all-gather.24.cloned.1.call-start = ((), (), s32[]{:S(2)}) async-start(), calls=%async_computation.13 | async-start | bytes 10616832 | tf_op jit(solution)/shard_map/all_gather | solution.py:168
  402.5 388.7 %all-gather.22.cloned.1.call-start = ((), (), s32[]{:S(2)}) async-start(), calls=%async_computation.12 | async-start | bytes 7864320 | tf_op jit(solution)/shard_map/all_gather | solution.py:39
  402.7 213.3 %copy-start.79 = (f32[1536]{0:T(1024)}, f32[1536]{0:T(1024)S(1)}, u32[]{:S(2)}) copy-start(f32[1536]{0:T(1024)S(1)} %get-tuple-element.160) | copy-start | bytes 18436
  402.7 1136.7 %copy-start.72 = (f32[1536]{0:T(1024)}, f32[1536]{0:T(1024)S(1)}, u32[]{:S(2)}) copy-start(f32[1536]{0:T(1024)S(1)} %get-tuple-element.159) | copy-start | bytes 18436
  402.8 213.6 %copy-start.96 = (f32[1,512]{1,0:T(1,128)}, f32[1,512]{1,0:T(1,128)S(1)}, u32[]{:S(2)}) copy-start(f32[1,512]{1,0:T(1,128)S(1)} %fusion.109) | copy-start | bytes 6148
  615.9 817.7 %copy-start.2 = (f32[512,1536]{1,0:T(8,128)}, f32[512,1536]{1,0:T(8,128)S(1)}, u32[]{:S(2)}) copy-start(f32[512,1536]{1,0:T(8,128)S(1)} %get-tuple-element.220) | copy-start | bytes 9437188
  625.4 224.9 %all-gather.26.cloned.1.call-start = ((), (), s32[]{:S(2)}) async-start(), calls=%async_computation.14 | async-start | bytes 10616832 | tf_op jit(solution)/shard_map/all_gather | solution.py:169
  626.1 341.7 %all-gather.28.cloned.1.call-start = ((), (), s32[]{:S(2)}) async-start(), calls=%async_computation.16 | async-start | bytes 7864320 | tf_op jit(solution)/shard_map/all_gather | solution.py:39
  626.9 591.5 %reduce-scatter.24.cloned.1.call-start = ((), (), s32[]{:S(2)}) async-start(), calls=%async_computation.17 | async-start | bytes 15728640 | tf_op jit(solution)/shard_map/reduce_scatter | solution.py:46
  628.2 379.9 %copy-start.110 = (f32[1536]{0:T(1024)}, f32[1536]{0:T(1024)S(1)}, u32[]{:S(2)}) copy-start(f32[1536]{0:T(1024)S(1)} %get-tuple-element.158) | copy-start | bytes 18436
  967.8 25.5 copy-start.125
  1008.1 425.5 %reduce-scatter.22.cloned.1.call-start = ((), (), s32[]{:S(2)}) async-start(), calls=%async_computation.15 | async-start | bytes 15728640 | tf_op jit(solution)/shard_map/reduce_scatter | solution.py:46
  1026.4 675.2 %all-gather.30.cloned.1.call-start = ((), (), s32[]{:S(2)}) async-start(), calls=%async_computation.18 | async-start | bytes 7864320 | tf_op jit(solution)/shard_map/all_gather | solution.py:39
  1027.7 406.0 %copy-start.74 = (f32[1536]{0:T(1024)}, f32[1536]{0:T(1024)S(1)}, u32[]{:S(2)}) copy-start(f32[1536]{0:T(1024)S(1)} %get-tuple-element.156) | copy-start | bytes 18436
  1031.3 402.4 %copy-start.82 = (f32[512]{0:T(512)S(1)}, f32[512]{0:T(512)}, u32[]{:S(2)}) copy-start(f32[512]{0:T(512)} %copy-done.81) | copy-start | bytes 6148
  1031.3 402.4 %copy-start.90 = (f32[512]{0:T(512)S(1)}, f32[512]{0:T(512)}, u32[]{:S(2)}) copy-start(f32[512]{0:T(512)} %copy-done.89) | copy-start | bytes 6148
  1031.3 402.4 %copy-start.97 = (f32[1,512]{1,0:T(1,128)S(1)}, f32[1,512]{1,0:T(1,128)}, u32[]{:S(2)}) copy-start(f32[1,512]{1,0:T(1,128)} %copy-done.96) | copy-start | bytes 6148
  1443.9 87.9 %copy-start.123 = (s32[77]{0:T(128)S(1)}, s32[77]{0:T(128)}, u32[]{:S(2)}) copy-start(s32[77]{0:T(128)} %copy-done.122) | copy-start | bytes 928
  1443.9 95.4 %copy-start.21 = (f32[77,6,1536]{2,0,1:T(8,128)S(1)}, f32[77,6,1536]{2,0,1:T(8,128)}, u32[]{:S(2)}) copy-start(f32[77,6,1536]{2,0,1:T(8,128)} %copy-done.20) | copy-start | bytes 8515588
  1444.0 803.9 %reduce-scatter.26.cloned.1.call-start = ((), (), s32[]{:S(2)}) async-start(), calls=%async_computation.19 | async-start | bytes 15728640 | tf_op jit(solution)/shard_map/reduce_scatter | solution.py:46
  1521.3 15.0 collective-permute-start
  1532.6 146.1 %copy-start.117 = (f32[77]{0:T(128)}, f32[77]{0:T(128)S(1)}, u32[]{:S(2)}) copy-start(f32[77]{0:T(128)S(1)} %convolution_bitcast_fusion.12) | copy-start | bytes 928
  1540.7 138.1 %copy-start.15 = (f32[77,1536]{1,0:T(8,128)}, f32[77,1536]{1,0:T(8,128)S(1)}, u32[]{:S(2)}) copy-start(f32[77,1536]{1,0:T(8,128)S(1)} %get-tuple-element.218) | copy-start | bytes 1419268
  1540.7 138.0 %copy-start.105 = (f32[77]{0:T(128)}, f32[77]{0:T(128)S(1)}, u32[]{:S(2)}) copy-start(f32[77]{0:T(128)S(1)} %broadcast_multiply_fusion.10) | copy-start | bytes 928
  1540.9 137.8 %copy-start.115 = (f32[77]{0:T(128)}, f32[77]{0:T(128)S(1)}, u32[]{:S(2)}) copy-start(f32[77]{0:T(128)S(1)} %add_rsqrt_fusion.2) | copy-start | bytes 928
  1543.4 80.5 %copy-start.112 = (f32[1536]{0:T(1024)S(1)}, f32[1536]{0:T(1024)}, u32[]{:S(2)}) copy-start(f32[1536]{0:T(1024)} %get-tuple-element.157) | copy-start | bytes 18436
  1623.9 11.7 slice-start
  1669.2 4.7 collective-permute-start.2
  1698.3 9.8 copy-start.53
  1817.3 9.7 copy-start.1
  1817.3 9.7 copy-start.29
  1817.3 9.7 copy-start.31
  1930.8 9.7 copy-start.1
  1930.8 9.7 copy-start.29
  1930.8 9.7 copy-start.31
  1945.7 416.2 %copy-start.39 = (bf16[2,1024,384]{2,1,0:T(8,128)(2,1)}, bf16[2,1024,384]{2,1,0:T(8,128)(2,1)S(1)}, u32[]{:S(2)}) copy-start(bf16[2,1024,384]{2,1,0:T(8,128)(2,1)S(1)} %copy.102) | copy-start | bytes 4718596
  1969.4 440.7 %reduce-scatter.30.cloned.1.call-start = ((), (), s32[]{:S(2)}) async-start(), calls=%async_computation.22 | async-start | bytes 983040
  1997.7 157.9 %copy-start.111 = (f32[1536]{0:T(1024)S(1)}, f32[1536]{0:T(1024)}, u32[]{:S(2)}) copy-start(f32[1536]{0:T(1024)} %copy-done.110) | copy-start | bytes 18436
  2127.5 28.1 copy-start.60
  2127.5 46.9 %copy-start.59 = (f32[80,1536]{1,0:T(8,128)}, f32[80,1536]{1,0:T(8,128)S(1)}, u32[]{:S(2)}) copy-start(f32[80,1536]{1,0:T(8,128)S(1)} %get-tuple-element.203) | copy-start | bytes 1474564
  2128.3 46.2 %collective-permute-start.3 = (f32[9,1536]{1,0:T(8,128)S(1)}, f32[9,1536]{1,0:T(8,128)}, u32[]{:S(2)}, u32[]{:S(2)}) collective-permute-start(f32[9,1536]{1,0:T(8,128)S(1)} %slice.252), channel_id=1, source_target_pairs={{0,1},{1,2},{2,3},{4,5},{5,6},{6,7},{8,9},{9,10},{10,11},{12,13},{... | collective-permute-start | bytes 165896
  2151.2 26.3 collective-permute-start.1
  2185.2 66.6 %copy-start.5 = (bf16[512,1536]{1,0:T(8,128)(2,1)S(1)}, bf16[512,1536]{1,0:T(8,128)(2,1)}, u32[]{:S(2)}) copy-start(bf16[512,1536]{1,0:T(8,128)(2,1)} %param.20) | copy-start | bytes 4718596
  2185.2 66.6 %copy-start.77 = (f32[512]{0:T(512)S(1)}, f32[512]{0:T(512)}, u32[]{:S(2)}) copy-start(f32[512]{0:T(512)} %copy-done.76) | copy-start | bytes 6148
  2185.2 66.6 %copy-start.87 = (f32[512]{0:T(512)S(1)}, f32[512]{0:T(512)}, u32[]{:S(2)}) copy-start(f32[512]{0:T(512)} %copy-done.86) | copy-start | bytes 6148
  2295.2 284.7 %all-reduce.25.cloned.1.call-start = ((), (), s32[]{:S(2)}) async-start(), calls=%async_computation.25 | async-start | bytes 37748736
  2338.3 486.0 %all-reduce.29.cloned.1.call-start = ((), (), s32[]{:S(2)}) async-start(), calls=%async_computation.27 | async-start | bytes 37748736
  2409.5 540.9 %all-reduce.21.cloned.1.call-start = ((), (), s32[]{:S(2)}) async-start(), calls=%async_computation.20 | async-start | bytes 196608 | tf_op jit(solution)/shard_map/psum | solution.py:449
  2410.1 567.2 %reduce-scatter.32.cloned.1.call-start = ((), (), s32[]{:S(2)}) async-start(), calls=%async_computation.23 | async-start | bytes 983040
  2412.6 15.6 copy-start.85
  2428.2 893.4 %all-reduce.23.cloned.1.call-start = ((), (), s32[]{:S(2)}) async-start(), calls=%async_computation.24 | async-start | bytes 56623104
  2485.0 966.9 %reduce-scatter.28.cloned.1.call-start = ((), (), s32[]{:S(2)}) async-start(), calls=%async_computation.21 | async-start | bytes 21233664 | tf_op jit(solution)/shard_map/reduce_scatter | solution.py:430
  2510.2 74.1 %copy-start.93 = (f32[1536]{0:T(1024)S(1)}, f32[1536]{0:T(1024)}, u32[]{:S(2)}) copy-start(f32[1536]{0:T(1024)} %get-tuple-element.209) | copy-start | bytes 18436
  2510.3 1070.3 %all-reduce.27.cloned.1.call-start = ((), (), s32[]{:S(2)}) async-start(), calls=%async_computation.26 | async-start | bytes 196608 | tf_op jit(solution)/shard_map/psum | solution.py:449
  2512.9 71.4 %copy-start.68 = (f32[2,6144]{1,0:T(2,128)}, f32[2,6144]{1,0:T(2,128)S(1)}, u32[]{:S(2)}) copy-start(f32[2,6144]{1,0:T(2,128)S(1)} %maximum_dynamic-update-slice_fusion) | copy-start | bytes 147460
  (101 other events, 373.7 us)
Sparse Core Ops, SparseCore 0:
  9.9 81.4 all-gather.13
  93.3 48.8 all-gather.17
  144.4 115.3 all-gather.15
  261.5 27.2 all-gather.19
  402.1 209.9 reduce-scatter.19
  613.8 59.8 all-gather.23
  675.9 115.3 all-gather.21
  793.2 57.0 all-gather.25
  852.4 115.3 all-gather.27
  1008.2 210.0 reduce-scatter.23
  1220.7 212.8 reduce-scatter.21
  1444.1 177.1 all-gather.29
  1969.6 278.2 reduce-scatter.25
  2295.3 25.2 reduce-scatter.29
  2338.4 241.4 all-reduce.24
  2584.3 239.9 all-reduce.28
  2829.7 120.6 all-reduce.20
  2953.1 24.1 reduce-scatter.31
  2981.1 340.4 all-reduce.22
  3325.6 126.2 reduce-scatter.27
  3458.5 122.0 all-reduce.26
where the time goes:
time: 3610 us; the launch traced here: 3590 us
  waiting for transfers between devices  2220 us (61%)
  matrix products  487 us (13%)
  blocking collectives  360 us (10%)
  local copies, waits for them, and re-layouts  271 us (8%)
  other arithmetic  198 us (5%)
  starting transfers between devices  41.8 us (1%)
    unnamed x30, waiting for transfers between devices  677 us
    reduce_scatter x4, waiting for transfers between devices, sum_rows(): lax.psum_scatter(first_rows, 'tensor', scatter_dimension=0, tiled=True)  671 us
    all_gather x4, waiting for transfers between devices, gather_rows(): lax.all_gather(first_rows, 'tensor', axis=0, tiled=True)  333 us
    psum x2, waiting for transfers between devices, body(): lax.psum((ada_bias_part, qv_whole, proj_bias_part, up_whole, down_bias_pa...  241 us
    unnamed x3, blocking collectives  233 us
    reduce_scatter x1, waiting for transfers between devices, body(): lax.psum_scatter(up_grads, 'dp', scatter_dimension=1, tiled=True)  125 us
    all_gather x4, blocking collectives, gather_rows(): lax.all_gather(second_rows, 'tensor', axis=0, tiled=True)  114 us
    unnamed x281, local copies, waits for them, and re-layouts  95.1 us
  transfers between devices with their start and end apart: 25, of which 19 were waited for; matrix products, arithmetic and copies ran while one was open for 22% of the time, Pallas kernels for 0%

commit v1 on v0

v1 whole, which is shorter than its diff:
```python
import functools

import jax
import jax.numpy as jnp
from jax import lax
from jax.experimental import pallas as pl
from jax.experimental.pallas import tpu as pltpu
from jax.sharding import Mesh
from jax.sharding import PartitionSpec as P

HEAD_DIM = 64
SCALE = HEAD_DIM ** (-0.5)
BF = jnp.bfloat16
F32 = jnp.float32
NEG = -1e30


def swap(v, axis):
    return lax.ppermute(v, axis, [(0, 1), (1, 0)])


def gather_bits(v, axes):
    for axis in axes:
        other = swap(v, axis)
        first = lax.axis_index(axis) == 0
        v = jnp.concatenate([jnp.where(first, v, other), jnp.where(first, other, v)], 0)
    return v


def scatter_bits(v, axes):
    for axis in axes:
        first = lax.axis_index(axis) == 0
        half = v.shape[0] // 2
        low, high = v[:half], v[half:]
        v = jnp.where(first, low, high) + swap(jnp.where(first, high, low), axis)
    return v


def sum_bits(v, axes):
    for axis in axes:
        v = v + swap(v, axis)
    return v


def index_of(axes):
    out = 0
    for axis in axes:
        out = out * 2 + lax.axis_index(axis)
    return out


def nt(a, b):
    return lax.dot_general(a, b, (((1,), (1,)), ((), ())), preferred_element_type=F32)


def nn(a, b):
    return lax.dot_general(a, b, (((1,), (0,)), ((), ())), preferred_element_type=F32)


def tn(a, b):
    return lax.dot_general(a, b, (((0,), (0,)), ((), ())), preferred_element_type=F32)


def flat(ref, h):
    whole = ref[...]
    merged = whole.reshape(whole.shape[0] * whole.shape[2], whole.shape[3])
    return merged[:, h * HEAD_DIM : (h + 1) * HEAD_DIM]


def pad_key(position, padded, real):
    return lax.rem(position, padded) >= real


def attend_kernel(
    chunk, txt, qi, ki, vi, qt, kt, vt, oi, ot, lse_i, lse_t
):
    rows = qi.shape[2]
    per = rows // chunk
    tp = qt.shape[2]
    keys_i = [flat(ki, h) for h in range(2)]
    vals_i = [flat(vi, h) for h in range(2)]
    keys_t = [flat(kt, h) for h in range(2)]
    vals_t = [flat(vt, h) for h in range(2)]
    mask = jnp.where(
        pad_key(lax.broadcasted_iota(jnp.int32, (1, 2 * tp), 1), tp, txt), NEG, 0.0
    ).astype(F32)

    def one(q_pair):
        outs, logs = [], []
        for h in range(2):
            q = q_pair[:, h * HEAD_DIM : (h + 1) * HEAD_DIM] * jnp.asarray(SCALE, BF)
            s_i = nt(q, keys_i[h])
            s_t = nt(q, keys_t[h]) + mask
            top = jnp.maximum(
                jnp.max(s_i, axis=1, keepdims=True), jnp.max(s_t, axis=1, keepdims=True)
            )
            p_i = jnp.exp(s_i - top)
            p_t = jnp.exp(s_t - top)
            total = jnp.sum(p_i, axis=1, keepdims=True) + jnp.sum(p_t, axis=1, keepdims=True)
            inv = 1.0 / total
            o = nn((p_i * inv).astype(BF), vals_i[h]) + nn((p_t * inv).astype(BF), vals_t[h])
            outs.append(o.astype(BF))
            logs.append((top + jnp.log(total)).reshape(1, -1))
        return jnp.concatenate(outs, axis=1), logs

    def step(c, carry):
        z = c // per
        r = pl.multiple_of(lax.rem(c, per) * chunk, chunk)
        o, logs = one(qi[z, 0, pl.ds(r, chunk), :])
        oi[z, 0, pl.ds(r, chunk), :] = o
        for h in range(2):
            lse_i[0, 0, h, pl.ds(c, 1), :] = logs[h]
        return carry

    lax.fori_loop(0, 2 * per, step, 0)
    whole = qt[...]
    o, logs = one(whole.reshape(2 * tp, whole.shape[3]))
    ot[...] = o.reshape(2, 1, tp, o.shape[1])
    for h in range(2):
        lse_t[0, 0, h, 0:1, :] = logs[h]


def attend_back_kernel(
    chunk, txt, qi, ki, vi, qt, kt, vt, gi, gt, lse_i, lse_t, di, dt, dk_i, dv_i, dk_t, dv_t
):
    rows = qi.shape[2]
    per = rows // chunk
    tp = qt.shape[2]
    hp = pl.program_id(1)
    pairs = pl.num_programs(1)
    width = 2 * HEAD_DIM
    keys_i = [flat(ki, h) for h in range(2)]
    vals_i = [flat(vi, h) for h in range(2)]
    keys_t = [flat(kt, h) for h in range(2)]
    vals_t = [flat(vt, h) for h in range(2)]
    mask = jnp.where(
        pad_key(lax.broadcasted_iota(jnp.int32, (2 * tp, 1), 0), tp, txt), NEG, 0.0
    ).astype(F32)
    dk_i[...] = jnp.zeros_like(dk_i)
    dv_i[...] = jnp.zeros_like(dv_i)
    dk_t[...] = jnp.zeros_like(dk_t)
    dv_t[...] = jnp.zeros_like(dv_t)

    def one(q_pair, g_pair, logs):
        outs = []
        for h in range(2):
            cols = slice(h * HEAD_DIM, (h + 1) * HEAD_DIM)
            q = q_pair[:, cols] * jnp.asarray(SCALE, BF)
            g = g_pair[:, cols]
            p_i = jnp.exp(nt(keys_i[h], q) - logs[h])
            p_t = jnp.exp(nt(keys_t[h], q) + mask - logs[h])
            dp_i = nt(vals_i[h], g)
            dp_t = nt(vals_t[h], g)
            delta = jnp.sum(p_i * dp_i, axis=0, keepdims=True) + jnp.sum(
                p_t * dp_t, axis=0, keepdims=True
            )
            dv_i[h] += nn(p_i.astype(BF), g)
            dv_t[h] += nn(p_t.astype(BF), g)
            ds_i = (p_i * (dp_i - delta)).astype(BF)
            ds_t = (p_t * (dp_t - delta)).astype(BF)
            dk_i[h] += nn(ds_i, q)
            dk_t[h] += nn(ds_t, q)
            dq = tn(ds_i, keys_i[h]) + tn(ds_t, keys_t[h])
            outs.append((dq * SCALE).astype(BF))
        return jnp.concatenate(outs, axis=1)

    def cols_of(kind):
        return pl.ds(pl.multiple_of((kind * pairs + hp) * width, width), width)

    def step(c, carry):
        z = c // per
        r = pl.multiple_of(lax.rem(c, per) * chunk, chunk)
        logs = [lse_i[0, 0, h, pl.ds(c, 1), :] for h in range(2)]
        dq = one(qi[z, 0, pl.ds(r, chunk), :], gi[z, 0, pl.ds(r, chunk), :], logs)
        di[z, 0, pl.ds(r, chunk), cols_of(0)] = dq
        return carry

    lax.fori_loop(0, 2 * per, step, 0)
    q_all, g_all = qt[...], gt[...]
    logs = [lse_t[0, 0, h, 0:1, :] for h in range(2)]
    dq = one(q_all.reshape(2 * tp, width), g_all.reshape(2 * tp, width), logs)
    dt[:, :, :, cols_of(0)] = dq.reshape(2, 1, tp, width)
    for kind, img, text in ((1, dk_i, dk_t), (2, dv_i, dv_t)):
        both = jnp.concatenate([img[0].astype(BF), img[1].astype(BF)], axis=1)
        di[:, :, :, cols_of(kind)] = both.reshape(2, 1, rows, width)
        both = jnp.concatenate([text[0].astype(BF), text[1].astype(BF)], axis=1)
        dt[:, :, :, cols_of(kind)] = both.reshape(2, 1, tp, width)


def qkv_specs(rows, tp, pairs):
    width = 2 * HEAD_DIM

    def spec(length, kind):
        return pl.BlockSpec(
            (2, 1, length, width), lambda s, h, kind=kind: (0, s, 0, kind * pairs + h)
        )

    return [spec(rows, kind) for kind in range(3)] + [spec(tp, kind) for kind in range(3)]


def lse_specs(n_chunks, chunk, tp):
    return [
        pl.BlockSpec((1, 1, 2, n_chunks, chunk), lambda s, h: (s, h, 0, 0, 0)),
        pl.BlockSpec((1, 1, 2, 1, 2 * tp), lambda s, h: (s, h, 0, 0, 0)),
    ]


def attention(img, text, txt, chunk):
    slots, rows, tp = img.shape[1], img.shape[2], text.shape[2]
    columns = img.shape[3] // 3
    width = 2 * HEAD_DIM
    pairs = columns // width
    n_chunks = 2 * rows // chunk
    keys = 2 * (rows + tp)
    out_spec = lambda length: pl.BlockSpec((2, 1, length, width), lambda s, h: (0, s, 0, h))
    return pl.pallas_call(
        functools.partial(attend_kernel, chunk, txt),
        grid=(slots, pairs),
        in_specs=qkv_specs(rows, tp, pairs),
        out_specs=[out_spec(rows), out_spec(tp)] + lse_specs(n_chunks, chunk, tp),
        out_shape=[
            jax.ShapeDtypeStruct((2, slots, rows, columns), BF),
            jax.ShapeDtypeStruct((2, slots, tp, columns), BF),
            jax.ShapeDtypeStruct((slots, pairs, 2, n_chunks, chunk), F32),
            jax.ShapeDtypeStruct((slots, pairs, 2, 1, 2 * tp), F32),
        ],
        compiler_params=pltpu.CompilerParams(vmem_limit_bytes=40 * 2**20),
        cost_estimate=pl.CostEstimate(
            flops=16 * slots * pairs * keys * keys * HEAD_DIM,
            bytes_accessed=slots * keys * columns * 8,
            transcendentals=2 * slots * pairs * keys * keys,
        ),
        name="attend",
    )(img, img, img, text, text, text)


def attention_back(img, text, grad_img, grad_text, lse_i, lse_t, txt, chunk):
    slots, rows, tp = img.shape[1], img.shape[2], text.shape[2]
    columns = img.shape[3] // 3
    width = 2 * HEAD_DIM
    pairs = columns // width
    n_chunks = 2 * rows // chunk
    keys = 2 * (rows + tp)
    g_spec = lambda length: pl.BlockSpec((2, 1, length, width), lambda s, h: (0, s, 0, h))
    d_spec = lambda length: pl.BlockSpec((2, 1, length, 3 * columns), lambda s, h: (0, s, 0, 0))
    return pl.pallas_call(
        functools.partial(attend_back_kernel, chunk, txt),
        grid=(slots, pairs),
        in_specs=qkv_specs(rows, tp, pairs)
        + [g_spec(rows), g_spec(tp)]
        + lse_specs(n_chunks, chunk, tp),
        out_specs=[d_spec(rows), d_spec(tp)],
        out_shape=[
            jax.ShapeDtypeStruct(img.shape, BF),
            jax.ShapeDtypeStruct(text.shape, BF),
        ],
        scratch_shapes=[
            pltpu.VMEM((2, 2 * rows, HEAD_DIM), F32),
            pltpu.VMEM((2, 2 * rows, HEAD_DIM), F32),
            pltpu.VMEM((2, 2 * tp, HEAD_DIM), F32),
            pltpu.VMEM((2, 2 * tp, HEAD_DIM), F32),
        ],
        compiler_params=pltpu.CompilerParams(vmem_limit_bytes=48 * 2**20),
        cost_estimate=pl.CostEstimate(
            flops=40 * slots * pairs * keys * keys * HEAD_DIM,
            bytes_accessed=slots * keys * columns * 16,
            transcendentals=2 * slots * pairs * keys * keys,
        ),
        name="attend_back",
    )(img, img, img, text, text, text, grad_img, grad_text, lse_i, lse_t)


class Layout:
    def __init__(self, dp_size, tensor_size):
        dp_bits = dp_size.bit_length() - 1
        t_bits = tensor_size.bit_length() - 1
        self.dp = tuple(f"d{i}" for i in range(dp_bits))
        self.tensor = tuple(f"t{i}" for i in range(t_bits))
        self.names = self.dp + self.tensor
        self.compact = dp_size == 8 and tensor_size == 4
        self.p = self.tensor[-1]
        if self.compact:
            self.y, self.x, self.q = self.dp
            self.zh = self.tensor[0]
            self.upper = ()
        else:
            self.q = self.tensor[-2]
            self.upper = self.tensor[:-2]
        self.rest = tuple(n for n in self.names if n not in (self.p, self.q))

    def my_columns(self, v):
        shards = 2 ** len(self.upper)
        part = v.shape[-1] // (4 * shards)
        v = v.reshape(v.shape[:-1] + (shards, 4, part))
        at = index_of((self.q, self.p))
        v = lax.dynamic_index_in_dim(v, at, v.ndim - 2, keepdims=False)
        return v.reshape(v.shape[:-2] + (shards * part,))

    def all_columns(self, v):
        shards = 2 ** len(self.upper)
        g = gather_bits(v[None], (self.p, self.q))
        g = g.reshape((4,) + v.shape[:-1] + (shards, v.shape[-1] // shards))
        g = jnp.moveaxis(g, 0, -2)
        return g.reshape(v.shape[:-1] + (4 * v.shape[-1],))

    def gather_rows(self, own):
        pair = swap(own, self.p)
        return jnp.concatenate([own, swap(own, self.q), pair, swap(pair, self.q)], 0)

    def sum_rows(self, product, factor):
        block = factor.shape[0] // 4
        far = product(factor[2 * block :])
        far = far[:block] + swap(far[block:].astype(BF), self.q).astype(F32)
        far = swap(far.astype(BF), self.p)
        near = product(factor[: 2 * block])
        near = near[:block] + swap(near[block:].astype(BF), self.q).astype(F32)
        return near + far.astype(F32)

    def gather_weight(self, w):
        two, part, kinds, columns = w.shape
        if not self.compact:
            w = lax.all_gather(w, self.dp, axis=1, tiled=True)
            if self.upper:
                w = lax.all_gather(w, self.upper, axis=3, tiled=True)
            return w.reshape(2, w.shape[1], -1)
        w = w.reshape(2, part, kinds * columns)
        joint = (self.q, self.zh)
        same = lax.axis_index(self.zh) == lax.axis_index(self.q)
        cross = lax.ppermute(w, joint, [(1, 2), (2, 1)])
        second = lax.ppermute(w, joint, [(0, 1), (3, 2), (2, 0), (1, 3)])
        first = jnp.where(same, w, cross)
        low = lax.axis_index(self.zh) == 0
        own = jnp.concatenate(
            [jnp.where(low, first, second), jnp.where(low, second, first)], axis=1
        )
        x, y = lax.axis_index(self.x), lax.axis_index(self.y)
        results = []
        for stream, (near_axis, far_axis) in enumerate(((self.x, self.y), (self.y, self.x))):
            mine = own[stream]
            near = swap(mine, near_axis)
            far, both = swap(mine, far_axis), swap(near, far_axis)
            dx, dy = (near, far) if stream == 0 else (far, near)
            whole = jnp.zeros((4,) + mine.shape, BF)
            for block, at in (
                (mine, 2 * y + x),
                (dx, 2 * y + 1 - x),
                (dy, 2 * (1 - y) + x),
                (both, 2 * (1 - y) + 1 - x),
            ):
                whole = lax.dynamic_update_index_in_dim(whole, block, at, 0)
            results.append(whole.reshape(-1, kinds * columns))
        return results

    def scatter_grad(self, grads, kinds):
        if not self.compact:
            d = grads[0].shape[0]
            g = jnp.stack(grads).astype(F32).reshape(2, d, kinds, -1)
            g = lax.psum_scatter(g, self.dp, scatter_dimension=1, tiled=True)
            if self.upper:
                g = lax.psum_scatter(g, self.upper, scatter_dimension=3, tiled=True)
            return g
        x, y = lax.axis_index(self.x), lax.axis_index(self.y)
        done = []
        for stream in range(2):
            g = grads[stream]
            n = g.shape[1]
            g = g.reshape(2, 2, -1, n)
            first = (self.x, x, 1, self.y, y) if stream == 0 else (self.y, y, 0, self.x, x)
            near_axis, near, dim, far_axis, far = first
            pick = lambda v, i, dim: lax.dynamic_index_in_dim(v, i, dim, keepdims=False)
            send = pick(g, 1 - near, dim).astype(BF)
            g = pick(g, near, dim).astype(F32) + swap(send, near_axis).astype(F32)
            g = pick(g, far, 0) + swap(pick(g, 1 - far, 0).astype(BF), far_axis).astype(F32)
            done.append(g)
        g = jnp.stack(done).reshape(2, 2, -1, n)
        zh = lax.axis_index(self.zh)
        joint = (self.q, self.zh)
        first = lax.dynamic_index_in_dim(g, zh, 1, keepdims=False)
        second = lax.dynamic_index_in_dim(g, 1 - zh, 1, keepdims=False)
        cross = lax.ppermute(first.astype(BF), joint, [(1, 2), (2, 1)])
        second = lax.ppermute(second.astype(BF), joint, [(1, 0), (2, 3), (0, 2), (3, 1)])
        same = zh == lax.axis_index(self.q)
        total = jnp.where(same, first, cross.astype(F32)) + second.astype(F32)
        return total.reshape(2, total.shape[1], kinds, -1)


def norm_parts(values):
    average = jnp.mean(values, axis=-1, keepdims=True)
    centred = values - average
    variance = jnp.mean(centred * centred, axis=-1, keepdims=True)
    inverse = lax.rsqrt(variance + 1e-06)
    return centred * inverse, inverse


def norm_back(normed, inverse, grad_in):
    first_mean = jnp.mean(grad_in, axis=-1, keepdims=True)
    cross_mean = jnp.mean(grad_in * normed, axis=-1, keepdims=True)
    return inverse * (grad_in - first_mean - normed * cross_mean)


def dot32(a, b):
    return jnp.dot(a, b, preferred_element_type=F32)


def dot_nt(a, b):
    return jnp.einsum("ij,kj->ik", a, b, preferred_element_type=F32)


def dot_tn(a, b):
    return jnp.einsum("ri,rj->ij", a, b, preferred_element_type=F32)


def gelu_slope(v):
    c = 0.7978845608028654
    inner = jnp.tanh(c * (v + 0.044715 * (v * v * v)))
    return 0.5 * (1.0 + inner) + 0.5 * v * (1.0 - inner * inner) * (
        c * (1.0 + 3 * 0.044715 * (v * v))
    )


def body(
    lay,
    image_in,
    text_in,
    condition,
    live_slots,
    ada_weight,
    ada_bias,
    qkv_weight,
    qv_bias,
    proj_weight,
    proj_bias,
    up_weight,
    up_bias,
    down_weight,
    down_bias,
    image_grad,
    text_grad,
):
    streams = range(2)
    width = image_in.shape[1]
    part = qkv_weight.shape[2]
    columns = qkv_weight.shape[3]
    img_rows, txt_rows = image_in.shape[0], text_in.shape[0]
    txt_pad = -(-txt_rows // 16) * 16
    group_slots = condition.shape[0]
    dp_index, t_index = index_of(lay.dp), index_of(lay.tensor)
    t_count = 2 ** len(lay.tensor)
    assert group_slots * 2 == t_count
    my_slot = t_index // 2
    dp_up, t_up = lay.dp[::-1], lay.tensor[::-1]

    def pad(v):
        return jnp.pad(v, ((0, txt_pad - txt_rows), (0, 0)))

    qkv_full = lay.gather_weight(jnp.swapaxes(qkv_weight, 1, 2))
    proj_full = lay.gather_weight(jnp.swapaxes(proj_weight, 1, 2)[:, :, None])
    up_full = lay.gather_weight(up_weight[:, :, None])
    down_full = lay.gather_weight(jnp.swapaxes(down_weight, 1, 2)[:, :, None])

    cond_all = gather_bits(condition, dp_up).astype(F32)
    silu_all = jax.nn.silu(cond_all).astype(BF)
    silu_mine = lax.dynamic_slice_in_dim(silu_all, dp_index * part, part, 1)
    mod = jnp.einsum("sd,tdkc->stkc", silu_mine, ada_weight, preferred_element_type=F32)
    mod = scatter_bits(mod, lay.dp)
    mod = gather_bits(mod[None], t_up)
    mod = lax.dynamic_index_in_dim(mod, my_slot, 1, keepdims=False)
    mod = jnp.moveaxis(mod, 0, 2).reshape(2, 6, width) + ada_bias.astype(F32)
    live = lax.dynamic_index_in_dim(live_slots, my_slot, 0, keepdims=False).astype(F32)

    inputs = (image_in.astype(F32), pad(text_in).astype(F32))
    grad_out = [live * g.astype(F32) for g in (image_grad, pad(text_grad))]
    grad_two = [(mod[s, 5] * grad_out[s]).astype(BF) for s in streams]

    first_norm = [norm_parts(inputs[s]) for s in streams]
    first_hidden = [
        (first_norm[s][0] * (1.0 + mod[s, 1]) + mod[s, 0]).astype(BF) for s in streams
    ]
    first_full = [lay.gather_rows(v) for v in first_hidden]
    qv = lay.my_columns(qv_bias.astype(F32))
    qkv_bias = jnp.concatenate([qv[:, 0], jnp.zeros_like(qv[:, 0]), qv[:, 1]], axis=1)
    qkv = [
        (dot32(first_full[s], qkv_full[s]) + qkv_bias[s])
        .astype(BF)
        .reshape(2, 2, first_hidden[s].shape[0], -1)
        for s in streams
    ]
    chunk = min(256, img_rows)
    heads_img, heads_txt, lse_i, lse_t = attention(qkv[0], qkv[1], txt_rows, chunk)
    heads_out = [v.reshape(-1, v.shape[3]) for v in (heads_img, heads_txt)]

    branch_one = [
        lay.sum_rows(lambda v, s=s: dot_nt(v, proj_full[s]), heads_out[s])
        + proj_bias[s].astype(F32)
        for s in streams
    ]
    middle = [inputs[s] + mod[s, 2] * branch_one[s] for s in streams]
    second_norm = [norm_parts(middle[s]) for s in streams]
    second_hidden = [
        (second_norm[s][0] * (1.0 + mod[s, 4]) + mod[s, 3]).astype(BF) for s in streams
    ]
    second_full = [lay.gather_rows(v) for v in second_hidden]
    grad_two_full = [lay.gather_rows(v) for v in grad_two]
    up_mine = lay.my_columns(up_bias.astype(F32))
    inner = [dot32(second_full[s], up_full[s]) + up_mine[s] for s in streams]
    activated = [jax.nn.gelu(v, approximate=True).astype(BF) for v in inner]
    branch_two = [
        lay.sum_rows(lambda v, s=s: dot_nt(v, down_full[s]), activated[s])
        + down_bias[s].astype(F32)
        for s in streams
    ]
    outputs = [(live * (middle[s] + mod[s, 5] * branch_two[s])).astype(BF) for s in streams]

    grad_inner = [
        (dot32(grad_two_full[s], down_full[s]) * gelu_slope(inner[s])).astype(BF) for s in streams
    ]
    grad_hidden_two = [
        lay.sum_rows(lambda v, s=s: dot_nt(v, up_full[s]), grad_inner[s]) for s in streams
    ]
    down_grads = [dot_tn(grad_two_full[s], activated[s]).astype(BF) for s in streams]
    up_grads = [dot_tn(second_full[s], grad_inner[s]).astype(BF) for s in streams]
    down_grad = jnp.swapaxes(lay.scatter_grad(down_grads, 1)[:, :, 0], 1, 2)
    up_grad = lay.scatter_grad(up_grads, 1)[:, :, 0]
    grad_middle = [
        grad_out[s]
        + norm_back(
            second_norm[s][0], second_norm[s][1], grad_hidden_two[s] * (1.0 + mod[s, 4])
        )
        for s in streams
    ]
    grad_one = [(mod[s, 2] * grad_middle[s]).astype(BF) for s in streams]
    grad_one_full = [lay.gather_rows(v) for v in grad_one]
    grad_heads = [dot32(grad_one_full[s], proj_full[s]).astype(BF) for s in streams]
    proj_grads = [dot_tn(grad_one_full[s], heads_out[s]).astype(BF) for s in streams]
    proj_grad = jnp.swapaxes(lay.scatter_grad(proj_grads, 1)[:, :, 0], 1, 2)
    grad_qkv = attention_back(
        qkv[0],
        qkv[1],
        grad_heads[0].reshape(heads_img.shape),
        grad_heads[1].reshape(heads_txt.shape),
        lse_i,
        lse_t,
        txt_rows,
        chunk,
    )
    grad_qkv = [v.reshape(-1, v.shape[3]) for v in grad_qkv]
    grad_hidden_one = [
        lay.sum_rows(lambda v, s=s: dot_nt(v, qkv_full[s]), grad_qkv[s]) for s in streams
    ]
    qkv_grads = [dot_tn(first_full[s], grad_qkv[s]).astype(BF) for s in streams]
    qkv_grad = jnp.swapaxes(lay.scatter_grad(qkv_grads, 3), 1, 2)
    input_grads = [
        grad_middle[s]
        + norm_back(first_norm[s][0], first_norm[s][1], grad_hidden_one[s] * (1.0 + mod[s, 1]))
        for s in streams
    ]

    total = lambda v: jnp.sum(v, axis=0)
    grad_mod = jnp.stack(
        [
            jnp.stack(
                [
                    total(grad_hidden_one[s]),
                    total(grad_hidden_one[s] * first_norm[s][0]),
                    total(branch_one[s] * grad_middle[s]),
                    total(grad_hidden_two[s]),
                    total(grad_hidden_two[s] * second_norm[s][0]),
                    total(branch_two[s] * grad_out[s]),
                ]
            )
            for s in streams
        ]
    )
    grad_mod = sum_bits(grad_mod, (lay.p,))
    grad_mod = gather_bits(grad_mod[None], t_up[1:])
    grad_mod = lax.dynamic_slice_in_dim(grad_mod, t_index * columns, columns, 3)
    grad_mod = gather_bits(grad_mod, dp_up)
    high = lax.Precision.HIGHEST
    ada_grad = jnp.einsum("sd,stkc->tdkc", silu_mine.astype(F32), grad_mod, precision=high)
    cond_terms = jnp.einsum("stkc,tdkc->sd", grad_mod, ada_weight.astype(F32), precision=high)
    cond_terms = gather_bits(sum_bits(cond_terms, t_up)[None], dp_up)
    cond_terms = lax.dynamic_slice_in_dim(cond_terms, dp_index * group_slots, group_slots, 1)
    cond_terms = jnp.swapaxes(cond_terms, 0, 1).reshape(group_slots, width)
    cond_terms = lax.dynamic_slice_in_dim(cond_terms, t_index * columns, columns, 1)
    cond_slice = lax.dynamic_slice_in_dim(condition.astype(F32), t_index * columns, columns, 1)
    unused, silu_pull = jax.vjp(jax.nn.silu, cond_slice)
    condition_grad = silu_pull(cond_terms)[0]
    ada_bias_grad = gather_bits(jnp.sum(grad_mod, axis=0)[None], t_up)
    ada_bias_grad = jnp.moveaxis(ada_bias_grad, 0, 2).reshape(2, 6, width)

    proj_bias_part = jnp.stack([total(grad_one[s].astype(F32)) for s in streams])
    down_bias_part = jnp.stack([total(grad_two[s].astype(F32)) for s in streams])
    own_part = sum_bits(jnp.stack([proj_bias_part, down_bias_part]), (lay.p, lay.q))
    heads = grad_qkv[0].shape[1] // 3
    qv_part = jnp.stack(
        [
            jnp.stack([total(grad_qkv[s][:, k * heads : (k + 1) * heads].astype(F32)) for k in (0, 2)])
            for s in streams
        ]
    )
    up_part = jnp.stack([total(grad_inner[s].astype(F32)) for s in streams])
    packed = jnp.concatenate([qv_part.reshape(-1), up_part.reshape(-1), own_part.reshape(-1)])
    packed = sum_bits(packed.reshape(-1, 128), lay.rest).reshape(-1)
    cut_one, cut_two = qv_part.size, qv_part.size + up_part.size
    qv_bias_grad = lay.all_columns(packed[:cut_one].reshape(qv_part.shape))
    up_bias_grad = lay.all_columns(packed[cut_one:cut_two].reshape(up_part.shape))
    own_part = packed[cut_two:].reshape(own_part.shape)
    return (
        outputs[0],
        outputs[1][:txt_rows],
        input_grads[0],
        input_grads[1][:txt_rows],
        condition_grad,
        ada_grad,
        ada_bias_grad,
        qkv_grad,
        qv_bias_grad,
        proj_grad,
        own_part[0],
        up_grad,
        up_bias_grad,
        down_grad,
        own_part[1],
    )


def solution(mesh):
    lay = Layout(mesh.shape["dp"], mesh.shape["tensor"])
    bits = Mesh(mesh.devices.reshape((2,) * len(lay.names)), lay.names)
    dp, tensor, every = lay.dp, lay.tensor, lay.names
    in_specs = (
        P(every, None),
        P(every, None),
        P(dp, None),
        P(dp),
        P(None, dp, None, tensor),
        P(),
        P(None, None, dp, tensor),
        P(),
        P(None, tensor, dp),
        P(),
        P(None, dp, tensor),
        P(),
        P(None, tensor, dp),
        P(),
        P(every, None),
        P(every, None),
    )
    out_specs = (
        P(every, None),
        P(every, None),
        P(every, None),
        P(every, None),
        P(dp, tensor),
        P(None, dp, None, tensor),
        P(),
        P(None, None, dp, tensor),
        P(),
        P(None, tensor, dp),
        P(),
        P(None, dp, tensor),
        P(),
        P(None, tensor, dp),
        P(),
    )
    return jax.shard_map(
        functools.partial(body, lay), mesh=bits, in_specs=in_specs, out_specs=out_specs, check_vma=False
    )
```

time: 3610 us -> 1360 us (0.38)
  waiting for transfers between devices: 2220 us -> 595 us
  blocking collectives: 360 us -> 0 us
  matrix products: 487 us -> 192 us
  starting transfers between devices: 41.8 us -> 258 us
  local copies, waits for them, and re-layouts: 271 us -> 77.6 us
  Pallas kernels: 0 us -> 125 us
  other arithmetic: 198 us -> 104 us
    reduce_scatter x5 -> x0, waiting for transfers between devices: 796 us -> none  [the longest x4 671 us: sum_rows(): lax.psum_scatter(first_rows, 'tensor', scatter_dimension=0, tiled=True)]
    unnamed x30 -> x0, waiting for transfers between devices: 677 us -> none
    ppermute x0 -> x133, waiting for transfers between devices: none -> 595 us  [the longest x117 481 us: swap(): return lax.ppermute(v, axis, [(0, 1), (1, 0)])]
    all_gather x9 -> x0, waiting for transfers between devices: 503 us -> none  [the longest x4 333 us: gather_rows(): lax.all_gather(first_rows, 'tensor', axis=0, tiled=True)]
    dot_general x47 -> x35, matrix products: 487 us -> 192 us  [the longest x8 73 us: dot32(): return jnp.dot(a, b, preferred_element_type=F32)]
    ppermute x0 -> x133, starting transfers between devices: none -> 258 us  [the longest x117 211 us: swap(): return lax.ppermute(v, axis, [(0, 1), (1, 0)])]
    psum x2 -> x0, waiting for transfers between devices: 241 us -> none  [body(): lax.psum((ada_bias_part, qv_whole, proj_bias_part, up_whole, down_bias_pa...]
    unnamed x3 -> x0, blocking collectives: 233 us -> none
  transfers between devices with their start and end apart: 25 -> 133, of which waited for: 19 -> 52; matrix products, arithmetic and copies ran while one was open for 22% -> 21% of each run, Pallas kernels for 0% -> 4%
where the time goes in v1:
time: 1360 us
  waiting for transfers between devices  595 us (44%)
  starting transfers between devices  258 us (19%)
  matrix products  192 us (14%)
  Pallas kernels  125 us (9%)
  other arithmetic  104 us (8%)
  local copies, waits for them, and re-layouts  77.6 us (6%)
    ppermute x117, waiting for transfers between devices, swap(): return lax.ppermute(v, axis, [(0, 1), (1, 0)])  481 us
    ppermute x117, starting transfers between devices, swap(): return lax.ppermute(v, axis, [(0, 1), (1, 0)])  211 us
    ppermute x4, waiting for transfers between devices, scatter_grad(): lax.ppermute(second.astype(BF), joint, [(1, 0), (2, 3), (0, 2), (3, 1)])  94.8 us
    dot_general x8, matrix products, dot32(): return jnp.dot(a, b, preferred_element_type=F32)  73 us
    pallas_call x1, Pallas kernels, attention_back(): pl.pallas_call(functools.partial(attend_back_kernel, chunk, txt), grid=(s...  71.2 us
    dot_general x16, matrix products, dot_nt(): return jnp.einsum('ij,kj->ik', a, b, preferred_element_type=F32)  58 us
    dot_general x8, matrix products, dot_tn(): return jnp.einsum('ri,rj->ij', a, b, preferred_element_type=F32)  55.1 us
    pallas_call x1, Pallas kernels, attention(): pl.pallas_call(functools.partial(attend_kernel, chunk, txt), grid=(slots,...  53.6 us
  transfers between devices with their start and end apart: 133, of which 52 were waited for; matrix products, arithmetic and copies ran while one was open for 21% of the time, Pallas kernels for 4%

profile of v1, /device:TPU:0, one launch (start us, length us, event | category | flops | bytes accessed | tf_op | source)
XLA Modules:
  0.0 1356.1 jit_solution(4565490527229626045)
XLA Ops:
  0.7 4.1 collective-permute-start.23
  43.1 10.2 collective-permute-done.6
  53.6 19.7 %collective-permute-done.7 = f32[2,2,2,6,384]{4,1,3,2,0:T(2,128)S(1)} collective-permute-done((f32[2,2,2,6,384]{4,1,3,2,0:T(2,128)S(1)}, f32[2,2,2,6,384]{4,1,3,2,0:T(2,128)S(1)}, u32[]{:S(2)}, u32[]{:S(2)}) %collective-permute-start.7) | collective-permute-done | bytes 73760 | tf_op jit(solution)/shard_map/ppermute | solution.py:19
  82.0 4.5 collective-permute-done.47
  97.3 16.9 %collective-permute-start.34 = (bf16[2,192,1536]{2,1,0:T(8,128)(2,1)S(1)}, bf16[2,192,1536]{2,1,0:T(8,128)(2,1)S(1)}, u32[]{:S(2)}, u32[]{:S(2)}) collective-permute-start(bf16[2,192,1536]{2,1,0:T(8,128)(2,1)S(1)} %copy-done.65), channel_id=1, source_target_pairs={{0,2},{6,4},{4,0},{2,6},{1,3},{7,5},{5,1},{3,7},{8,10},{14,12},{12... | collective-permute-start | bytes 3538952 | tf_op jit(solution)/shard_map/ppermute | solution.py:330
  121.4 19.2 %collective-permute-done.34 = bf16[2,192,1536]{2,1,0:T(8,128)(2,1)S(1)} collective-permute-done((bf16[2,192,1536]{2,1,0:T(8,128)(2,1)S(1)}, bf16[2,192,1536]{2,1,0:T(8,128)(2,1)S(1)}, u32[]{:S(2)}, u32[]{:S(2)}) %collective-permute-start.34) | collective-permute-done | bytes 1179680 | tf_op jit(solution)/shard_map/ppermute | solution.py:330
  150.9 8.3 collective-permute-done.13
  161.4 10.4 collective-permute-done.58
  172.4 10.1 collective-permute-done.59
  185.9 21.3 %collective-permute-done.41 = bf16[384,1536]{1,0:T(8,128)(2,1)S(1)} collective-permute-done((bf16[384,1536]{1,0:T(8,128)(2,1)S(1)}, bf16[384,1536]{1,0:T(8,128)(2,1)S(1)}, u32[]{:S(2)}, u32[]{:S(2)}) %collective-permute-start.41) | collective-permute-done | bytes 1179680 | tf_op jit(solution)/shard_map/ppermute | solution.py:19
  209.3 51.1 %collective-permute-start.9 = (bf16[512,1536]{1,0:T(8,128)(2,1)S(1)}, bf16[512,1536]{1,0:T(8,128)(2,1)S(1)}, u32[]{:S(2)}, u32[]{:S(2)}) collective-permute-start(bf16[512,1536]{1,0:T(8,128)(2,1)S(1)} %fusion.17), channel_id=1, source_target_pairs={{0,1},{1,0},{2,3},{3,2},{4,5},{5,4},{6,7},{7,6},{8,9},{9,8},{10,11... | collective-permute-start | bytes 4718600 | tf_op jit(solution)/shard_map/ppermute | solution.py:19
  260.4 31.1 %collective-permute-start.18 = (bf16[80,1536]{1,0:T(8,128)(2,1)S(1)}, bf16[80,1536]{1,0:T(8,128)(2,1)S(1)}, u32[]{:S(2)}, u32[]{:S(2)}) collective-permute-start(bf16[80,1536]{1,0:T(8,128)(2,1)S(1)} %collective-permute-done.17), channel_id=1, source_target_pairs={{0,4},{4,0},{1,5},{5,1},{2,6},{6,2},{3,7},{7,3},{8,12},{12,8},{9,1... | collective-permute-start | bytes 737288 | tf_op jit(solution)/shard_map/ppermute | solution.py:19
  293.6 19.9 %collective-permute-done.21 = bf16[384,1152]{1,0:T(8,128)(2,1)S(1)} collective-permute-done((bf16[384,1152]{1,0:T(8,128)(2,1)}, bf16[384,1152]{1,0:T(8,128)(2,1)S(1)}, u32[]{:S(2)}, u32[]{:S(2)}) %collective-permute-start.21) | collective-permute-done | bytes 884768 | tf_op jit(solution)/shard_map/ppermute | solution.py:19
  319.1 23.3 %collective-permute-done.60 = bf16[384,1536]{1,0:T(8,128)(2,1)S(1)} collective-permute-done((bf16[384,1536]{1,0:T(8,128)(2,1)S(1)}, bf16[384,1536]{1,0:T(8,128)(2,1)S(1)}, u32[]{:S(2)}, u32[]{:S(2)}) %collective-permute-start.60) | collective-permute-done | bytes 1179680 | tf_op jit(solution)/shard_map/ppermute | solution.py:19
  344.2 14.8 %collective-permute-start.10 = (bf16[512,1536]{1,0:T(8,128)(2,1)S(1)}, bf16[512,1536]{1,0:T(8,128)(2,1)S(1)}, u32[]{:S(2)}, u32[]{:S(2)}) collective-permute-start(bf16[512,1536]{1,0:T(8,128)(2,1)S(1)} %collective-permute-done.9), channel_id=1, source_target_pairs={{0,4},{4,0},{1,5},{5,1},{2,6},{6,2},{3,7},{7,3},{8,12},{12,8},{9,1... | collective-permute-start | bytes 4718600 | tf_op jit(solution)/shard_map/ppermute | solution.py:19
  359.2 6.6 collective-permute-done.57
  365.9 9.6 collective-permute-start.65
  378.8 13.1 add_convert_fusion
  392.0 53.6 %attend.1 = (bf16[2,2,512,384]{3,2,1,0:T(8,128)(2,1)S(1)}, bf16[2,2,80,384]{3,2,1,0:T(8,128)(2,1)S(1)}, f32[2,3,2,4,256]{4,3,2,1,0:T(4,128)S(1)}, f32[2,3,2,1,160]{4,3,2,1,0:T(1,128)S(1)}) custom-call(bf16[2,2,512,1152]{3,2,1,0:T(8,128)(2,1)S(1)} %bitcast.344, bf16[2,2,512,1152]{3,2,1,0:T(8,128)(2,1)S(1)} %bitcast.345, ...), custom_call_target="tpu_custom_call" | custom-call | flops 8613003264 | bytes 7274496 | tf_op jit(solution)/shard_map/attend/pallas_call | solution.py:216
  450.8 6.1 collective-permute-done.51
  471.2 4.4 convert_reduce_fusion.6
  483.7 4.4 convolution_convert_fusion
  488.1 4.2 convolution_convert_fusion.1
  495.6 6.6 collective-permute-done.78
  504.0 5.6 collective-permute-done.63
  524.3 61.0 %collective-permute-done.115 = bf16[2,384,384]{2,1,0:T(8,128)(2,1)S(1)} collective-permute-done((bf16[2,384,384]{2,1,0:T(8,128)(2,1)S(1)}, bf16[2,384,384]{2,1,0:T(8,128)(2,1)S(1)}, u32[]{:S(2)}, u32[]{:S(2)}) %collective-permute-start.115) | collective-permute-done | bytes 589856 | tf_op jit(solution)/shard_map/ppermute | solution.py:19
  596.5 42.0 %collective-permute-done.121 = bf16[2,384,1536]{2,1,0:T(8,128)(2,1)} collective-permute-done((bf16[2,384,1536]{2,1,0:T(8,128)(2,1)}, bf16[2,384,1536]{2,1,0:T(8,128)(2,1)}, u32[]{:S(2)}, u32[]{:S(2)}) %collective-permute-start.121) | collective-permute-done | bytes 2359328 | tf_op jit(solution)/shard_map/ppermute | solution.py:19
  649.4 18.4 %collective-permute-done.122 = bf16[384,1536]{1,0:T(8,128)(2,1)S(1)} collective-permute-done((bf16[384,1536]{1,0:T(8,128)(2,1)S(1)}, bf16[384,1536]{1,0:T(8,128)(2,1)S(1)}, u32[]{:S(2)}, u32[]{:S(2)}) %collective-permute-start.122) | collective-permute-done | bytes 1179680 | tf_op jit(solution)/shard_map/ppermute | solution.py:19
  671.9 19.6 %multiply_convert_fusion = (bf16[2048,1536]{1,0:T(8,128)(2,1)}, f32[2048,1536]{1,0:T(8,128)}) fusion(f32[1536]{0:T(1024)S(1)} %copy-done.131, bf16[1536,1536]{1,0:T(8,128)(2,1)S(1)} %bitcast.407, bf16[512,1536]{1,0:T(8,128)(2,1)} %copy-done.145, bf16[512,1536]{1,0:T(8,128)(2,1)} %copy-done.143, bf16[512,1536]{1,0:T(8,128)(2,1)} %copy-done.144, ...), kind=kOutput, calls=%fused_computation.13 | convolution fusion | flops 9720299520 | bytes 29890560 | tf_op jit(solution)/shard_map/dot_general | solution.py:402
  691.5 24.6 %convert_reduce_fusion = (f32[1536]{0:T(1024)S(1)}, bf16[2048,1536]{1,0:T(8,128)(2,1)}) fusion(f32[2048,1536]{1,0:T(8,128)} %get-tuple-element.241, f32[1536]{0:T(1024)S(1)} %copy-done.131, bf16[1536,1536]{1,0:T(8,128)(2,1)} %bitcast.398, bf16[512,1536]{1,0:T(8,128)(2,1)} %collective-permute-done.66, bf16[512,1536]{1,0:T(8,128)(2,1)} %collective-permute-done.65, ...), kind=kOutput, calls=%fused_computation.12 | convolution fusion | flops 9754900480 | bytes 29896704 | tf_op jit(solution)/shard_map/dot_general | solution.py:402
  716.1 8.0 fusion.27
  724.2 11.6 fusion.30
  735.8 13.9 %convolution_convert_fusion.5 = bf16[1536,1536]{1,0:T(8,128)(2,1)S(1)} fusion(bf16[2048,1536]{1,0:T(8,128)(2,1)} %get-tuple-element.247, bf16[512,1536]{1,0:T(8,128)(2,1)} %copy-done.145, bf16[512,1536]{1,0:T(8,128)(2,1)} %copy-done.143, bf16[512,1536]{1,0:T(8,128)(2,1)} %copy-done.144, bf16[512,1536]{1,0:T(8,128)(2,1)S(1)} %copy-done.62), kind=kOutput, calls=%fused_computation.21 | convolution fusion | flops 9691201536 | bytes 17301504 | tf_op jit(solution)/shard_map/ri,rj->ij/dot_general | solution.py:410
  753.0 8.9 fusion.33
  761.8 14.2 %convolution_convert_fusion.4 = bf16[1536,1536]{1,0:T(8,128)(2,1)S(1)} fusion(bf16[2048,1536]{1,0:T(8,128)(2,1)} %get-tuple-element.240, bf16[512,1536]{1,0:T(8,128)(2,1)} %collective-permute-done.66, bf16[512,1536]{1,0:T(8,128)(2,1)} %collective-permute-done.65, bf16[512,1536]{1,0:T(8,128)(2,1)} %collective-permute-done.64, ...), kind=kOutput, calls=%fused_computation.20 | convolution fusion | flops 9691201536 | bytes 17301504 | tf_op jit(solution)/shard_map/ri,rj->ij/dot_general | solution.py:410
  781.4 6.9 fusion.37
  788.4 4.3 slice.754
  799.8 4.0 fusion.32
  810.5 42.6 %collective-permute-done.127 = bf16[2,384,1536]{2,1,0:T(8,128)(2,1)S(1)} collective-permute-done((bf16[2,384,1536]{2,1,0:T(8,128)(2,1)S(1)}, bf16[2,384,1536]{2,1,0:T(8,128)(2,1)S(1)}, u32[]{:S(2)}, u32[]{:S(2)}) %collective-permute-start.127) | collective-permute-done | bytes 2359328 | tf_op jit(solution)/shard_map/ppermute | solution.py:19
  859.4 3.9 multiply_reduce_fusion.1
  863.4 5.1 collective-permute-done.45
  868.5 6.4 multiply_reduce_fusion
  877.1 6.4 collective-permute-done.120
  886.7 9.5 collective-permute-start.107
  896.3 8.5 collective-permute-done.128
  909.2 9.0 collective-permute-start.132
  923.8 10.0 collective-permute-done.71
  934.5 39.2 %collective-permute-done.124 = bf16[2,192,1536]{2,1,0:T(8,128)(2,1)} collective-permute-done((bf16[2,192,1536]{2,1,0:T(8,128)(2,1)}, bf16[2,192,1536]{2,1,0:T(8,128)(2,1)}, u32[]{:S(2)}, u32[]{:S(2)}) %collective-permute-start.124) | collective-permute-done | bytes 1179680 | tf_op jit(solution)/shard_map/ppermute | solution.py:381
  973.7 3.9 convert_add_fusion.7
  977.6 21.4 %collective-permute-done.132 = bf16[2,192,1536]{2,1,0:T(8,128)(2,1)} collective-permute-done((bf16[2,192,1536]{2,1,0:T(8,128)(2,1)}, bf16[2,192,1536]{2,1,0:T(8,128)(2,1)}, u32[]{:S(2)}, u32[]{:S(2)}) %collective-permute-start.132) | collective-permute-done | bytes 1179680 | tf_op jit(solution)/shard_map/ppermute | solution.py:381
  1002.6 5.8 convolution_convert_fusion.8
  1008.5 71.2 %attend_back.1 = (bf16[2,2,512,1152]{3,2,1,0:T(8,128)(2,1)}, bf16[2,2,80,1152]{3,2,1,0:T(8,128)(2,1)S(1)}) custom-call(bf16[2,2,512,1152]{3,2,1,0:T(8,128)(2,1)} %bitcast.347, bf16[2,2,512,1152]{3,2,1,0:T(8,128)(2,1)} %bitcast.348, bf16[2,2,512,1152]{3,2,1,0:T(8,128)(2,1)} %bitcast.349, bf16[2,2,80,1152]{3,2,1,0:T(8,128)(2,1)S(1)} %bitcast.354, ...), custom_call_target="tpu_custom_call" | custom-call | flops 21532508160 | bytes 14548992 | tf_op jit(solution)/shard_map/attend_back/pallas_call | solution.py:246
  1079.9 5.2 fusion.178
  1087.0 6.2 convolution_convert_fusion.7
  1099.5 9.0 convolution_convert_fusion.3
  1112.5 4.2 fusion.189
  1116.8 4.2 fusion.188
  1124.6 26.8 %collective-permute-done.109 = f32[84,128]{1,0:T(8,128)S(1)} collective-permute-done((f32[84,128]{1,0:T(8,128)S(1)}, f32[84,128]{1,0:T(8,128)S(1)}, u32[]{:S(2)}, u32[]{:S(2)}) %collective-permute-start.109) | collective-permute-done | bytes 43040 | tf_op jit(solution)/shard_map/ppermute | solution.py:19
  1172.1 5.9 collective-permute-done.87
  1183.5 30.3 %collective-permute-done.114 = bf16[384,384]{1,0:T(8,128)(2,1)S(1)} collective-permute-done((bf16[384,384]{1,0:T(8,128)(2,1)S(1)}, bf16[384,384]{1,0:T(8,128)(2,1)S(1)}, u32[]{:S(2)}, u32[]{:S(2)}) %collective-permute-start.114) | collective-permute-done | bytes 294944 | tf_op jit(solution)/shard_map/ppermute | solution.py:19
  1233.3 30.6 %collective-permute-done.84 = bf16[512,1536]{1,0:T(8,128)(2,1)S(1)} collective-permute-done((bf16[512,1536]{1,0:T(8,128)(2,1)S(1)}, bf16[512,1536]{1,0:T(8,128)(2,1)S(1)}, u32[]{:S(2)}, u32[]{:S(2)}) %collective-permute-start.84) | collective-permute-done | bytes 1572896 | tf_op jit(solution)/shard_map/ppermute | solution.py:19
  1291.3 34.2 %collective-permute-done.105 = bf16[2,192,1152]{2,1,0:T(8,128)(2,1)S(1)} collective-permute-done((bf16[2,192,1152]{2,1,0:T(8,128)(2,1)S(1)}, bf16[2,192,1152]{2,1,0:T(8,128)(2,1)S(1)}, u32[]{:S(2)}, u32[]{:S(2)}) %collective-permute-start.105) | collective-permute-done | bytes 884768 | tf_op jit(solution)/shard_map/ppermute | solution.py:381
  1335.5 4.2 convolution_bitcast_fusion
  1339.8 4.6 collective-permute-done.94
  (870 shorter events, 326.1 us)
Async XLA Ops:
  0.7 37.6 %collective-permute-start.23 = (bf16[2,192,384]{2,1,0:T(8,128)(2,1)}, bf16[2,192,384]{2,1,0:T(8,128)(2,1)}, u32[]{:S(2)}, u32[]{:S(2)}) collective-permute-start(bf16[2,192,384]{2,1,0:T(8,128)(2,1)} %bitcast.440), channel_id=1, source_target_pairs={{0,2},{6,4},{4,0},{2,6},{1,3},{7,5},{5,1},{3,7},{8,10},{14,12},{12... | collective-permute-start | bytes 884744 | tf_op jit(solution)/shard_map/ppermute | solution.py:330
  4.8 33.6 %collective-permute-start.22 = (bf16[2,192,384]{2,1,0:T(8,128)(2,1)}, bf16[2,192,384]{2,1,0:T(8,128)(2,1)}, u32[]{:S(2)}, u32[]{:S(2)}) collective-permute-start(bf16[2,192,384]{2,1,0:T(8,128)(2,1)} %bitcast.441), channel_id=1, source_target_pairs={{2,4},{4,2},{3,5},{5,3},{10,12},{12,10},{11,13},{13,11},{18,20},{2... | collective-permute-start | bytes 884744 | tf_op jit(solution)/shard_map/ppermute | solution.py:329
  8.3 82.2 %collective-permute-start.12 = (bf16[2,192,1152]{2,1,0:T(8,128)(2,1)}, bf16[2,192,1152]{2,1,0:T(8,128)(2,1)}, u32[]{:S(2)}, u32[]{:S(2)}) collective-permute-start(bf16[2,192,1152]{2,1,0:T(8,128)(2,1)} %bitcast.164), channel_id=1, source_target_pairs={{0,2},{6,4},{4,0},{2,6},{1,3},{7,5},{5,1},{3,7},{8,10},{14,12},{12... | collective-permute-start | bytes 2654216 | tf_op jit(solution)/shard_map/ppermute | solution.py:330
  9.2 82.0 %collective-permute-start.11 = (bf16[2,192,1152]{2,1,0:T(8,128)(2,1)}, bf16[2,192,1152]{2,1,0:T(8,128)(2,1)}, u32[]{:S(2)}, u32[]{:S(2)}) collective-permute-start(bf16[2,192,1152]{2,1,0:T(8,128)(2,1)} %bitcast.164), channel_id=1, source_target_pairs={{2,4},{4,2},{3,5},{5,3},{10,12},{12,10},{11,13},{13,11},{18,20},{2... | collective-permute-start | bytes 2654216 | tf_op jit(solution)/shard_map/ppermute | solution.py:329
  35.9 82.6 %collective-permute-start.39 = (bf16[2,192,1536]{2,1,0:T(8,128)(2,1)}, bf16[2,192,1536]{2,1,0:T(8,128)(2,1)S(1)}, u32[]{:S(2)}, u32[]{:S(2)}) collective-permute-start(bf16[2,192,1536]{2,1,0:T(8,128)(2,1)} %bitcast.435), channel_id=1, source_target_pairs={{0,2},{6,4},{4,0},{2,6},{1,3},{7,5},{5,1},{3,7},{8,10},{14,12},{12... | collective-permute-start | bytes 3538952 | tf_op jit(solution)/shard_map/ppermute | solution.py:330
  41.5 38.3 %collective-permute-start.46 = (bf16[384,384]{1,0:T(8,128)(2,1)S(1)}, bf16[384,384]{1,0:T(8,128)(2,1)S(1)}, u32[]{:S(2)}, u32[]{:S(2)}) collective-permute-start(bf16[384,384]{1,0:T(8,128)(2,1)S(1)} %get-tuple-element.191), channel_id=1, source_target_pairs={{0,8},{8,0},{1,9},{9,1},{2,10},{10,2},{3,11},{11,3},{4,12},{12,4},... | collective-permute-start | bytes 884744 | tf_op jit(solution)/shard_map/ppermute | solution.py:19
  86.6 32.0 %collective-permute-start.38 = (bf16[2,192,1536]{2,1,0:T(8,128)(2,1)S(1)}, bf16[2,192,1536]{2,1,0:T(8,128)(2,1)S(1)}, u32[]{:S(2)}, u32[]{:S(2)}) collective-permute-start(bf16[2,192,1536]{2,1,0:T(8,128)(2,1)S(1)} %bitcast.436), channel_id=1, source_target_pairs={{2,4},{4,2},{3,5},{5,3},{10,12},{12,10},{11,13},{13,11},{18,20},{2... | collective-permute-start | bytes 3538952 | tf_op jit(solution)/shard_map/ppermute | solution.py:329
  97.3 43.3 %collective-permute-start.34 = (bf16[2,192,1536]{2,1,0:T(8,128)(2,1)S(1)}, bf16[2,192,1536]{2,1,0:T(8,128)(2,1)S(1)}, u32[]{:S(2)}, u32[]{:S(2)}) collective-permute-start(bf16[2,192,1536]{2,1,0:T(8,128)(2,1)S(1)} %copy-done.65), channel_id=1, source_target_pairs={{0,2},{6,4},{4,0},{2,6},{1,3},{7,5},{5,1},{3,7},{8,10},{14,12},{12... | collective-permute-start | bytes 3538952 | tf_op jit(solution)/shard_map/ppermute | solution.py:330
  114.2 95.1 %collective-permute-start.17 = (bf16[80,1536]{1,0:T(8,128)(2,1)S(1)}, bf16[80,1536]{1,0:T(8,128)(2,1)S(1)}, u32[]{:S(2)}, u32[]{:S(2)}) collective-permute-start(bf16[80,1536]{1,0:T(8,128)(2,1)S(1)} %add_convert_fusion.3), channel_id=1, source_target_pairs={{0,1},{1,0},{2,3},{3,2},{4,5},{5,4},{6,7},{7,6},{8,9},{9,8},{10,11... | collective-permute-start | bytes 737288 | tf_op jit(solution)/shard_map/ppermute | solution.py:19
  118.6 197.1 %collective-permute-start.16 = (bf16[80,1536]{1,0:T(8,128)(2,1)S(1)}, bf16[80,1536]{1,0:T(8,128)(2,1)S(1)}, u32[]{:S(2)}, u32[]{:S(2)}) collective-permute-start(bf16[80,1536]{1,0:T(8,128)(2,1)S(1)} %add_convert_fusion.3), channel_id=1, source_target_pairs={{0,4},{4,0},{1,5},{5,1},{2,6},{6,2},{3,7},{7,3},{8,12},{12,8},{9,1... | collective-permute-start | bytes 737288 | tf_op jit(solution)/shard_map/ppermute | solution.py:19
  171.8 35.4 %collective-permute-start.41 = (bf16[384,1536]{1,0:T(8,128)(2,1)S(1)}, bf16[384,1536]{1,0:T(8,128)(2,1)S(1)}, u32[]{:S(2)}, u32[]{:S(2)}) collective-permute-start(bf16[384,1536]{1,0:T(8,128)(2,1)S(1)} %copy-done.66), channel_id=1, source_target_pairs={{0,16},{16,0},{1,17},{17,1},{2,18},{18,2},{3,19},{19,3},{4,20},{20... | collective-permute-start | bytes 3538952 | tf_op jit(solution)/shard_map/ppermute | solution.py:19
  185.8 74.6 %collective-permute-start.56 = (bf16[384,1536]{1,0:T(8,128)(2,1)S(1)}, bf16[384,1536]{1,0:T(8,128)(2,1)S(1)}, u32[]{:S(2)}, u32[]{:S(2)}) collective-permute-start(bf16[384,1536]{1,0:T(8,128)(2,1)S(1)} %get-tuple-element.174), channel_id=1, source_target_pairs={{0,16},{16,0},{1,17},{17,1},{2,18},{18,2},{3,19},{19,3},{4,20},{20... | collective-permute-start | bytes 3538952 | tf_op jit(solution)/shard_map/ppermute | solution.py:19
  207.2 84.5 %collective-permute-start.35 = (bf16[384,1536]{1,0:T(8,128)(2,1)S(1)}, bf16[384,1536]{1,0:T(8,128)(2,1)S(1)}, u32[]{:S(2)}, u32[]{:S(2)}) collective-permute-start(bf16[384,1536]{1,0:T(8,128)(2,1)S(1)} %get-tuple-element.175), channel_id=1, source_target_pairs={{0,8},{8,0},{1,9},{9,1},{2,10},{10,2},{3,11},{11,3},{4,12},{12,4},... | collective-permute-start | bytes 3538952 | tf_op jit(solution)/shard_map/ppermute | solution.py:19
  209.2 82.6 %collective-permute-start.36 = (bf16[384,1536]{1,0:T(8,128)(2,1)S(1)}, bf16[384,1536]{1,0:T(8,128)(2,1)S(1)}, u32[]{:S(2)}, u32[]{:S(2)}) collective-permute-start(bf16[384,1536]{1,0:T(8,128)(2,1)S(1)} %get-tuple-element.175), channel_id=1, source_target_pairs={{0,16},{16,0},{1,17},{17,1},{2,18},{18,2},{3,19},{19,3},{4,20},{20... | collective-permute-start | bytes 3538952 | tf_op jit(solution)/shard_map/ppermute | solution.py:19
  209.3 134.7 %collective-permute-start.9 = (bf16[512,1536]{1,0:T(8,128)(2,1)S(1)}, bf16[512,1536]{1,0:T(8,128)(2,1)S(1)}, u32[]{:S(2)}, u32[]{:S(2)}) collective-permute-start(bf16[512,1536]{1,0:T(8,128)(2,1)S(1)} %fusion.17), channel_id=1, source_target_pairs={{0,1},{1,0},{2,3},{3,2},{4,5},{5,4},{6,7},{7,6},{8,9},{9,8},{10,11... | collective-permute-start | bytes 4718600 | tf_op jit(solution)/shard_map/ppermute | solution.py:19
  260.4 55.4 %collective-permute-start.18 = (bf16[80,1536]{1,0:T(8,128)(2,1)S(1)}, bf16[80,1536]{1,0:T(8,128)(2,1)S(1)}, u32[]{:S(2)}, u32[]{:S(2)}) collective-permute-start(bf16[80,1536]{1,0:T(8,128)(2,1)S(1)} %collective-permute-done.17), channel_id=1, source_target_pairs={{0,4},{4,0},{1,5},{5,1},{2,6},{6,2},{3,7},{7,3},{8,12},{12,8},{9,1... | collective-permute-start | bytes 737288 | tf_op jit(solution)/shard_map/ppermute | solution.py:19
  315.7 60.0 %collective-permute-start.8 = (bf16[512,1536]{1,0:T(8,128)(2,1)S(1)}, bf16[512,1536]{1,0:T(8,128)(2,1)S(1)}, u32[]{:S(2)}, u32[]{:S(2)}) collective-permute-start(bf16[512,1536]{1,0:T(8,128)(2,1)S(1)} %fusion.17), channel_id=1, source_target_pairs={{0,4},{4,0},{1,5},{5,1},{2,6},{6,2},{3,7},{7,3},{8,12},{12,8},{9,1... | collective-permute-start | bytes 4718600 | tf_op jit(solution)/shard_map/ppermute | solution.py:19
  315.8 50.0 %collective-permute-start.57 = (bf16[384,1536]{1,0:T(8,128)(2,1)S(1)}, bf16[384,1536]{1,0:T(8,128)(2,1)S(1)}, u32[]{:S(2)}, u32[]{:S(2)}) collective-permute-start(bf16[384,1536]{1,0:T(8,128)(2,1)S(1)} %collective-permute-done.56), channel_id=1, source_target_pairs={{0,8},{8,0},{1,9},{9,1},{2,10},{10,2},{3,11},{11,3},{4,12},{12,4},... | collective-permute-start | bytes 3538952 | tf_op jit(solution)/shard_map/ppermute | solution.py:19
  342.4 33.2 %collective-permute-start.37 = (bf16[384,1536]{1,0:T(8,128)(2,1)S(1)}, bf16[384,1536]{1,0:T(8,128)(2,1)S(1)}, u32[]{:S(2)}, u32[]{:S(2)}) collective-permute-start(bf16[384,1536]{1,0:T(8,128)(2,1)S(1)} %collective-permute-done.35), channel_id=1, source_target_pairs={{0,16},{16,0},{1,17},{17,1},{2,18},{18,2},{3,19},{19,3},{4,20},{20... | collective-permute-start | bytes 3538952 | tf_op jit(solution)/shard_map/ppermute | solution.py:19
  365.8 105.4 %collective-permute-start.73 = (bf16[80,1536]{1,0:T(8,128)(2,1)}, bf16[80,1536]{1,0:T(8,128)(2,1)}, u32[]{:S(2)}, u32[]{:S(2)}) collective-permute-start(bf16[80,1536]{1,0:T(8,128)(2,1)} %get-tuple-element.138), channel_id=1, source_target_pairs={{0,4},{4,0},{1,5},{5,1},{2,6},{6,2},{3,7},{7,3},{8,12},{12,8},{9,1... | collective-permute-start | bytes 737288 | tf_op jit(solution)/shard_map/ppermute | solution.py:19
  365.9 281.2 %collective-permute-start.65 = (bf16[512,1536]{1,0:T(8,128)(2,1)}, bf16[512,1536]{1,0:T(8,128)(2,1)}, u32[]{:S(2)}, u32[]{:S(2)}) collective-permute-start(bf16[512,1536]{1,0:T(8,128)(2,1)} %get-tuple-element.136), channel_id=1, source_target_pairs={{0,1},{1,0},{2,3},{3,2},{4,5},{5,4},{6,7},{7,6},{8,9},{9,8},{10,11... | collective-permute-start | bytes 4718600 | tf_op jit(solution)/shard_map/ppermute | solution.py:19
  375.5 95.6 %collective-permute-start.75 = (bf16[80,1536]{1,0:T(8,128)(2,1)}, bf16[80,1536]{1,0:T(8,128)(2,1)}, u32[]{:S(2)}, u32[]{:S(2)}) collective-permute-start(bf16[80,1536]{1,0:T(8,128)(2,1)} %collective-permute-done.74), channel_id=1, source_target_pairs={{0,4},{4,0},{1,5},{5,1},{2,6},{6,2},{3,7},{7,3},{8,12},{12,8},{9,1... | collective-permute-start | bytes 737288 | tf_op jit(solution)/shard_map/ppermute | solution.py:19
  467.2 119.4 %collective-permute-start.27 = (bf16[512,1536]{1,0:T(8,128)(2,1)S(1)}, bf16[512,1536]{1,0:T(8,128)(2,1)S(1)}, u32[]{:S(2)}, u32[]{:S(2)}) collective-permute-start(bf16[512,1536]{1,0:T(8,128)(2,1)S(1)} %slice.758), channel_id=1, source_target_pairs={{0,4},{4,0},{1,5},{5,1},{2,6},{6,2},{3,7},{7,3},{8,12},{12,8},{9,1... | collective-permute-start | bytes 4718600 | tf_op jit(solution)/shard_map/ppermute | solution.py:19
  467.8 43.8 %collective-permute-start.28 = (bf16[512,1536]{1,0:T(8,128)(2,1)S(1)}, bf16[512,1536]{1,0:T(8,128)(2,1)}, u32[]{:S(2)}, u32[]{:S(2)}) collective-permute-start(bf16[512,1536]{1,0:T(8,128)(2,1)S(1)} %slice.757), channel_id=1, source_target_pairs={{0,4},{4,0},{1,5},{5,1},{2,6},{6,2},{3,7},{7,3},{8,12},{12,8},{9,1... | collective-permute-start | bytes 4718600 | tf_op jit(solution)/shard_map/ppermute | solution.py:19
  513.4 73.3 %collective-permute-start.29 = (bf16[512,1536]{1,0:T(8,128)(2,1)S(1)}, bf16[512,1536]{1,0:T(8,128)(2,1)S(1)}, u32[]{:S(2)}, u32[]{:S(2)}) collective-permute-start(bf16[512,1536]{1,0:T(8,128)(2,1)S(1)} %fusion.39), channel_id=1, source_target_pairs={{0,1},{1,0},{2,3},{3,2},{4,5},{5,4},{6,7},{7,6},{8,9},{9,8},{10,11... | collective-permute-start | bytes 4718600 | tf_op jit(solution)/shard_map/ppermute | solution.py:19
  518.8 73.3 %collective-permute-start.129 = (bf16[2,384,1536]{2,1,0:T(8,128)(2,1)}, bf16[2,384,1536]{2,1,0:T(8,128)(2,1)}, u32[]{:S(2)}, u32[]{:S(2)}) collective-permute-start(bf16[2,384,1536]{2,1,0:T(8,128)(2,1)} %dynamic-slice_bitcast_fusion), channel_id=1, source_target_pairs={{0,16},{16,0},{1,17},{17,1},{2,18},{18,2},{3,19},{19,3},{4,20},{20... | collective-permute-start | bytes 7077896 | tf_op jit(solution)/shard_map/ppermute | solution.py:19
  521.0 64.4 %collective-permute-start.115 = (bf16[2,384,384]{2,1,0:T(8,128)(2,1)S(1)}, bf16[2,384,384]{2,1,0:T(8,128)(2,1)S(1)}, u32[]{:S(2)}, u32[]{:S(2)}) collective-permute-start(bf16[2,384,384]{2,1,0:T(8,128)(2,1)S(1)} %dynamic-slice_bitcast_fusion.6), channel_id=1, source_target_pairs={{0,16},{16,0},{1,17},{17,1},{2,18},{18,2},{3,19},{19,3},{4,20},{20... | collective-permute-start | bytes 1769480 | tf_op jit(solution)/shard_map/ppermute | solution.py:19
  585.3 53.2 %collective-permute-start.121 = (bf16[2,384,1536]{2,1,0:T(8,128)(2,1)}, bf16[2,384,1536]{2,1,0:T(8,128)(2,1)}, u32[]{:S(2)}, u32[]{:S(2)}) collective-permute-start(bf16[2,384,1536]{2,1,0:T(8,128)(2,1)} %dynamic-slice_bitcast_fusion.2), channel_id=1, source_target_pairs={{0,16},{16,0},{1,17},{17,1},{2,18},{18,2},{3,19},{19,3},{4,20},{20... | collective-permute-start | bytes 7077896 | tf_op jit(solution)/shard_map/ppermute | solution.py:19
  586.6 58.4 %collective-permute-start.116 = (bf16[384,384]{1,0:T(8,128)(2,1)S(1)}, bf16[384,384]{1,0:T(8,128)(2,1)S(1)}, u32[]{:S(2)}, u32[]{:S(2)}) collective-permute-start(bf16[384,384]{1,0:T(8,128)(2,1)S(1)} %fusion.112), channel_id=1, source_target_pairs={{0,8},{8,0},{1,9},{9,1},{2,10},{10,2},{3,11},{11,3},{4,12},{12,4},... | collective-permute-start | bytes 884744 | tf_op jit(solution)/shard_map/ppermute | solution.py:19
  589.9 55.1 %collective-permute-start.31 = (bf16[512,1536]{1,0:T(8,128)(2,1)S(1)}, bf16[512,1536]{1,0:T(8,128)(2,1)S(1)}, u32[]{:S(2)}, u32[]{:S(2)}) collective-permute-start(bf16[512,1536]{1,0:T(8,128)(2,1)S(1)} %add_convert_fusion.1), channel_id=1, source_target_pairs={{0,1},{1,0},{2,3},{3,2},{4,5},{5,4},{6,7},{7,6},{8,9},{9,8},{10,11... | collective-permute-start | bytes 4718600 | tf_op jit(solution)/shard_map/ppermute | solution.py:19
  594.6 53.0 %collective-permute-start.130 = (bf16[384,1536]{1,0:T(8,128)(2,1)S(1)}, bf16[384,1536]{1,0:T(8,128)(2,1)S(1)}, u32[]{:S(2)}, u32[]{:S(2)}) collective-permute-start(bf16[384,1536]{1,0:T(8,128)(2,1)S(1)} %fusion.69), channel_id=1, source_target_pairs={{0,8},{8,0},{1,9},{9,1},{2,10},{10,2},{3,11},{11,3},{4,12},{12,4},... | collective-permute-start | bytes 3538952 | tf_op jit(solution)/shard_map/ppermute | solution.py:19
  647.1 44.4 %collective-permute-start.64 = (bf16[512,1536]{1,0:T(8,128)(2,1)}, bf16[512,1536]{1,0:T(8,128)(2,1)}, u32[]{:S(2)}, u32[]{:S(2)}) collective-permute-start(bf16[512,1536]{1,0:T(8,128)(2,1)} %get-tuple-element.136), channel_id=1, source_target_pairs={{0,4},{4,0},{1,5},{5,1},{2,6},{6,2},{3,7},{7,3},{8,12},{12,8},{9,1... | collective-permute-start | bytes 4718600 | tf_op jit(solution)/shard_map/ppermute | solution.py:19
  647.5 44.0 %collective-permute-start.66 = (bf16[512,1536]{1,0:T(8,128)(2,1)}, bf16[512,1536]{1,0:T(8,128)(2,1)}, u32[]{:S(2)}, u32[]{:S(2)}) collective-permute-start(bf16[512,1536]{1,0:T(8,128)(2,1)} %collective-permute-done.65), channel_id=1, source_target_pairs={{0,4},{4,0},{1,5},{5,1},{2,6},{6,2},{3,7},{7,3},{8,12},{12,8},{9,1... | collective-permute-start | bytes 4718600 | tf_op jit(solution)/shard_map/ppermute | solution.py:19
  751.3 54.5 %collective-permute-start.119 = (bf16[2,384,1536]{2,1,0:T(8,128)(2,1)}, bf16[2,384,1536]{2,1,0:T(8,128)(2,1)}, u32[]{:S(2)}, u32[]{:S(2)}) collective-permute-start(bf16[2,384,1536]{2,1,0:T(8,128)(2,1)} %dynamic-slice_bitcast_fusion.3), channel_id=1, source_target_pairs={{0,8},{8,0},{1,9},{9,1},{2,10},{10,2},{3,11},{11,3},{4,12},{12,4},... | collective-permute-start | bytes 7077896 | tf_op jit(solution)/shard_map/ppermute | solution.py:19
  752.9 41.5 %collective-permute-start.68 = (bf16[512,1536]{1,0:T(8,128)(2,1)}, bf16[512,1536]{1,0:T(8,128)(2,1)}, u32[]{:S(2)}, u32[]{:S(2)}) collective-permute-start(bf16[512,1536]{1,0:T(8,128)(2,1)} %slice.753), channel_id=1, source_target_pairs={{0,4},{4,0},{1,5},{5,1},{2,6},{6,2},{3,7},{7,3},{8,12},{12,8},{9,1... | collective-permute-start | bytes 4718600 | tf_op jit(solution)/shard_map/ppermute | solution.py:19
  776.2 77.0 %collective-permute-start.127 = (bf16[2,384,1536]{2,1,0:T(8,128)(2,1)S(1)}, bf16[2,384,1536]{2,1,0:T(8,128)(2,1)S(1)}, u32[]{:S(2)}, u32[]{:S(2)}) collective-permute-start(bf16[2,384,1536]{2,1,0:T(8,128)(2,1)S(1)} %dynamic-slice_bitcast_fusion.1), channel_id=1, source_target_pairs={{0,8},{8,0},{1,9},{9,1},{2,10},{10,2},{3,11},{11,3},{4,12},{12,4},... | collective-permute-start | bytes 7077896 | tf_op jit(solution)/shard_map/ppermute | solution.py:19
  792.7 65.7 %collective-permute-start.67 = (bf16[512,1536]{1,0:T(8,128)(2,1)S(1)}, bf16[512,1536]{1,0:T(8,128)(2,1)S(1)}, u32[]{:S(2)}, u32[]{:S(2)}) collective-permute-start(bf16[512,1536]{1,0:T(8,128)(2,1)S(1)} %slice.754), channel_id=1, source_target_pairs={{0,4},{4,0},{1,5},{5,1},{2,6},{6,2},{3,7},{7,3},{8,12},{12,8},{9,1... | collective-permute-start | bytes 4718600 | tf_op jit(solution)/shard_map/ppermute | solution.py:19
  794.5 68.9 %collective-permute-start.43 = (bf16[512,1536]{1,0:T(8,128)(2,1)}, bf16[512,1536]{1,0:T(8,128)(2,1)}, u32[]{:S(2)}, u32[]{:S(2)}) collective-permute-start(bf16[512,1536]{1,0:T(8,128)(2,1)} %slice.756), channel_id=1, source_target_pairs={{0,4},{4,0},{1,5},{5,1},{2,6},{6,2},{3,7},{7,3},{8,12},{12,8},{9,1... | collective-permute-start | bytes 4718600 | tf_op jit(solution)/shard_map/ppermute | solution.py:19
  797.5 61.9 %collective-permute-start.69 = (bf16[512,1536]{1,0:T(8,128)(2,1)S(1)}, bf16[512,1536]{1,0:T(8,128)(2,1)S(1)}, u32[]{:S(2)}, u32[]{:S(2)}) collective-permute-start(bf16[512,1536]{1,0:T(8,128)(2,1)S(1)} %fusion.26), channel_id=1, source_target_pairs={{0,1},{1,0},{2,3},{3,2},{4,5},{5,4},{6,7},{7,6},{8,9},{9,8},{10,11... | collective-permute-start | bytes 4718600 | tf_op jit(solution)/shard_map/ppermute | solution.py:19
  805.8 62.7 %collective-permute-start.45 = (bf16[512,1536]{1,0:T(8,128)(2,1)}, bf16[512,1536]{1,0:T(8,128)(2,1)}, u32[]{:S(2)}, u32[]{:S(2)}) collective-permute-start(bf16[512,1536]{1,0:T(8,128)(2,1)} %fusion.32), channel_id=1, source_target_pairs={{0,1},{1,0},{2,3},{3,2},{4,5},{5,4},{6,7},{7,6},{8,9},{9,8},{10,11... | collective-permute-start | bytes 4718600 | tf_op jit(solution)/shard_map/ppermute | solution.py:19
  858.4 46.4 %collective-permute-start.128 = (bf16[384,1536]{1,0:T(8,128)(2,1)S(1)}, bf16[384,1536]{1,0:T(8,128)(2,1)S(1)}, u32[]{:S(2)}, u32[]{:S(2)}) collective-permute-start(bf16[384,1536]{1,0:T(8,128)(2,1)S(1)} %fusion.68), channel_id=1, source_target_pairs={{0,16},{16,0},{1,17},{17,1},{2,18},{18,2},{3,19},{19,3},{4,20},{20... | collective-permute-start | bytes 3538952 | tf_op jit(solution)/shard_map/ppermute | solution.py:19
  876.8 57.0 %collective-permute-start.71 = (bf16[512,1536]{1,0:T(8,128)(2,1)}, bf16[512,1536]{1,0:T(8,128)(2,1)}, u32[]{:S(2)}, u32[]{:S(2)}) collective-permute-start(bf16[512,1536]{1,0:T(8,128)(2,1)} %get-tuple-element.156), channel_id=1, source_target_pairs={{0,1},{1,0},{2,3},{3,2},{4,5},{5,4},{6,7},{7,6},{8,9},{9,8},{10,11... | collective-permute-start | bytes 4718600 | tf_op jit(solution)/shard_map/ppermute | solution.py:19
  885.9 34.7 %collective-permute-start.123 = (bf16[2,192,1536]{2,1,0:T(8,128)(2,1)}, bf16[2,192,1536]{2,1,0:T(8,128)(2,1)S(1)}, u32[]{:S(2)}, u32[]{:S(2)}) collective-permute-start(bf16[2,192,1536]{2,1,0:T(8,128)(2,1)} %get-tuple-element.160), channel_id=1, source_target_pairs={{2,4},{4,2},{3,5},{5,3},{10,12},{12,10},{11,13},{13,11},{18,20},{2... | collective-permute-start | bytes 3538952 | tf_op jit(solution)/shard_map/ppermute | solution.py:380
  896.2 77.5 %collective-permute-start.124 = (bf16[2,192,1536]{2,1,0:T(8,128)(2,1)}, bf16[2,192,1536]{2,1,0:T(8,128)(2,1)}, u32[]{:S(2)}, u32[]{:S(2)}) collective-permute-start(bf16[2,192,1536]{2,1,0:T(8,128)(2,1)} %get-tuple-element.161), channel_id=1, source_target_pairs={{2,0},{4,6},{0,4},{6,2},{3,1},{5,7},{1,5},{7,3},{10,8},{12,14},{8,... | collective-permute-start | bytes 3538952 | tf_op jit(solution)/shard_map/ppermute | solution.py:381
  907.4 70.2 %collective-permute-start.131 = (bf16[2,192,1536]{2,1,0:T(8,128)(2,1)}, bf16[2,192,1536]{2,1,0:T(8,128)(2,1)}, u32[]{:S(2)}, u32[]{:S(2)}) collective-permute-start(bf16[2,192,1536]{2,1,0:T(8,128)(2,1)} %get-tuple-element.158), channel_id=1, source_target_pairs={{2,4},{4,2},{3,5},{5,3},{10,12},{12,10},{11,13},{13,11},{18,20},{2... | collective-permute-start | bytes 3538952 | tf_op jit(solution)/shard_map/ppermute | solution.py:380
  909.2 89.9 %collective-permute-start.132 = (bf16[2,192,1536]{2,1,0:T(8,128)(2,1)}, bf16[2,192,1536]{2,1,0:T(8,128)(2,1)}, u32[]{:S(2)}, u32[]{:S(2)}) collective-permute-start(bf16[2,192,1536]{2,1,0:T(8,128)(2,1)} %get-tuple-element.159), channel_id=1, source_target_pairs={{2,0},{4,6},{0,4},{6,2},{3,1},{5,7},{1,5},{7,3},{10,8},{12,14},{8,... | collective-permute-start | bytes 3538952 | tf_op jit(solution)/shard_map/ppermute | solution.py:381
  920.6 82.0 %collective-permute-start.70 = (bf16[512,1536]{1,0:T(8,128)(2,1)}, bf16[512,1536]{1,0:T(8,128)(2,1)}, u32[]{:S(2)}, u32[]{:S(2)}) collective-permute-start(bf16[512,1536]{1,0:T(8,128)(2,1)} %get-tuple-element.156), channel_id=1, source_target_pairs={{0,4},{4,0},{1,5},{5,1},{2,6},{6,2},{3,7},{7,3},{8,12},{12,8},{9,1... | collective-permute-start | bytes 4718600 | tf_op jit(solution)/shard_map/ppermute | solution.py:19
  933.8 68.8 %collective-permute-start.72 = (bf16[512,1536]{1,0:T(8,128)(2,1)}, bf16[512,1536]{1,0:T(8,128)(2,1)}, u32[]{:S(2)}, u32[]{:S(2)}) collective-permute-start(bf16[512,1536]{1,0:T(8,128)(2,1)} %collective-permute-done.71), channel_id=1, source_target_pairs={{0,4},{4,0},{1,5},{5,1},{2,6},{6,2},{3,7},{7,3},{8,12},{12,8},{9,1... | collective-permute-start | bytes 4718600 | tf_op jit(solution)/shard_map/ppermute | solution.py:19
  1086.5 34.6 %collective-permute-start.108 = (f32[84,128]{1,0:T(8,128)}, f32[84,128]{1,0:T(8,128)S(1)}, u32[]{:S(2)}, u32[]{:S(2)}) collective-permute-start(f32[84,128]{1,0:T(8,128)} %maximum_bitcast_fusion.2), channel_id=1, source_target_pairs={{0,16},{16,0},{1,17},{17,1},{2,18},{18,2},{3,19},{19,3},{4,20},{20... | collective-permute-start | bytes 129032 | tf_op jit(solution)/shard_map/ppermute | solution.py:19
  1094.1 86.4 %collective-permute-start.113 = (bf16[2,384,384]{2,1,0:T(8,128)(2,1)}, bf16[2,384,384]{2,1,0:T(8,128)(2,1)}, u32[]{:S(2)}, u32[]{:S(2)}) collective-permute-start(bf16[2,384,384]{2,1,0:T(8,128)(2,1)} %dynamic-slice_bitcast_fusion.7), channel_id=1, source_target_pairs={{0,8},{8,0},{1,9},{9,1},{2,10},{10,2},{3,11},{11,3},{4,12},{12,4},... | collective-permute-start | bytes 1769480 | tf_op jit(solution)/shard_map/ppermute | solution.py:19
  1098.4 70.1 %collective-permute-start.86 = (bf16[80,1536]{1,0:T(8,128)(2,1)}, bf16[80,1536]{1,0:T(8,128)(2,1)}, u32[]{:S(2)}, u32[]{:S(2)}) collective-permute-start(bf16[80,1536]{1,0:T(8,128)(2,1)} %slice.759), channel_id=1, source_target_pairs={{0,4},{4,0},{1,5},{5,1},{2,6},{6,2},{3,7},{7,3},{8,12},{12,8},{9,1... | collective-permute-start | bytes 737288 | tf_op jit(solution)/shard_map/ppermute | solution.py:19
  1098.7 73.3 %collective-permute-start.85 = (bf16[80,1536]{1,0:T(8,128)(2,1)S(1)}, bf16[80,1536]{1,0:T(8,128)(2,1)S(1)}, u32[]{:S(2)}, u32[]{:S(2)}) collective-permute-start(bf16[80,1536]{1,0:T(8,128)(2,1)S(1)} %slice.760), channel_id=1, source_target_pairs={{0,4},{4,0},{1,5},{5,1},{2,6},{6,2},{3,7},{7,3},{8,12},{12,8},{9,1... | collective-permute-start | bytes 737288 | tf_op jit(solution)/shard_map/ppermute | solution.py:19
  1109.9 112.0 %collective-permute-start.100 = (bf16[2,384,1152]{2,1,0:T(8,128)(2,1)}, bf16[2,384,1152]{2,1,0:T(8,128)(2,1)}, u32[]{:S(2)}, u32[]{:S(2)}) collective-permute-start(bf16[2,384,1152]{2,1,0:T(8,128)(2,1)} %dynamic-slice_bitcast_fusion.5), channel_id=1, source_target_pairs={{0,8},{8,0},{1,9},{9,1},{2,10},{10,2},{3,11},{11,3},{4,12},{12,4},... | collective-permute-start | bytes 5308424 | tf_op jit(solution)/shard_map/ppermute | solution.py:19
  1166.2 60.1 %collective-permute-start.102 = (bf16[2,384,1152]{2,1,0:T(8,128)(2,1)}, bf16[2,384,1152]{2,1,0:T(8,128)(2,1)}, u32[]{:S(2)}, u32[]{:S(2)}) collective-permute-start(bf16[2,384,1152]{2,1,0:T(8,128)(2,1)} %dynamic-slice_bitcast_fusion.4), channel_id=1, source_target_pairs={{0,16},{16,0},{1,17},{17,1},{2,18},{18,2},{3,19},{19,3},{4,20},{20... | collective-permute-start | bytes 5308424 | tf_op jit(solution)/shard_map/ppermute | solution.py:19
  1172.0 43.5 %collective-permute-start.83 = (bf16[512,1536]{1,0:T(8,128)(2,1)}, bf16[512,1536]{1,0:T(8,128)(2,1)}, u32[]{:S(2)}, u32[]{:S(2)}) collective-permute-start(bf16[512,1536]{1,0:T(8,128)(2,1)} %slice.751), channel_id=1, source_target_pairs={{0,4},{4,0},{1,5},{5,1},{2,6},{6,2},{3,7},{7,3},{8,12},{12,8},{9,1... | collective-permute-start | bytes 4718600 | tf_op jit(solution)/shard_map/ppermute | solution.py:19
  1178.0 54.1 %collective-permute-start.82 = (bf16[512,1536]{1,0:T(8,128)(2,1)}, bf16[512,1536]{1,0:T(8,128)(2,1)}, u32[]{:S(2)}, u32[]{:S(2)}) collective-permute-start(bf16[512,1536]{1,0:T(8,128)(2,1)} %slice.752), channel_id=1, source_target_pairs={{0,4},{4,0},{1,5},{5,1},{2,6},{6,2},{3,7},{7,3},{8,12},{12,8},{9,1... | collective-permute-start | bytes 4718600 | tf_op jit(solution)/shard_map/ppermute | solution.py:19
  1182.0 31.7 %collective-permute-start.114 = (bf16[384,384]{1,0:T(8,128)(2,1)S(1)}, bf16[384,384]{1,0:T(8,128)(2,1)S(1)}, u32[]{:S(2)}, u32[]{:S(2)}) collective-permute-start(bf16[384,384]{1,0:T(8,128)(2,1)S(1)} %fusion.111), channel_id=1, source_target_pairs={{0,16},{16,0},{1,17},{17,1},{2,18},{18,2},{3,19},{19,3},{4,20},{20... | collective-permute-start | bytes 884744 | tf_op jit(solution)/shard_map/ppermute | solution.py:19
  1214.8 71.0 %collective-permute-start.117 = (bf16[2,192,384]{2,1,0:T(8,128)(2,1)}, bf16[2,192,384]{2,1,0:T(8,128)(2,1)S(1)}, u32[]{:S(2)}, u32[]{:S(2)}) collective-permute-start(bf16[2,192,384]{2,1,0:T(8,128)(2,1)} %get-tuple-element.185), channel_id=1, source_target_pairs={{2,4},{4,2},{3,5},{5,3},{10,12},{12,10},{11,13},{13,11},{18,20},{2... | collective-permute-start | bytes 884744 | tf_op jit(solution)/shard_map/ppermute | solution.py:380
  1215.5 70.4 %collective-permute-start.118 = (bf16[2,192,384]{2,1,0:T(8,128)(2,1)}, bf16[2,192,384]{2,1,0:T(8,128)(2,1)}, u32[]{:S(2)}, u32[]{:S(2)}) collective-permute-start(bf16[2,192,384]{2,1,0:T(8,128)(2,1)} %get-tuple-element.186), channel_id=1, source_target_pairs={{2,0},{4,6},{0,4},{6,2},{3,1},{5,7},{1,5},{7,3},{10,8},{12,14},{8,... | collective-permute-start | bytes 884744 | tf_op jit(solution)/shard_map/ppermute | solution.py:381
  1221.9 42.0 %collective-permute-start.84 = (bf16[512,1536]{1,0:T(8,128)(2,1)S(1)}, bf16[512,1536]{1,0:T(8,128)(2,1)S(1)}, u32[]{:S(2)}, u32[]{:S(2)}) collective-permute-start(bf16[512,1536]{1,0:T(8,128)(2,1)S(1)} %fusion.24), channel_id=1, source_target_pairs={{0,1},{1,0},{2,3},{3,2},{4,5},{5,4},{6,7},{7,6},{8,9},{9,8},{10,11... | collective-permute-start | bytes 4718600 | tf_op jit(solution)/shard_map/ppermute | solution.py:19
  1227.6 43.6 %collective-permute-start.101 = (bf16[384,1152]{1,0:T(8,128)(2,1)}, bf16[384,1152]{1,0:T(8,128)(2,1)}, u32[]{:S(2)}, u32[]{:S(2)}) collective-permute-start(bf16[384,1152]{1,0:T(8,128)(2,1)} %fusion.78), channel_id=1, source_target_pairs={{0,16},{16,0},{1,17},{17,1},{2,18},{18,2},{3,19},{19,3},{4,20},{20... | collective-permute-start | bytes 2654216 | tf_op jit(solution)/shard_map/ppermute | solution.py:19
  1232.0 44.1 %collective-permute-start.103 = (bf16[384,1152]{1,0:T(8,128)(2,1)}, bf16[384,1152]{1,0:T(8,128)(2,1)}, u32[]{:S(2)}, u32[]{:S(2)}) collective-permute-start(bf16[384,1152]{1,0:T(8,128)(2,1)} %fusion.79), channel_id=1, source_target_pairs={{0,8},{8,0},{1,9},{9,1},{2,10},{10,2},{3,11},{11,3},{4,12},{12,4},... | collective-permute-start | bytes 2654216 | tf_op jit(solution)/shard_map/ppermute | solution.py:19
  1282.6 42.9 %collective-permute-start.105 = (bf16[2,192,1152]{2,1,0:T(8,128)(2,1)S(1)}, bf16[2,192,1152]{2,1,0:T(8,128)(2,1)S(1)}, u32[]{:S(2)}, u32[]{:S(2)}) collective-permute-start(bf16[2,192,1152]{2,1,0:T(8,128)(2,1)S(1)} %get-tuple-element.165), channel_id=1, source_target_pairs={{2,0},{4,6},{0,4},{6,2},{3,1},{5,7},{1,5},{7,3},{10,8},{12,14},{8,... | collective-permute-start | bytes 2654216 | tf_op jit(solution)/shard_map/ppermute | solution.py:381
  1289.7 41.3 %collective-permute-start.92 = (f32[8,2,6,384]{3,0,2,1:T(8,128)}, f32[8,2,6,384]{3,0,2,1:T(8,128)}, u32[]{:S(2)}, u32[]{:S(2)}) collective-permute-start(f32[8,2,6,384]{3,0,2,1:T(8,128)} %pad_maximum_fusion.29), channel_id=1, source_target_pairs={{0,16},{16,0},{1,17},{17,1},{2,18},{18,2},{3,19},{19,3},{4,20},{20... | collective-permute-start | bytes 442376 | tf_op jit(solution)/shard_map/ppermute | solution.py:19
  (244 other events, 5492.7 us)

commit v2 on v1

v2 whole, which is shorter than its diff:
```python
import functools

import jax
import jax.numpy as jnp
from jax import lax
from jax.experimental import pallas as pl
from jax.experimental.pallas import tpu as pltpu
from jax.sharding import Mesh
from jax.sharding import PartitionSpec as P

HEAD_DIM = 64
SCALE = HEAD_DIM ** (-0.5)
BF = jnp.bfloat16
F32 = jnp.float32
NEG = -1e30


def swap(v, axis):
    return lax.ppermute(v, axis, [(0, 1), (1, 0)])


def gather_bits(v, axes):
    for axis in axes:
        other = swap(v, axis)
        first = lax.axis_index(axis) == 0
        v = jnp.concatenate([jnp.where(first, v, other), jnp.where(first, other, v)], 0)
    return v


def scatter_bits(v, axes):
    for axis in axes:
        first = lax.axis_index(axis) == 0
        half = v.shape[0] // 2
        low, high = v[:half], v[half:]
        v = jnp.where(first, low, high) + swap(jnp.where(first, high, low), axis)
    return v


def sum_bits(v, axes):
    for axis in axes:
        v = v + swap(v, axis)
    return v


def after(v, *deps):
    return lax.optimization_barrier((v,) + deps)[0]


def index_of(axes):
    out = 0
    for axis in axes:
        out = out * 2 + lax.axis_index(axis)
    return out


def nt(a, b):
    return lax.dot_general(a, b, (((1,), (1,)), ((), ())), preferred_element_type=F32)


def nn(a, b):
    return lax.dot_general(a, b, (((1,), (0,)), ((), ())), preferred_element_type=F32)


def tn(a, b):
    return lax.dot_general(a, b, (((0,), (0,)), ((), ())), preferred_element_type=F32)


VMEM_LIMIT = 52 * 2**20
GELU_C = 0.7978845608028654


def launch(kernel, grid, in_specs, out_specs, out_shape, args, name, flops, scratch=(), rides=(), cid=None):
    n_in, n_out = len(args), len(out_shape)
    params = dict(vmem_limit_bytes=VMEM_LIMIT)
    cost = pl.CostEstimate(flops=flops, bytes_accessed=flops // 512, transcendentals=0)
    if not rides:
        outs = pl.pallas_call(
            kernel,
            grid=grid,
            in_specs=in_specs,
            out_specs=out_specs,
            out_shape=out_shape,
            scratch_shapes=list(scratch),
            compiler_params=pltpu.CompilerParams(**params),
            cost_estimate=cost,
            name=name,
        )(*args)
        return list(outs), []
    partners = sorted({partner for ride in rides for partner in ride.partners})
    n_rides, sems = len(rides), sum(ride.sems for ride in rides)

    def body(*refs):
        ins, rest = refs[:n_in], refs[n_in:]
        sources, rest = rest[:n_rides], rest[n_rides:]
        outs, rest = rest[:n_out], rest[n_out:]
        targets, rest = rest[:n_rides], rest[n_rides:]
        own, (send, recv) = rest[:-2], rest[-2:]
        steps, at = [], 0
        for source, target, ride in zip(sources, targets, rides):
            steps.append(ride.moves(source, target, lambda k, at=at: send.at[at + k], lambda k, at=at: recv.at[at + k]))
            at += ride.sems

        @pl.when(pl.program_id(0) == 0)
        def _():
            barrier = pltpu.get_barrier_semaphore()
            for partner in partners:
                pl.semaphore_signal(
                    barrier,
                    1,
                    device_id={axis: 1 - lax.axis_index(axis) for axis in partner},
                    device_id_type=pl.DeviceIdType.MESH,
                )
            pl.semaphore_wait(barrier, len(partners))
            for start, unused in steps:
                start()

        kernel(*ins, *outs, *own)

        @pl.when(pl.program_id(0) == grid[0] - 1)
        def _():
            for unused, wait in steps:
                wait()

    anywhere = pl.BlockSpec(memory_space=pl.ANY)
    outs = pl.pallas_call(
        body,
        grid=grid,
        in_specs=list(in_specs) + [anywhere] * n_rides,
        out_specs=list(out_specs) + [anywhere] * n_rides,
        out_shape=list(out_shape) + [ride.shape for ride in rides],
        scratch_shapes=list(scratch)
        + [pltpu.SemaphoreType.DMA((sems,)), pltpu.SemaphoreType.DMA((sems,))],
        compiler_params=pltpu.CompilerParams(collective_id=cid, has_side_effects=True, **params),
        cost_estimate=cost,
        name=f"{name}_{cid}",
    )(*args, *[ride.array for ride in rides])
    return list(outs[:n_out]), list(outs[n_out:])


class NeighbourRide:
    def __init__(self, array, axis, shape, views, sems):
        self.array, self.axis, self.views, self.sems = array, axis, views, sems
        self.shape = jax.ShapeDtypeStruct(shape, array.dtype)
        self.partners = [(axis,)]

    def moves(self, source, target, send, recv):
        other = {self.axis: 1 - lax.axis_index(self.axis)}
        made = [
            pltpu.make_async_remote_copy(
                src_ref=src,
                dst_ref=dst,
                send_sem=send(k),
                recv_sem=recv(k),
                device_id=other,
                device_id_type=pl.DeviceIdType.MESH,
            )
            for k, (src, dst) in enumerate(self.views(source, target))
        ]

        def start():
            for move in made:
                move.start()

        def wait():
            for move in made:
                move.wait()

        return start, wait


def row_ride(array, axis, start, stop):
    views = lambda source, target: [(source.at[pl.ds(start, stop - start)], target)]
    return NeighbourRide(array, axis, (stop - start,) + array.shape[1:], views, 1)


class TradeRide:
    sems = 3

    def __init__(self, array, zh, q, back):
        self.array, self.zh, self.q, self.back = array, zh, q, back
        streams, part, n = array.shape[0], array.shape[-2], array.shape[-1]
        shape = (2, streams, part, n) if back else (streams, 2, part, n)
        self.shape = jax.ShapeDtypeStruct(shape, array.dtype)
        self.partners = [(q,), (zh,), (q, zh)]

    def moves(self, source, target, send, recv):
        zh, q = lax.axis_index(self.zh), lax.axis_index(self.q)
        same = zh == q

        def remote(k, src, dst, at, to_zh, to_q):
            return pltpu.make_async_remote_copy(
                src_ref=src,
                dst_ref=dst,
                send_sem=send(k),
                recv_sem=recv(at),
                device_id={self.zh: to_zh, self.q: to_q},
                device_id_type=pl.DeviceIdType.MESH,
            )

        if self.back:
            outgoing = [remote(j, source.at[:, j], target.at[zh], zh, q, j) for j in range(2)]
            arriving = [remote(j, source.at[:, j], target.at[j], j, q, j) for j in range(2)]
            local = pltpu.make_async_copy(source.at[:, q], target.at[zh], send(2))
            mine = [jnp.logical_and(same, q == j) for j in range(2)]
        else:
            outgoing = [remote(j, source, target.at[:, q], q, j, zh) for j in range(2)]
            arriving = [remote(j, source, target.at[:, j], j, j, zh) for j in range(2)]
            local = pltpu.make_async_copy(source, target.at[:, q], send(2))
            mine = [jnp.logical_and(same, zh == j) for j in range(2)]

        def start():
            for move, own in zip(outgoing, mine):
                pl.when(jnp.logical_not(own))(move.start)
            pl.when(same)(local.start)

        def wait():
            for move, own in zip(outgoing, mine):
                pl.when(jnp.logical_not(own))(move.wait_send)
            for move, own in zip(arriving, mine):
                pl.when(jnp.logical_not(own))(move.wait_recv)
            pl.when(same)(local.wait)

        return start, wait


def once(shape, index):
    return pl.BlockSpec(shape, index, pipeline_mode=pl.Buffered(1))


def by_stream(w):
    return [(w[0], 0), (w[1], 0)] if isinstance(w, (list, tuple)) else [(w, 0), (w, 1)]


def rows_nn_kernel(nb, img, mode, *refs):
    xs, w0, w1 = refs[:nb], refs[nb], refs[nb + 1]
    rest = refs[nb + 2 :]
    depth, tile = xs[0].shape[1], w0.shape[3]
    text = xs[0].shape[0] - img
    y_text = nn(
        jnp.concatenate([x[img:, :] for x in xs], axis=0), w1[:, 0].reshape(depth, tile)
    )
    w_img = w0[:, 0].reshape(depth, tile)
    if mode == "slope":
        sums = rest[2 * nb]
        total = [jnp.zeros((1, tile), F32), jnp.zeros((1, tile), F32)]
    for b in range(nb):
        for stream, rows in ((0, slice(0, img)), (1, slice(img, img + text))):
            y = nn(xs[b][rows, :], w_img) if stream == 0 else y_text[b * text : (b + 1) * text]
            if mode == "plain":
                rest[b][rows, :] = y.astype(BF)
            elif mode == "bias":
                rest[1 + b][rows, :] = (y + rest[0][stream]).astype(BF)
            elif mode == "gelu":
                v = y + rest[0][stream]
                inner = jnp.tanh(GELU_C * (v + 0.044715 * (v * v * v)))
                half = 0.5 * (1.0 + inner)
                rest[1 + b][rows, :] = (v * half).astype(BF)
                rest[1 + nb + b][rows, :] = half + 0.5 * v * (1.0 - inner * inner) * (
                    GELU_C * (1.0 + 3 * 0.044715 * (v * v))
                )
            else:
                y = (y * rest[b][rows, :]).astype(BF)
                rest[nb + b][rows, :] = y
                total[stream] += jnp.sum(y.astype(F32), axis=0, keepdims=True)
    if mode == "slope":
        sums[0] = total[0]
        sums[1] = total[1]


def rows_nn(xs, w, img, mode, bias=None, slopes=(), tile=384, rides=(), cid=None):
    (w0, s0), (w1, s1) = by_stream(w)
    n = w0.shape[3]
    nb, (rows, depth) = len(xs), xs[0].shape
    in_specs = [once((rows, depth), lambda j: (0, 0))] * nb
    in_specs += [
        pl.BlockSpec((4, 1, depth // 4, tile), lambda j, at=at: (0, at, 0, j)) for at in (s0, s1)
    ]
    args = list(xs) + [w0, w1]
    out_tile = pl.BlockSpec((rows, tile), lambda j: (0, j))
    vector = pl.BlockSpec((2, 1, tile), lambda j: (0, 0, j))
    shape = lambda dtype: jax.ShapeDtypeStruct((rows, n), dtype)
    if bias is not None:
        in_specs.append(vector)
        args.append(bias.reshape(2, 1, n))
    in_specs += [out_tile] * len(slopes)
    args += list(slopes)
    out_specs, out_shape = [out_tile] * nb, [shape(BF)] * nb
    if mode == "gelu":
        out_specs, out_shape = out_specs + [out_tile] * nb, out_shape + [shape(F32)] * nb
    if mode == "slope":
        out_specs.append(vector)
        out_shape.append(jax.ShapeDtypeStruct((2, 1, n), F32))
    return launch(
        functools.partial(rows_nn_kernel, nb, img, mode),
        (n // tile,),
        in_specs,
        out_specs,
        out_shape,
        args,
        f"rows_{mode}",
        2 * nb * rows * depth * n,
        rides=rides,
        cid=cid,
    )


def rows_nt_kernel(nb, img, *refs):
    xs, w0, w1, outs = refs[:nb], refs[nb], refs[nb + 1], refs[nb + 2 :]
    text = xs[0].shape[0] - img
    y_text = nt(jnp.concatenate([x[img:, :] for x in xs], axis=0), w1[0, 0])
    w_img = w0[0, 0]
    for b in range(nb):
        outs[b][:img, :] = nt(xs[b][:img, :], w_img).astype(outs[b].dtype)
        outs[b][img:, :] = y_text[b * text : (b + 1) * text].astype(outs[b].dtype)


def rows_nt(xs, w, img, dtypes, rides=(), cid=None):
    nb, (rows, n) = len(xs), xs[0].shape
    (w0, s0), (w1, s1) = by_stream(w)
    quarter = w0.shape[2]
    return launch(
        functools.partial(rows_nt_kernel, nb, img),
        (4,),
        [once((rows, n), lambda j: (0, 0))] * nb
        + [
            pl.BlockSpec((1, 1, quarter, n), lambda j, at=at: (j, at, 0, 0)) for at in (s0, s1)
        ],
        [pl.BlockSpec((rows, quarter), lambda j: (0, j))] * nb,
        [jax.ShapeDtypeStruct((rows, 4 * quarter), t) for t in dtypes],
        list(xs) + [w0, w1],
        "rows_back",
        8 * nb * rows * quarter * n,
        rides=rides,
        cid=cid,
    )


def weight_grad_kernel(nb, img, *refs):
    xs, ys, out = refs[:nb], refs[nb : 2 * nb], refs[2 * nb]
    total = tn(xs[0][:img, :], ys[0][:img, :])
    for b in range(1, nb):
        total += tn(xs[b][:img, :], ys[b][:img, :])
    out[0, 0] = total.astype(BF)
    x_text = jnp.concatenate([x[img:, :] for x in xs], axis=0)
    y_text = jnp.concatenate([y[img:, :] for y in ys], axis=0)
    out[0, 1] = tn(x_text, y_text).astype(BF)


def weight_grad(xs, ys, img, rides=(), cid=None):
    nb, (rows, d), n = len(xs), xs[0].shape, ys[0].shape[1]
    (out,), rode = launch(
        functools.partial(weight_grad_kernel, nb, img),
        (4,),
        [pl.BlockSpec((rows, d // 4), lambda j: (0, j))] * nb
        + [once((rows, n), lambda j: (0, 0))] * nb,
        [pl.BlockSpec((1, 2, d // 4, n), lambda j: (j, 0, 0, 0))],
        [jax.ShapeDtypeStruct((4, 2, d // 4, n), BF)],
        list(xs) + list(ys),
        "weight_grad",
        2 * nb * rows * d * n,
        rides=rides,
        cid=cid,
    )
    return out, rode


def pad_key(position, padded, real):
    return lax.rem(position, padded) >= real


def head_of(refs, img, h):
    cols = slice(h * HEAD_DIM, (h + 1) * HEAD_DIM)
    whole = [r[...] for r in refs]
    return (
        jnp.concatenate([w[:img, cols] for w in whole], axis=0),
        jnp.concatenate([w[img:, cols] for w in whole], axis=0),
    )


def attend_kernel(chunk, img, txt, q0, k0, v0, q1, k1, v1, o0, o1, lse_i, lse_t):
    per = img // chunk
    tp = q0.shape[0] - img
    keys = [head_of((k0, k1), img, h) for h in range(2)]
    vals = [head_of((v0, v1), img, h) for h in range(2)]
    mask = jnp.where(
        pad_key(lax.broadcasted_iota(jnp.int32, (1, 2 * tp), 1), tp, txt), NEG, 0.0
    ).astype(F32)

    def one(q_pair):
        outs, logs = [], []
        for h in range(2):
            q = q_pair[:, h * HEAD_DIM : (h + 1) * HEAD_DIM] * jnp.asarray(SCALE, BF)
            s_i = nt(q, keys[h][0])
            s_t = nt(q, keys[h][1]) + mask
            top = jnp.maximum(
                jnp.max(s_i, axis=1, keepdims=True), jnp.max(s_t, axis=1, keepdims=True)
            )
            p_i = jnp.exp(s_i - top)
            p_t = jnp.exp(s_t - top)
            total = jnp.sum(p_i, axis=1, keepdims=True) + jnp.sum(p_t, axis=1, keepdims=True)
            inv = 1.0 / total
            o = nn((p_i * inv).astype(BF), vals[h][0]) + nn((p_t * inv).astype(BF), vals[h][1])
            outs.append(o.astype(BF))
            logs.append((top + jnp.log(total)).reshape(1, -1))
        return jnp.concatenate(outs, axis=1), logs

    for z, (q_ref, o_ref) in enumerate(((q0, o0), (q1, o1))):

        def step(c, carry, z=z, q_ref=q_ref, o_ref=o_ref):
            r = pl.multiple_of(c * chunk, chunk)
            o, logs = one(q_ref[pl.ds(r, chunk), :])
            o_ref[pl.ds(r, chunk), :] = o
            for h in range(2):
                lse_i[0, h, pl.ds(z * per + c, 1), :] = logs[h]
            return carry

        lax.fori_loop(0, per, step, 0)
    o, logs = one(jnp.concatenate([q0[img:, :], q1[img:, :]], axis=0))
    o0[img:, :] = o[:tp]
    o1[img:, :] = o[tp:]
    for h in range(2):
        lse_t[0, h, 0:1, :] = logs[h]


def attend_back_kernel(
    chunk, img, txt, q0, k0, v0, q1, k1, v1, g0, g1, lse_i, lse_t, d0, d1, sums, dk_i, dv_i, dk_t, dv_t
):
    per = img // chunk
    tp = q0.shape[0] - img
    hp = pl.program_id(0)
    pairs = pl.num_programs(0)
    width = 2 * HEAD_DIM
    keys = [head_of((k0, k1), img, h) for h in range(2)]
    vals = [head_of((v0, v1), img, h) for h in range(2)]
    mask = jnp.where(
        pad_key(lax.broadcasted_iota(jnp.int32, (2 * tp, 1), 0), tp, txt), NEG, 0.0
    ).astype(F32)
    dk_i[...] = jnp.zeros_like(dk_i)
    dv_i[...] = jnp.zeros_like(dv_i)
    dk_t[...] = jnp.zeros_like(dk_t)
    dv_t[...] = jnp.zeros_like(dv_t)

    def one(q_pair, g_pair, logs):
        outs = []
        for h in range(2):
            cols = slice(h * HEAD_DIM, (h + 1) * HEAD_DIM)
            q = q_pair[:, cols] * jnp.asarray(SCALE, BF)
            g = g_pair[:, cols]
            p_i = jnp.exp(nt(keys[h][0], q) - logs[h])
            p_t = jnp.exp(nt(keys[h][1], q) + mask - logs[h])
            dp_i = nt(vals[h][0], g)
            dp_t = nt(vals[h][1], g)
            delta = jnp.sum(p_i * dp_i, axis=0, keepdims=True) + jnp.sum(
                p_t * dp_t, axis=0, keepdims=True
            )
            dv_i[h] += nn(p_i.astype(BF), g)
            dv_t[h] += nn(p_t.astype(BF), g)
            ds_i = (p_i * (dp_i - delta)).astype(BF)
            ds_t = (p_t * (dp_t - delta)).astype(BF)
            dk_i[h] += nn(ds_i, q)
            dk_t[h] += nn(ds_t, q)
            dq = tn(ds_i, keys[h][0]) + tn(ds_t, keys[h][1])
            outs.append((dq * SCALE).astype(BF))
        return jnp.concatenate(outs, axis=1)

    def cols_of(kind):
        return pl.ds(pl.multiple_of((kind * pairs + hp) * width, width), width)

    def column_sum(v):
        return jnp.sum(v.astype(F32), axis=0, keepdims=True)

    q_sum = jnp.zeros((1, width), F32)
    for z, (q_ref, g_ref, d_ref) in enumerate(((q0, g0, d0), (q1, g1, d1))):

        def step(c, total, z=z, q_ref=q_ref, g_ref=g_ref, d_ref=d_ref):
            r = pl.multiple_of(c * chunk, chunk)
            logs = [lse_i[0, h, pl.ds(z * per + c, 1), :] for h in range(2)]
            dq = one(q_ref[pl.ds(r, chunk), :], g_ref[pl.ds(r, chunk), :], logs)
            d_ref[pl.ds(r, chunk), cols_of(0)] = dq
            return total + column_sum(dq)

        q_sum = lax.fori_loop(0, per, step, q_sum)
    logs = [lse_t[0, h, 0:1, :] for h in range(2)]
    dq = one(
        jnp.concatenate([q0[img:, :], q1[img:, :]], axis=0),
        jnp.concatenate([g0[img:, :], g1[img:, :]], axis=0),
        logs,
    )
    d0[img:, cols_of(0)] = dq[:tp]
    d1[img:, cols_of(0)] = dq[tp:]
    sums[0, 0:1] = q_sum
    sums[0, 1:2] = column_sum(dq)
    for kind, image, text in ((1, dk_i, dk_t), (2, dv_i, dv_t)):
        both = jnp.concatenate([image[0].astype(BF), image[1].astype(BF)], axis=1)
        d0[:img, cols_of(kind)] = both[:img]
        d1[:img, cols_of(kind)] = both[img:]
        both_t = jnp.concatenate([text[0].astype(BF), text[1].astype(BF)], axis=1)
        d0[img:, cols_of(kind)] = both_t[:tp]
        d1[img:, cols_of(kind)] = both_t[tp:]
        if kind == 2:
            sums[0, 2:3] = column_sum(both)
            sums[0, 3:4] = column_sum(both_t)


def qkv_specs(rows, pairs):
    width = 2 * HEAD_DIM
    return [
        pl.BlockSpec((rows, width), lambda h, kind=kind: (0, kind * pairs + h)) for kind in range(3)
    ] * 2


def lse_specs(n_chunks, chunk, tp):
    return [
        pl.BlockSpec((1, 2, n_chunks, chunk), lambda h: (h, 0, 0, 0)),
        pl.BlockSpec((1, 2, 1, 2 * tp), lambda h: (h, 0, 0, 0)),
    ]


def attention(near, far, img, txt, chunk, slot, rides=(), cid=None):
    rows, columns = near.shape[0], near.shape[1] // 3
    tp, width = rows - img, 2 * HEAD_DIM
    pairs, n_chunks = columns // width, 2 * img // chunk
    tile = pl.BlockSpec((rows, width), lambda h: (0, h))
    return launch(
        functools.partial(attend_kernel, chunk, img, txt),
        (pairs,),
        qkv_specs(rows, pairs),
        [tile, tile] + lse_specs(n_chunks, chunk, tp),
        [jax.ShapeDtypeStruct((rows, columns), BF)] * 2
        + [
            jax.ShapeDtypeStruct((pairs, 2, n_chunks, chunk), F32),
            jax.ShapeDtypeStruct((pairs, 2, 1, 2 * tp), F32),
        ],
        [near, near, near, far, far, far],
        f"attend_{slot}",
        80 * pairs * rows * rows * HEAD_DIM,
        rides=rides,
        cid=cid,
    )


def attention_back(
    near, far, grad_near, grad_far, lse_i, lse_t, img, txt, chunk, slot, rides=(), cid=None
):
    rows, columns = near.shape[0], near.shape[1] // 3
    tp, width = rows - img, 2 * HEAD_DIM
    pairs, n_chunks = columns // width, 2 * img // chunk
    tile = pl.BlockSpec((rows, width), lambda h: (0, h))
    whole = pl.BlockSpec((rows, 3 * columns), lambda h: (0, 0))
    return launch(
        functools.partial(attend_back_kernel, chunk, img, txt),
        (pairs,),
        qkv_specs(rows, pairs) + [tile, tile] + lse_specs(n_chunks, chunk, tp),
        [whole, whole, pl.BlockSpec((1, 4, width), lambda h: (h, 0, 0))],
        [jax.ShapeDtypeStruct((rows, 3 * columns), BF)] * 2
        + [jax.ShapeDtypeStruct((pairs, 4, width), F32)],
        [near, near, near, far, far, far, grad_near, grad_far, lse_i, lse_t],
        f"attend_back_{slot}",
        200 * pairs * rows * rows * HEAD_DIM,
        scratch=[
            pltpu.VMEM((2, 2 * img, HEAD_DIM), F32),
            pltpu.VMEM((2, 2 * img, HEAD_DIM), F32),
            pltpu.VMEM((2, 2 * tp, HEAD_DIM), F32),
            pltpu.VMEM((2, 2 * tp, HEAD_DIM), F32),
        ],
        rides=rides,
        cid=cid,
    )


class Layout:
    def __init__(self, dp_size, tensor_size):
        dp_bits = dp_size.bit_length() - 1
        t_bits = tensor_size.bit_length() - 1
        self.dp = tuple(f"d{i}" for i in range(dp_bits))
        self.tensor = tuple(f"t{i}" for i in range(t_bits))
        self.names = self.dp + self.tensor
        self.compact = dp_size == 8 and tensor_size == 4
        self.p = self.tensor[-1]
        if self.compact:
            self.y, self.x, self.q = self.dp
            self.zh = self.tensor[0]
            self.upper = ()
        else:
            self.q = self.tensor[-2]
            self.upper = self.tensor[:-2]
        self.rest = tuple(n for n in self.names if n not in (self.p, self.q))

    def my_columns(self, v):
        shards = 2 ** len(self.upper)
        part = v.shape[-1] // (4 * shards)
        v = v.reshape(v.shape[:-1] + (shards, 4, part))
        at = index_of((self.q, self.p))
        v = lax.dynamic_index_in_dim(v, at, v.ndim - 2, keepdims=False)
        return v.reshape(v.shape[:-2] + (shards * part,))

    def all_columns(self, v):
        shards = 2 ** len(self.upper)
        g = gather_bits(v[None], (self.p, self.q))
        g = g.reshape((4,) + v.shape[:-1] + (shards, v.shape[-1] // shards))
        g = jnp.moveaxis(g, 0, -2)
        return g.reshape(v.shape[:-1] + (4 * v.shape[-1],))

    def gather_rows(self, own, end=()):
        pair = after(swap(own, self.p), *end)
        return [[own, swap(own, self.q)], [pair, swap(pair, self.q)]]

    def sum_far(self, w, blocks, img):
        (send, keep), unused = rows_nt([blocks[1][1], blocks[1][0]], w, img, (BF, F32))
        return (keep + swap(send, self.q).astype(F32)).astype(BF)

    def sum_near(self, w, blocks, img, rides=(), cid=None):
        (send, keep), rode = rows_nt([blocks[0][1], blocks[0][0]], w, img, (BF, F32), rides, cid)
        return keep + swap(send, self.q).astype(F32), rode

    def gather_weight(self, w):
        w = lax.all_gather(w, self.dp, axis=1, tiled=True)
        if self.upper:
            w = lax.all_gather(w, self.upper, axis=3, tiled=True)
        return jnp.swapaxes(w.reshape(2, 4, w.shape[1] // 4, -1), 0, 1)

    def trade_shards(self, w, end=()):
        w = w.reshape(w.shape[0], w.shape[1], -1)
        joint = (self.q, self.zh)
        same = lax.axis_index(self.zh) == lax.axis_index(self.q)
        cross = lax.ppermute(w, joint, [(1, 2), (2, 1)])
        second = lax.ppermute(w, joint, [(0, 1), (3, 2), (2, 0), (1, 3)])
        cross, second = after((cross, second), *end)
        first = jnp.where(same, w, cross)
        low = lax.axis_index(self.zh) == 0
        return jnp.concatenate(
            [jnp.where(low, first, second), jnp.where(low, second, first)], axis=1
        )

    def spread_near(self, own):
        return [swap(own[0], self.x), swap(own[1], self.y)]

    def spread_rows(self, own, nears):
        x, y = lax.axis_index(self.x), lax.axis_index(self.y)
        whole = jnp.zeros((4,) + own.shape, BF)
        for stream, far_axis in enumerate((self.y, self.x)):
            mine, near = own[stream], nears[stream]
            both, far = swap(near, far_axis), swap(mine, far_axis)
            dx, dy = (near, far) if stream == 0 else (far, near)
            for block, at in (
                (mine, 2 * y + x),
                (dx, 2 * y + 1 - x),
                (dy, 2 * (1 - y) + x),
                (both, 2 * (1 - y) + 1 - x),
            ):
                whole = lax.dynamic_update_slice(whole, block[None, None], (at, stream, 0, 0))
        return whole

    def spread_rows_async(self, own):
        own = own.reshape(own.shape[0], -1, own.shape[-1])
        return lax.all_gather(own, (self.y, self.x), axis=0, tiled=False)

    def trade_ride(self, array, back=False):
        if back:
            array = array.reshape(2, 2, -1, array.shape[-1])
        return TradeRide(array, self.zh, self.q, back)

    def scatter_generic(self, g, kinds):
        g = jnp.swapaxes(g.astype(F32), 0, 1).reshape(2, 4 * g.shape[2], kinds, -1)
        g = lax.psum_scatter(g, self.dp, scatter_dimension=1, tiled=True)
        if self.upper:
            g = lax.psum_scatter(g, self.upper, scatter_dimension=3, tiled=True)
        return g

    def sum_plane_async(self, g):
        return lax.psum_scatter(g, (self.y, self.x), scatter_dimension=0, tiled=False)

    def plane_rides(self, g):
        g = g.reshape((2, 2) + g.shape[1:])
        shape = (2,) + g.shape[3:]

        def along_x(source, target):
            x = 1 - lax.axis_index(self.x)
            return [(source.at[k, x, 0], target.at[k]) for k in range(2)]

        def along_y(source, target):
            y = 1 - lax.axis_index(self.y)
            return [(source.at[y, k, 1], target.at[k]) for k in range(2)]

        return [
            NeighbourRide(g, self.x, shape, along_x, 2),
            NeighbourRide(g, self.y, shape, along_y, 2),
        ]

    def sum_plane(self, g, arrived):
        x, y = lax.axis_index(self.x), lax.axis_index(self.y)
        pick = lambda v, i, dim: lax.dynamic_index_in_dim(v, i, dim, keepdims=False)
        g = g.reshape((2, 2) + g.shape[1:])
        done = []
        for stream in range(2):
            near, dim, far_axis, far = ((x, 1, self.y, y), (y, 0, self.x, x))[stream]
            v = pick(g[:, :, stream], near, dim).astype(F32) + arrived[stream].astype(F32)
            v = pick(v, far, 0) + swap(pick(v, 1 - far, 0).astype(BF), far_axis).astype(F32)
            done.append(v)
        return jnp.stack(done)

    def trade_sums(self, g, kinds, end=()):
        g = g.reshape(2, 2, -1, g.shape[2])
        zh = lax.axis_index(self.zh)
        joint = (self.q, self.zh)
        first = lax.dynamic_index_in_dim(g, zh, 1, keepdims=False)
        second = lax.dynamic_index_in_dim(g, 1 - zh, 1, keepdims=False)
        cross = lax.ppermute(first.astype(BF), joint, [(1, 2), (2, 1)])
        second = lax.ppermute(second.astype(BF), joint, [(1, 0), (2, 3), (0, 2), (3, 1)])
        cross, second = after((cross, second), *end)
        same = zh == lax.axis_index(self.q)
        total = jnp.where(same, first.astype(F32), cross.astype(F32)) + second.astype(F32)
        return total.reshape(2, total.shape[1], kinds, -1)


def norm_parts(values):
    average = jnp.mean(values, axis=-1, keepdims=True)
    centred = values - average
    variance = jnp.mean(centred * centred, axis=-1, keepdims=True)
    inverse = lax.rsqrt(variance + 1e-06)
    return centred * inverse, inverse


def norm_back(normed, inverse, grad_in):
    first_mean = jnp.mean(grad_in, axis=-1, keepdims=True)
    cross_mean = jnp.mean(grad_in * normed, axis=-1, keepdims=True)
    return inverse * (grad_in - first_mean - normed * cross_mean)


def body(
    lay,
    image_in,
    text_in,
    condition,
    live_slots,
    ada_weight,
    ada_bias,
    qkv_weight,
    qv_bias,
    proj_weight,
    proj_bias,
    up_weight,
    up_bias,
    down_weight,
    down_bias,
    image_grad,
    text_grad,
):
    width = image_in.shape[1]
    part = qkv_weight.shape[2]
    columns = qkv_weight.shape[3]
    img_rows, txt_rows = image_in.shape[0], text_in.shape[0]
    txt_pad = -(-txt_rows // 16) * 16
    group_slots = condition.shape[0]
    dp_index, t_index = index_of(lay.dp), index_of(lay.tensor)
    t_count = 2 ** len(lay.tensor)
    assert group_slots * 2 == t_count
    my_slot = t_index // 2
    dp_up, t_up = lay.dp[::-1], lay.tensor[::-1]

    rows = img_rows + txt_pad
    is_image = lax.broadcasted_iota(jnp.int32, (rows, 1), 0) < img_rows

    def pack(image, text):
        return jnp.concatenate([image, jnp.pad(text, ((0, txt_pad - txt_rows), (0, 0)))], axis=0)

    def spread(per_stream):
        return jnp.where(is_image, per_stream[0], per_stream[1])

    def total(v):
        return jnp.stack([jnp.sum(v[:img_rows], axis=0), jnp.sum(v[img_rows:], axis=0)])

    def flat(blocks):
        return blocks[0] + blocks[1]

    def unflat(v):
        return [list(v[:2]), list(v[2:4])]

    qkv_local = jnp.swapaxes(qkv_weight, 1, 2)
    proj_local = jnp.swapaxes(proj_weight, 1, 2)[:, :, None]
    up_local = up_weight[:, :, None]
    down_local = jnp.swapaxes(down_weight, 1, 2)[:, :, None]
    compact = lay.compact
    if compact:
        qkv_own = lay.trade_shards(qkv_local)
        qkv_near = lay.spread_near(qkv_own)
    else:
        qkv_full, up_full, proj_full, down_full = [
            lay.gather_weight(w) for w in (qkv_local, up_local, proj_local, down_local)
        ]

    cond_all = gather_bits(condition, dp_up).astype(F32)
    silu_all = jax.nn.silu(cond_all).astype(BF)
    silu_mine = lax.dynamic_slice_in_dim(silu_all, dp_index * part, part, 1)
    mod = jnp.einsum("sd,tdkc->stkc", silu_mine, ada_weight, preferred_element_type=F32)
    mod = scatter_bits(mod, lay.dp)
    if compact:
        mod = after(mod, qkv_own)
    mod = gather_bits(mod[None], t_up)
    mod = lax.dynamic_index_in_dim(mod, my_slot, 1, keepdims=False)
    mod = jnp.moveaxis(mod, 0, 2).reshape(2, 6, width) + ada_bias.astype(F32)
    live = lax.dynamic_index_in_dim(live_slots, my_slot, 0, keepdims=False).astype(F32)

    mods = [spread(mod[:, k]) for k in range(6)]
    shift_one, scale_one, gate_one, shift_two, scale_two, gate_two = mods

    inputs = pack(image_in, text_in).astype(F32)
    grad_out = live * pack(image_grad, text_grad).astype(F32)
    grad_two = (gate_two * grad_out).astype(BF)

    first_norm = norm_parts(inputs)
    first_hidden = (first_norm[0] * (1.0 + scale_one) + shift_one).astype(BF)
    if compact:
        first_hidden = after(first_hidden, qkv_near)
    first = lay.gather_rows(first_hidden)
    if compact:
        qkv_full = lay.spread_rows(qkv_own, qkv_near)
    qv = lay.my_columns(qv_bias.astype(F32))
    qkv_bias = jnp.concatenate([qv[:, 0], jnp.zeros_like(qv[:, 0]), qv[:, 1]], axis=1)
    heads_n = qv.shape[2]
    img = img_rows

    def ride(array, start, stop):
        return row_ride(array, lay.p, start, stop)

    def thirds(n):
        return [0] + [n * k // 3 // 16 * 16 for k in (1, 2)] + [n]

    cut = thirds(rows)
    rides = [ride(grad_two, cut[k], cut[k + 1]) for k in range(3)]
    extra = [[], [], []]
    if compact:
        extra = [
            [lay.trade_ride(w.reshape(w.shape[0], part, -1))]
            for w in (proj_local, up_local[:1], up_local[1:])
        ]
    qkv, rode = rows_nn(
        flat(first), qkv_full, img, "bias", bias=qkv_bias, rides=[rides[0]] + extra[0], cid=1
    )
    grad_two_pair = rode[:1]
    qkv = unflat(qkv)
    chunk = min(256, img_rows)
    if compact:
        proj_full = lay.spread_rows_async(rode[1])
    other, rode = attention(
        qkv[0][1], qkv[1][1], img, txt_rows, chunk, 1, rides=[rides[1]] + extra[1], cid=2
    )
    grad_two_pair += rode[:1]
    if compact:
        up_full = [lay.spread_rows_async(rode[1])]
        qkv, other = after((qkv, other), proj_full)
    mine, rode = attention(
        qkv[0][0], qkv[1][0], img, txt_rows, chunk, 0, rides=[rides[2]] + extra[2], cid=10
    )
    grad_two_pair = jnp.concatenate(grad_two_pair + rode[:1], axis=0)
    heads_out = [[mine[z], other[z]] for z in range(2)]
    grad_two_blocks = [
        [grad_two, swap(grad_two, lay.q)], [grad_two_pair, swap(grad_two_pair, lay.q)]
    ]
    if compact:
        up_full.append(lay.spread_rows_async(rode[1]))
        down_local = after(down_local, mine)

    far = swap(lay.sum_far(proj_full, heads_out, img), lay.p)
    near, unused = lay.sum_near(proj_full, heads_out, img)
    branch_one = near + far.astype(F32) + spread(proj_bias.astype(F32))
    middle = inputs + gate_one * branch_one
    second_norm = norm_parts(middle)
    second_hidden = (second_norm[0] * (1.0 + scale_two) + shift_two).astype(BF)
    if compact:
        down_own = lay.trade_shards(down_local, (second_hidden,))
        down_full = lay.spread_rows_async(down_own)
    second = lay.gather_rows(second_hidden)
    up_mine = lay.my_columns(up_bias.astype(F32))
    up_n = up_mine.shape[1]
    up_out, unused = rows_nn(flat(second), up_full, img, "gelu", bias=up_mine)
    activated, slopes = up_out[:4], up_out[4:]
    far = lay.sum_far(down_full, unflat(activated), img)
    cut = rows * 21 // 37 // 16 * 16
    back_out, rode = rows_nn(
        flat(grad_two_blocks), down_full, img, "slope", slopes=slopes, rides=[ride(far, 0, cut)], cid=3
    )
    grad_inner, up_part = back_out[:4], back_out[4].reshape(2, up_n)
    down_grads, rode_two = weight_grad(
        after(flat(grad_two_blocks), grad_inner), activated, img, rides=[ride(far, cut, rows)], cid=4
    )
    far = jnp.concatenate(rode + rode_two, axis=0)
    if compact:
        down_plane = lay.sum_plane_async(down_grads)
    far_two = lay.sum_far(up_full, after(unflat(grad_inner), down_grads), img)
    cut, cut_two = rows * 11 // 37 // 16 * 16, rows * 22 // 37 // 16 * 16
    near_two, rode = lay.sum_near(up_full, unflat(grad_inner), img, [ride(far_two, 0, cut)], 5)
    up_grads, rode_two = weight_grad(
        after(flat(second), near_two), grad_inner, img, rides=[ride(far_two, cut_two, rows)], cid=6
    )
    if compact:
        up_plane = lay.sum_plane_async(up_grads)
    near, rode_three = lay.sum_near(
        down_full, after(unflat(activated), up_grads), img, [ride(far_two, cut, cut_two)], 7
    )
    far_two = jnp.concatenate(rode + rode_three + rode_two, axis=0)
    branch_two = near + far.astype(F32) + spread(down_bias.astype(F32))
    outputs = (live * (middle + gate_two * branch_two)).astype(BF)
    grad_hidden_two = near_two + far_two.astype(F32)
    grad_middle = grad_out + norm_back(
        second_norm[0], second_norm[1], grad_hidden_two * (1.0 + scale_two)
    )
    grad_one = (gate_one * grad_middle).astype(BF)
    if compact:
        grad_one = after(grad_one, down_plane)
    grad_one_blocks = lay.gather_rows(grad_one)
    grad_heads = unflat(rows_nn(flat(grad_one_blocks), proj_full, img, "plain")[0])

    def back(c, saved, heads, rides, cid):
        return attention_back(
            qkv[0][c],
            qkv[1][c],
            heads[0][c],
            heads[1][c],
            saved[2],
            saved[3],
            img,
            txt_rows,
            chunk,
            c,
            rides,
            cid,
        )

    grad_other, down_sums = back(
        1, other, grad_heads, [lay.trade_ride(down_plane, True)] if compact else (), 11
    )
    proj_grads, unused = weight_grad(
        after(flat(grad_one_blocks), grad_other), flat(heads_out), img
    )
    if compact:
        proj_plane = lay.sum_plane_async(proj_grads)
    grad_mine, up_sums = back(
        0,
        mine,
        after(grad_heads, proj_grads),
        [lay.trade_ride(up_plane, True)] if compact else (),
        12,
    )
    grad_qkv = [[grad_mine[z], grad_other[z]] for z in range(2)]
    far = lay.sum_far(qkv_full, grad_qkv, img)
    cut = rows * 20 // 37 // 16 * 16
    qkv_grads, rode = weight_grad(
        flat(first), flat(grad_qkv), img, rides=[ride(far, 0, cut)], cid=8
    )
    rides = [ride(far, cut, rows)]
    if compact:
        rides += lay.plane_rides(qkv_grads) + [lay.trade_ride(proj_plane, True)]
    near, rode_two = lay.sum_near(qkv_full, after(grad_qkv, qkv_grads), img, rides, 9)
    far = jnp.concatenate(rode + rode_two[:1], axis=0)
    if compact:
        down_grad, up_grad, proj_grad = [
            (v[0].astype(F32) + v[1].astype(F32))[:, :, None]
            for v in (down_sums[0], up_sums[0], rode_two[3])
        ]
        qkv_plane = lay.sum_plane(qkv_grads, rode_two[1:3])
    else:
        down_grad, up_grad, proj_grad = [
            lay.scatter_generic(g, 1) for g in (down_grads, up_grads, proj_grads)
        ]
        qkv_grad = lay.scatter_generic(qkv_grads, 3)
    grad_hidden_one = near + far.astype(F32)
    input_grads = grad_middle + norm_back(
        first_norm[0], first_norm[1], grad_hidden_one * (1.0 + scale_one)
    )

    grad_mod = jnp.stack(
        [
            total(grad_hidden_one),
            total(grad_hidden_one * first_norm[0]),
            total(branch_one * grad_middle),
            total(grad_hidden_two),
            total(grad_hidden_two * second_norm[0]),
            total(branch_two * grad_out),
        ],
        axis=1,
    )
    grad_mod = sum_bits(grad_mod, (lay.p,))
    grad_mod = gather_bits(grad_mod[None], t_up[1:])
    if compact:
        qkv_grad = lay.trade_sums(after(qkv_plane, grad_mod), 3)
    down_grad = jnp.swapaxes(down_grad[:, :, 0], 1, 2)
    proj_grad = jnp.swapaxes(proj_grad[:, :, 0], 1, 2)
    up_grad = up_grad[:, :, 0]
    qkv_grad = jnp.swapaxes(qkv_grad, 1, 2)
    grad_mod = lax.dynamic_slice_in_dim(grad_mod, t_index * columns, columns, 3)
    grad_mod = gather_bits(grad_mod, dp_up)
    high = lax.Precision.HIGHEST
    ada_grad = jnp.einsum("sd,stkc->tdkc", silu_mine.astype(F32), grad_mod, precision=high)
    cond_terms = jnp.einsum("stkc,tdkc->sd", grad_mod, ada_weight.astype(F32), precision=high)
    cond_terms = gather_bits(sum_bits(cond_terms, t_up)[None], dp_up)
    cond_terms = lax.dynamic_slice_in_dim(cond_terms, dp_index * group_slots, group_slots, 1)
    cond_terms = jnp.swapaxes(cond_terms, 0, 1).reshape(group_slots, width)
    cond_terms = lax.dynamic_slice_in_dim(cond_terms, t_index * columns, columns, 1)
    cond_slice = lax.dynamic_slice_in_dim(condition.astype(F32), t_index * columns, columns, 1)
    unused, silu_pull = jax.vjp(jax.nn.silu, cond_slice)
    condition_grad = silu_pull(cond_terms)[0]
    ada_bias_grad = gather_bits(jnp.sum(grad_mod, axis=0)[None], t_up)
    ada_bias_grad = jnp.moveaxis(ada_bias_grad, 0, 2).reshape(2, 6, width)

    own_part = sum_bits(
        jnp.stack([total(grad_one.astype(F32)), total(grad_two.astype(F32))]), (lay.p, lay.q)
    )
    sums = grad_mine[2] + grad_other[2]
    pairs = sums.shape[0]
    qv_part = jnp.transpose(sums.reshape(pairs, 2, 2, -1), (2, 1, 0, 3)).reshape(2, 2, heads_n)
    if compact:
        qv_part = after(qv_part, near)
    packed = jnp.concatenate([qv_part.reshape(-1), up_part.reshape(-1), own_part.reshape(-1)])
    packed = sum_bits(packed.reshape(-1, 128), lay.rest).reshape(-1)
    cut_one, cut_two = qv_part.size, qv_part.size + up_part.size
    qv_bias_grad = lay.all_columns(packed[:cut_one].reshape(qv_part.shape))
    up_bias_grad = lay.all_columns(packed[cut_one:cut_two].reshape(up_part.shape))
    own_part = packed[cut_two:].reshape(own_part.shape)
    return (
        outputs[:img_rows],
        outputs[img_rows : img_rows + txt_rows],
        input_grads[:img_rows],
        input_grads[img_rows : img_rows + txt_rows],
        condition_grad,
        ada_grad,
        ada_bias_grad,
        qkv_grad,
        qv_bias_grad,
        proj_grad,
        own_part[0],
        up_grad,
        up_bias_grad,
        down_grad,
        own_part[1],
    )


def solution(mesh):
    lay = Layout(mesh.shape["dp"], mesh.shape["tensor"])
    bits = Mesh(mesh.devices.reshape((2,) * len(lay.names)), lay.names)
    dp, tensor, every = lay.dp, lay.tensor, lay.names
    in_specs = (
        P(every, None),
        P(every, None),
        P(dp, None),
        P(dp),
        P(None, dp, None, tensor),
        P(),
        P(None, None, dp, tensor),
        P(),
        P(None, tensor, dp),
        P(),
        P(None, dp, tensor),
        P(),
        P(None, tensor, dp),
        P(),
        P(every, None),
        P(every, None),
    )
    out_specs = (
        P(every, None),
        P(every, None),
        P(every, None),
        P(every, None),
        P(dp, tensor),
        P(None, dp, None, tensor),
        P(),
        P(None, None, dp, tensor),
        P(),
        P(None, tensor, dp),
        P(),
        P(None, dp, tensor),
        P(),
        P(None, tensor, dp),
        P(),
    )
    return jax.shard_map(
        functools.partial(body, lay), mesh=bits, in_specs=in_specs, out_specs=out_specs, check_vma=False
    )
```

time: 1360 us -> 1070 us (0.79)
  Pallas kernels: 125 us -> 477 us
  waiting for transfers between devices: 595 us -> 314 us
  matrix products: 192 us -> 6.06 us
  starting transfers between devices: 258 us -> 86 us
  local copies, waits for them, and re-layouts: 77.6 us -> 61.1 us
    pallas_call x2 -> x20, Pallas kernels: 125 us -> 477 us  [the longest x12 386 us: launch(): pl.pallas_call(body, grid=grid, in_specs=list(in_specs) + [anywhere] * n_...]
    ppermute x117 -> x57, waiting for transfers between devices: 481 us -> 264 us  [swap(): return lax.ppermute(v, axis, [(0, 1), (1, 0)])]
    dot_general x32 -> x0, matrix products: 186 us -> none  [the longest x8 73 us: dot32(): return jnp.dot(a, b, preferred_element_type=F32)]
    ppermute x117 -> x57, starting transfers between devices: 211 us -> 64.8 us  [swap(): return lax.ppermute(v, axis, [(0, 1), (1, 0)])]
    ppermute x16 -> x6, waiting for transfers between devices: 114 us -> 25.5 us  [the longest x1 25.5 us: trade_sums(): lax.ppermute(second.astype(BF), joint, [(1, 0), (2, 3), (0, 2), (3, 1)])]
    mul x0 -> x4, other arithmetic: none -> 28.4 us  [the longest x1 9.21 us: body(): branch_two * grad_out]
    ppermute x16 -> x6, starting transfers between devices: 46.8 us -> 20.2 us  [the longest x2 12.6 us: trade_shards(): cross = lax.ppermute(w, joint, [(1, 2), (2, 1)])]
    all_gather x0 -> x4, waiting for transfers between devices: none -> 24 us  [spread_rows_async(): return lax.all_gather(own, (self.y, self.x), axis=0, tiled=False)]
  transfers between devices with their start and end apart: 133 -> 70, of which waited for: 52 -> 38; matrix products, arithmetic and copies ran while one was open for 21% -> 12% of each run, Pallas kernels for 4% -> 37%
where the time goes in v2:
time: 1070 us; the launch traced here: 1060 us
  Pallas kernels  477 us (45%)
  waiting for transfers between devices  314 us (29%)
  other arithmetic  98.2 us (9%)
  starting transfers between devices  86 us (8%)
  local copies, waits for them, and re-layouts  61.1 us (6%)
  between operations  16.7 us (2%)
    pallas_call x12, Pallas kernels, launch(): pl.pallas_call(body, grid=grid, in_specs=list(in_specs) + [anywhere] * n_...  386 us
    ppermute x57, waiting for transfers between devices, swap(): return lax.ppermute(v, axis, [(0, 1), (1, 0)])  264 us
    pallas_call x8, Pallas kernels, launch(): pl.pallas_call(kernel, grid=grid, in_specs=in_specs, out_specs=out_specs,...  91.3 us
    ppermute x57, starting transfers between devices, swap(): return lax.ppermute(v, axis, [(0, 1), (1, 0)])  64.8 us
    unnamed x189, local copies, waits for them, and re-layouts  31.6 us
    ppermute x1, waiting for transfers between devices, trade_sums(): lax.ppermute(second.astype(BF), joint, [(1, 0), (2, 3), (0, 2), (3, 1)])  25.5 us
    all_gather x4, waiting for transfers between devices, spread_rows_async(): return lax.all_gather(own, (self.y, self.x), axis=0, tiled=False)  24 us
  transfers between devices with their start and end apart: 70, of which 38 were waited for; matrix products, arithmetic and copies ran while one was open for 12% of the time, Pallas kernels for 37%

profile of v2, /device:TPU:0, one launch (start us, length us, event | category | flops | bytes accessed | tf_op | source)
XLA Modules:
  0.0 1059.2 jit_solution(4205998751750295722)
XLA Ops:
  9.6 4.0 collective-permute-start.7
  33.1 2.9 collective-permute-done.4
  40.3 12.9 %collective-permute-done.8 = f32[1,2,2,6,384]{4,1,3,2,0:T(2,128)S(1)} collective-permute-done((f32[1,2,2,6,384]{4,1,3,2,0:T(2,128)S(1)}, f32[1,2,2,6,384]{4,1,3,2,0:T(2,128)S(1)}, u32[]{:S(2)}, u32[]{:S(2)}) %collective-permute-start.8) | collective-permute-done | bytes 36896 | tf_op jit(solution)/shard_map/ppermute | solution.py:19
  53.3 2.8 collective-permute-start.9
  56.1 2.5 collective-permute-done.9
  64.8 6.2 fusion.59
  71.5 12.0 %collective-permute-done.11 = bf16[384,1152]{1,0:T(8,128)(2,1)S(1)} collective-permute-done((bf16[384,1152]{1,0:T(8,128)(2,1)S(1)}, bf16[384,1152]{1,0:T(8,128)(2,1)S(1)}, u32[]{:S(2)}, u32[]{:S(2)}) %collective-permute-start.11) | collective-permute-done | bytes 884768 | tf_op jit(solution)/shard_map/ppermute | solution.py:19
  89.3 13.2 %collective-permute-done.15 = bf16[384,1152]{1,0:T(8,128)(2,1)S(1)} collective-permute-done((bf16[384,1152]{1,0:T(8,128)(2,1)S(1)}, bf16[384,1152]{1,0:T(8,128)(2,1)S(1)}, u32[]{:S(2)}, u32[]{:S(2)}) %collective-permute-start.15) | collective-permute-done | bytes 884768 | tf_op jit(solution)/shard_map/ppermute | solution.py:19
  104.1 15.1 %collective-permute-done.16 = bf16[384,1152]{1,0:T(8,128)(2,1)S(1)} collective-permute-done((bf16[384,1152]{1,0:T(8,128)(2,1)S(1)}, bf16[384,1152]{1,0:T(8,128)(2,1)S(1)}, u32[]{:S(2)}, u32[]{:S(2)}) %collective-permute-start.16) | collective-permute-done | bytes 884768 | tf_op jit(solution)/shard_map/ppermute | solution.py:19
  119.4 5.1 collective-permute-done.13.refs_2_
  125.8 2.5 collective-permute-done.14.refs_3_
  129.7 29.9 %rows_bias_1.1 = (bf16[592,1152]{1,0:T(8,128)(2,1)}, bf16[592,1152]{1,0:T(8,128)(2,1)}, bf16[592,1152]{1,0:T(8,128)(2,1)}, bf16[592,1152]{1,0:T(8,128)(2,1)}, bf...) custom-call(bf16[592,1536]{1,0:T(8,128)(2,1)} %copy-done.70, bf16[592,1536]{1,0:T(8,128)(2,1)} %copy-done.89, ...), custom_call_target="tpu_custom_call" | custom-call | flops 8380219392 | bytes 16367616 | tf_op jit(solution)/shard_map/rows_bias_1/pallas_call | solution.py:125
  161.9 30.1 %attend_1_2.1 = (bf16[592,384]{1,0:T(8,128)(2,1)S(1)}, bf16[592,384]{1,0:T(8,128)(2,1)S(1)}, f32[3,2,4,256]{3,2,1,0:T(4,128)S(1)}, f32[3,2,1,160]{3,2,1,0:T(1,12...) custom-call(bf16[592,1152]{1,0:T(8,128)(2,1)} %get-tuple-element.202.refs_0_.refs_1_.refs_2_, ...), custom_call_target="tpu_custom_call" | custom-call | flops 5383127040 | bytes 10513920 | tf_op jit(solution)/shard_map/attend_1_2/pallas_call | solution.py:125
  193.0 3.8 all-gather.6.cloned.1.call-done.refs_2_.refs_3_.refs_4_.refs_5_
  197.9 32.2 %attend_0_10.1 = (bf16[592,384]{1,0:T(8,128)(2,1)S(1)}, bf16[592,384]{1,0:T(8,128)(2,1)S(1)}, f32[3,2,4,256]{3,2,1,0:T(4,128)S(1)}, f32[3,2,1,160]{3,2,1,0:T(1,1...) custom-call(bf16[592,1152]{1,0:T(8,128)(2,1)} %get-tuple-element.140.refs_0_.refs_1_.refs_2_, ...), custom_call_target="tpu_custom_call" | custom-call | flops 5383127040 | bytes 10513920 | tf_op jit(solution)/shard_map/attend_0_10/pallas_call | solution.py:125
  230.1 5.9 rows_back.6
  236.8 6.1 rows_back.5
  248.2 11.1 %collective-permute-start.27 = (bf16[2,192,1536]{2,1,0:T(8,128)(2,1)S(1)}, bf16[2,192,1536]{2,1,0:T(8,128)(2,1)S(1)}, u32[]{:S(2)}, u32[]{:S(2)}) collective-permute-start(bf16[2,192,1536]{2,1,0:T(8,128)(2,1)S(1)} %bitcast.208), channel_id=1, source_target_pairs={{2,4},{4,2},{3,5},{5,3},{10,12},{12,10},{11,13},{13,11},{18,20},{2... | collective-permute-start | bytes 3538952 | tf_op jit(solution)/shard_map/ppermute | solution.py:626
  259.3 53.3 %collective-permute-done.21 = bf16[592,1536]{1,0:T(8,128)(2,1)S(1)} collective-permute-done((bf16[592,1536]{1,0:T(8,128)(2,1)S(1)}, bf16[592,1536]{1,0:T(8,128)(2,1)S(1)}, u32[]{:S(2)}, u32[]{:S(2)}) %collective-permute-start.21) | collective-permute-done | bytes 1818656 | tf_op jit(solution)/shard_map/ppermute | solution.py:19
  314.9 2.4 add_convert_fusion.3.refs_0_
  319.3 41.1 %collective-permute-done.23.refs_2_ = bf16[592,1536]{1,0:T(8,128)(2,1)} collective-permute-done((bf16[592,1536]{1,0:T(8,128)(2,1)}, bf16[592,1536]{1,0:T(8,128)(2,1)}, u32[]{:S(2)}, u32[]{:S(2)}) %collective-permute-start.23) | collective-permute-done | bytes 1818656 | tf_op jit(solution)/shard_map/ppermute | solution.py:19
  361.1 3.4 collective-permute-done.24.refs_3_
  364.6 28.4 %rows_gelu.1 = (bf16[592,1536]{1,0:T(8,128)(2,1)S(1)}, bf16[592,1536]{1,0:T(8,128)(2,1)}, bf16[592,1536]{1,0:T(8,128)(2,1)}, bf16[592,1536]{1,0:T(8,128)(2,1)}, ...) custom-call(bf16[592,1536]{1,0:T(8,128)(2,1)} %add_convert_fusion.3.refs_0_, ...), custom_call_target="tpu_custom_call" | custom-call | flops 11173625856 | bytes 21823488 | tf_op jit(solution)/shard_map/rows_gelu/pallas_call | solution.py:77
  394.2 20.1 %all-gather.12.cloned.1.call-done = bf16[8,384,1536]{2,1,0:T(8,128)(2,1)} async-done(((bf16[2,384,1536]{2,1,0:T(8,128)(2,1)}), bf16[8,384,1536]{2,1,0:T(8,128)(2,1)}) %all-gather.12.cloned.1.call-update) | async-done | bytes 9437200 | tf_op jit(solution)/shard_map/all_gather | solution.py:656
  414.3 12.6 %rows_back.7 = (bf16[592,1536]{1,0:T(8,128)(2,1)S(1)}, f32[592,1536]{1,0:T(8,128)}) custom-call(bf16[592,1536]{1,0:T(8,128)(2,1)} %get-tuple-element.154.refs_0_.refs_7_, bf16[592,1536]{1,0:T(8,128)(2,1)} %get-tuple-element.153.refs_1_.refs_6_, bf16[4,2,384,1536]{3,2,1,0:T(8,128)(2,1)} %bitcast.193, bf16[4,2,384,1536]{3,2,1,0:T(8,128)(2,1)} %bitcast.194), custom_call_target="tpu_custom_call" | custom-call | flops 5586812928 | bytes 10911744 | tf_op jit(solution)/shard_map/rows_back/pallas_call | solution.py:77
  434.5 31.4 %rows_slope_3.1 = (bf16[592,1536]{1,0:T(8,128)(2,1)}, bf16[592,1536]{1,0:T(8,128)(2,1)}, bf16[592,1536]{1,0:T(8,128)(2,1)}, bf16[592,1536]{1,0:T(8,128)(2,1)}, f...) custom-call(bf16[592,1536]{1,0:T(8,128)(2,1)} %get-tuple-element.173.refs_7_.refs_6_.refs_0_, ...), custom_call_target="tpu_custom_call" | custom-call | flops 11173625856 | bytes 21823488 | tf_op jit(solution)/shard_map/rows_slope_3/pallas_call | solution.py:125
  466.9 24.2 %weight_grad_4.1 = (bf16[4,2,384,1536]{3,2,1,0:T(8,128)(2,1)}, bf16[256,1536]{1,0:T(8,128)(2,1)S(1)}) custom-call(bf16[592,1536]{1,0:T(8,128)(2,1)} %get-tuple-element.173.refs_7_.refs_6_.refs_0_, bf16[592,1536]{1,0:T(8,128)(2,1)} %collective-permute-done.25.refs_1_, bf16[592,1536]{1,0:T(8,128)(2,1)} %copy-done.66, bf16[592,1536]{1,0:T(8,128)(2,1)} %copy-done.71, ...), custom_call_target="tpu_custom_call" | custom-call | flops 11173625856 | bytes 21823488 | tf_op jit(solution)/shard_map/weight_grad_4/pallas_call | solution.py:125
  492.4 12.8 %rows_back.8 = (bf16[592,1536]{1,0:T(8,128)(2,1)S(1)}, f32[592,1536]{1,0:T(8,128)}) custom-call(bf16[592,1536]{1,0:T(8,128)(2,1)} %get-tuple-element.178.refs_0_.refs_7_, bf16[592,1536]{1,0:T(8,128)(2,1)} %get-tuple-element.179.refs_1_.refs_6_, bf16[4,1,384,1536]{3,2,1,0:T(8,128)(2,1)} %all-gather.8.cloned.1.call-done.refs_4_.refs_2_, ...), custom_call_target="tpu_custom_call" | custom-call | flops 5586812928 | bytes 10911744 | tf_op jit(solution)/shard_map/rows_back/pallas_call | solution.py:77
  505.3 3.8 collective-permute-done.30
  509.0 3.8 add_convert_fusion.1.refs_4_.refs_8_
  512.8 18.8 %rows_back_5.1 = (bf16[592,1536]{1,0:T(8,128)(2,1)}, f32[592,1536]{1,0:T(8,128)}, bf16[176,1536]{1,0:T(8,128)(2,1)S(1)}) custom-call(bf16[592,1536]{1,0:T(8,128)(2,1)} %get-tuple-element.169.refs_0_.refs_5_, bf16[592,1536]{1,0:T(8,128)(2,1)} %get-tuple-element.170.refs_1_.refs_4_, bf16[4,1,384,1536]{3,2,1,0:T(8,128)(2,1)} %all-gather.8.cloned.1.call-done.refs_4_.refs_2_, ...), custom_call_target="tpu_custom_call" | custom-call | flops 5586812928 | bytes 10911744 | tf_op jit(solution)/shard_map/rows_back_5/pallas_call | solution.py:125
  532.4 4.0 collective-permute-done.31
  536.4 4.6 convert_add_fusion.4
  541.0 24.0 %weight_grad_6.1 = (bf16[4,2,384,1536]{3,2,1,0:T(8,128)(2,1)}, bf16[240,1536]{1,0:T(8,128)(2,1)S(1)}) custom-call(bf16[592,1536]{1,0:T(8,128)(2,1)} %add_convert_fusion.3.refs_0_, bf16[592,1536]{1,0:T(8,128)(2,1)} %collective-permute-done.22.refs_1_, bf16[592,1536]{1,0:T(8,128)(2,1)} %collective-permute-done.23.refs_2_, ...), custom_call_target="tpu_custom_call" | custom-call | flops 11173625856 | bytes 21823488 | tf_op jit(solution)/shard_map/weight_grad_6/pallas_call | solution.py:125
  566.6 18.0 %rows_back_7.1 = (bf16[592,1536]{1,0:T(8,128)(2,1)}, f32[592,1536]{1,0:T(8,128)}, bf16[176,1536]{1,0:T(8,128)(2,1)S(1)}) custom-call(bf16[592,1536]{1,0:T(8,128)(2,1)} %get-tuple-element.189.refs_5_.refs_0_, bf16[592,1536]{1,0:T(8,128)(2,1)} %copy-done.1, bf16[4,2,384,1536]{3,2,1,0:T(8,128)(2,1)} %bitcast.197, bf16[4,2,384,1536]{3,2,1,0:T(8,128)(2,1)} %bitcast.198, ...), custom_call_target="tpu_custom_call" | custom-call | flops 5586812928 | bytes 10911744 | tf_op jit(solution)/shard_map/rows_back_7/pallas_call | solution.py:125
  584.8 5.7 fusion.23
  594.9 7.2 fusion.42
  602.1 9.2 fusion.21
  612.9 40.8 %collective-permute-done.34.refs_2_ = bf16[592,1536]{1,0:T(8,128)(2,1)} collective-permute-done((bf16[592,1536]{1,0:T(8,128)(2,1)}, bf16[592,1536]{1,0:T(8,128)(2,1)}, u32[]{:S(2)}, u32[]{:S(2)}) %collective-permute-start.34) | collective-permute-done | bytes 1818656 | tf_op jit(solution)/shard_map/ppermute | solution.py:19
  661.8 8.0 rows_plain.1
  674.9 46.0 %attend_back_1_11.1 = (bf16[592,1152]{1,0:T(8,128)(2,1)}, bf16[592,1152]{1,0:T(8,128)(2,1)}, f32[3,4,128]{2,1,0:T(4,128)S(1)}, bf16[2,2,192,1536]{3,2,1,0:T(8,128)(2,1)}) custom-call(bf16[592,1152]{1,0:T(8,128)(2,1)} %get-tuple-element.202.refs_0_.refs_1_.refs_2_, bf16[592,1152]{1,0:T(8,128)(2,1)} %get-tuple-element.202.refs_0_.refs_1_.refs_2_, ...), custom_call_target="tpu_custom_call" | custom-call | flops 13457817600 | bytes 26284800 | tf_op jit(solution)/shard_map/attend_back_1_11/pallas_call | solution.py:125
  721.0 7.7 weight_grad.1
  730.8 57.9 %attend_back_0_12.1 = (bf16[592,1152]{1,0:T(8,128)(2,1)}, bf16[592,1152]{1,0:T(8,128)(2,1)}, f32[3,4,128]{2,1,0:T(4,128)S(1)}, bf16[2,2,192,1536]{3,2,1,0:T(8,128)(2,1)}) custom-call(bf16[592,1152]{1,0:T(8,128)(2,1)} %get-tuple-element.140.refs_0_.refs_1_.refs_2_, bf16[592,1152]{1,0:T(8,128)(2,1)} %get-tuple-element.140.refs_0_.refs_1_.refs_2_, ...), custom_call_target="tpu_custom_call" | custom-call | flops 13457817600 | bytes 26284800 | tf_op jit(solution)/shard_map/attend_back_0_12/pallas_call | solution.py:125
  788.7 9.9 rows_back.9
  798.6 12.5 %collective-permute-start.36 = (bf16[592,1536]{1,0:T(8,128)(2,1)}, bf16[592,1536]{1,0:T(8,128)(2,1)S(1)}, u32[]{:S(2)}, u32[]{:S(2)}) collective-permute-start(bf16[592,1536]{1,0:T(8,128)(2,1)} %get-tuple-element.218), channel_id=1, source_target_pairs={{0,4},{4,0},{1,5},{5,1},{2,6},{6,2},{3,7},{7,3},{8,12},{12,8},{9,1... | collective-permute-start | bytes 5455880 | tf_op jit(solution)/shard_map/ppermute | solution.py:19
  821.7 29.1 %weight_grad_8.1 = (bf16[4,2,384,1152]{3,2,1,0:T(8,128)(2,1)}, bf16[320,1536]{1,0:T(8,128)(2,1)S(1)}) custom-call(bf16[592,1536]{1,0:T(8,128)(2,1)} %copy-done.70, bf16[592,1536]{1,0:T(8,128)(2,1)} %copy-done.89, bf16[592,1536]{1,0:T(8,128)(2,1)} %copy-done.88, bf16[592,1536]{1,0:T(8,128)(2,1)} %copy-done.90, ...), custom_call_target="tpu_custom_call" | custom-call | flops 8380219392 | bytes 16367616 | tf_op jit(solution)/shard_map/weight_grad_8/pallas_call | solution.py:125
  850.8 6.6 fusion.64
  858.4 44.5 %rows_back_9.1 = (bf16[592,1536]{1,0:T(8,128)(2,1)}, f32[592,1536]{1,0:T(8,128)}, bf16[272,1536]{1,0:T(8,128)(2,1)S(1)}, bf16[2,384,1152]{2,1,0:T(8,128)(2,1)}, ...) custom-call(bf16[592,1152]{1,0:T(8,128)(2,1)} %get-tuple-element.220.refs_5_.refs_0_, ...), custom_call_target="tpu_custom_call" | custom-call | flops 4190109696 | bytes 8183808 | tf_op jit(solution)/shard_map/rows_back_9/pallas_call | solution.py:125
  910.7 16.3 %collective-permute-done.50 = bf16[384,1152]{1,0:T(8,128)(2,1)} collective-permute-done((bf16[384,1152]{1,0:T(8,128)(2,1)}, bf16[384,1152]{1,0:T(8,128)(2,1)}, u32[]{:S(2)}, u32[]{:S(2)}) %collective-permute-start.50) | collective-permute-done | bytes 884768 | tf_op jit(solution)/shard_map/ppermute | solution.py:19
  936.7 3.5 add_bitcast_fusion.1
  941.1 25.5 %collective-permute-done.53 = bf16[2,192,1152]{2,1,0:T(8,128)(2,1)} collective-permute-done((bf16[2,192,1152]{2,1,0:T(8,128)(2,1)}, bf16[2,192,1152]{2,1,0:T(8,128)(2,1)}, u32[]{:S(2)}, u32[]{:S(2)}) %collective-permute-start.53) | collective-permute-done | bytes 884768 | tf_op jit(solution)/shard_map/ppermute | solution.py:709
  966.6 3.0 fusion.28
  969.5 3.9 reshape.234
  973.5 3.1 copy.128
  976.7 6.3 fusion.2
  987.3 4.3 fusion.11
  995.9 10.1 collective-permute-start.58
  1006.1 3.0 collective-permute-start.39
  1019.0 3.6 collective-permute-done.41
  1024.3 3.7 collective-permute-done.42
  1031.6 4.2 convolution_bitcast_fusion
  1036.6 3.9 collective-permute-done.44
  1042.7 3.6 collective-permute-done.49
  1048.2 2.5 collective-permute-done.47
  (481 shorter events, 152.0 us)
Async XLA Ops:
  7.2 189.6 %all-gather.6.cloned.1.call-start = ((), (), s32[]{:S(2)}) async-start(), calls=%async_computation.3 | async-start | bytes 2949120 | tf_op jit(solution)/shard_map/all_gather | solution.py:656
  9.6 49.4 %collective-permute-start.7 = (bf16[2,192,1152]{2,1,0:T(8,128)(2,1)}, bf16[2,192,1152]{2,1,0:T(8,128)(2,1)}, u32[]{:S(2)}, u32[]{:S(2)}) collective-permute-start(bf16[2,192,1152]{2,1,0:T(8,128)(2,1)} %bitcast.92), channel_id=1, source_target_pairs={{0,2},{6,4},{4,0},{2,6},{1,3},{7,5},{5,1},{3,7},{8,10},{14,12},{12... | collective-permute-start | bytes 2654216 | tf_op jit(solution)/shard_map/ppermute | solution.py:627
  13.6 45.3 %collective-permute-start.6 = (bf16[2,192,1152]{2,1,0:T(8,128)(2,1)}, bf16[2,192,1152]{2,1,0:T(8,128)(2,1)}, u32[]{:S(2)}, u32[]{:S(2)}) collective-permute-start(bf16[2,192,1152]{2,1,0:T(8,128)(2,1)} %bitcast.92), channel_id=1, source_target_pairs={{2,4},{4,2},{3,5},{5,3},{10,12},{12,10},{11,13},{13,11},{18,20},{2... | collective-permute-start | bytes 2654216 | tf_op jit(solution)/shard_map/ppermute | solution.py:626
  17.5 3.8 collective-permute-start.1
  21.3 3.9 collective-permute-start.2
  26.3 5.2 collective-permute-start.3
  31.6 4.4 collective-permute-start.4
  37.4 15.8 %collective-permute-start.8 = (f32[1,2,2,6,384]{4,1,3,2,0:T(2,128)S(1)}, f32[1,2,2,6,384]{4,1,3,2,0:T(2,128)S(1)}, u32[]{:S(2)}, u32[]{:S(2)}) collective-permute-start(f32[1,2,2,6,384]{4,1,3,2,0:T(2,128)S(1)} %bitcast.213), channel_id=1, source_target_pairs={{0,1},{1,0},{2,3},{3,2},{4,5},{5,4},{6,7},{7,6},{8,9},{9,8},{10,11... | collective-permute-start | bytes 110600 | tf_op jit(solution)/shard_map/ppermute | solution.py:19
  53.3 5.3 collective-permute-start.9
  60.9 22.7 %collective-permute-start.11 = (bf16[384,1152]{1,0:T(8,128)(2,1)S(1)}, bf16[384,1152]{1,0:T(8,128)(2,1)S(1)}, u32[]{:S(2)}, u32[]{:S(2)}) collective-permute-start(bf16[384,1152]{1,0:T(8,128)(2,1)S(1)} %get-tuple-element.342), channel_id=1, source_target_pairs={{0,16},{16,0},{1,17},{17,1},{2,18},{18,2},{3,19},{19,3},{4,20},{20... | collective-permute-start | bytes 2654216 | tf_op jit(solution)/shard_map/ppermute | solution.py:19
  62.5 22.6 %collective-permute-start.10 = (bf16[384,1152]{1,0:T(8,128)(2,1)S(1)}, bf16[384,1152]{1,0:T(8,128)(2,1)S(1)}, u32[]{:S(2)}, u32[]{:S(2)}) collective-permute-start(bf16[384,1152]{1,0:T(8,128)(2,1)S(1)} %get-tuple-element.343), channel_id=1, source_target_pairs={{0,8},{8,0},{1,9},{9,1},{2,10},{10,2},{3,11},{11,3},{4,12},{12,4},... | collective-permute-start | bytes 2654216 | tf_op jit(solution)/shard_map/ppermute | solution.py:19
  64.2 38.3 %collective-permute-start.15 = (bf16[384,1152]{1,0:T(8,128)(2,1)S(1)}, bf16[384,1152]{1,0:T(8,128)(2,1)S(1)}, u32[]{:S(2)}, u32[]{:S(2)}) collective-permute-start(bf16[384,1152]{1,0:T(8,128)(2,1)S(1)} %get-tuple-element.343), channel_id=1, source_target_pairs={{0,16},{16,0},{1,17},{17,1},{2,18},{18,2},{3,19},{19,3},{4,20},{20... | collective-permute-start | bytes 2654216 | tf_op jit(solution)/shard_map/ppermute | solution.py:19
  71.0 53.7 %collective-permute-start.17 = (bf16[384,1152]{1,0:T(8,128)(2,1)S(1)}, bf16[384,1152]{1,0:T(8,128)(2,1)S(1)}, u32[]{:S(2)}, u32[]{:S(2)}) collective-permute-start(bf16[384,1152]{1,0:T(8,128)(2,1)S(1)} %get-tuple-element.342), channel_id=1, source_target_pairs={{0,8},{8,0},{1,9},{9,1},{2,10},{10,2},{3,11},{11,3},{4,12},{12,4},... | collective-permute-start | bytes 2654216 | tf_op jit(solution)/shard_map/ppermute | solution.py:19
  85.1 39.5 %collective-permute-start.13 = (bf16[592,1536]{1,0:T(8,128)(2,1)S(1)}, bf16[592,1536]{1,0:T(8,128)(2,1)S(1)}, u32[]{:S(2)}, u32[]{:S(2)}) collective-permute-start(bf16[592,1536]{1,0:T(8,128)(2,1)S(1)} %get-tuple-element.129.refs_0_), channel_id=1, source_target_pairs={{0,1},{1,0},{2,3},{3,2},{4,5},{5,4},{6,7},{7,6},{8,9},{9,8},{10,11... | collective-permute-start | bytes 5455880 | tf_op jit(solution)/shard_map/ppermute | solution.py:19
  88.5 37.3 %collective-permute-start.12 = (bf16[592,1536]{1,0:T(8,128)(2,1)S(1)}, bf16[592,1536]{1,0:T(8,128)(2,1)S(1)}, u32[]{:S(2)}, u32[]{:S(2)}) collective-permute-start(bf16[592,1536]{1,0:T(8,128)(2,1)S(1)} %get-tuple-element.129.refs_0_), channel_id=1, source_target_pairs={{0,4},{4,0},{1,5},{5,1},{2,6},{6,2},{3,7},{7,3},{8,12},{12,8},{9,1... | collective-permute-start | bytes 5455880 | tf_op jit(solution)/shard_map/ppermute | solution.py:19
  88.6 30.7 %collective-permute-start.16 = (bf16[384,1152]{1,0:T(8,128)(2,1)S(1)}, bf16[384,1152]{1,0:T(8,128)(2,1)S(1)}, u32[]{:S(2)}, u32[]{:S(2)}) collective-permute-start(bf16[384,1152]{1,0:T(8,128)(2,1)S(1)} %collective-permute-done.10), channel_id=1, source_target_pairs={{0,16},{16,0},{1,17},{17,1},{2,18},{18,2},{3,19},{19,3},{4,20},{20... | collective-permute-start | bytes 2654216 | tf_op jit(solution)/shard_map/ppermute | solution.py:19
  102.5 22.5 %collective-permute-start.18 = (bf16[384,1152]{1,0:T(8,128)(2,1)S(1)}, bf16[384,1152]{1,0:T(8,128)(2,1)S(1)}, u32[]{:S(2)}, u32[]{:S(2)}) collective-permute-start(bf16[384,1152]{1,0:T(8,128)(2,1)S(1)} %collective-permute-done.11), channel_id=1, source_target_pairs={{0,8},{8,0},{1,9},{9,1},{2,10},{10,2},{3,11},{11,3},{4,12},{12,4},... | collective-permute-start | bytes 2654216 | tf_op jit(solution)/shard_map/ppermute | solution.py:19
  124.6 3.8 collective-permute-start.14
  160.5 200.6 %all-gather.8.cloned.1.call-start = ((), (), s32[]{:S(2)}) async-start(), calls=%async_computation.4 | async-start | bytes 5898240 | tf_op jit(solution)/shard_map/all_gather | solution.py:656
  192.9 168.2 %all-gather.10.cloned.1.call-start = ((), (), s32[]{:S(2)}) async-start(), calls=%async_computation.5 | async-start | bytes 5898240 | tf_op jit(solution)/shard_map/all_gather | solution.py:656
  236.7 6.7 collective-permute-start.20
  236.8 177.6 %all-gather.12.cloned.1.call-start = ((), (), s32[]{:S(2)}) async-start(), calls=%async_computation.6 | async-start | bytes 11796480 | tf_op jit(solution)/shard_map/all_gather | solution.py:656
  242.9 16.4 %collective-permute-start.19 = (bf16[592,1536]{1,0:T(8,128)(2,1)}, bf16[592,1536]{1,0:T(8,128)(2,1)S(1)}, u32[]{:S(2)}, u32[]{:S(2)}) collective-permute-start(bf16[592,1536]{1,0:T(8,128)(2,1)} %get-tuple-element.144), channel_id=1, source_target_pairs={{0,4},{4,0},{1,5},{5,1},{2,6},{6,2},{3,7},{7,3},{8,12},{12,8},{9,1... | collective-permute-start | bytes 5455880 | tf_op jit(solution)/shard_map/ppermute | solution.py:19
  245.6 67.0 %collective-permute-start.21 = (bf16[592,1536]{1,0:T(8,128)(2,1)S(1)}, bf16[592,1536]{1,0:T(8,128)(2,1)S(1)}, u32[]{:S(2)}, u32[]{:S(2)}) collective-permute-start(bf16[592,1536]{1,0:T(8,128)(2,1)S(1)} %add_convert_fusion.4), channel_id=1, source_target_pairs={{0,1},{1,0},{2,3},{3,2},{4,5},{5,4},{6,7},{7,6},{8,9},{9,8},{10,11... | collective-permute-start | bytes 5455880 | tf_op jit(solution)/shard_map/ppermute | solution.py:19
  246.4 70.9 %collective-permute-start.28 = (bf16[2,192,1536]{2,1,0:T(8,128)(2,1)S(1)}, bf16[2,192,1536]{2,1,0:T(8,128)(2,1)S(1)}, u32[]{:S(2)}, u32[]{:S(2)}) collective-permute-start(bf16[2,192,1536]{2,1,0:T(8,128)(2,1)S(1)} %bitcast.207), channel_id=1, source_target_pairs={{0,2},{6,4},{4,0},{2,6},{1,3},{7,5},{5,1},{3,7},{8,10},{14,12},{12... | collective-permute-start | bytes 3538952 | tf_op jit(solution)/shard_map/ppermute | solution.py:627
  248.2 69.1 %collective-permute-start.27 = (bf16[2,192,1536]{2,1,0:T(8,128)(2,1)S(1)}, bf16[2,192,1536]{2,1,0:T(8,128)(2,1)S(1)}, u32[]{:S(2)}, u32[]{:S(2)}) collective-permute-start(bf16[2,192,1536]{2,1,0:T(8,128)(2,1)S(1)} %bitcast.208), channel_id=1, source_target_pairs={{2,4},{4,2},{3,5},{5,3},{10,12},{12,10},{11,13},{13,11},{18,20},{2... | collective-permute-start | bytes 3538952 | tf_op jit(solution)/shard_map/ppermute | solution.py:626
  319.1 353.8 %reduce-scatter.10.cloned.1.call-start = ((), (), s32[]{:S(2)}) async-start(), calls=%async_computation.7 | async-start | bytes 11796480
  319.2 41.3 %collective-permute-start.23 = (bf16[592,1536]{1,0:T(8,128)(2,1)}, bf16[592,1536]{1,0:T(8,128)(2,1)}, u32[]{:S(2)}, u32[]{:S(2)}) collective-permute-start(bf16[592,1536]{1,0:T(8,128)(2,1)} %add_convert_fusion.3.refs_0_), channel_id=1, source_target_pairs={{0,1},{1,0},{2,3},{3,2},{4,5},{5,4},{6,7},{7,6},{8,9},{9,8},{10,11... | collective-permute-start | bytes 5455880 | tf_op jit(solution)/shard_map/ppermute | solution.py:19
  319.3 41.8 %collective-permute-start.22 = (bf16[592,1536]{1,0:T(8,128)(2,1)}, bf16[592,1536]{1,0:T(8,128)(2,1)}, u32[]{:S(2)}, u32[]{:S(2)}) collective-permute-start(bf16[592,1536]{1,0:T(8,128)(2,1)} %add_convert_fusion.3.refs_0_), channel_id=1, source_target_pairs={{0,4},{4,0},{1,5},{5,1},{2,6},{6,2},{3,7},{7,3},{8,12},{12,8},{9,1... | collective-permute-start | bytes 5455880 | tf_op jit(solution)/shard_map/ppermute | solution.py:19
  360.4 4.1 collective-permute-start.24
  360.5 71.9 %collective-permute-start.25 = (bf16[592,1536]{1,0:T(8,128)(2,1)}, bf16[592,1536]{1,0:T(8,128)(2,1)}, u32[]{:S(2)}, u32[]{:S(2)}) collective-permute-start(bf16[592,1536]{1,0:T(8,128)(2,1)} %get-tuple-element.173.refs_7_.refs_6_.refs_0_), channel_id=1, source_target_pairs={{0,4},{4,0},{1,5},{5,1},{2,6},{6,2},{3,7},{7,3},{8,12},{12,8},{9,1... | collective-permute-start | bytes 5455880 | tf_op jit(solution)/shard_map/ppermute | solution.py:19
  426.9 3.8 collective-permute-start.29
  428.3 5.0 collective-permute-start.26
  492.0 236.7 %reduce-scatter.12.cloned.1.call-start = ((), (), s32[]{:S(2)}) async-start(), calls=%async_computation.8 | async-start | bytes 11796480
  505.3 3.8 collective-permute-start.30
  532.4 4.0 collective-permute-start.31
  565.9 291.5 %reduce-scatter.14.cloned.1.call-start = ((), (), s32[]{:S(2)}) async-start(), calls=%async_computation.9 | async-start | bytes 2949120
  584.7 17.4 %collective-permute-start.32 = (bf16[592,1536]{1,0:T(8,128)(2,1)}, bf16[592,1536]{1,0:T(8,128)(2,1)}, u32[]{:S(2)}, u32[]{:S(2)}) collective-permute-start(bf16[592,1536]{1,0:T(8,128)(2,1)} %get-tuple-element.192), channel_id=1, source_target_pairs={{0,4},{4,0},{1,5},{5,1},{2,6},{6,2},{3,7},{7,3},{8,12},{12,8},{9,1... | collective-permute-start | bytes 5455880 | tf_op jit(solution)/shard_map/ppermute | solution.py:19
  611.3 42.4 %collective-permute-start.34 = (bf16[592,1536]{1,0:T(8,128)(2,1)}, bf16[592,1536]{1,0:T(8,128)(2,1)}, u32[]{:S(2)}, u32[]{:S(2)}) collective-permute-start(bf16[592,1536]{1,0:T(8,128)(2,1)} %get-tuple-element.209.refs_0_), channel_id=1, source_target_pairs={{0,1},{1,0},{2,3},{3,2},{4,5},{5,4},{6,7},{7,6},{8,9},{9,8},{10,11... | collective-permute-start | bytes 5455880 | tf_op jit(solution)/shard_map/ppermute | solution.py:19
  612.7 49.1 %collective-permute-start.33 = (bf16[592,1536]{1,0:T(8,128)(2,1)}, bf16[592,1536]{1,0:T(8,128)(2,1)}, u32[]{:S(2)}, u32[]{:S(2)}) collective-permute-start(bf16[592,1536]{1,0:T(8,128)(2,1)} %get-tuple-element.209.refs_0_), channel_id=1, source_target_pairs={{0,4},{4,0},{1,5},{5,1},{2,6},{6,2},{3,7},{7,3},{8,12},{12,8},{9,1... | collective-permute-start | bytes 5455880 | tf_op jit(solution)/shard_map/ppermute | solution.py:19
  653.7 8.2 collective-permute-start.35
  798.6 21.3 %collective-permute-start.36 = (bf16[592,1536]{1,0:T(8,128)(2,1)}, bf16[592,1536]{1,0:T(8,128)(2,1)S(1)}, u32[]{:S(2)}, u32[]{:S(2)}) collective-permute-start(bf16[592,1536]{1,0:T(8,128)(2,1)} %get-tuple-element.218), channel_id=1, source_target_pairs={{0,4},{4,0},{1,5},{5,1},{2,6},{6,2},{3,7},{7,3},{8,12},{12,8},{9,1... | collective-permute-start | bytes 5455880 | tf_op jit(solution)/shard_map/ppermute | solution.py:19
  815.9 3.9 collective-permute-start.54
  819.8 90.8 %collective-permute-start.55 = (f32[2,2,1536]{2,1,0:T(2,128)S(1)}, f32[2,2,1536]{2,1,0:T(2,128)S(1)}, u32[]{:S(2)}, u32[]{:S(2)}) collective-permute-start(f32[2,2,1536]{2,1,0:T(2,128)S(1)} %fusion.56), channel_id=1, source_target_pairs={{0,4},{4,0},{1,5},{5,1},{2,6},{6,2},{3,7},{7,3},{8,12},{12,8},{9,1... | collective-permute-start | bytes 73736 | tf_op jit(solution)/shard_map/ppermute | solution.py:19
  906.1 20.9 %collective-permute-start.50 = (bf16[384,1152]{1,0:T(8,128)(2,1)}, bf16[384,1152]{1,0:T(8,128)(2,1)}, u32[]{:S(2)}, u32[]{:S(2)}) collective-permute-start(bf16[384,1152]{1,0:T(8,128)(2,1)} %fusion.36), channel_id=1, source_target_pairs={{0,16},{16,0},{1,17},{17,1},{2,18},{18,2},{3,19},{19,3},{4,20},{20... | collective-permute-start | bytes 2654216 | tf_op jit(solution)/shard_map/ppermute | solution.py:19
  909.5 20.7 %collective-permute-start.51 = (bf16[384,1152]{1,0:T(8,128)(2,1)}, bf16[384,1152]{1,0:T(8,128)(2,1)}, u32[]{:S(2)}, u32[]{:S(2)}) collective-permute-start(bf16[384,1152]{1,0:T(8,128)(2,1)} %fusion.37), channel_id=1, source_target_pairs={{0,8},{8,0},{1,9},{9,1},{2,10},{10,2},{3,11},{11,3},{4,12},{12,4},... | collective-permute-start | bytes 2654216 | tf_op jit(solution)/shard_map/ppermute | solution.py:19
  910.7 66.0 %collective-permute-start.37 = (bf16[592,1536]{1,0:T(8,128)(2,1)}, bf16[592,1536]{1,0:T(8,128)(2,1)}, u32[]{:S(2)}, u32[]{:S(2)}) collective-permute-start(bf16[592,1536]{1,0:T(8,128)(2,1)} %get-tuple-element.223), channel_id=1, source_target_pairs={{0,4},{4,0},{1,5},{5,1},{2,6},{6,2},{3,7},{7,3},{8,12},{12,8},{9,1... | collective-permute-start | bytes 5455880 | tf_op jit(solution)/shard_map/ppermute | solution.py:19
  933.2 33.4 %collective-permute-start.53 = (bf16[2,192,1152]{2,1,0:T(8,128)(2,1)}, bf16[2,192,1152]{2,1,0:T(8,128)(2,1)}, u32[]{:S(2)}, u32[]{:S(2)}) collective-permute-start(bf16[2,192,1152]{2,1,0:T(8,128)(2,1)} %get-tuple-element.336), channel_id=1, source_target_pairs={{2,0},{4,6},{0,4},{6,2},{3,1},{5,7},{1,5},{7,3},{10,8},{12,14},{8,... | collective-permute-start | bytes 2654216 | tf_op jit(solution)/shard_map/ppermute | solution.py:709
  933.2 33.4 %collective-permute-start.52 = (bf16[2,192,1152]{2,1,0:T(8,128)(2,1)}, bf16[2,192,1152]{2,1,0:T(8,128)(2,1)}, u32[]{:S(2)}, u32[]{:S(2)}) collective-permute-start(bf16[2,192,1152]{2,1,0:T(8,128)(2,1)} %get-tuple-element.337), channel_id=1, source_target_pairs={{2,4},{4,2},{3,5},{5,3},{10,12},{12,10},{11,13},{13,11},{18,20},{2... | collective-permute-start | bytes 2654216 | tf_op jit(solution)/shard_map/ppermute | solution.py:708
  986.3 5.5 collective-permute-start.56
  991.8 4.1 collective-permute-start.57
  995.6 10.4 collective-permute-start.38
  995.9 13.2 %collective-permute-start.58 = (f32[84,128]{1,0:T(8,128)S(1)}, f32[84,128]{1,0:T(8,128)S(1)}, u32[]{:S(2)}, u32[]{:S(2)}) collective-permute-start(f32[84,128]{1,0:T(8,128)S(1)} %fusion.68), channel_id=1, source_target_pairs={{0,2},{2,0},{1,3},{3,1},{4,6},{6,4},{5,7},{7,5},{8,10},{10,8},{9,1... | collective-permute-start | bytes 129032 | tf_op jit(solution)/shard_map/ppermute | solution.py:19
  1006.1 10.0 collective-permute-start.39
  1009.2 4.3 collective-permute-start.59
  1012.3 3.7 collective-permute-start.61
  1017.9 4.6 collective-permute-start.41
  1022.6 5.4 collective-permute-start.42
  1029.6 6.2 collective-permute-start.43
  1029.8 6.8 collective-permute-start.48
  1035.8 4.7 collective-permute-start.44
  1040.5 5.8 collective-permute-start.49
  1041.7 4.6 collective-permute-start.46
  1046.4 4.3 collective-permute-start.47
  (98 other events, 1007.4 us)
Sparse Core Ops, SparseCore 0:
  160.7 36.1 all-gather.5
  198.7 57.0 all-gather.7
  257.6 57.0 all-gather.9
  319.2 95.0 all-gather.11
  492.1 95.0 reduce-scatter.9
  590.1 95.0 reduce-scatter.11
  728.8 48.7 reduce-scatter.13

commit v3 on v2

--- a/solution.py
+++ b/solution.py
@@ -44,6 +44,10 @@
 
 def after(v, *deps):
     return lax.optimization_barrier((v,) + deps)[0]
+
+
+def tie(*vs):
+    return lax.optimization_barrier(vs)
 
 
 def index_of(axes):
@@ -100,33 +104,31 @@
             steps.append(ride.moves(source, target, lambda k, at=at: send.at[at + k], lambda k, at=at: recv.at[at + k]))
             at += ride.sems
 
-        @pl.when(pl.program_id(0) == 0)
-        def _():
-            barrier = pltpu.get_barrier_semaphore()
-            for partner in partners:
-                pl.semaphore_signal(
-                    barrier,
-                    1,
-                    device_id={axis: 1 - lax.axis_index(axis) for axis in partner},
-                    device_id_type=pl.DeviceIdType.MESH,
-                )
-            pl.semaphore_wait(barrier, len(partners))
-            for start, unused in steps:
-                start()
-
-        kernel(*ins, *outs, *own)
-
-        @pl.when(pl.program_id(0) == grid[0] - 1)
-        def _():
-            for unused, wait in steps:
-                wait()
+        barrier = pltpu.get_barrier_semaphore()
+        for partner in partners:
+            pl.semaphore_signal(
+                barrier,
+                1,
+                device_id={axis: 1 - lax.axis_index(axis) for axis in partner},
+                device_id_type=pl.DeviceIdType.MESH,
+            )
+        pl.semaphore_wait(barrier, len(partners))
+        for start, unused in steps:
+            start()
+        pltpu.emit_pipeline(
+            lambda *blocks: kernel(*blocks, *own),
+            grid=grid,
+            in_specs=list(in_specs),
+            out_specs=list(out_specs),
+        )(*ins, *outs)
+        for unused, wait in steps:
+            wait()
 
     anywhere = pl.BlockSpec(memory_space=pl.ANY)
     outs = pl.pallas_call(
         body,
-        grid=grid,
-        in_specs=list(in_specs) + [anywhere] * n_rides,
-        out_specs=list(out_specs) + [anywhere] * n_rides,
+        in_specs=[anywhere] * (n_in + n_rides),
+        out_specs=[anywhere] * (n_out + n_rides),
         out_shape=list(out_shape) + [ride.shape for ride in rides],
         scratch_shapes=list(scratch)
         + [pltpu.SemaphoreType.DMA((sems,)), pltpu.SemaphoreType.DMA((sems,))],
@@ -169,8 +171,16 @@
 
 
 def row_ride(array, axis, start, stop):
-    views = lambda source, target: [(source.at[pl.ds(start, stop - start)], target)]
-    return NeighbourRide(array, axis, (stop - start,) + array.shape[1:], views, 1)
+    count = min(4, (stop - start) // 16)
+    cuts = [start + (stop - start) // 16 * k // count * 16 for k in range(count)] + [stop]
+
+    def views(source, target):
+        return [
+            (source.at[pl.ds(a, b - a)], target.at[pl.ds(a - start, b - a)])
+            for a, b in zip(cuts, cuts[1:])
+        ]
+
+    return NeighbourRide(array, axis, (stop - start,) + array.shape[1:], views, count)
 
 
 class TradeRide:
@@ -267,9 +277,10 @@
         sums[1] = total[1]
 
 
-def rows_nn(xs, w, img, mode, bias=None, slopes=(), tile=384, rides=(), cid=None):
+def rows_nn(xs, w, img, mode, bias=None, slopes=(), rides=(), cid=None):
     (w0, s0), (w1, s1) = by_stream(w)
     n = w0.shape[3]
+    tile = 768 if n % 768 == 0 else 384
     nb, (rows, depth) = len(xs), xs[0].shape
     in_specs = [once((rows, depth), lambda j: (0, 0))] * nb
     in_specs += [
@@ -307,8 +318,8 @@
 def rows_nt_kernel(nb, img, *refs):
     xs, w0, w1, outs = refs[:nb], refs[nb], refs[nb + 1], refs[nb + 2 :]
     text = xs[0].shape[0] - img
-    y_text = nt(jnp.concatenate([x[img:, :] for x in xs], axis=0), w1[0, 0])
-    w_img = w0[0, 0]
+    y_text = nt(jnp.concatenate([x[img:, :] for x in xs], axis=0), w1[:, 0].reshape(-1, xs[0].shape[1]))
+    w_img = w0[:, 0].reshape(-1, xs[0].shape[1])
     for b in range(nb):
         outs[b][:img, :] = nt(xs[b][:img, :], w_img).astype(outs[b].dtype)
         outs[b][img:, :] = y_text[b * text : (b + 1) * text].astype(outs[b].dtype)
@@ -320,12 +331,12 @@
     quarter = w0.shape[2]
     return launch(
         functools.partial(rows_nt_kernel, nb, img),
-        (4,),
+        (2,),
         [once((rows, n), lambda j: (0, 0))] * nb
         + [
-            pl.BlockSpec((1, 1, quarter, n), lambda j, at=at: (j, at, 0, 0)) for at in (s0, s1)
+            pl.BlockSpec((2, 1, quarter, n), lambda j, at=at: (j, at, 0, 0)) for at in (s0, s1)
         ],
-        [pl.BlockSpec((rows, quarter), lambda j: (0, j))] * nb,
+        [pl.BlockSpec((rows, 2 * quarter), lambda j: (0, j))] * nb,
         [jax.ShapeDtypeStruct((rows, 4 * quarter), t) for t in dtypes],
         list(xs) + [w0, w1],
         "rows_back",
@@ -337,13 +348,19 @@
 
 def weight_grad_kernel(nb, img, *refs):
     xs, ys, out = refs[:nb], refs[nb : 2 * nb], refs[2 * nb]
-    total = tn(xs[0][:img, :], ys[0][:img, :])
-    for b in range(1, nb):
-        total += tn(xs[b][:img, :], ys[b][:img, :])
-    out[0, 0] = total.astype(BF)
+    y_img, y_text = refs[2 * nb + 1 :]
+    text = xs[0].shape[0] - img
+
+    @pl.when(pl.program_id(0) == 0)
+    def _():
+        for b in range(nb):
+            y_img[b * img : (b + 1) * img, :] = ys[b][:img, :]
+            y_text[b * text : (b + 1) * text, :] = ys[b][img:, :]
+
+    x_img = jnp.concatenate([x[:img, :] for x in xs], axis=0)
     x_text = jnp.concatenate([x[img:, :] for x in xs], axis=0)
-    y_text = jnp.concatenate([y[img:, :] for y in ys], axis=0)
-    out[0, 1] = tn(x_text, y_text).astype(BF)
+    out[0, 0] = tn(x_img, y_img[...]).astype(BF)
+    out[0, 1] = tn(x_text, y_text[...]).astype(BF)
 
 
 def weight_grad(xs, ys, img, rides=(), cid=None):
@@ -358,6 +375,7 @@
         list(xs) + list(ys),
         "weight_grad",
         2 * nb * rows * d * n,
+        scratch=[pltpu.VMEM((nb * img, n), BF), pltpu.VMEM((nb * (rows - img), n), BF)],
         rides=rides,
         cid=cid,
     )
@@ -694,22 +712,31 @@
         done = []
         for stream in range(2):
             near, dim, far_axis, far = ((x, 1, self.y, y), (y, 0, self.x, x))[stream]
-            v = pick(g[:, :, stream], near, dim).astype(F32) + arrived[stream].astype(F32)
+            at = (0, near, stream, 0, 0) if dim == 1 else (near, 0, stream, 0, 0)
+            size = (2, 1) if dim == 1 else (1, 2)
+            v = lax.dynamic_slice(g, at, size + (1,) + g.shape[3:]).reshape(arrived[stream].shape)
+            v = v.astype(F32) + arrived[stream].astype(F32)
             v = pick(v, far, 0) + swap(pick(v, 1 - far, 0).astype(BF), far_axis).astype(F32)
             done.append(v)
         return jnp.stack(done)
 
-    def trade_sums(self, g, kinds, end=()):
-        g = g.reshape(2, 2, -1, g.shape[2])
+    def trade_parts(self, g):
+        g = g.reshape(2, 2, -1, g.shape[-1])
         zh = lax.axis_index(self.zh)
+        return [lax.dynamic_index_in_dim(g, k, 1, keepdims=False) for k in (zh, 1 - zh)]
+
+    def trade_sends(self, g):
+        first, second = self.trade_parts(g)
         joint = (self.q, self.zh)
-        first = lax.dynamic_index_in_dim(g, zh, 1, keepdims=False)
-        second = lax.dynamic_index_in_dim(g, 1 - zh, 1, keepdims=False)
-        cross = lax.ppermute(first.astype(BF), joint, [(1, 2), (2, 1)])
-        second = lax.ppermute(second.astype(BF), joint, [(1, 0), (2, 3), (0, 2), (3, 1)])
-        cross, second = after((cross, second), *end)
-        same = zh == lax.axis_index(self.q)
-        total = jnp.where(same, first.astype(F32), cross.astype(F32)) + second.astype(F32)
+        return [
+            lax.ppermute(first.astype(BF), joint, [(1, 2), (2, 1)]),
+            lax.ppermute(second.astype(BF), joint, [(1, 0), (2, 3), (0, 2), (3, 1)]),
+        ]
+
+    def trade_adds(self, g, arrived, kinds):
+        same = lax.axis_index(self.zh) == lax.axis_index(self.q)
+        total = jnp.where(same, self.trade_parts(g)[0].astype(F32), arrived[0].astype(F32))
+        total += arrived[1].astype(F32)
         return total.reshape(2, total.shape[1], kinds, -1)
 
 
@@ -823,11 +850,7 @@
     def ride(array, start, stop):
         return row_ride(array, lay.p, start, stop)
 
-    def thirds(n):
-        return [0] + [n * k // 3 // 16 * 16 for k in (1, 2)] + [n]
-
-    cut = thirds(rows)
-    rides = [ride(grad_two, cut[k], cut[k + 1]) for k in range(3)]
+    cut = rows // 3 // 16 * 16
     extra = [[], [], []]
     if compact:
         extra = [
@@ -835,31 +858,33 @@
             for w in (proj_local, up_local[:1], up_local[1:])
         ]
     qkv, rode = rows_nn(
-        flat(first), qkv_full, img, "bias", bias=qkv_bias, rides=[rides[0]] + extra[0], cid=1
-    )
-    grad_two_pair = rode[:1]
+        flat(first), qkv_full, img, "bias", bias=qkv_bias, rides=extra[0], cid=1
+    )
     qkv = unflat(qkv)
     chunk = min(256, img_rows)
     if compact:
-        proj_full = lay.spread_rows_async(rode[1])
+        proj_full = lay.spread_rows_async(rode[0])
     other, rode = attention(
-        qkv[0][1], qkv[1][1], img, txt_rows, chunk, 1, rides=[rides[1]] + extra[1], cid=2
-    )
-    grad_two_pair += rode[:1]
-    if compact:
-        up_full = [lay.spread_rows_async(rode[1])]
+        qkv[0][1], qkv[1][1], img, txt_rows, chunk, 1, rides=extra[1], cid=2
+    )
+    if compact:
+        up_full = [lay.spread_rows_async(rode[0])]
         qkv, other = after((qkv, other), proj_full)
     mine, rode = attention(
-        qkv[0][0], qkv[1][0], img, txt_rows, chunk, 0, rides=[rides[2]] + extra[2], cid=10
-    )
-    grad_two_pair = jnp.concatenate(grad_two_pair + rode[:1], axis=0)
+        qkv[0][0],
+        qkv[1][0],
+        img,
+        txt_rows,
+        chunk,
+        0,
+        rides=[ride(grad_two, 0, cut)] + extra[2],
+        cid=10,
+    )
+    grad_two_pair = rode[:1]
     heads_out = [[mine[z], other[z]] for z in range(2)]
-    grad_two_blocks = [
-        [grad_two, swap(grad_two, lay.q)], [grad_two_pair, swap(grad_two_pair, lay.q)]
-    ]
     if compact:
         up_full.append(lay.spread_rows_async(rode[1]))
-        down_local = after(down_local, mine)
+        down_own = lay.trade_shards(after(down_local, mine))
 
     far = swap(lay.sum_far(proj_full, heads_out, img), lay.p)
     near, unused = lay.sum_near(proj_full, heads_out, img)
@@ -868,12 +893,18 @@
     second_norm = norm_parts(middle)
     second_hidden = (second_norm[0] * (1.0 + scale_two) + shift_two).astype(BF)
     if compact:
-        down_own = lay.trade_shards(down_local, (second_hidden,))
+        second_hidden, down_own = tie(second_hidden, down_own)
         down_full = lay.spread_rows_async(down_own)
     second = lay.gather_rows(second_hidden)
     up_mine = lay.my_columns(up_bias.astype(F32))
     up_n = up_mine.shape[1]
-    up_out, unused = rows_nn(flat(second), up_full, img, "gelu", bias=up_mine)
+    up_out, rode = rows_nn(
+        flat(second), up_full, img, "gelu", bias=up_mine, rides=[ride(grad_two, cut, rows)], cid=13
+    )
+    grad_two_pair = jnp.concatenate(grad_two_pair + rode, axis=0)
+    grad_two_blocks = [
+        [grad_two, swap(grad_two, lay.q)], [grad_two_pair, swap(grad_two_pair, lay.q)]
+    ]
     activated, slopes = up_out[:4], up_out[4:]
     far = lay.sum_far(down_full, unflat(activated), img)
     cut = rows * 21 // 37 // 16 * 16
@@ -944,19 +975,21 @@
     )
     grad_qkv = [[grad_mine[z], grad_other[z]] for z in range(2)]
     far = lay.sum_far(qkv_full, grad_qkv, img)
-    cut = rows * 20 // 37 // 16 * 16
-    qkv_grads, rode = weight_grad(
-        flat(first), flat(grad_qkv), img, rides=[ride(far, 0, cut)], cid=8
-    )
+    cut = rows * 16 // 37 // 16 * 16
+    rides = [ride(far, 0, cut)]
+    if compact:
+        rides.append(lay.trade_ride(proj_plane, True))
+    qkv_grads, rode = weight_grad(flat(first), flat(grad_qkv), img, rides=rides, cid=8)
     rides = [ride(far, cut, rows)]
     if compact:
-        rides += lay.plane_rides(qkv_grads) + [lay.trade_ride(proj_plane, True)]
+        proj_sums = rode[1]
+        rides += lay.plane_rides(qkv_grads)
     near, rode_two = lay.sum_near(qkv_full, after(grad_qkv, qkv_grads), img, rides, 9)
-    far = jnp.concatenate(rode + rode_two[:1], axis=0)
+    far = jnp.concatenate(rode[:1] + rode_two[:1], axis=0)
     if compact:
         down_grad, up_grad, proj_grad = [
             (v[0].astype(F32) + v[1].astype(F32))[:, :, None]
-            for v in (down_sums[0], up_sums[0], rode_two[3])
+            for v in (down_sums[0], up_sums[0], proj_sums)
         ]
         qkv_plane = lay.sum_plane(qkv_grads, rode_two[1:3])
     else:
@@ -983,19 +1016,24 @@
     grad_mod = sum_bits(grad_mod, (lay.p,))
     grad_mod = gather_bits(grad_mod[None], t_up[1:])
     if compact:
-        qkv_grad = lay.trade_sums(after(qkv_plane, grad_mod), 3)
-    down_grad = jnp.swapaxes(down_grad[:, :, 0], 1, 2)
-    proj_grad = jnp.swapaxes(proj_grad[:, :, 0], 1, 2)
-    up_grad = up_grad[:, :, 0]
-    qkv_grad = jnp.swapaxes(qkv_grad, 1, 2)
+        qkv_plane, grad_mod = tie(qkv_plane, grad_mod)
     grad_mod = lax.dynamic_slice_in_dim(grad_mod, t_index * columns, columns, 3)
     grad_mod = gather_bits(grad_mod, dp_up)
     high = lax.Precision.HIGHEST
     ada_grad = jnp.einsum("sd,stkc->tdkc", silu_mine.astype(F32), grad_mod, precision=high)
     cond_terms = jnp.einsum("stkc,tdkc->sd", grad_mod, ada_weight.astype(F32), precision=high)
-    cond_terms = gather_bits(sum_bits(cond_terms, t_up)[None], dp_up)
+    cond_terms = gather_bits(cond_terms[None], dp_up)
     cond_terms = lax.dynamic_slice_in_dim(cond_terms, dp_index * group_slots, group_slots, 1)
     cond_terms = jnp.swapaxes(cond_terms, 0, 1).reshape(group_slots, width)
+    if compact:
+        arrived = lay.trade_sends(qkv_plane)
+        cond_terms, arrived = tie(cond_terms, arrived)
+        qkv_grad = lay.trade_adds(qkv_plane, arrived, 3)
+    down_grad = jnp.swapaxes(down_grad[:, :, 0], 1, 2)
+    proj_grad = jnp.swapaxes(proj_grad[:, :, 0], 1, 2)
+    up_grad = up_grad[:, :, 0]
+    qkv_grad = jnp.swapaxes(qkv_grad, 1, 2)
+    cond_terms = sum_bits(cond_terms, t_up)
     cond_terms = lax.dynamic_slice_in_dim(cond_terms, t_index * columns, columns, 1)
     cond_slice = lax.dynamic_slice_in_dim(condition.astype(F32), t_index * columns, columns, 1)
     unused, silu_pull = jax.vjp(jax.nn.silu, cond_slice)

time: 1070 us -> 1030 us (0.963)
  Pallas kernels: 477 us -> 440 us
    pallas_call x8 -> x7, Pallas kernels: 91.3 us -> 59.4 us  [launch(): pl.pallas_call(kernel, grid=grid, in_specs=in_specs, out_specs=out_specs,...]
    ppermute x2, waiting for transfers between devices: 25.5 us -> 0.01 us  [the longest x1 0.01 us: trade_sends(): lax.ppermute(second.astype(BF), joint, [(1, 0), (2, 3), (0, 2), (3, 1)])]
    ppermute x57, waiting for transfers between devices: 264 us -> 285 us  [swap(): return lax.ppermute(v, axis, [(0, 1), (1, 0)])]
    pallas_call x12 -> x13, Pallas kernels: 386 us -> 381 us  [launch(): pl.pallas_call(body, in_specs=[anywhere] * (n_in + n_rides), out_specs=[a...]
    unnamed x189 -> x186, local copies, waits for them, and re-layouts: 31.6 us -> 32.9 us
  transfers between devices with their start and end apart: 70 -> 70, of which waited for: 38 -> 36; matrix products, arithmetic and copies ran while one was open for 12% -> 12% of each run, Pallas kernels for 37% -> 28%
where the time goes in v3:
time: 1030 us; the launch traced here: 1020 us
  Pallas kernels  440 us (43%)
  waiting for transfers between devices  316 us (31%)
  other arithmetic  105 us (10%)
  starting transfers between devices  81.3 us (8%)
  local copies, waits for them, and re-layouts  57.3 us (6%)
  between operations  16.7 us (2%)
    pallas_call x13, Pallas kernels, launch(): pl.pallas_call(body, in_specs=[anywhere] * (n_in + n_rides), out_specs=[a...  381 us
    ppermute x57, waiting for transfers between devices, swap(): return lax.ppermute(v, axis, [(0, 1), (1, 0)])  285 us
    ppermute x57, starting transfers between devices, swap(): return lax.ppermute(v, axis, [(0, 1), (1, 0)])  59.5 us
    pallas_call x7, Pallas kernels, launch(): pl.pallas_call(kernel, grid=grid, in_specs=in_specs, out_specs=out_specs,...  59.4 us
    unnamed x186, local copies, waits for them, and re-layouts  32.9 us
    all_gather x4, waiting for transfers between devices, spread_rows_async(): return lax.all_gather(own, (self.y, self.x), axis=0, tiled=False)  27.3 us
  transfers between devices with their start and end apart: 70, of which 36 were waited for; matrix products, arithmetic and copies ran while one was open for 12% of the time, Pallas kernels for 28%

profile of v3, /device:TPU:0, one launch (start us, length us, event | category | flops | bytes accessed | tf_op | source)
XLA Modules:
  0.0 1022.7 jit_solution(3484790513125042221)
XLA Ops:
  9.6 4.0 collective-permute-start.7
  33.1 2.9 collective-permute-done.4
  40.3 12.9 %collective-permute-done.8 = f32[1,2,2,6,384]{4,1,3,2,0:T(2,128)S(1)} collective-permute-done((f32[1,2,2,6,384]{4,1,3,2,0:T(2,128)S(1)}, f32[1,2,2,6,384]{4,1,3,2,0:T(2,128)S(1)}, u32[]{:S(2)}, u32[]{:S(2)}) %collective-permute-start.8) | collective-permute-done | bytes 36896 | tf_op jit(solution)/shard_map/ppermute | solution.py:19
  53.3 2.8 collective-permute-start.9
  56.1 2.5 collective-permute-done.9
  64.8 6.2 fusion.59
  71.6 11.9 %collective-permute-done.11 = bf16[384,1152]{1,0:T(8,128)(2,1)S(1)} collective-permute-done((bf16[384,1152]{1,0:T(8,128)(2,1)S(1)}, bf16[384,1152]{1,0:T(8,128)(2,1)S(1)}, u32[]{:S(2)}, u32[]{:S(2)}) %collective-permute-start.11) | collective-permute-done | bytes 884768 | tf_op jit(solution)/shard_map/ppermute | solution.py:19
  89.3 13.2 %collective-permute-done.15 = bf16[384,1152]{1,0:T(8,128)(2,1)S(1)} collective-permute-done((bf16[384,1152]{1,0:T(8,128)(2,1)S(1)}, bf16[384,1152]{1,0:T(8,128)(2,1)S(1)}, u32[]{:S(2)}, u32[]{:S(2)}) %collective-permute-start.15) | collective-permute-done | bytes 884768 | tf_op jit(solution)/shard_map/ppermute | solution.py:19
  104.1 15.1 %collective-permute-done.16 = bf16[384,1152]{1,0:T(8,128)(2,1)S(1)} collective-permute-done((bf16[384,1152]{1,0:T(8,128)(2,1)S(1)}, bf16[384,1152]{1,0:T(8,128)(2,1)S(1)}, u32[]{:S(2)}, u32[]{:S(2)}) %collective-permute-start.16) | collective-permute-done | bytes 884768 | tf_op jit(solution)/shard_map/ppermute | solution.py:19
  119.4 5.1 collective-permute-done.13.refs_2_
  125.8 2.5 collective-permute-done.14.refs_3_
  129.7 24.5 %rows_bias_1.1 = (bf16[592,1152]{1,0:T(8,128)(2,1)}, bf16[592,1152]{1,0:T(8,128)(2,1)}, bf16[592,1152]{1,0:T(8,128)(2,1)}, bf16[592,1152]{1,0:T(8,128)(2,1)}, bf16[2,2,192,384]{3,2,1,0:T(8,128)(2,1)}) custom-call(bf16[592,1536]{1,0:T(8,128)(2,1)} %copy-done.64, bf16[592,1536]{1,0:T(8,128)(2,1)} %copy-done.88, bf16[592,1536]{1,0:T(8,128)(2,1)} %copy-done.87, ...), custom_call_target="tpu_custom_call" | custom-call | flops 8380219392 | bytes 16367616 | tf_op jit(solution)/shard_map/rows_bias_1/pallas_call | solution.py:128
  155.4 27.4 %attend_1_2.1 = (bf16[592,384]{1,0:T(8,128)(2,1)S(1)}, bf16[592,384]{1,0:T(8,128)(2,1)S(1)}, f32[3,2,4,256]{3,2,1,0:T(4,128)S(1)}, f32[3,2,1,160]{3,2,1,0:T(1,128)S(1)}, bf16[1,2,192,1536]{3,2,1,0:T(8,128)(2,1)}) custom-call(bf16[592,1152]{1,0:T(8,128)(2,1)} %get-tuple-element.206.refs_0_.refs_1_.refs_2_, ...), custom_call_target="tpu_custom_call" | custom-call | flops 5383127040 | bytes 10513920 | tf_op jit(solution)/shard_map/attend_1_2/pallas_call | solution.py:128
  182.9 7.4 all-gather.6.cloned.1.call-done.refs_2_.refs_3_.refs_4_.refs_5_
  190.4 30.1 %attend_0_10.1 = (bf16[592,384]{1,0:T(8,128)(2,1)S(1)}, bf16[592,384]{1,0:T(8,128)(2,1)S(1)}, f32[3,2,4,256]{3,2,1,0:T(4,128)S(1)}, f32[3,2,1,160]{3,2,1,0:T(1,1...) custom-call(bf16[592,1152]{1,0:T(8,128)(2,1)} %get-tuple-element.143.refs_0_.refs_1_.refs_2_, ...), custom_call_target="tpu_custom_call" | custom-call | flops 5383127040 | bytes 10513920 | tf_op jit(solution)/shard_map/attend_0_10/pallas_call | solution.py:128
  223.3 5.1 rows_back.6
  230.4 12.0 %collective-permute-start.22 = (bf16[2,192,1536]{2,1,0:T(8,128)(2,1)S(1)}, bf16[2,192,1536]{2,1,0:T(8,128)(2,1)}, u32[]{:S(2)}, u32[]{:S(2)}) collective-permute-start(bf16[2,192,1536]{2,1,0:T(8,128)(2,1)S(1)} %bitcast.208), channel_id=1, source_target_pairs={{2,4},{4,2},{3,5},{5,3},{10,12},{12,10},{11,13},{13,11},{18,20},{2... | collective-permute-start | bytes 3538952 | tf_op jit(solution)/shard_map/ppermute | solution.py:644
  242.4 5.0 rows_back.5
  251.9 3.0 collective-permute-done.23
  256.7 60.1 %collective-permute-done.21 = bf16[592,1536]{1,0:T(8,128)(2,1)} collective-permute-done((bf16[592,1536]{1,0:T(8,128)(2,1)}, bf16[592,1536]{1,0:T(8,128)(2,1)}, u32[]{:S(2)}, u32[]{:S(2)}) %collective-permute-start.21) | collective-permute-done | bytes 1818656 | tf_op jit(solution)/shard_map/ppermute | solution.py:19
  316.9 4.4 fusion.63
  325.8 41.0 %collective-permute-done.25.refs_2_ = bf16[592,1536]{1,0:T(8,128)(2,1)} collective-permute-done((bf16[592,1536]{1,0:T(8,128)(2,1)}, bf16[592,1536]{1,0:T(8,128)(2,1)}, u32[]{:S(2)}, u32[]{:S(2)}) %collective-permute-start.25) | collective-permute-done | bytes 1818656 | tf_op jit(solution)/shard_map/ppermute | solution.py:19
  366.9 4.0 collective-permute-done.26.refs_3_
  370.8 29.3 %rows_gelu_13.1 = (bf16[592,1536]{1,0:T(8,128)(2,1)}, bf16[592,1536]{1,0:T(8,128)(2,1)}, bf16[592,1536]{1,0:T(8,128)(2,1)}, bf16[592,1536]{1,0:T(8,128)(2,1)}, f...) custom-call(bf16[592,1536]{1,0:T(8,128)(2,1)} %add_convert_fusion.3., ...), custom_call_target="tpu_custom_call" | custom-call | flops 11173625856 | bytes 21823488 | tf_op jit(solution)/shard_map/rows_gelu_13/pallas_call | solution.py:128
  401.2 19.8 %all-gather.12.cloned.1.call-done = bf16[8,384,1536]{2,1,0:T(8,128)(2,1)} async-done(((bf16[2,384,1536]{2,1,0:T(8,128)(2,1)}), bf16[8,384,1536]{2,1,0:T(8,128)(2,1)}) %all-gather.12.cloned.1.call-update) | async-done | bytes 9437200 | tf_op jit(solution)/shard_map/all_gather | solution.py:674
  421.0 11.8 %rows_back.7 = (bf16[592,1536]{1,0:T(8,128)(2,1)S(1)}, f32[592,1536]{1,0:T(8,128)}) custom-call(bf16[592,1536]{1,0:T(8,128)(2,1)} %get-tuple-element.163.refs_0_.refs_7_, bf16[592,1536]{1,0:T(8,128)(2,1)} %get-tuple-element.162.refs_1_.refs_6_, bf16[4,2,384,1536]{3,2,1,0:T(8,128)(2,1)} %bitcast.193, bf16[4,2,384,1536]{3,2,1,0:T(8,128)(2,1)} %bitcast.194), custom_call_target="tpu_custom_call" | custom-call | flops 5586812928 | bytes 10911744 | tf_op jit(solution)/shard_map/rows_back/pallas_call | solution.py:81
  433.6 2.9 collective-permute-done.29
  439.2 2.6 collective-permute-done.28.refs_3_
  443.0 25.9 %rows_slope_3.1 = (bf16[592,1536]{1,0:T(8,128)(2,1)}, bf16[592,1536]{1,0:T(8,128)(2,1)}, bf16[592,1536]{1,0:T(8,128)(2,1)}, bf16[592,1536]{1,0:T(8,128)(2,1)}, f...) custom-call(bf16[592,1536]{1,0:T(8,128)(2,1)} %get-tuple-element.177.refs_6_.refs_7_.refs_0_, ...), custom_call_target="tpu_custom_call" | custom-call | flops 11173625856 | bytes 21823488 | tf_op jit(solution)/shard_map/rows_slope_3/pallas_call | solution.py:128
  469.8 23.3 %weight_grad_4.1 = (bf16[4,2,384,1536]{3,2,1,0:T(8,128)(2,1)}, bf16[256,1536]{1,0:T(8,128)(2,1)S(1)}) custom-call(bf16[592,1536]{1,0:T(8,128)(2,1)} %get-tuple-element.177.refs_6_.refs_7_.refs_0_, bf16[592,1536]{1,0:T(8,128)(2,1)} %copy-done.65, bf16[592,1536]{1,0:T(8,128)(2,1)} %copy-done.60, bf16[592,1536]{1,0:T(8,128)(2,1)} %copy-done.66, ...), custom_call_target="tpu_custom_call" | custom-call | flops 11173625856 | bytes 21823488 | tf_op jit(solution)/shard_map/weight_grad_4/pallas_call | solution.py:128
  494.1 12.1 %rows_back.8 = (bf16[592,1536]{1,0:T(8,128)(2,1)S(1)}, f32[592,1536]{1,0:T(8,128)}) custom-call(bf16[592,1536]{1,0:T(8,128)(2,1)} %get-tuple-element.182.refs_0_.refs_7_, bf16[592,1536]{1,0:T(8,128)(2,1)} %get-tuple-element.183.refs_1_.refs_6_, bf16[4,1,384,1536]{3,2,1,0:T(8,128)(2,1)} %all-gather.8.cloned.1.call-done.refs_4_.refs_2_, ...), custom_call_target="tpu_custom_call" | custom-call | flops 5586812928 | bytes 10911744 | tf_op jit(solution)/shard_map/rows_back/pallas_call | solution.py:81
  506.1 3.8 collective-permute-done.30
  509.9 4.0 add_convert_fusion.1.refs_4_.refs_8_
  513.9 15.4 %rows_back_5.1 = (bf16[592,1536]{1,0:T(8,128)(2,1)}, f32[592,1536]{1,0:T(8,128)}, bf16[176,1536]{1,0:T(8,128)(2,1)S(1)}) custom-call(bf16[592,1536]{1,0:T(8,128)(2,1)} %get-tuple-element.173.refs_0_.refs_5_, bf16[592,1536]{1,0:T(8,128)(2,1)} %get-tuple-element.174.refs_1_.refs_4_, bf16[4,1,384,1536]{3,2,1,0:T(8,128)(2,1)} %all-gather.8.cloned.1.call-done.refs_4_.refs_2_, ...), custom_call_target="tpu_custom_call" | custom-call | flops 5586812928 | bytes 10911744 | tf_op jit(solution)/shard_map/rows_back_5/pallas_call | solution.py:128
  530.2 4.0 collective-permute-done.31
  534.1 4.4 convert_add_fusion.4
  538.6 23.2 %weight_grad_6.1 = (bf16[4,2,384,1536]{3,2,1,0:T(8,128)(2,1)}, bf16[240,1536]{1,0:T(8,128)(2,1)S(1)}) custom-call(bf16[592,1536]{1,0:T(8,128)(2,1)} %add_convert_fusion.3.refs_0_, bf16[592,1536]{1,0:T(8,128)(2,1)} %collective-permute-done.24.refs_1_, bf16[592,1536]{1,0:T(8,128)(2,1)} %collective-permute-done.25.refs_2_, ...), custom_call_target="tpu_custom_call" | custom-call | flops 11173625856 | bytes 21823488 | tf_op jit(solution)/shard_map/weight_grad_6/pallas_call | solution.py:128
  563.4 15.8 %rows_back_7.1 = (bf16[592,1536]{1,0:T(8,128)(2,1)}, f32[592,1536]{1,0:T(8,128)}, bf16[176,1536]{1,0:T(8,128)(2,1)S(1)}) custom-call(bf16[592,1536]{1,0:T(8,128)(2,1)} %get-tuple-element.193.refs_5_.refs_0_, bf16[592,1536]{1,0:T(8,128)(2,1)} %get-tuple-element.194.refs_4_.refs_1_, bf16[4,2,384,1536]{3,2,1,0:T(8,128)(2,1)} %bitcast.197, ...), custom_call_target="tpu_custom_call" | custom-call | flops 5586812928 | bytes 10911744 | tf_op jit(solution)/shard_map/rows_back_7/pallas_call | solution.py:128
  579.3 5.7 fusion.23
  588.9 8.2 fusion.42
  597.2 7.5 fusion.21
  605.4 41.8 %collective-permute-done.34.refs_2_ = bf16[592,1536]{1,0:T(8,128)(2,1)} collective-permute-done((bf16[592,1536]{1,0:T(8,128)(2,1)}, bf16[592,1536]{1,0:T(8,128)(2,1)}, u32[]{:S(2)}, u32[]{:S(2)}) %collective-permute-start.34) | collective-permute-done | bytes 1818656 | tf_op jit(solution)/shard_map/ppermute | solution.py:19
  659.4 7.8 rows_plain.1
  672.4 42.7 %attend_back_1_11.1 = (bf16[592,1152]{1,0:T(8,128)(2,1)}, bf16[592,1152]{1,0:T(8,128)(2,1)}, f32[3,4,128]{2,1,0:T(4,128)S(1)}, bf16[2,2,192,1536]{3,2,1,0:T(8,128)(2,1)}) custom-call(bf16[592,1152]{1,0:T(8,128)(2,1)} %get-tuple-element.206.refs_0_.refs_1_.refs_2_, bf16[592,1152]{1,0:T(8,128)(2,1)} %get-tuple-element.206.refs_0_.refs_1_.refs_2_, ...), custom_call_target="tpu_custom_call" | custom-call | flops 13457817600 | bytes 26284800 | tf_op jit(solution)/shard_map/attend_back_1_11/pallas_call | solution.py:128
  715.1 8.3 weight_grad.1
  726.7 54.8 %attend_back_0_12.1 = (bf16[592,1152]{1,0:T(8,128)(2,1)}, bf16[592,1152]{1,0:T(8,128)(2,1)}, f32[3,4,128]{2,1,0:T(4,128)S(1)}, bf16[2,2,192,1536]{3,2,1,0:T(8,128)(2,1)}) custom-call(bf16[592,1152]{1,0:T(8,128)(2,1)} %get-tuple-element.143.refs_0_.refs_1_.refs_2_, bf16[592,1152]{1,0:T(8,128)(2,1)} %get-tuple-element.143.refs_0_.refs_1_.refs_2_, ...), custom_call_target="tpu_custom_call" | custom-call | flops 13457817600 | bytes 26284800 | tf_op jit(solution)/shard_map/attend_back_0_12/pallas_call | solution.py:128
  781.6 9.4 rows_back.9
  791.0 12.5 %collective-permute-start.36 = (bf16[592,1536]{1,0:T(8,128)(2,1)}, bf16[592,1536]{1,0:T(8,128)(2,1)}, u32[]{:S(2)}, u32[]{:S(2)}) collective-permute-start(bf16[592,1536]{1,0:T(8,128)(2,1)} %get-tuple-element.222), channel_id=1, source_target_pairs={{0,4},{4,0},{1,5},{5,1},{2,6},{6,2},{3,7},{7,3},{8,12},{12,8},{9,1... | collective-permute-start | bytes 5455880 | tf_op jit(solution)/shard_map/ppermute | solution.py:19
  807.1 3.5 add_bitcast_fusion
  810.6 3.3 add_convert_fusion.refs_8_.refs_4_
  815.0 27.2 %weight_grad_8.1 = (bf16[4,2,384,1152]{3,2,1,0:T(8,128)(2,1)}, bf16[256,1536]{1,0:T(8,128)(2,1)S(1)}, bf16[2,2,192,384]{3,2,1,0:T(8,128)(2,1)S(1)}) custom-call(bf16[592,1536]{1,0:T(8,128)(2,1)} %copy-done.64, bf16[592,1536]{1,0:T(8,128)(2,1)} %copy-done.88, bf16[592,1536]{1,0:T(8,128)(2,1)} %copy-done.87, bf16[592,1536]{1,0:T(8,128)(2,1)} %copy-done.89, ...), custom_call_target="tpu_custom_call" | custom-call | flops 8380219392 | bytes 16367616 | tf_op jit(solution)/shard_map/weight_grad_8/pallas_call | solution.py:128
  842.2 41.1 %rows_back_9.1 = (bf16[592,1536]{1,0:T(8,128)(2,1)}, f32[592,1536]{1,0:T(8,128)}, bf16[336,1536]{1,0:T(8,128)(2,1)S(1)}, bf16[2,384,1152]{2,1,0:T(8,128)(2,1)}, bf16[2,384,1152]{2,1,0:T(8,128)(2,1)}) custom-call(bf16[592,1152]{1,0:T(8,128)(2,1)} %get-tuple-element.224.refs_5_.refs_0_, bf16[592,1152]{1,0:T(8,128)(2,1)} %get-tuple-element.225.refs_4_.refs_1_, ...), custom_call_target="tpu_custom_call" | custom-call | flops 4190109696 | bytes 8183808 | tf_op jit(solution)/shard_map/rows_back_9/pallas_call | solution.py:128
  883.3 2.7 convert_add_fusion.6
  892.8 14.9 %collective-permute-done.39 = bf16[384,1152]{1,0:T(8,128)(2,1)} collective-permute-done((bf16[384,1152]{1,0:T(8,128)(2,1)}, bf16[384,1152]{1,0:T(8,128)(2,1)}, u32[]{:S(2)}, u32[]{:S(2)}) %collective-permute-start.39) | collective-permute-done | bytes 884768 | tf_op jit(solution)/shard_map/ppermute | solution.py:19
  915.1 5.6 fusion.2
  925.3 4.5 fusion.11
  934.9 2.4 collective-permute-start.58
  938.1 2.8 collective-permute-start.41
  957.5 2.5 collective-permute-done.43
  961.9 3.4 collective-permute-done.44
  968.8 4.2 convolution_bitcast_fusion
  975.0 19.1 %collective-permute-done.52 = f32[1,2,6,384]{3,2,1,0:T(8,128)S(1)} collective-permute-done((f32[1,2,6,384]{3,2,1,0:T(8,128)S(1)}, f32[1,2,6,384]{3,2,1,0:T(8,128)S(1)}, u32[]{:S(2)}, u32[]{:S(2)}) %collective-permute-start.52) | collective-permute-done | bytes 18464 | tf_op jit(solution)/shard_map/ppermute | solution.py:19
  995.3 3.9 collective-permute-done.53
  1011.3 3.0 copy.128
  (476 shorter events, 161.5 us)
Async XLA Ops:
  7.2 183.1 %all-gather.6.cloned.1.call-start = ((), (), s32[]{:S(2)}) async-start(), calls=%async_computation.3 | async-start | bytes 2949120 | tf_op jit(solution)/shard_map/all_gather | solution.py:674
  9.6 49.4 %collective-permute-start.7 = (bf16[2,192,1152]{2,1,0:T(8,128)(2,1)}, bf16[2,192,1152]{2,1,0:T(8,128)(2,1)}, u32[]{:S(2)}, u32[]{:S(2)}) collective-permute-start(bf16[2,192,1152]{2,1,0:T(8,128)(2,1)} %bitcast.93), channel_id=1, source_target_pairs={{0,2},{6,4},{4,0},{2,6},{1,3},{7,5},{5,1},{3,7},{8,10},{14,12},{12... | collective-permute-start | bytes 2654216 | tf_op jit(solution)/shard_map/ppermute | solution.py:645
  13.6 45.3 %collective-permute-start.6 = (bf16[2,192,1152]{2,1,0:T(8,128)(2,1)}, bf16[2,192,1152]{2,1,0:T(8,128)(2,1)}, u32[]{:S(2)}, u32[]{:S(2)}) collective-permute-start(bf16[2,192,1152]{2,1,0:T(8,128)(2,1)} %bitcast.93), channel_id=1, source_target_pairs={{2,4},{4,2},{3,5},{5,3},{10,12},{12,10},{11,13},{13,11},{18,20},{2... | collective-permute-start | bytes 2654216 | tf_op jit(solution)/shard_map/ppermute | solution.py:644
  21.3 3.9 collective-permute-start.2
  26.3 5.2 collective-permute-start.3
  31.6 4.4 collective-permute-start.4
  37.4 15.8 %collective-permute-start.8 = (f32[1,2,2,6,384]{4,1,3,2,0:T(2,128)S(1)}, f32[1,2,2,6,384]{4,1,3,2,0:T(2,128)S(1)}, u32[]{:S(2)}, u32[]{:S(2)}) collective-permute-start(f32[1,2,2,6,384]{4,1,3,2,0:T(2,128)S(1)} %bitcast.213), channel_id=1, source_target_pairs={{0,1},{1,0},{2,3},{3,2},{4,5},{5,4},{6,7},{7,6},{8,9},{9,8},{10,11... | collective-permute-start | bytes 110600 | tf_op jit(solution)/shard_map/ppermute | solution.py:19
  53.3 5.3 collective-permute-start.9
  60.9 22.7 %collective-permute-start.11 = (bf16[384,1152]{1,0:T(8,128)(2,1)S(1)}, bf16[384,1152]{1,0:T(8,128)(2,1)S(1)}, u32[]{:S(2)}, u32[]{:S(2)}) collective-permute-start(bf16[384,1152]{1,0:T(8,128)(2,1)S(1)} %get-tuple-element.348), channel_id=1, source_target_pairs={{0,16},{16,0},{1,17},{17,1},{2,18},{18,2},{3,19},{19,3},{4,20},{20... | collective-permute-start | bytes 2654216 | tf_op jit(solution)/shard_map/ppermute | solution.py:19
  62.5 22.6 %collective-permute-start.10 = (bf16[384,1152]{1,0:T(8,128)(2,1)S(1)}, bf16[384,1152]{1,0:T(8,128)(2,1)S(1)}, u32[]{:S(2)}, u32[]{:S(2)}) collective-permute-start(bf16[384,1152]{1,0:T(8,128)(2,1)S(1)} %get-tuple-element.349), channel_id=1, source_target_pairs={{0,8},{8,0},{1,9},{9,1},{2,10},{10,2},{3,11},{11,3},{4,12},{12,4},... | collective-permute-start | bytes 2654216 | tf_op jit(solution)/shard_map/ppermute | solution.py:19
  64.2 38.3 %collective-permute-start.15 = (bf16[384,1152]{1,0:T(8,128)(2,1)S(1)}, bf16[384,1152]{1,0:T(8,128)(2,1)S(1)}, u32[]{:S(2)}, u32[]{:S(2)}) collective-permute-start(bf16[384,1152]{1,0:T(8,128)(2,1)S(1)} %get-tuple-element.349), channel_id=1, source_target_pairs={{0,16},{16,0},{1,17},{17,1},{2,18},{18,2},{3,19},{19,3},{4,20},{20... | collective-permute-start | bytes 2654216 | tf_op jit(solution)/shard_map/ppermute | solution.py:19
  71.0 53.6 %collective-permute-start.17 = (bf16[384,1152]{1,0:T(8,128)(2,1)S(1)}, bf16[384,1152]{1,0:T(8,128)(2,1)S(1)}, u32[]{:S(2)}, u32[]{:S(2)}) collective-permute-start(bf16[384,1152]{1,0:T(8,128)(2,1)S(1)} %get-tuple-element.348), channel_id=1, source_target_pairs={{0,8},{8,0},{1,9},{9,1},{2,10},{10,2},{3,11},{11,3},{4,12},{12,4},... | collective-permute-start | bytes 2654216 | tf_op jit(solution)/shard_map/ppermute | solution.py:19
  85.1 39.5 %collective-permute-start.13 = (bf16[592,1536]{1,0:T(8,128)(2,1)S(1)}, bf16[592,1536]{1,0:T(8,128)(2,1)S(1)}, u32[]{:S(2)}, u32[]{:S(2)}) collective-permute-start(bf16[592,1536]{1,0:T(8,128)(2,1)S(1)} %get-tuple-element.132.refs_0_), channel_id=1, source_target_pairs={{0,1},{1,0},{2,3},{3,2},{4,5},{5,4},{6,7},{7,6},{8,9},{9,8},{10,11... | collective-permute-start | bytes 5455880 | tf_op jit(solution)/shard_map/ppermute | solution.py:19
  88.5 37.3 %collective-permute-start.12 = (bf16[592,1536]{1,0:T(8,128)(2,1)S(1)}, bf16[592,1536]{1,0:T(8,128)(2,1)S(1)}, u32[]{:S(2)}, u32[]{:S(2)}) collective-permute-start(bf16[592,1536]{1,0:T(8,128)(2,1)S(1)} %get-tuple-element.132.refs_0_), channel_id=1, source_target_pairs={{0,4},{4,0},{1,5},{5,1},{2,6},{6,2},{3,7},{7,3},{8,12},{12,8},{9,1... | collective-permute-start | bytes 5455880 | tf_op jit(solution)/shard_map/ppermute | solution.py:19
  88.6 30.7 %collective-permute-start.16 = (bf16[384,1152]{1,0:T(8,128)(2,1)S(1)}, bf16[384,1152]{1,0:T(8,128)(2,1)S(1)}, u32[]{:S(2)}, u32[]{:S(2)}) collective-permute-start(bf16[384,1152]{1,0:T(8,128)(2,1)S(1)} %collective-permute-done.10), channel_id=1, source_target_pairs={{0,16},{16,0},{1,17},{17,1},{2,18},{18,2},{3,19},{19,3},{4,20},{20... | collective-permute-start | bytes 2654216 | tf_op jit(solution)/shard_map/ppermute | solution.py:19
  102.5 22.5 %collective-permute-start.18 = (bf16[384,1152]{1,0:T(8,128)(2,1)S(1)}, bf16[384,1152]{1,0:T(8,128)(2,1)S(1)}, u32[]{:S(2)}, u32[]{:S(2)}) collective-permute-start(bf16[384,1152]{1,0:T(8,128)(2,1)S(1)} %collective-permute-done.11), channel_id=1, source_target_pairs={{0,8},{8,0},{1,9},{9,1},{2,10},{10,2},{3,11},{11,3},{4,12},{12,4},... | collective-permute-start | bytes 2654216 | tf_op jit(solution)/shard_map/ppermute | solution.py:19
  124.6 3.8 collective-permute-start.14
  154.2 212.6 %all-gather.8.cloned.1.call-start = ((), (), s32[]{:S(2)}) async-start(), calls=%async_computation.4 | async-start | bytes 5898240 | tf_op jit(solution)/shard_map/all_gather | solution.py:674
  182.9 184.0 %all-gather.10.cloned.1.call-start = ((), (), s32[]{:S(2)}) async-start(), calls=%async_computation.5 | async-start | bytes 5898240 | tf_op jit(solution)/shard_map/all_gather | solution.py:674
  222.1 198.9 %all-gather.12.cloned.1.call-start = ((), (), s32[]{:S(2)}) async-start(), calls=%async_computation.6 | async-start | bytes 11796480 | tf_op jit(solution)/shard_map/all_gather | solution.py:674
  228.3 20.2 %collective-permute-start.20 = (bf16[592,1536]{1,0:T(8,128)(2,1)}, bf16[592,1536]{1,0:T(8,128)(2,1)S(1)}, u32[]{:S(2)}, u32[]{:S(2)}) collective-permute-start(bf16[592,1536]{1,0:T(8,128)(2,1)} %get-tuple-element.151), channel_id=1, source_target_pairs={{0,4},{4,0},{1,5},{5,1},{2,6},{6,2},{3,7},{7,3},{8,12},{12,8},{9,1... | collective-permute-start | bytes 5455880 | tf_op jit(solution)/shard_map/ppermute | solution.py:19
  228.4 26.5 %collective-permute-start.23 = (bf16[2,192,1536]{2,1,0:T(8,128)(2,1)S(1)}, bf16[2,192,1536]{2,1,0:T(8,128)(2,1)S(1)}, u32[]{:S(2)}, u32[]{:S(2)}) collective-permute-start(bf16[2,192,1536]{2,1,0:T(8,128)(2,1)S(1)} %bitcast.207), channel_id=1, source_target_pairs={{0,2},{6,4},{4,0},{2,6},{1,3},{7,5},{5,1},{3,7},{8,10},{14,12},{12... | collective-permute-start | bytes 3538952 | tf_op jit(solution)/shard_map/ppermute | solution.py:645
  230.4 24.5 %collective-permute-start.22 = (bf16[2,192,1536]{2,1,0:T(8,128)(2,1)S(1)}, bf16[2,192,1536]{2,1,0:T(8,128)(2,1)}, u32[]{:S(2)}, u32[]{:S(2)}) collective-permute-start(bf16[2,192,1536]{2,1,0:T(8,128)(2,1)S(1)} %bitcast.208), channel_id=1, source_target_pairs={{2,4},{4,2},{3,5},{5,3},{10,12},{12,10},{11,13},{13,11},{18,20},{2... | collective-permute-start | bytes 3538952 | tf_op jit(solution)/shard_map/ppermute | solution.py:644
  247.4 9.3 collective-permute-start.19
  250.3 66.5 %collective-permute-start.21 = (bf16[592,1536]{1,0:T(8,128)(2,1)}, bf16[592,1536]{1,0:T(8,128)(2,1)}, u32[]{:S(2)}, u32[]{:S(2)}) collective-permute-start(bf16[592,1536]{1,0:T(8,128)(2,1)} %add_convert_fusion.4), channel_id=1, source_target_pairs={{0,1},{1,0},{2,3},{3,2},{4,5},{5,4},{6,7},{7,6},{8,9},{9,8},{10,11... | collective-permute-start | bytes 5455880 | tf_op jit(solution)/shard_map/ppermute | solution.py:19
  325.5 344.8 %reduce-scatter.10.cloned.1.call-start = ((), (), s32[]{:S(2)}) async-start(), calls=%async_computation.7 | async-start | bytes 11796480
  325.6 41.1 %collective-permute-start.25 = (bf16[592,1536]{1,0:T(8,128)(2,1)}, bf16[592,1536]{1,0:T(8,128)(2,1)}, u32[]{:S(2)}, u32[]{:S(2)}) collective-permute-start(bf16[592,1536]{1,0:T(8,128)(2,1)} %add_convert_fusion.3.refs_0_), channel_id=1, source_target_pairs={{0,1},{1,0},{2,3},{3,2},{4,5},{5,4},{6,7},{7,6},{8,9},{9,8},{10,11... | collective-permute-start | bytes 5455880 | tf_op jit(solution)/shard_map/ppermute | solution.py:19
  325.7 41.2 %collective-permute-start.24 = (bf16[592,1536]{1,0:T(8,128)(2,1)}, bf16[592,1536]{1,0:T(8,128)(2,1)}, u32[]{:S(2)}, u32[]{:S(2)}) collective-permute-start(bf16[592,1536]{1,0:T(8,128)(2,1)} %add_convert_fusion.3.refs_0_), channel_id=1, source_target_pairs={{0,4},{4,0},{1,5},{5,1},{2,6},{6,2},{3,7},{7,3},{8,12},{12,8},{9,1... | collective-permute-start | bytes 5455880 | tf_op jit(solution)/shard_map/ppermute | solution.py:19
  366.7 4.1 collective-permute-start.26
  432.8 3.8 collective-permute-start.29
  432.8 6.3 collective-permute-start.27
  433.5 8.3 collective-permute-start.28
  494.0 230.7 %reduce-scatter.12.cloned.1.call-start = ((), (), s32[]{:S(2)}) async-start(), calls=%async_computation.8 | async-start | bytes 11796480
  506.1 3.8 collective-permute-start.30
  530.2 4.0 collective-permute-start.31
  562.6 251.3 %reduce-scatter.14.cloned.1.call-start = ((), (), s32[]{:S(2)}) async-start(), calls=%async_computation.9 | async-start | bytes 2949120
  579.2 17.9 %collective-permute-start.32 = (bf16[592,1536]{1,0:T(8,128)(2,1)}, bf16[592,1536]{1,0:T(8,128)(2,1)S(1)}, u32[]{:S(2)}, u32[]{:S(2)}) collective-permute-start(bf16[592,1536]{1,0:T(8,128)(2,1)} %get-tuple-element.196), channel_id=1, source_target_pairs={{0,4},{4,0},{1,5},{5,1},{2,6},{6,2},{3,7},{7,3},{8,12},{12,8},{9,1... | collective-permute-start | bytes 5455880 | tf_op jit(solution)/shard_map/ppermute | solution.py:19
  604.7 42.5 %collective-permute-start.34 = (bf16[592,1536]{1,0:T(8,128)(2,1)}, bf16[592,1536]{1,0:T(8,128)(2,1)}, u32[]{:S(2)}, u32[]{:S(2)}) collective-permute-start(bf16[592,1536]{1,0:T(8,128)(2,1)} %get-tuple-element.213.refs_0_), channel_id=1, source_target_pairs={{0,1},{1,0},{2,3},{3,2},{4,5},{5,4},{6,7},{7,6},{8,9},{9,8},{10,11... | collective-permute-start | bytes 5455880 | tf_op jit(solution)/shard_map/ppermute | solution.py:19
  605.3 52.5 %collective-permute-start.33 = (bf16[592,1536]{1,0:T(8,128)(2,1)}, bf16[592,1536]{1,0:T(8,128)(2,1)}, u32[]{:S(2)}, u32[]{:S(2)}) collective-permute-start(bf16[592,1536]{1,0:T(8,128)(2,1)} %get-tuple-element.213.refs_0_), channel_id=1, source_target_pairs={{0,4},{4,0},{1,5},{5,1},{2,6},{6,2},{3,7},{7,3},{8,12},{12,8},{9,1... | collective-permute-start | bytes 5455880 | tf_op jit(solution)/shard_map/ppermute | solution.py:19
  647.2 12.2 %collective-permute-start.35 = (bf16[592,1536]{1,0:T(8,128)(2,1)}, bf16[592,1536]{1,0:T(8,128)(2,1)}, u32[]{:S(2)}, u32[]{:S(2)}) collective-permute-start(bf16[592,1536]{1,0:T(8,128)(2,1)} %collective-permute-done.34.refs_2_), channel_id=1, source_target_pairs={{0,4},{4,0},{1,5},{5,1},{2,6},{6,2},{3,7},{7,3},{8,12},{12,8},{9,1... | collective-permute-start | bytes 5455880 | tf_op jit(solution)/shard_map/ppermute | solution.py:19
  724.6 79.1 %collective-permute-start.54 = (f32[2,2,1536]{2,1,0:T(2,128)S(1)}, f32[2,2,1536]{2,1,0:T(2,128)S(1)}, u32[]{:S(2)}, u32[]{:S(2)}) collective-permute-start(f32[2,2,1536]{2,1,0:T(2,128)S(1)} %pad_maximum_fusion.12), channel_id=1, source_target_pairs={{0,1},{1,0},{2,3},{3,2},{4,5},{5,4},{6,7},{7,6},{8,9},{9,8},{10,11... | collective-permute-start | bytes 73736 | tf_op jit(solution)/shard_map/ppermute | solution.py:19
  791.0 19.6 %collective-permute-start.36 = (bf16[592,1536]{1,0:T(8,128)(2,1)}, bf16[592,1536]{1,0:T(8,128)(2,1)}, u32[]{:S(2)}, u32[]{:S(2)}) collective-permute-start(bf16[592,1536]{1,0:T(8,128)(2,1)} %get-tuple-element.222), channel_id=1, source_target_pairs={{0,4},{4,0},{1,5},{5,1},{2,6},{6,2},{3,7},{7,3},{8,12},{12,8},{9,1... | collective-permute-start | bytes 5455880 | tf_op jit(solution)/shard_map/ppermute | solution.py:19
  887.1 20.6 %collective-permute-start.39 = (bf16[384,1152]{1,0:T(8,128)(2,1)}, bf16[384,1152]{1,0:T(8,128)(2,1)}, u32[]{:S(2)}, u32[]{:S(2)}) collective-permute-start(bf16[384,1152]{1,0:T(8,128)(2,1)} %fusion.37), channel_id=1, source_target_pairs={{0,8},{8,0},{1,9},{9,1},{2,10},{10,2},{3,11},{11,3},{4,12},{12,4},... | collective-permute-start | bytes 2654216 | tf_op jit(solution)/shard_map/ppermute | solution.py:19
  889.2 20.5 %collective-permute-start.38 = (bf16[384,1152]{1,0:T(8,128)(2,1)}, bf16[384,1152]{1,0:T(8,128)(2,1)}, u32[]{:S(2)}, u32[]{:S(2)}) collective-permute-start(bf16[384,1152]{1,0:T(8,128)(2,1)} %fusion.36), channel_id=1, source_target_pairs={{0,16},{16,0},{1,17},{17,1},{2,18},{18,2},{3,19},{19,3},{4,20},{20... | collective-permute-start | bytes 2654216 | tf_op jit(solution)/shard_map/ppermute | solution.py:19
  890.1 23.0 %collective-permute-start.37 = (bf16[592,1536]{1,0:T(8,128)(2,1)}, bf16[592,1536]{1,0:T(8,128)(2,1)}, u32[]{:S(2)}, u32[]{:S(2)}) collective-permute-start(bf16[592,1536]{1,0:T(8,128)(2,1)} %get-tuple-element.227), channel_id=1, source_target_pairs={{0,4},{4,0},{1,5},{5,1},{2,6},{6,2},{3,7},{7,3},{8,12},{12,8},{9,1... | collective-permute-start | bytes 5455880 | tf_op jit(solution)/shard_map/ppermute | solution.py:19
  924.1 5.9 collective-permute-start.56
  930.0 4.8 collective-permute-start.57
  933.6 4.4 collective-permute-start.40
  934.9 6.1 collective-permute-start.58
  938.1 9.3 collective-permute-start.41
  944.7 8.1 collective-permute-start.60
  947.4 9.3 collective-permute-start.62
  948.4 6.4 collective-permute-start.42
  951.1 49.5 %collective-permute-start.49 = (bf16[2,192,1152]{2,1,0:T(8,128)(2,1)S(1)}, bf16[2,192,1152]{2,1,0:T(8,128)(2,1)}, u32[]{:S(2)}, u32[]{:S(2)}) collective-permute-start(bf16[2,192,1152]{2,1,0:T(8,128)(2,1)S(1)} %get-tuple-element.342), channel_id=1, source_target_pairs={{2,0},{4,6},{0,4},{6,2},{3,1},{5,7},{1,5},{7,3},{10,8},{12,14},{8,... | collective-permute-start | bytes 2654216 | tf_op jit(solution)/shard_map/ppermute | solution.py:733
  951.2 49.4 %collective-permute-start.48 = (bf16[2,192,1152]{2,1,0:T(8,128)(2,1)S(1)}, bf16[2,192,1152]{2,1,0:T(8,128)(2,1)}, u32[]{:S(2)}, u32[]{:S(2)}) collective-permute-start(bf16[2,192,1152]{2,1,0:T(8,128)(2,1)S(1)} %get-tuple-element.343), channel_id=1, source_target_pairs={{2,4},{4,2},{3,5},{5,3},{10,12},{12,10},{11,13},{13,11},{18,20},{2... | collective-permute-start | bytes 2654216 | tf_op jit(solution)/shard_map/ppermute | solution.py:732
  955.7 4.4 collective-permute-start.43
  960.2 5.2 collective-permute-start.44
  967.0 6.9 collective-permute-start.45
  973.0 21.0 %collective-permute-start.52 = (f32[1,2,6,384]{3,2,1,0:T(8,128)S(1)}, f32[1,2,6,384]{3,2,1,0:T(8,128)S(1)}, u32[]{:S(2)}, u32[]{:S(2)}) collective-permute-start(f32[1,2,6,384]{3,2,1,0:T(8,128)S(1)} %add_bitcast_fusion.4), channel_id=1, source_target_pairs={{0,1},{1,0},{2,3},{3,2},{4,5},{5,4},{6,7},{7,6},{8,9},{9,8},{10,11... | collective-permute-start | bytes 55304 | tf_op jit(solution)/shard_map/ppermute | solution.py:19
  973.9 20.3 %collective-permute-start.46 = (f32[2,16,192]{2,1,0:T(8,128)S(1)}, f32[2,16,192]{2,1,0:T(8,128)S(1)}, u32[]{:S(2)}, u32[]{:S(2)}) collective-permute-start(f32[2,16,192]{2,1,0:T(8,128)S(1)} %pad_maximum_fusion.10), channel_id=1, source_target_pairs={{0,8},{8,0},{1,9},{9,1},{2,10},{10,2},{3,11},{11,3},{4,12},{12,4},... | collective-permute-start | bytes 73736 | tf_op jit(solution)/shard_map/ppermute | solution.py:19
  994.1 5.1 collective-permute-start.53
  994.2 5.7 collective-permute-start.47
  1000.6 3.9 collective-permute-start.50
  1005.2 9.1 collective-permute-start.51
  (97 other events, 881.3 us)
Sparse Core Ops, SparseCore 0:
  154.4 35.9 all-gather.5
  192.2 57.1 all-gather.7
  251.2 57.0 all-gather.9
  325.7 95.3 all-gather.11
  494.1 94.8 reduce-scatter.9
  591.9 95.0 reduce-scatter.11
  723.6 48.4 reduce-scatter.13

commit v4 on v3

--- a/solution.py
+++ b/solution.py
@@ -705,19 +705,24 @@
             NeighbourRide(g, self.y, shape, along_y, 2),
         ]
 
-    def sum_plane(self, g, arrived):
+    def sum_plane_first(self, g, arrived):
         x, y = lax.axis_index(self.x), lax.axis_index(self.y)
-        pick = lambda v, i, dim: lax.dynamic_index_in_dim(v, i, dim, keepdims=False)
         g = g.reshape((2, 2) + g.shape[1:])
+        sums = []
+        for stream in range(2):
+            at, size = (((0, x, 0), (2, 1)), ((y, 0, 1), (1, 2)))[stream]
+            v = lax.dynamic_slice(g, at + (0, 0), size + (1,) + g.shape[3:])
+            v = v.reshape(arrived[stream].shape)
+            sums.append(v.astype(F32) + arrived[stream].astype(F32))
+        return sums
+
+    def sum_plane_last(self, sums):
         done = []
-        for stream in range(2):
-            near, dim, far_axis, far = ((x, 1, self.y, y), (y, 0, self.x, x))[stream]
-            at = (0, near, stream, 0, 0) if dim == 1 else (near, 0, stream, 0, 0)
-            size = (2, 1) if dim == 1 else (1, 2)
-            v = lax.dynamic_slice(g, at, size + (1,) + g.shape[3:]).reshape(arrived[stream].shape)
-            v = v.astype(F32) + arrived[stream].astype(F32)
-            v = pick(v, far, 0) + swap(pick(v, 1 - far, 0).astype(BF), far_axis).astype(F32)
-            done.append(v)
+        for v, axis in zip(sums, (self.y, self.x)):
+            at = lax.axis_index(axis)
+            low, high = v[0], v[1]
+            keep, send = jnp.where(at == 0, low, high), jnp.where(at == 0, high, low)
+            done.append(keep + swap(send.astype(BF), axis).astype(F32))
         return jnp.stack(done)
 
     def trade_parts(self, g):
@@ -991,7 +996,7 @@
             (v[0].astype(F32) + v[1].astype(F32))[:, :, None]
             for v in (down_sums[0], up_sums[0], proj_sums)
         ]
-        qkv_plane = lay.sum_plane(qkv_grads, rode_two[1:3])
+        plane_sums = lay.sum_plane_first(qkv_grads, rode_two[1:3])
     else:
         down_grad, up_grad, proj_grad = [
             lay.scatter_generic(g, 1) for g in (down_grads, up_grads, proj_grads)
@@ -1013,6 +1018,10 @@
         ],
         axis=1,
     )
+    if compact:
+        plane_sums, grad_mod = tie(plane_sums, grad_mod)
+        qkv_plane = lay.sum_plane_last(plane_sums)
+    grad_mod_own = grad_mod
     grad_mod = sum_bits(grad_mod, (lay.p,))
     grad_mod = gather_bits(grad_mod[None], t_up[1:])
     if compact:
@@ -1038,12 +1047,8 @@
     cond_slice = lax.dynamic_slice_in_dim(condition.astype(F32), t_index * columns, columns, 1)
     unused, silu_pull = jax.vjp(jax.nn.silu, cond_slice)
     condition_grad = silu_pull(cond_terms)[0]
-    ada_bias_grad = gather_bits(jnp.sum(grad_mod, axis=0)[None], t_up)
-    ada_bias_grad = jnp.moveaxis(ada_bias_grad, 0, 2).reshape(2, 6, width)
-
-    own_part = sum_bits(
-        jnp.stack([total(grad_one.astype(F32)), total(grad_two.astype(F32))]), (lay.p, lay.q)
-    )
+    own_part = [total(grad_one.astype(F32))[:, None], total(grad_two.astype(F32))[:, None]]
+    own_part = sum_bits(jnp.concatenate(own_part + [grad_mod_own], axis=1), (lay.p, lay.q))
     sums = grad_mine[2] + grad_other[2]
     pairs = sums.shape[0]
     qv_part = jnp.transpose(sums.reshape(pairs, 2, 2, -1), (2, 1, 0, 3)).reshape(2, 2, heads_n)
@@ -1062,15 +1067,15 @@
         input_grads[img_rows : img_rows + txt_rows],
         condition_grad,
         ada_grad,
-        ada_bias_grad,
+        own_part[:, 2:],
         qkv_grad,
         qv_bias_grad,
         proj_grad,
-        own_part[0],
+        own_part[:, 0],
         up_grad,
         up_bias_grad,
         down_grad,
-        own_part[1],
+        own_part[:, 1],
     )
 
 

time: 1030 us -> 1050 us (1.019)
  waiting for transfers between devices: 316 us -> 334 us
    ppermute x1, waiting for transfers between devices: 0.01 us -> 26.2 us  [trade_sends(): lax.ppermute(second.astype(BF), joint, [(1, 0), (2, 3), (0, 2), (3, 1)])]
    ppermute x57 -> x55, waiting for transfers between devices: 285 us -> 277 us  [swap(): return lax.ppermute(v, axis, [(0, 1), (1, 0)])]
    ppermute x57 -> x55, starting transfers between devices: 59.5 us -> 62.1 us  [swap(): return lax.ppermute(v, axis, [(0, 1), (1, 0)])]
    unnamed x186 -> x189, local copies, waits for them, and re-layouts: 32.9 us -> 31 us
  transfers between devices with their start and end apart: 70 -> 68, of which waited for: 36 -> 38; matrix products, arithmetic and copies ran while one was open for 12% -> 12% of each run, Pallas kernels for 28% -> 27%
where the time goes in v4:
time: 1050 us; the launch traced here: 1040 us
  Pallas kernels  438 us (42%)
  waiting for transfers between devices  334 us (32%)
  other arithmetic  109 us (10%)
  starting transfers between devices  83.8 us (8%)
  local copies, waits for them, and re-layouts  53.4 us (5%)
  between operations  16.8 us (2%)
    pallas_call x13, Pallas kernels, launch(): pl.pallas_call(body, in_specs=[anywhere] * (n_in + n_rides), out_specs=[a...  379 us
    ppermute x55, waiting for transfers between devices, swap(): return lax.ppermute(v, axis, [(0, 1), (1, 0)])  277 us
    ppermute x55, starting transfers between devices, swap(): return lax.ppermute(v, axis, [(0, 1), (1, 0)])  62.1 us
    pallas_call x7, Pallas kernels, launch(): pl.pallas_call(kernel, grid=grid, in_specs=in_specs, out_specs=out_specs,...  59 us
    unnamed x189, local copies, waits for them, and re-layouts  31 us
    all_gather x4, waiting for transfers between devices, spread_rows_async(): return lax.all_gather(own, (self.y, self.x), axis=0, tiled=False)  27.3 us
    ppermute x1, waiting for transfers between devices, trade_sends(): lax.ppermute(second.astype(BF), joint, [(1, 0), (2, 3), (0, 2), (3, 1)])  26.2 us
  transfers between devices with their start and end apart: 68, of which 38 were waited for; matrix products, arithmetic and copies ran while one was open for 12% of the time, Pallas kernels for 27%

profile of v4, /device:TPU:0, one launch (start us, length us, event | category | flops | bytes accessed | tf_op | source)
XLA Modules:
  0.0 1041.4 jit_solution(13688221361650510312)
XLA Ops:
  9.6 4.0 collective-permute-start.7
  33.1 2.9 collective-permute-done.4
  40.3 12.9 %collective-permute-done.8 = f32[1,2,2,6,384]{4,1,3,2,0:T(2,128)S(1)} collective-permute-done((f32[1,2,2,6,384]{4,1,3,2,0:T(2,128)S(1)}, f32[1,2,2,6,384]{4,1,3,2,0:T(2,128)S(1)}, u32[]{:S(2)}, u32[]{:S(2)}) %collective-permute-start.8) | collective-permute-done | bytes 36896 | tf_op jit(solution)/shard_map/ppermute | solution.py:19
  53.3 2.8 collective-permute-start.9
  64.8 6.2 fusion.58
  71.6 11.9 %collective-permute-done.11 = bf16[384,1152]{1,0:T(8,128)(2,1)S(1)} collective-permute-done((bf16[384,1152]{1,0:T(8,128)(2,1)S(1)}, bf16[384,1152]{1,0:T(8,128)(2,1)S(1)}, u32[]{:S(2)}, u32[]{:S(2)}) %collective-permute-start.11) | collective-permute-done | bytes 884768 | tf_op jit(solution)/shard_map/ppermute | solution.py:19
  89.3 13.2 %collective-permute-done.15 = bf16[384,1152]{1,0:T(8,128)(2,1)S(1)} collective-permute-done((bf16[384,1152]{1,0:T(8,128)(2,1)S(1)}, bf16[384,1152]{1,0:T(8,128)(2,1)S(1)}, u32[]{:S(2)}, u32[]{:S(2)}) %collective-permute-start.15) | collective-permute-done | bytes 884768 | tf_op jit(solution)/shard_map/ppermute | solution.py:19
  104.1 15.1 %collective-permute-done.16 = bf16[384,1152]{1,0:T(8,128)(2,1)S(1)} collective-permute-done((bf16[384,1152]{1,0:T(8,128)(2,1)S(1)}, bf16[384,1152]{1,0:T(8,128)(2,1)S(1)}, u32[]{:S(2)}, u32[]{:S(2)}) %collective-permute-start.16) | collective-permute-done | bytes 884768 | tf_op jit(solution)/shard_map/ppermute | solution.py:19
  119.4 5.1 collective-permute-done.13.refs_2_
  129.7 24.5 %rows_bias_1.1 = (bf16[592,1152]{1,0:T(8,128)(2,1)}, bf16[592,1152]{1,0:T(8,128)(2,1)}, bf16[592,1152]{1,0:T(8,128)(2,1)}, bf16[592,1152]{1,0:T(8,128)(2,1)}, bf16[2,2,192,384]{3,2,1,0:T(8,128)(2,1)}) custom-call(bf16[592,1536]{1,0:T(8,128)(2,1)} %copy-done.62, bf16[592,1536]{1,0:T(8,128)(2,1)} %copy-done.88, bf16[592,1536]{1,0:T(8,128)(2,1)} %copy-done.87, ...), custom_call_target="tpu_custom_call" | custom-call | flops 8380219392 | bytes 16367616 | tf_op jit(solution)/shard_map/rows_bias_1/pallas_call | solution.py:128
  155.5 27.4 %attend_1_2.1 = (bf16[592,384]{1,0:T(8,128)(2,1)S(1)}, bf16[592,384]{1,0:T(8,128)(2,1)S(1)}, f32[3,2,4,256]{3,2,1,0:T(4,128)S(1)}, f32[3,2,1,160]{3,2,1,0:T(1,128)S(1)}, bf16[1,2,192,1536]{3,2,1,0:T(8,128)(2,1)}) custom-call(bf16[592,1152]{1,0:T(8,128)(2,1)} %get-tuple-element.209.refs_0_.refs_1_.refs_2_, ...), custom_call_target="tpu_custom_call" | custom-call | flops 5383127040 | bytes 10513920 | tf_op jit(solution)/shard_map/attend_1_2/pallas_call | solution.py:128
  183.0 7.4 all-gather.6.cloned.1.call-done.refs_2_.refs_3_.refs_4_.refs_5_
  190.4 30.1 %attend_0_10.1 = (bf16[592,384]{1,0:T(8,128)(2,1)S(1)}, bf16[592,384]{1,0:T(8,128)(2,1)S(1)}, f32[3,2,4,256]{3,2,1,0:T(4,128)S(1)}, f32[3,2,1,160]{3,2,1,0:T(1,1...) custom-call(bf16[592,1152]{1,0:T(8,128)(2,1)} %get-tuple-element.146.refs_0_.refs_1_.refs_2_, ...), custom_call_target="tpu_custom_call" | custom-call | flops 5383127040 | bytes 10513920 | tf_op jit(solution)/shard_map/attend_0_10/pallas_call | solution.py:128
  223.3 5.0 rows_back.6
  230.4 11.9 %collective-permute-start.22 = (bf16[2,192,1536]{2,1,0:T(8,128)(2,1)S(1)}, bf16[2,192,1536]{2,1,0:T(8,128)(2,1)}, u32[]{:S(2)}, u32[]{:S(2)}) collective-permute-start(bf16[2,192,1536]{2,1,0:T(8,128)(2,1)S(1)} %bitcast.181), channel_id=1, source_target_pairs={{2,4},{4,2},{3,5},{5,3},{10,12},{12,10},{11,13},{13,11},{18,20},{2... | collective-permute-start | bytes 3538952 | tf_op jit(solution)/shard_map/ppermute | solution.py:644
  242.4 5.0 rows_back.5
  251.8 3.1 collective-permute-done.23
  256.7 60.1 %collective-permute-done.21 = bf16[592,1536]{1,0:T(8,128)(2,1)} collective-permute-done((bf16[592,1536]{1,0:T(8,128)(2,1)}, bf16[592,1536]{1,0:T(8,128)(2,1)}, u32[]{:S(2)}, u32[]{:S(2)}) %collective-permute-start.21) | collective-permute-done | bytes 1818656 | tf_op jit(solution)/shard_map/ppermute | solution.py:19
  316.8 4.4 fusion.60
  325.7 41.0 %collective-permute-done.25.refs_2_ = bf16[592,1536]{1,0:T(8,128)(2,1)} collective-permute-done((bf16[592,1536]{1,0:T(8,128)(2,1)}, bf16[592,1536]{1,0:T(8,128)(2,1)}, u32[]{:S(2)}, u32[]{:S(2)}) %collective-permute-start.25) | collective-permute-done | bytes 1818656 | tf_op jit(solution)/shard_map/ppermute | solution.py:19
  366.8 4.0 collective-permute-done.26.refs_3_
  370.8 29.3 %rows_gelu_13.1 = (bf16[592,1536]{1,0:T(8,128)(2,1)}, bf16[592,1536]{1,0:T(8,128)(2,1)}, bf16[592,1536]{1,0:T(8,128)(2,1)}, bf16[592,1536]{1,0:T(8,128)(2,1)}, f...) custom-call(bf16[592,1536]{1,0:T(8,128)(2,1)} %add_convert_fusion.3., ...), custom_call_target="tpu_custom_call" | custom-call | flops 11173625856 | bytes 21823488 | tf_op jit(solution)/shard_map/rows_gelu_13/pallas_call | solution.py:128
  401.1 19.8 %all-gather.12.cloned.1.call-done = bf16[8,384,1536]{2,1,0:T(8,128)(2,1)} async-done(((bf16[2,384,1536]{2,1,0:T(8,128)(2,1)}), bf16[8,384,1536]{2,1,0:T(8,128)(2,1)}) %all-gather.12.cloned.1.call-update) | async-done | bytes 9437200 | tf_op jit(solution)/shard_map/all_gather | solution.py:674
  421.0 11.8 %rows_back.7 = (bf16[592,1536]{1,0:T(8,128)(2,1)S(1)}, f32[592,1536]{1,0:T(8,128)}) custom-call(bf16[592,1536]{1,0:T(8,128)(2,1)} %get-tuple-element.166.refs_0_.refs_7_, bf16[592,1536]{1,0:T(8,128)(2,1)} %get-tuple-element.165.refs_1_.refs_6_, bf16[4,2,384,1536]{3,2,1,0:T(8,128)(2,1)} %bitcast.166, bf16[4,2,384,1536]{3,2,1,0:T(8,128)(2,1)} %bitcast.167), custom_call_target="tpu_custom_call" | custom-call | flops 5586812928 | bytes 10911744 | tf_op jit(solution)/shard_map/rows_back/pallas_call | solution.py:81
  433.6 2.9 collective-permute-done.29
  442.9 25.8 %rows_slope_3.1 = (bf16[592,1536]{1,0:T(8,128)(2,1)}, bf16[592,1536]{1,0:T(8,128)(2,1)}, bf16[592,1536]{1,0:T(8,128)(2,1)}, bf16[592,1536]{1,0:T(8,128)(2,1)}, f...) custom-call(bf16[592,1536]{1,0:T(8,128)(2,1)} %get-tuple-element.180.refs_6_.refs_7_.refs_0_, ...), custom_call_target="tpu_custom_call" | custom-call | flops 11173625856 | bytes 21823488 | tf_op jit(solution)/shard_map/rows_slope_3/pallas_call | solution.py:128
  469.7 23.4 %weight_grad_4.1 = (bf16[4,2,384,1536]{3,2,1,0:T(8,128)(2,1)}, bf16[256,1536]{1,0:T(8,128)(2,1)S(1)}) custom-call(bf16[592,1536]{1,0:T(8,128)(2,1)} %get-tuple-element.180.refs_6_.refs_7_.refs_0_, bf16[592,1536]{1,0:T(8,128)(2,1)} %copy-done.63, bf16[592,1536]{1,0:T(8,128)(2,1)} %copy-done.58, bf16[592,1536]{1,0:T(8,128)(2,1)} %copy-done.64, ...), custom_call_target="tpu_custom_call" | custom-call | flops 11173625856 | bytes 21823488 | tf_op jit(solution)/shard_map/weight_grad_4/pallas_call | solution.py:128
  494.0 12.1 %rows_back.8 = (bf16[592,1536]{1,0:T(8,128)(2,1)S(1)}, f32[592,1536]{1,0:T(8,128)}) custom-call(bf16[592,1536]{1,0:T(8,128)(2,1)} %get-tuple-element.185.refs_0_.refs_7_, bf16[592,1536]{1,0:T(8,128)(2,1)} %get-tuple-element.186.refs_1_.refs_6_, bf16[4,1,384,1536]{3,2,1,0:T(8,128)(2,1)} %all-gather.8.cloned.1.call-done.refs_4_.refs_2_, ...), custom_call_target="tpu_custom_call" | custom-call | flops 5586812928 | bytes 10911744 | tf_op jit(solution)/shard_map/rows_back/pallas_call | solution.py:81
  506.1 3.8 collective-permute-done.30
  509.9 4.0 add_convert_fusion.1.refs_4_.refs_8_
  513.9 15.5 %rows_back_5.1 = (bf16[592,1536]{1,0:T(8,128)(2,1)}, f32[592,1536]{1,0:T(8,128)}, bf16[176,1536]{1,0:T(8,128)(2,1)S(1)}) custom-call(bf16[592,1536]{1,0:T(8,128)(2,1)} %get-tuple-element.176.refs_0_.refs_5_, bf16[592,1536]{1,0:T(8,128)(2,1)} %get-tuple-element.177.refs_1_.refs_4_, bf16[4,1,384,1536]{3,2,1,0:T(8,128)(2,1)} %all-gather.8.cloned.1.call-done.refs_4_.refs_2_, ...), custom_call_target="tpu_custom_call" | custom-call | flops 5586812928 | bytes 10911744 | tf_op jit(solution)/shard_map/rows_back_5/pallas_call | solution.py:128
  530.2 4.0 collective-permute-done.31
  534.2 4.5 convert_add_fusion.4
  538.7 23.1 %weight_grad_6.1 = (bf16[4,2,384,1536]{3,2,1,0:T(8,128)(2,1)}, bf16[240,1536]{1,0:T(8,128)(2,1)S(1)}) custom-call(bf16[592,1536]{1,0:T(8,128)(2,1)} %add_convert_fusion.3.refs_0_, bf16[592,1536]{1,0:T(8,128)(2,1)} %collective-permute-done.24.refs_1_, bf16[592,1536]{1,0:T(8,128)(2,1)} %collective-permute-done.25.refs_2_, ...), custom_call_target="tpu_custom_call" | custom-call | flops 11173625856 | bytes 21823488 | tf_op jit(solution)/shard_map/weight_grad_6/pallas_call | solution.py:128
  563.4 16.0 %rows_back_7.1 = (bf16[592,1536]{1,0:T(8,128)(2,1)}, f32[592,1536]{1,0:T(8,128)}, bf16[176,1536]{1,0:T(8,128)(2,1)S(1)}) custom-call(bf16[592,1536]{1,0:T(8,128)(2,1)} %get-tuple-element.196.refs_5_.refs_0_, bf16[592,1536]{1,0:T(8,128)(2,1)} %get-tuple-element.197.refs_4_.refs_1_, bf16[4,2,384,1536]{3,2,1,0:T(8,128)(2,1)} %bitcast.170, ...), custom_call_target="tpu_custom_call" | custom-call | flops 5586812928 | bytes 10911744 | tf_op jit(solution)/shard_map/rows_back_7/pallas_call | solution.py:128
  579.5 5.7 fusion.23
  589.1 8.1 fusion.42
  597.3 7.5 fusion.21
  605.7 41.7 %collective-permute-done.34.refs_2_ = bf16[592,1536]{1,0:T(8,128)(2,1)} collective-permute-done((bf16[592,1536]{1,0:T(8,128)(2,1)}, bf16[592,1536]{1,0:T(8,128)(2,1)}, u32[]{:S(2)}, u32[]{:S(2)}) %collective-permute-start.34) | collective-permute-done | bytes 1818656 | tf_op jit(solution)/shard_map/ppermute | solution.py:19
  651.5 7.8 rows_plain.1
  664.4 42.7 %attend_back_1_11.1 = (bf16[592,1152]{1,0:T(8,128)(2,1)}, bf16[592,1152]{1,0:T(8,128)(2,1)}, f32[3,4,128]{2,1,0:T(4,128)S(1)}, bf16[2,2,192,1536]{3,2,1,0:T(8,128)(2,1)}) custom-call(bf16[592,1152]{1,0:T(8,128)(2,1)} %get-tuple-element.209.refs_0_.refs_1_.refs_2_, bf16[592,1152]{1,0:T(8,128)(2,1)} %get-tuple-element.209.refs_0_.refs_1_.refs_2_, ...), custom_call_target="tpu_custom_call" | custom-call | flops 13457817600 | bytes 26284800 | tf_op jit(solution)/shard_map/attend_back_1_11/pallas_call | solution.py:128
  707.1 7.9 weight_grad.1
  716.1 3.2 slice_reduce_fusion.3
  721.4 54.1 %attend_back_0_12.1 = (bf16[592,1152]{1,0:T(8,128)(2,1)}, bf16[592,1152]{1,0:T(8,128)(2,1)}, f32[3,4,128]{2,1,0:T(4,128)S(1)}, bf16[2,2,192,1536]{3,2,1,0:T(8,128)(2,1)}) custom-call(bf16[592,1152]{1,0:T(8,128)(2,1)} %get-tuple-element.146.refs_0_.refs_1_.refs_2_, bf16[592,1152]{1,0:T(8,128)(2,1)} %get-tuple-element.146.refs_0_.refs_1_.refs_2_, ...), custom_call_target="tpu_custom_call" | custom-call | flops 13457817600 | bytes 26284800 | tf_op jit(solution)/shard_map/attend_back_0_12/pallas_call | solution.py:128
  775.5 9.4 rows_back.9
  784.9 12.5 %collective-permute-start.36 = (bf16[592,1536]{1,0:T(8,128)(2,1)}, bf16[592,1536]{1,0:T(8,128)(2,1)S(1)}, u32[]{:S(2)}, u32[]{:S(2)}) collective-permute-start(bf16[592,1536]{1,0:T(8,128)(2,1)} %get-tuple-element.225), channel_id=1, source_target_pairs={{0,4},{4,0},{1,5},{5,1},{2,6},{6,2},{3,7},{7,3},{8,12},{12,8},{9,1... | collective-permute-start | bytes 5455880 | tf_op jit(solution)/shard_map/ppermute | solution.py:19
  808.6 26.4 %weight_grad_8.1 = (bf16[4,2,384,1152]{3,2,1,0:T(8,128)(2,1)}, bf16[256,1536]{1,0:T(8,128)(2,1)S(1)}, bf16[2,2,192,384]{3,2,1,0:T(8,128)(2,1)S(1)}) custom-call(bf16[592,1536]{1,0:T(8,128)(2,1)} %copy-done.62, bf16[592,1536]{1,0:T(8,128)(2,1)} %copy-done.88, bf16[592,1536]{1,0:T(8,128)(2,1)} %copy-done.87, bf16[592,1536]{1,0:T(8,128)(2,1)} %copy-done.89, ...), custom_call_target="tpu_custom_call" | custom-call | flops 8380219392 | bytes 16367616 | tf_op jit(solution)/shard_map/weight_grad_8/pallas_call | solution.py:128
  835.1 40.6 %rows_back_9.1 = (bf16[592,1536]{1,0:T(8,128)(2,1)}, f32[592,1536]{1,0:T(8,128)}, bf16[336,1536]{1,0:T(8,128)(2,1)S(1)}, bf16[2,384,1152]{2,1,0:T(8,128)(2,1)}, bf16[2,384,1152]{2,1,0:T(8,128)(2,1)}) custom-call(bf16[592,1152]{1,0:T(8,128)(2,1)} %get-tuple-element.227.refs_5_.refs_0_, bf16[592,1152]{1,0:T(8,128)(2,1)} %get-tuple-element.228.refs_4_.refs_1_, ...), custom_call_target="tpu_custom_call" | custom-call | flops 4190109696 | bytes 8183808 | tf_op jit(solution)/shard_map/rows_back_9/pallas_call | solution.py:128
  878.2 3.5 add_bitcast_fusion.1
  882.7 5.8 convert_add_fusion.5
  888.5 5.7 fusion.2
  901.3 6.1 fusion.11
  909.9 3.1 fusion.37
  923.3 2.8 collective-permute-done.41
  926.2 14.9 %collective-permute-done.55 = f32[228,128]{1,0:T(8,128)S(1)} collective-permute-done((f32[228,128]{1,0:T(8,128)S(1)}, f32[228,128]{1,0:T(8,128)S(1)}, u32[]{:S(2)}, u32[]{:S(2)}) %collective-permute-start.55) | collective-permute-done | bytes 116768 | tf_op jit(solution)/shard_map/ppermute | solution.py:19
  943.7 5.4 collective-permute-done.56
  962.3 3.3 collective-permute-done.43
  967.5 3.6 collective-permute-done.44
  980.5 2.6 collective-permute-done.47
  983.9 26.2 %collective-permute-done.49 = bf16[2,192,1152]{2,1,0:T(8,128)(2,1)} collective-permute-done((bf16[2,192,1152]{2,1,0:T(8,128)(2,1)S(1)}, bf16[2,192,1152]{2,1,0:T(8,128)(2,1)}, u32[]{:S(2)}, u32[]{:S(2)}) %collective-permute-start.49) | collective-permute-done | bytes 884768 | tf_op jit(solution)/shard_map/ppermute | solution.py:738
  1010.1 4.4 convolution_bitcast_fusion
  1014.5 5.1 collective-permute-done.50
  1019.6 6.4 collective-permute-start.51
  1030.0 3.0 copy.105
  (480 shorter events, 161.0 us)
Async XLA Ops:
  7.2 183.2 %all-gather.6.cloned.1.call-start = ((), (), s32[]{:S(2)}) async-start(), calls=%async_computation.3 | async-start | bytes 2949120 | tf_op jit(solution)/shard_map/all_gather | solution.py:674
  9.6 49.4 %collective-permute-start.7 = (bf16[2,192,1152]{2,1,0:T(8,128)(2,1)}, bf16[2,192,1152]{2,1,0:T(8,128)(2,1)}, u32[]{:S(2)}, u32[]{:S(2)}) collective-permute-start(bf16[2,192,1152]{2,1,0:T(8,128)(2,1)} %bitcast.85), channel_id=1, source_target_pairs={{0,2},{6,4},{4,0},{2,6},{1,3},{7,5},{5,1},{3,7},{8,10},{14,12},{12... | collective-permute-start | bytes 2654216 | tf_op jit(solution)/shard_map/ppermute | solution.py:645
  13.6 45.3 %collective-permute-start.6 = (bf16[2,192,1152]{2,1,0:T(8,128)(2,1)}, bf16[2,192,1152]{2,1,0:T(8,128)(2,1)}, u32[]{:S(2)}, u32[]{:S(2)}) collective-permute-start(bf16[2,192,1152]{2,1,0:T(8,128)(2,1)} %bitcast.85), channel_id=1, source_target_pairs={{2,4},{4,2},{3,5},{5,3},{10,12},{12,10},{11,13},{13,11},{18,20},{2... | collective-permute-start | bytes 2654216 | tf_op jit(solution)/shard_map/ppermute | solution.py:644
  15.2 1.6 collective-permute-start
  17.5 3.8 collective-permute-start.1
  21.3 3.9 collective-permute-start.2
  26.3 5.2 collective-permute-start.3
  31.6 4.4 collective-permute-start.4
  37.4 15.9 %collective-permute-start.8 = (f32[1,2,2,6,384]{4,1,3,2,0:T(2,128)S(1)}, f32[1,2,2,6,384]{4,1,3,2,0:T(2,128)S(1)}, u32[]{:S(2)}, u32[]{:S(2)}) collective-permute-start(f32[1,2,2,6,384]{4,1,3,2,0:T(2,128)S(1)} %bitcast.188), channel_id=1, source_target_pairs={{0,1},{1,0},{2,3},{3,2},{4,5},{5,4},{6,7},{7,6},{8,9},{9,8},{10,11... | collective-permute-start | bytes 110600 | tf_op jit(solution)/shard_map/ppermute | solution.py:19
  53.3 5.3 collective-permute-start.9
  60.9 22.7 %collective-permute-start.11 = (bf16[384,1152]{1,0:T(8,128)(2,1)S(1)}, bf16[384,1152]{1,0:T(8,128)(2,1)S(1)}, u32[]{:S(2)}, u32[]{:S(2)}) collective-permute-start(bf16[384,1152]{1,0:T(8,128)(2,1)S(1)} %get-tuple-element.335), channel_id=1, source_target_pairs={{0,16},{16,0},{1,17},{17,1},{2,18},{18,2},{3,19},{19,3},{4,20},{20... | collective-permute-start | bytes 2654216 | tf_op jit(solution)/shard_map/ppermute | solution.py:19
  62.5 22.6 %collective-permute-start.10 = (bf16[384,1152]{1,0:T(8,128)(2,1)S(1)}, bf16[384,1152]{1,0:T(8,128)(2,1)S(1)}, u32[]{:S(2)}, u32[]{:S(2)}) collective-permute-start(bf16[384,1152]{1,0:T(8,128)(2,1)S(1)} %get-tuple-element.336), channel_id=1, source_target_pairs={{0,8},{8,0},{1,9},{9,1},{2,10},{10,2},{3,11},{11,3},{4,12},{12,4},... | collective-permute-start | bytes 2654216 | tf_op jit(solution)/shard_map/ppermute | solution.py:19
  64.2 38.3 %collective-permute-start.15 = (bf16[384,1152]{1,0:T(8,128)(2,1)S(1)}, bf16[384,1152]{1,0:T(8,128)(2,1)S(1)}, u32[]{:S(2)}, u32[]{:S(2)}) collective-permute-start(bf16[384,1152]{1,0:T(8,128)(2,1)S(1)} %get-tuple-element.336), channel_id=1, source_target_pairs={{0,16},{16,0},{1,17},{17,1},{2,18},{18,2},{3,19},{19,3},{4,20},{20... | collective-permute-start | bytes 2654216 | tf_op jit(solution)/shard_map/ppermute | solution.py:19
  71.1 53.6 %collective-permute-start.17 = (bf16[384,1152]{1,0:T(8,128)(2,1)S(1)}, bf16[384,1152]{1,0:T(8,128)(2,1)S(1)}, u32[]{:S(2)}, u32[]{:S(2)}) collective-permute-start(bf16[384,1152]{1,0:T(8,128)(2,1)S(1)} %get-tuple-element.335), channel_id=1, source_target_pairs={{0,8},{8,0},{1,9},{9,1},{2,10},{10,2},{3,11},{11,3},{4,12},{12,4},... | collective-permute-start | bytes 2654216 | tf_op jit(solution)/shard_map/ppermute | solution.py:19
  85.1 39.5 %collective-permute-start.13 = (bf16[592,1536]{1,0:T(8,128)(2,1)S(1)}, bf16[592,1536]{1,0:T(8,128)(2,1)S(1)}, u32[]{:S(2)}, u32[]{:S(2)}) collective-permute-start(bf16[592,1536]{1,0:T(8,128)(2,1)S(1)} %get-tuple-element.135.refs_0_), channel_id=1, source_target_pairs={{0,1},{1,0},{2,3},{3,2},{4,5},{5,4},{6,7},{7,6},{8,9},{9,8},{10,11... | collective-permute-start | bytes 5455880 | tf_op jit(solution)/shard_map/ppermute | solution.py:19
  88.5 37.3 %collective-permute-start.12 = (bf16[592,1536]{1,0:T(8,128)(2,1)S(1)}, bf16[592,1536]{1,0:T(8,128)(2,1)S(1)}, u32[]{:S(2)}, u32[]{:S(2)}) collective-permute-start(bf16[592,1536]{1,0:T(8,128)(2,1)S(1)} %get-tuple-element.135.refs_0_), channel_id=1, source_target_pairs={{0,4},{4,0},{1,5},{5,1},{2,6},{6,2},{3,7},{7,3},{8,12},{12,8},{9,1... | collective-permute-start | bytes 5455880 | tf_op jit(solution)/shard_map/ppermute | solution.py:19
  88.6 30.7 %collective-permute-start.16 = (bf16[384,1152]{1,0:T(8,128)(2,1)S(1)}, bf16[384,1152]{1,0:T(8,128)(2,1)S(1)}, u32[]{:S(2)}, u32[]{:S(2)}) collective-permute-start(bf16[384,1152]{1,0:T(8,128)(2,1)S(1)} %collective-permute-done.10), channel_id=1, source_target_pairs={{0,16},{16,0},{1,17},{17,1},{2,18},{18,2},{3,19},{19,3},{4,20},{20... | collective-permute-start | bytes 2654216 | tf_op jit(solution)/shard_map/ppermute | solution.py:19
  102.5 22.5 %collective-permute-start.18 = (bf16[384,1152]{1,0:T(8,128)(2,1)S(1)}, bf16[384,1152]{1,0:T(8,128)(2,1)S(1)}, u32[]{:S(2)}, u32[]{:S(2)}) collective-permute-start(bf16[384,1152]{1,0:T(8,128)(2,1)S(1)} %collective-permute-done.11), channel_id=1, source_target_pairs={{0,8},{8,0},{1,9},{9,1},{2,10},{10,2},{3,11},{11,3},{4,12},{12,4},... | collective-permute-start | bytes 2654216 | tf_op jit(solution)/shard_map/ppermute | solution.py:19
  124.6 3.8 collective-permute-start.14
  154.3 212.5 %all-gather.8.cloned.1.call-start = ((), (), s32[]{:S(2)}) async-start(), calls=%async_computation.4 | async-start | bytes 5898240 | tf_op jit(solution)/shard_map/all_gather | solution.py:674
  182.9 183.9 %all-gather.10.cloned.1.call-start = ((), (), s32[]{:S(2)}) async-start(), calls=%async_computation.5 | async-start | bytes 5898240 | tf_op jit(solution)/shard_map/all_gather | solution.py:674
  222.1 198.9 %all-gather.12.cloned.1.call-start = ((), (), s32[]{:S(2)}) async-start(), calls=%async_computation.6 | async-start | bytes 11796480 | tf_op jit(solution)/shard_map/all_gather | solution.py:674
  228.4 20.1 %collective-permute-start.20 = (bf16[592,1536]{1,0:T(8,128)(2,1)}, bf16[592,1536]{1,0:T(8,128)(2,1)S(1)}, u32[]{:S(2)}, u32[]{:S(2)}) collective-permute-start(bf16[592,1536]{1,0:T(8,128)(2,1)} %get-tuple-element.154), channel_id=1, source_target_pairs={{0,4},{4,0},{1,5},{5,1},{2,6},{6,2},{3,7},{7,3},{8,12},{12,8},{9,1... | collective-permute-start | bytes 5455880 | tf_op jit(solution)/shard_map/ppermute | solution.py:19
  228.4 26.5 %collective-permute-start.23 = (bf16[2,192,1536]{2,1,0:T(8,128)(2,1)S(1)}, bf16[2,192,1536]{2,1,0:T(8,128)(2,1)S(1)}, u32[]{:S(2)}, u32[]{:S(2)}) collective-permute-start(bf16[2,192,1536]{2,1,0:T(8,128)(2,1)S(1)} %bitcast.180), channel_id=1, source_target_pairs={{0,2},{6,4},{4,0},{2,6},{1,3},{7,5},{5,1},{3,7},{8,10},{14,12},{12... | collective-permute-start | bytes 3538952 | tf_op jit(solution)/shard_map/ppermute | solution.py:645
  230.4 24.5 %collective-permute-start.22 = (bf16[2,192,1536]{2,1,0:T(8,128)(2,1)S(1)}, bf16[2,192,1536]{2,1,0:T(8,128)(2,1)}, u32[]{:S(2)}, u32[]{:S(2)}) collective-permute-start(bf16[2,192,1536]{2,1,0:T(8,128)(2,1)S(1)} %bitcast.181), channel_id=1, source_target_pairs={{2,4},{4,2},{3,5},{5,3},{10,12},{12,10},{11,13},{13,11},{18,20},{2... | collective-permute-start | bytes 3538952 | tf_op jit(solution)/shard_map/ppermute | solution.py:644
  247.4 9.4 collective-permute-start.19
  250.3 66.5 %collective-permute-start.21 = (bf16[592,1536]{1,0:T(8,128)(2,1)}, bf16[592,1536]{1,0:T(8,128)(2,1)}, u32[]{:S(2)}, u32[]{:S(2)}) collective-permute-start(bf16[592,1536]{1,0:T(8,128)(2,1)} %add_convert_fusion.4), channel_id=1, source_target_pairs={{0,1},{1,0},{2,3},{3,2},{4,5},{5,4},{6,7},{7,6},{8,9},{9,8},{10,11... | collective-permute-start | bytes 5455880 | tf_op jit(solution)/shard_map/ppermute | solution.py:19
  325.5 336.9 %reduce-scatter.10.cloned.1.call-start = ((), (), s32[]{:S(2)}) async-start(), calls=%async_computation.7 | async-start | bytes 11796480
  325.5 41.1 %collective-permute-start.25 = (bf16[592,1536]{1,0:T(8,128)(2,1)}, bf16[592,1536]{1,0:T(8,128)(2,1)}, u32[]{:S(2)}, u32[]{:S(2)}) collective-permute-start(bf16[592,1536]{1,0:T(8,128)(2,1)} %add_convert_fusion.3.refs_0_), channel_id=1, source_target_pairs={{0,1},{1,0},{2,3},{3,2},{4,5},{5,4},{6,7},{7,6},{8,9},{9,8},{10,11... | collective-permute-start | bytes 5455880 | tf_op jit(solution)/shard_map/ppermute | solution.py:19
  325.6 41.2 %collective-permute-start.24 = (bf16[592,1536]{1,0:T(8,128)(2,1)}, bf16[592,1536]{1,0:T(8,128)(2,1)}, u32[]{:S(2)}, u32[]{:S(2)}) collective-permute-start(bf16[592,1536]{1,0:T(8,128)(2,1)} %add_convert_fusion.3.refs_0_), channel_id=1, source_target_pairs={{0,4},{4,0},{1,5},{5,1},{2,6},{6,2},{3,7},{7,3},{8,12},{12,8},{9,1... | collective-permute-start | bytes 5455880 | tf_op jit(solution)/shard_map/ppermute | solution.py:19
  366.7 4.1 collective-permute-start.26
  432.7 3.8 collective-permute-start.29
  432.8 6.3 collective-permute-start.27
  433.4 8.3 collective-permute-start.28
  494.0 225.3 %reduce-scatter.12.cloned.1.call-start = ((), (), s32[]{:S(2)}) async-start(), calls=%async_computation.8 | async-start | bytes 11796480
  506.1 3.8 collective-permute-start.30
  530.2 4.0 collective-permute-start.31
  562.7 244.9 %reduce-scatter.14.cloned.1.call-start = ((), (), s32[]{:S(2)}) async-start(), calls=%async_computation.9 | async-start | bytes 2949120
  579.4 17.9 %collective-permute-start.32 = (bf16[592,1536]{1,0:T(8,128)(2,1)}, bf16[592,1536]{1,0:T(8,128)(2,1)S(1)}, u32[]{:S(2)}, u32[]{:S(2)}) collective-permute-start(bf16[592,1536]{1,0:T(8,128)(2,1)} %get-tuple-element.199), channel_id=1, source_target_pairs={{0,4},{4,0},{1,5},{5,1},{2,6},{6,2},{3,7},{7,3},{8,12},{12,8},{9,1... | collective-permute-start | bytes 5455880 | tf_op jit(solution)/shard_map/ppermute | solution.py:19
  604.9 42.5 %collective-permute-start.34 = (bf16[592,1536]{1,0:T(8,128)(2,1)}, bf16[592,1536]{1,0:T(8,128)(2,1)}, u32[]{:S(2)}, u32[]{:S(2)}) collective-permute-start(bf16[592,1536]{1,0:T(8,128)(2,1)} %get-tuple-element.216.refs_0_), channel_id=1, source_target_pairs={{0,1},{1,0},{2,3},{3,2},{4,5},{5,4},{6,7},{7,6},{8,9},{9,8},{10,11... | collective-permute-start | bytes 5455880 | tf_op jit(solution)/shard_map/ppermute | solution.py:19
  605.7 45.3 %collective-permute-start.33 = (bf16[592,1536]{1,0:T(8,128)(2,1)}, bf16[592,1536]{1,0:T(8,128)(2,1)}, u32[]{:S(2)}, u32[]{:S(2)}) collective-permute-start(bf16[592,1536]{1,0:T(8,128)(2,1)} %get-tuple-element.216.refs_0_), channel_id=1, source_target_pairs={{0,4},{4,0},{1,5},{5,1},{2,6},{6,2},{3,7},{7,3},{8,12},{12,8},{9,1... | collective-permute-start | bytes 5455880 | tf_op jit(solution)/shard_map/ppermute | solution.py:19
  647.4 4.1 collective-permute-start.35
  784.9 20.0 %collective-permute-start.36 = (bf16[592,1536]{1,0:T(8,128)(2,1)}, bf16[592,1536]{1,0:T(8,128)(2,1)S(1)}, u32[]{:S(2)}, u32[]{:S(2)}) collective-permute-start(bf16[592,1536]{1,0:T(8,128)(2,1)} %get-tuple-element.225), channel_id=1, source_target_pairs={{0,4},{4,0},{1,5},{5,1},{2,6},{6,2},{3,7},{7,3},{8,12},{12,8},{9,1... | collective-permute-start | bytes 5455880 | tf_op jit(solution)/shard_map/ppermute | solution.py:19
  875.7 12.7 %collective-permute-start.37 = (bf16[592,1536]{1,0:T(8,128)(2,1)}, bf16[592,1536]{1,0:T(8,128)(2,1)}, u32[]{:S(2)}, u32[]{:S(2)}) collective-permute-start(bf16[592,1536]{1,0:T(8,128)(2,1)} %get-tuple-element.230), channel_id=1, source_target_pairs={{0,4},{4,0},{1,5},{5,1},{2,6},{6,2},{3,7},{7,3},{8,12},{12,8},{9,1... | collective-permute-start | bytes 5455880 | tf_op jit(solution)/shard_map/ppermute | solution.py:19
  899.0 19.7 %collective-permute-start.40 = (f32[2,6,1536]{2,1,0:T(8,128)S(1)}, f32[2,6,1536]{2,1,0:T(8,128)}, u32[]{:S(2)}, u32[]{:S(2)}) collective-permute-start(f32[2,6,1536]{2,1,0:T(8,128)S(1)} %stack.126), channel_id=1, source_target_pairs={{0,1},{1,0},{2,3},{3,2},{4,5},{5,4},{6,7},{7,6},{8,9},{9,8},{10,11... | collective-permute-start | bytes 221192 | tf_op jit(solution)/shard_map/ppermute | solution.py:19
  900.4 6.9 collective-permute-start.52
  908.8 13.4 %collective-permute-start.54 = (f32[228,128]{1,0:T(8,128)S(1)}, f32[228,128]{1,0:T(8,128)S(1)}, u32[]{:S(2)}, u32[]{:S(2)}) collective-permute-start(f32[228,128]{1,0:T(8,128)S(1)} %maximum_bitcast_fusion), channel_id=1, source_target_pairs={{0,16},{16,0},{1,17},{17,1},{2,18},{18,2},{3,19},{19,3},{4,20},{20... | collective-permute-start | bytes 350216 | tf_op jit(solution)/shard_map/ppermute | solution.py:19
  916.7 36.7 %collective-permute-start.39 = (bf16[384,1152]{1,0:T(8,128)(2,1)}, bf16[384,1152]{1,0:T(8,128)(2,1)}, u32[]{:S(2)}, u32[]{:S(2)}) collective-permute-start(bf16[384,1152]{1,0:T(8,128)(2,1)} %fusion.37), channel_id=1, source_target_pairs={{0,8},{8,0},{1,9},{9,1},{2,10},{10,2},{3,11},{11,3},{4,12},{12,4},... | collective-permute-start | bytes 2654216 | tf_op jit(solution)/shard_map/ppermute | solution.py:19
  917.8 38.2 %collective-permute-start.38 = (bf16[384,1152]{1,0:T(8,128)(2,1)S(1)}, bf16[384,1152]{1,0:T(8,128)(2,1)}, u32[]{:S(2)}, u32[]{:S(2)}) collective-permute-start(bf16[384,1152]{1,0:T(8,128)(2,1)S(1)} %fusion.36), channel_id=1, source_target_pairs={{0,16},{16,0},{1,17},{17,1},{2,18},{18,2},{3,19},{19,3},{4,20},{20... | collective-permute-start | bytes 2654216 | tf_op jit(solution)/shard_map/ppermute | solution.py:19
  919.8 6.3 collective-permute-start.41
  922.3 18.9 %collective-permute-start.55 = (f32[228,128]{1,0:T(8,128)S(1)}, f32[228,128]{1,0:T(8,128)S(1)}, u32[]{:S(2)}, u32[]{:S(2)}) collective-permute-start(f32[228,128]{1,0:T(8,128)S(1)} %fusion.55), channel_id=1, source_target_pairs={{0,8},{8,0},{1,9},{9,1},{2,10},{10,2},{3,11},{11,3},{4,12},{12,4},... | collective-permute-start | bytes 350216 | tf_op jit(solution)/shard_map/ppermute | solution.py:19
  941.2 7.9 collective-permute-start.56
  949.2 4.1 collective-permute-start.57
  949.4 10.7 %collective-permute-start.59 = (f32[1,2,1536]{2,0,1:T(1,128)S(1)}, f32[1,2,1536]{2,0,1:T(1,128)S(1)}, u32[]{:S(2)}, u32[]{:S(2)}) collective-permute-start(f32[1,2,1536]{2,0,1:T(1,128)S(1)} %bitcast.190), channel_id=1, source_target_pairs={{0,1},{1,0},{2,3},{3,2},{4,5},{5,4},{6,7},{7,6},{8,9},{9,8},{10,11... | collective-permute-start | bytes 36872 | tf_op jit(solution)/shard_map/ppermute | solution.py:19
  953.4 13.4 %collective-permute-start.58 = (f32[2,2,2,384]{3,0,2,1:T(2,128)S(1)}, f32[2,2,2,384]{3,0,2,1:T(2,128)S(1)}, u32[]{:S(2)}, u32[]{:S(2)}) collective-permute-start(f32[2,2,2,384]{3,0,2,1:T(2,128)S(1)} %pad_maximum_fusion.22), channel_id=1, source_target_pairs={{0,4},{4,0},{1,5},{5,1},{2,6},{6,2},{3,7},{7,3},{8,12},{12,8},{9,1... | collective-permute-start | bytes 36872 | tf_op jit(solution)/shard_map/ppermute | solution.py:19
  961.0 4.6 collective-permute-start.43
  962.1 10.5 %collective-permute-start.60 = (f32[2,2,1536]{2,0,1:T(2,128)S(1)}, f32[2,2,1536]{2,0,1:T(2,128)S(1)}, u32[]{:S(2)}, u32[]{:S(2)}) collective-permute-start(f32[2,2,1536]{2,0,1:T(2,128)S(1)} %pad_maximum_fusion.12), channel_id=1, source_target_pairs={{0,4},{4,0},{1,5},{5,1},{2,6},{6,2},{3,7},{7,3},{8,12},{12,8},{9,1... | collective-permute-start | bytes 73736 | tf_op jit(solution)/shard_map/ppermute | solution.py:19
  965.7 5.4 collective-permute-start.44
  973.8 5.0 collective-permute-start.46
  977.1 33.0 %collective-permute-start.49 = (bf16[2,192,1152]{2,1,0:T(8,128)(2,1)S(1)}, bf16[2,192,1152]{2,1,0:T(8,128)(2,1)}, u32[]{:S(2)}, u32[]{:S(2)}) collective-permute-start(bf16[2,192,1152]{2,1,0:T(8,128)(2,1)S(1)} %get-tuple-element.329), channel_id=1, source_target_pairs={{2,0},{4,6},{0,4},{6,2},{3,1},{5,7},{1,5},{7,3},{10,8},{12,14},{8,... | collective-permute-start | bytes 2654216 | tf_op jit(solution)/shard_map/ppermute | solution.py:738
  977.2 32.9 %collective-permute-start.48 = (bf16[2,192,1152]{2,1,0:T(8,128)(2,1)S(1)}, bf16[2,192,1152]{2,1,0:T(8,128)(2,1)}, u32[]{:S(2)}, u32[]{:S(2)}) collective-permute-start(bf16[2,192,1152]{2,1,0:T(8,128)(2,1)S(1)} %get-tuple-element.330), channel_id=1, source_target_pairs={{2,4},{4,2},{3,5},{5,3},{10,12},{12,10},{11,13},{13,11},{18,20},{2... | collective-permute-start | bytes 2654216 | tf_op jit(solution)/shard_map/ppermute | solution.py:737
  978.8 4.3 collective-permute-start.47
  1010.1 9.5 collective-permute-start.50
  1019.6 13.4 %collective-permute-start.51 = (f32[2,1536]{1,0:T(2,128)S(1)}, f32[2,1536]{1,0:T(2,128)}, u32[]{:S(2)}, u32[]{:S(2)}) collective-permute-start(f32[2,1536]{1,0:T(2,128)S(1)} %add.310), channel_id=1, source_target_pairs={{0,2},{2,0},{1,3},{3,1},{4,6},{6,4},{5,7},{7,5},{8,10},{10,8},{9,1... | collective-permute-start | bytes 36872 | tf_op jit(solution)/shard_map/ppermute | solution.py:19
  (95 other events, 940.2 us)
Sparse Core Ops, SparseCore 0:
  154.4 35.9 all-gather.5
  192.2 57.1 all-gather.7
  251.3 57.0 all-gather.9
  325.6 95.3 all-gather.11
  494.1 94.7 reduce-scatter.9
  591.8 95.0 reduce-scatter.11
  715.1 48.0 reduce-scatter.13

commit v5 on v3

--- a/solution.py
+++ b/solution.py
@@ -623,9 +623,9 @@
         pair = after(swap(own, self.p), *end)
         return [[own, swap(own, self.q)], [pair, swap(pair, self.q)]]
 
-    def sum_far(self, w, blocks, img):
-        (send, keep), unused = rows_nt([blocks[1][1], blocks[1][0]], w, img, (BF, F32))
-        return (keep + swap(send, self.q).astype(F32)).astype(BF)
+    def sum_far(self, w, blocks, img, rides=(), cid=None):
+        (send, keep), rode = rows_nt([blocks[1][1], blocks[1][0]], w, img, (BF, F32), rides, cid)
+        return (keep + swap(send, self.q).astype(F32)).astype(BF), rode
 
     def sum_near(self, w, blocks, img, rides=(), cid=None):
         (send, keep), rode = rows_nt([blocks[0][1], blocks[0][0]], w, img, (BF, F32), rides, cid)
@@ -886,7 +886,7 @@
         up_full.append(lay.spread_rows_async(rode[1]))
         down_own = lay.trade_shards(after(down_local, mine))
 
-    far = swap(lay.sum_far(proj_full, heads_out, img), lay.p)
+    far = swap(lay.sum_far(proj_full, heads_out, img)[0], lay.p)
     near, unused = lay.sum_near(proj_full, heads_out, img)
     branch_one = near + far.astype(F32) + spread(proj_bias.astype(F32))
     middle = inputs + gate_one * branch_one
@@ -906,40 +906,39 @@
         [grad_two, swap(grad_two, lay.q)], [grad_two_pair, swap(grad_two_pair, lay.q)]
     ]
     activated, slopes = up_out[:4], up_out[4:]
-    far = lay.sum_far(down_full, unflat(activated), img)
-    cut = rows * 21 // 37 // 16 * 16
-    back_out, rode = rows_nn(
-        flat(grad_two_blocks), down_full, img, "slope", slopes=slopes, rides=[ride(far, 0, cut)], cid=3
-    )
+    grad_two_flat = flat(grad_two_blocks)
+    back_out, unused = rows_nn(grad_two_flat, down_full, img, "slope", slopes=slopes)
     grad_inner, up_part = back_out[:4], back_out[4].reshape(2, up_n)
+    far_two, unused = lay.sum_far(up_full, unflat(grad_inner), img)
+    cut = rows * 15 // 37 // 16 * 16
+    near_two, rode = lay.sum_near(up_full, unflat(grad_inner), img, [ride(far_two, 0, cut)], 5)
     down_grads, rode_two = weight_grad(
-        after(flat(grad_two_blocks), grad_inner), activated, img, rides=[ride(far, cut, rows)], cid=4
-    )
-    far = jnp.concatenate(rode + rode_two, axis=0)
+        after(grad_two_flat, near_two), activated, img, rides=[ride(far_two, cut, rows)], cid=4
+    )
     if compact:
         down_plane = lay.sum_plane_async(down_grads)
-    far_two = lay.sum_far(up_full, after(unflat(grad_inner), down_grads), img)
-    cut, cut_two = rows * 11 // 37 // 16 * 16, rows * 22 // 37 // 16 * 16
-    near_two, rode = lay.sum_near(up_full, unflat(grad_inner), img, [ride(far_two, 0, cut)], 5)
-    up_grads, rode_two = weight_grad(
-        after(flat(second), near_two), grad_inner, img, rides=[ride(far_two, cut_two, rows)], cid=6
-    )
-    if compact:
-        up_plane = lay.sum_plane_async(up_grads)
-    near, rode_three = lay.sum_near(
-        down_full, after(unflat(activated), up_grads), img, [ride(far_two, cut, cut_two)], 7
-    )
-    far_two = jnp.concatenate(rode + rode_three + rode_two, axis=0)
-    branch_two = near + far.astype(F32) + spread(down_bias.astype(F32))
-    outputs = (live * (middle + gate_two * branch_two)).astype(BF)
-    grad_hidden_two = near_two + far_two.astype(F32)
+    grad_hidden_two = near_two + jnp.concatenate(rode + rode_two, axis=0).astype(F32)
     grad_middle = grad_out + norm_back(
         second_norm[0], second_norm[1], grad_hidden_two * (1.0 + scale_two)
     )
     grad_one = (gate_one * grad_middle).astype(BF)
-    if compact:
-        grad_one = after(grad_one, down_plane)
-    grad_one_blocks = lay.gather_rows(grad_one)
+    cut, cut_two = rows * 17 // 37 // 16 * 16, rows * 27 // 37 // 16 * 16
+    up_grads, rode = weight_grad(
+        after(flat(second), grad_one), grad_inner, img, rides=[ride(grad_one, 0, cut)], cid=6
+    )
+    if compact:
+        up_plane = lay.sum_plane_async(up_grads)
+    near, rode_two = lay.sum_near(
+        down_full, after(unflat(activated), up_grads), img, [ride(grad_one, cut, cut_two)], 7
+    )
+    deps = (near, down_plane) if compact else (near,)
+    far, rode_three = lay.sum_far(
+        down_full, after(unflat(activated), *deps), img, [ride(grad_one, cut_two, rows)], 3
+    )
+    grad_one_pair = jnp.concatenate(rode + rode_two + rode_three, axis=0)
+    grad_one_blocks = [
+        [grad_one, swap(grad_one, lay.q)], [grad_one_pair, swap(grad_one_pair, lay.q)]
+    ]
     grad_heads = unflat(rows_nn(flat(grad_one_blocks), proj_full, img, "plain")[0])
 
     def back(c, saved, heads, rides, cid):
@@ -958,9 +957,12 @@
             cid,
         )
 
-    grad_other, down_sums = back(
-        1, other, grad_heads, [lay.trade_ride(down_plane, True)] if compact else (), 11
-    )
+    half = rows // 32 * 16
+    rides, rides_two = [ride(far, 0, half)], [ride(far, half, rows)]
+    if compact:
+        rides.append(lay.trade_ride(down_plane, True))
+        rides_two.append(lay.trade_ride(up_plane, True))
+    grad_other, down_sums = back(1, other, grad_heads, rides, 11)
     proj_grads, unused = weight_grad(
         after(flat(grad_one_blocks), grad_other), flat(heads_out), img
     )
@@ -970,11 +972,14 @@
         0,
         mine,
         after(grad_heads, proj_grads),
-        [lay.trade_ride(up_plane, True)] if compact else (),
+        rides_two,
         12,
     )
+    far = jnp.concatenate(down_sums[:1] + up_sums[:1], axis=0)
+    branch_two = near + far.astype(F32) + spread(down_bias.astype(F32))
+    outputs = (live * (middle + gate_two * branch_two)).astype(BF)
     grad_qkv = [[grad_mine[z], grad_other[z]] for z in range(2)]
-    far = lay.sum_far(qkv_full, grad_qkv, img)
+    far, unused = lay.sum_far(qkv_full, grad_qkv, img)
     cut = rows * 16 // 37 // 16 * 16
     rides = [ride(far, 0, cut)]
     if compact:
@@ -989,7 +994,7 @@
     if compact:
         down_grad, up_grad, proj_grad = [
             (v[0].astype(F32) + v[1].astype(F32))[:, :, None]
-            for v in (down_sums[0], up_sums[0], proj_sums)
+            for v in (down_sums[1], up_sums[1], proj_sums)
         ]
         qkv_plane = lay.sum_plane(qkv_grads, rode_two[1:3])
     else:

time: 1030 us -> 1010 us (0.981)
  waiting for transfers between devices: 316 us -> 290 us
    ppermute x57 -> x56, waiting for transfers between devices: 285 us -> 232 us  [swap(): return lax.ppermute(v, axis, [(0, 1), (1, 0)])]
    unnamed x10, waiting for transfers between devices: 0.14 us -> 21.7 us
    pallas_call x13, Pallas kernels: 381 us -> 365 us  [launch(): pl.pallas_call(body, in_specs=[anywhere] * (n_in + n_rides), out_specs=[a...]
    ppermute x57 -> x56, starting transfers between devices: 59.5 us -> 71.7 us  [swap(): return lax.ppermute(v, axis, [(0, 1), (1, 0)])]
    ppermute x2, waiting for transfers between devices: 3.02 us -> 15 us  [trade_shards(): second = lax.ppermute(w, joint, [(0, 1), (3, 2), (2, 0), (1, 3)])]
    unnamed x186 -> x184, local copies, waits for them, and re-layouts: 32.9 us -> 38.5 us
  transfers between devices with their start and end apart: 70 -> 69, of which waited for: 36 -> 35; matrix products, arithmetic and copies ran while one was open for 12% -> 12% of each run, Pallas kernels for 28% -> 26%
where the time goes in v5:
time: 1010 us; the launch traced here: 1000 us
  Pallas kernels  432 us (43%)
  waiting for transfers between devices  290 us (29%)
  other arithmetic  108 us (11%)
  starting transfers between devices  83.6 us (8%)
  local copies, waits for them, and re-layouts  64.8 us (6%)
  between operations  16.7 us (2%)
    pallas_call x13, Pallas kernels, launch(): pl.pallas_call(body, in_specs=[anywhere] * (n_in + n_rides), out_specs=[a...  365 us
    ppermute x56, waiting for transfers between devices, swap(): return lax.ppermute(v, axis, [(0, 1), (1, 0)])  232 us
    ppermute x56, starting transfers between devices, swap(): return lax.ppermute(v, axis, [(0, 1), (1, 0)])  71.7 us
    pallas_call x7, Pallas kernels, launch(): pl.pallas_call(kernel, grid=grid, in_specs=in_specs, out_specs=out_specs,...  67 us
    unnamed x184, local copies, waits for them, and re-layouts  38.5 us
    unnamed x10, waiting for transfers between devices  21.7 us
    all_gather x4, waiting for transfers between devices, spread_rows_async(): return lax.all_gather(own, (self.y, self.x), axis=0, tiled=False)  21.3 us
  transfers between devices with their start and end apart: 69, of which 35 were waited for; matrix products, arithmetic and copies ran while one was open for 12% of the time, Pallas kernels for 26%

profile of v5, /device:TPU:0, one launch (start us, length us, event | category | flops | bytes accessed | tf_op | source)
XLA Modules:
  0.0 1001.2 jit_solution(5549798638763652858)
XLA Ops:
  9.6 4.0 collective-permute-start.7
  33.1 2.9 collective-permute-done.4
  40.3 12.9 %collective-permute-done.8 = f32[1,2,2,6,384]{4,1,3,2,0:T(2,128)S(1)} collective-permute-done((f32[1,2,2,6,384]{4,1,3,2,0:T(2,128)S(1)}, f32[1,2,2,6,384]{4,1,3,2,0:T(2,128)S(1)}, u32[]{:S(2)}, u32[]{:S(2)}) %collective-permute-start.8) | collective-permute-done | bytes 36896 | tf_op jit(solution)/shard_map/ppermute | solution.py:19
  53.3 2.8 collective-permute-start.9
  64.8 6.2 fusion.61
  71.6 11.9 %collective-permute-done.11 = bf16[384,1152]{1,0:T(8,128)(2,1)S(1)} collective-permute-done((bf16[384,1152]{1,0:T(8,128)(2,1)S(1)}, bf16[384,1152]{1,0:T(8,128)(2,1)S(1)}, u32[]{:S(2)}, u32[]{:S(2)}) %collective-permute-start.11) | collective-permute-done | bytes 884768 | tf_op jit(solution)/shard_map/ppermute | solution.py:19
  89.3 13.2 %collective-permute-done.15 = bf16[384,1152]{1,0:T(8,128)(2,1)S(1)} collective-permute-done((bf16[384,1152]{1,0:T(8,128)(2,1)S(1)}, bf16[384,1152]{1,0:T(8,128)(2,1)S(1)}, u32[]{:S(2)}, u32[]{:S(2)}) %collective-permute-start.15) | collective-permute-done | bytes 884768 | tf_op jit(solution)/shard_map/ppermute | solution.py:19
  104.1 15.1 %collective-permute-done.16 = bf16[384,1152]{1,0:T(8,128)(2,1)S(1)} collective-permute-done((bf16[384,1152]{1,0:T(8,128)(2,1)S(1)}, bf16[384,1152]{1,0:T(8,128)(2,1)S(1)}, u32[]{:S(2)}, u32[]{:S(2)}) %collective-permute-start.16) | collective-permute-done | bytes 884768 | tf_op jit(solution)/shard_map/ppermute | solution.py:19
  119.4 5.1 collective-permute-done.13.refs_2_
  129.8 24.5 %rows_bias_1.1 = (bf16[592,1152]{1,0:T(8,128)(2,1)}, bf16[592,1152]{1,0:T(8,128)(2,1)}, bf16[592,1152]{1,0:T(8,128)(2,1)}, bf16[592,1152]{1,0:T(8,128)(2,1)}, bf16[2,2,192,384]{3,2,1,0:T(8,128)(2,1)}) custom-call(bf16[592,1536]{1,0:T(8,128)(2,1)} %copy-done.57, bf16[592,1536]{1,0:T(8,128)(2,1)} %copy-done.86, bf16[592,1536]{1,0:T(8,128)(2,1)} %copy-done.85, ...), custom_call_target="tpu_custom_call" | custom-call | flops 8380219392 | bytes 16367616 | tf_op jit(solution)/shard_map/rows_bias_1/pallas_call | solution.py:128
  155.8 27.4 %attend_1_2.1 = (bf16[592,384]{1,0:T(8,128)(2,1)S(1)}, bf16[592,384]{1,0:T(8,128)(2,1)S(1)}, f32[3,2,4,256]{3,2,1,0:T(4,128)S(1)}, f32[3,2,1,160]{3,2,1,0:T(1,128)S(1)}, bf16[1,2,192,1536]{3,2,1,0:T(8,128)(2,1)}) custom-call(bf16[592,1152]{1,0:T(8,128)(2,1)} %get-tuple-element.196.refs_0_.refs_1_.refs_2_, ...), custom_call_target="tpu_custom_call" | custom-call | flops 5383127040 | bytes 10513920 | tf_op jit(solution)/shard_map/attend_1_2/pallas_call | solution.py:128
  183.3 7.3 all-gather.6.cloned.1.call-done.refs_2_.refs_3_.refs_4_.refs_5_
  190.6 29.9 %attend_0_10.1 = (bf16[592,384]{1,0:T(8,128)(2,1)S(1)}, bf16[592,384]{1,0:T(8,128)(2,1)S(1)}, f32[3,2,4,256]{3,2,1,0:T(4,128)S(1)}, f32[3,2,1,160]{3,2,1,0:T(1,1...) custom-call(bf16[592,1152]{1,0:T(8,128)(2,1)} %get-tuple-element.145.refs_0_.refs_1_.refs_2_, ...), custom_call_target="tpu_custom_call" | custom-call | flops 5383127040 | bytes 10513920 | tf_op jit(solution)/shard_map/attend_0_10/pallas_call | solution.py:128
  223.4 5.1 rows_back.5
  232.4 5.0 rows_back.4
  240.2 15.0 %collective-permute-done.23 = bf16[2,192,1536]{2,1,0:T(8,128)(2,1)S(1)} collective-permute-done((bf16[2,192,1536]{2,1,0:T(8,128)(2,1)S(1)}, bf16[2,192,1536]{2,1,0:T(8,128)(2,1)S(1)}, u32[]{:S(2)}, u32[]{:S(2)}) %collective-permute-start.23) | collective-permute-done | bytes 1179680 | tf_op jit(solution)/shard_map/ppermute | solution.py:645
  257.0 49.5 %collective-permute-done.21 = bf16[592,1536]{1,0:T(8,128)(2,1)} collective-permute-done((bf16[592,1536]{1,0:T(8,128)(2,1)}, bf16[592,1536]{1,0:T(8,128)(2,1)}, u32[]{:S(2)}, u32[]{:S(2)}) %collective-permute-start.21) | collective-permute-done | bytes 1818656 | tf_op jit(solution)/shard_map/ppermute | solution.py:19
  306.5 4.4 fusion.65
  315.3 41.0 %collective-permute-done.25.refs_2_ = bf16[592,1536]{1,0:T(8,128)(2,1)} collective-permute-done((bf16[592,1536]{1,0:T(8,128)(2,1)}, bf16[592,1536]{1,0:T(8,128)(2,1)}, u32[]{:S(2)}, u32[]{:S(2)}) %collective-permute-start.25) | collective-permute-done | bytes 1818656 | tf_op jit(solution)/shard_map/ppermute | solution.py:19
  360.4 29.3 %rows_gelu_13.1 = (bf16[592,1536]{1,0:T(8,128)(2,1)}, bf16[592,1536]{1,0:T(8,128)(2,1)}, bf16[592,1536]{1,0:T(8,128)(2,1)}, bf16[592,1536]{1,0:T(8,128)(2,1)}, f...) custom-call(bf16[592,1536]{1,0:T(8,128)(2,1)} %add_convert_fusion.3., ...), custom_call_target="tpu_custom_call" | custom-call | flops 11173625856 | bytes 21823488 | tf_op jit(solution)/shard_map/rows_gelu_13/pallas_call | solution.py:128
  391.2 3.9 collective-permute-done.28.refs_3_
  395.1 14.0 %all-gather.12.cloned.1.call-done = bf16[8,384,1536]{2,1,0:T(8,128)(2,1)} async-done(((bf16[2,384,1536]{2,1,0:T(8,128)(2,1)}), bf16[8,384,1536]{2,1,0:T(8,128)(2,1)}) %all-gather.12.cloned.1.call-update) | async-done | bytes 9437200 | tf_op jit(solution)/shard_map/all_gather | solution.py:674
  409.0 20.1 %rows_slope.1 = (bf16[592,1536]{1,0:T(8,128)(2,1)S(1)}, bf16[592,1536]{1,0:T(8,128)(2,1)}, bf16[592,1536]{1,0:T(8,128)(2,1)}, bf16[592,1536]{1,0:T(8,128)(2,1)}, f32[2,1,1536]{2,1,0:T(1,128)S(1)}) custom-call(bf16[592,1536]{1,0:T(8,128)(2,1)} %get-tuple-element.182.refs_6_.refs_7_.refs_0_, bf16[592,1536]{1,0:T(8,128)(2,1)} %collective-permute-done.27.refs_1_, ...), custom_call_target="tpu_custom_call" | custom-call | flops 11173625856 | bytes 21823488 | tf_op jit(solution)/shard_map/rows_slope/pallas_call | solution.py:81
  430.4 11.8 %rows_back.6 = (bf16[592,1536]{1,0:T(8,128)(2,1)S(1)}, f32[592,1536]{1,0:T(8,128)}) custom-call(bf16[592,1536]{1,0:T(8,128)(2,1)} %get-tuple-element.175.refs_0_.refs_7_, bf16[592,1536]{1,0:T(8,128)(2,1)} %get-tuple-element.176.refs_1_.refs_6_, bf16[4,1,384,1536]{3,2,1,0:T(8,128)(2,1)} %all-gather.8.cloned.1.call-done.refs_4_.refs_2_, ...), custom_call_target="tpu_custom_call" | custom-call | flops 5586812928 | bytes 10911744 | tf_op jit(solution)/shard_map/rows_back/pallas_call | solution.py:81
  442.1 3.8 collective-permute-done.29
  445.9 3.8 add_convert_fusion.2.refs_4_.refs_8_
  449.7 18.8 %rows_back_5.1 = (bf16[592,1536]{1,0:T(8,128)(2,1)}, f32[592,1536]{1,0:T(8,128)}, bf16[240,1536]{1,0:T(8,128)(2,1)S(1)}) custom-call(bf16[592,1536]{1,0:T(8,128)(2,1)} %get-tuple-element.173.refs_0_.refs_5_, bf16[592,1536]{1,0:T(8,128)(2,1)} %copy-done.24, bf16[4,1,384,1536]{3,2,1,0:T(8,128)(2,1)} %all-gather.8.cloned.1.call-done.refs_4_.refs_2_, ...), custom_call_target="tpu_custom_call" | custom-call | flops 5586812928 | bytes 10911744 | tf_op jit(solution)/shard_map/rows_back_5/pallas_call | solution.py:128
  468.6 4.0 collective-permute-done.30
  472.6 4.3 convert_add_fusion.5
  476.9 26.2 %weight_grad_4.1 = (bf16[4,2,384,1536]{3,2,1,0:T(8,128)(2,1)}, bf16[352,1536]{1,0:T(8,128)(2,1)S(1)}) custom-call(bf16[592,1536]{1,0:T(8,128)(2,1)} %get-tuple-element.182.refs_6_.refs_7_.refs_0_, bf16[592,1536]{1,0:T(8,128)(2,1)} %collective-permute-done.27.refs_1_, bf16[592,1536]{1,0:T(8,128)(2,1)} %copy-done.62, ...), custom_call_target="tpu_custom_call" | custom-call | flops 11173625856 | bytes 21823488 | tf_op jit(solution)/shard_map/weight_grad_4/pallas_call | solution.py:128
  504.2 6.2 fusion.23
  513.2 6.6 fusion.59
  519.8 24.1 %weight_grad_6.1 = (bf16[4,2,384,1536]{3,2,1,0:T(8,128)(2,1)}, bf16[272,1536]{1,0:T(8,128)(2,1)S(1)}) custom-call(bf16[592,1536]{1,0:T(8,128)(2,1)} %add_convert_fusion.3.refs_0_, bf16[592,1536]{1,0:T(8,128)(2,1)} %collective-permute-done.24.refs_1_, bf16[592,1536]{1,0:T(8,128)(2,1)} %collective-permute-done.25.refs_2_, ...), custom_call_target="tpu_custom_call" | custom-call | flops 11173625856 | bytes 21823488 | tf_op jit(solution)/shard_map/weight_grad_6/pallas_call | solution.py:128
  544.9 15.1 %rows_back_7.1 = (bf16[592,1536]{1,0:T(8,128)(2,1)}, f32[592,1536]{1,0:T(8,128)}, bf16[160,1536]{1,0:T(8,128)(2,1)S(1)}) custom-call(bf16[592,1536]{1,0:T(8,128)(2,1)} %get-tuple-element.192.refs_5_.refs_0_, bf16[592,1536]{1,0:T(8,128)(2,1)} %get-tuple-element.193.refs_4_.refs_1_, bf16[4,2,384,1536]{3,2,1,0:T(8,128)(2,1)} %bitcast.195, ...), custom_call_target="tpu_custom_call" | custom-call | flops 5586812928 | bytes 10911744 | tf_op jit(solution)/shard_map/rows_back_7/pallas_call | solution.py:128
  565.5 4.9 convert_add_fusion.3
  570.5 15.0 %rows_back_3.1 = (bf16[592,1536]{1,0:T(8,128)(2,1)}, f32[592,1536]{1,0:T(8,128)}, bf16[160,1536]{1,0:T(8,128)(2,1)S(1)}) custom-call(bf16[592,1536]{1,0:T(8,128)(2,1)} %get-tuple-element.200.refs_7_.refs_0_, bf16[592,1536]{1,0:T(8,128)(2,1)} %get-tuple-element.201.refs_6_.refs_1_, bf16[4,2,384,1536]{3,2,1,0:T(8,128)(2,1)} %bitcast.197, ...), custom_call_target="tpu_custom_call" | custom-call | flops 5586812928 | bytes 10911744 | tf_op jit(solution)/shard_map/rows_back_3/pallas_call | solution.py:128
  586.5 2.7 slice_reduce_fusion
  594.4 7.8 rows_plain.1
  605.2 3.3 add_convert_fusion.1.refs_10_
  610.7 42.4 %attend_back_1_11.1 = (bf16[592,1152]{1,0:T(8,128)(2,1)}, bf16[592,1152]{1,0:T(8,128)(2,1)}, f32[3,4,128]{2,1,0:T(4,128)S(1)}, bf16[288,1536]{1,0:T(8,128)(2,1)S(1)}, bf16[2,2,192,1536]{3,2,1,0:T(8,128)(2,1)}) custom-call(bf16[592,1152]{1,0:T(8,128)(2,1)} %get-tuple-element.196.refs_0_.refs_1_.refs_2_, ...), custom_call_target="tpu_custom_call" | custom-call | flops 13457817600 | bytes 26284800 | tf_op jit(solution)/shard_map/attend_back_1_11/pallas_call | solution.py:128
  654.0 7.9 weight_grad.1
  661.9 13.8 %collective-permute-start.54 = (f32[2,2,1536]{2,1,0:T(2,128)S(1)}, f32[2,2,1536]{2,1,0:T(2,128)S(1)}, u32[]{:S(2)}, u32[]{:S(2)}) collective-permute-start(f32[2,2,1536]{2,1,0:T(2,128)S(1)} %fusion.56), channel_id=1, source_target_pairs={{0,4},{4,0},{1,5},{5,1},{2,6},{6,2},{3,7},{7,3},{8,12},{12,8},{9,1... | collective-permute-start | bytes 73736 | tf_op jit(solution)/shard_map/ppermute | solution.py:19
  675.7 21.6 %reduce-scatter.12.cloned.1.call-done = bf16[1,2,384,1536]{3,2,1,0:T(8,128)(2,1)} async-done(((bf16[4,2,384,1536]{3,2,1,0:T(8,128)(2,1)}), bf16[1,2,384,1536]{3,2,1,0:T(8,128)(2,1)}) %reduce-scatter.12.cloned.1.call-update) | async-done | bytes 2359312
  699.4 44.7 %attend_back_0_12.1 = (bf16[592,1152]{1,0:T(8,128)(2,1)}, bf16[592,1152]{1,0:T(8,128)(2,1)}, f32[3,4,128]{2,1,0:T(4,128)S(1)}, bf16[304,1536]{1,0:T(8,128)(2,1)S(1)}, bf16[2,2,192,1536]{3,2,1,0:T(8,128)(2,1)}) custom-call(bf16[592,1152]{1,0:T(8,128)(2,1)} %get-tuple-element.145.refs_0_.refs_1_.refs_2_, ...), custom_call_target="tpu_custom_call" | custom-call | flops 13457817600 | bytes 26284800 | tf_op jit(solution)/shard_map/attend_back_0_12/pallas_call | solution.py:128
  744.1 9.4 rows_back.7
  753.5 11.7 %collective-permute-start.35 = (bf16[592,1536]{1,0:T(8,128)(2,1)}, bf16[592,1536]{1,0:T(8,128)(2,1)}, u32[]{:S(2)}, u32[]{:S(2)}) collective-permute-start(bf16[592,1536]{1,0:T(8,128)(2,1)} %get-tuple-element.226), channel_id=1, source_target_pairs={{0,4},{4,0},{1,5},{5,1},{2,6},{6,2},{3,7},{7,3},{8,12},{12,8},{9,1... | collective-permute-start | bytes 5455880 | tf_op jit(solution)/shard_map/ppermute | solution.py:19
  765.3 3.5 add_bitcast_fusion.1
  768.9 8.8 fusion.21
  777.7 3.5 add_convert_fusion.refs_8_.refs_4_
  782.3 26.8 %weight_grad_8.1 = (bf16[4,2,384,1152]{3,2,1,0:T(8,128)(2,1)}, bf16[256,1536]{1,0:T(8,128)(2,1)S(1)}, bf16[2,2,192,384]{3,2,1,0:T(8,128)(2,1)S(1)}) custom-call(bf16[592,1536]{1,0:T(8,128)(2,1)} %copy-done.57, bf16[592,1536]{1,0:T(8,128)(2,1)} %copy-done.86, bf16[592,1536]{1,0:T(8,128)(2,1)} %copy-done.85, bf16[592,1536]{1,0:T(8,128)(2,1)} %copy-done.87, ...), custom_call_target="tpu_custom_call" | custom-call | flops 8380219392 | bytes 16367616 | tf_op jit(solution)/shard_map/weight_grad_8/pallas_call | solution.py:128
  809.1 40.6 %rows_back_9.1 = (bf16[592,1536]{1,0:T(8,128)(2,1)}, f32[592,1536]{1,0:T(8,128)}, bf16[336,1536]{1,0:T(8,128)(2,1)S(1)}, bf16[2,384,1152]{2,1,0:T(8,128)(2,1)}, bf16[2,384,1152]{2,1,0:T(8,128)(2,1)}) custom-call(bf16[592,1152]{1,0:T(8,128)(2,1)} %get-tuple-element.228.refs_5_.refs_0_, bf16[592,1152]{1,0:T(8,128)(2,1)} %get-tuple-element.229.refs_4_.refs_1_, ...), custom_call_target="tpu_custom_call" | custom-call | flops 4190109696 | bytes 8183808 | tf_op jit(solution)/shard_map/rows_back_9/pallas_call | solution.py:128
  849.8 2.9 convert_add_fusion.7
  863.0 11.1 %collective-permute-done.38 = bf16[384,1152]{1,0:T(8,128)(2,1)} collective-permute-done((bf16[384,1152]{1,0:T(8,128)(2,1)}, bf16[384,1152]{1,0:T(8,128)(2,1)}, u32[]{:S(2)}, u32[]{:S(2)}) %collective-permute-start.38) | collective-permute-done | bytes 884768 | tf_op jit(solution)/shard_map/ppermute | solution.py:19
  876.1 3.2 collective-permute-done.37
  884.7 5.7 fusion.2
  893.9 6.9 fusion.42
  908.5 3.8 slice.304
  913.0 2.7 collective-permute-start.57
  922.7 3.1 collective-permute-done.60
  940.8 3.6 collective-permute-done.43
  947.8 4.2 convolution_bitcast_fusion
  953.2 19.4 %collective-permute-done.51 = f32[1,2,6,384]{3,2,1,0:T(8,128)S(1)} collective-permute-done((f32[1,2,6,384]{3,2,1,0:T(8,128)S(1)}, f32[1,2,6,384]{3,2,1,0:T(8,128)S(1)}, u32[]{:S(2)}, u32[]{:S(2)}) %collective-permute-start.51) | collective-permute-done | bytes 18464 | tf_op jit(solution)/shard_map/ppermute | solution.py:19
  974.2 3.6 collective-permute-done.52
  989.9 3.0 copy.128
  (473 shorter events, 167.7 us)
Async XLA Ops:
  7.2 183.4 %all-gather.6.cloned.1.call-start = ((), (), s32[]{:S(2)}) async-start(), calls=%async_computation.3 | async-start | bytes 2949120 | tf_op jit(solution)/shard_map/all_gather | solution.py:674
  9.6 49.4 %collective-permute-start.7 = (bf16[2,192,1152]{2,1,0:T(8,128)(2,1)}, bf16[2,192,1152]{2,1,0:T(8,128)(2,1)}, u32[]{:S(2)}, u32[]{:S(2)}) collective-permute-start(bf16[2,192,1152]{2,1,0:T(8,128)(2,1)} %bitcast.93), channel_id=1, source_target_pairs={{0,2},{6,4},{4,0},{2,6},{1,3},{7,5},{5,1},{3,7},{8,10},{14,12},{12... | collective-permute-start | bytes 2654216 | tf_op jit(solution)/shard_map/ppermute | solution.py:645
  13.6 45.3 %collective-permute-start.6 = (bf16[2,192,1152]{2,1,0:T(8,128)(2,1)}, bf16[2,192,1152]{2,1,0:T(8,128)(2,1)}, u32[]{:S(2)}, u32[]{:S(2)}) collective-permute-start(bf16[2,192,1152]{2,1,0:T(8,128)(2,1)} %bitcast.93), channel_id=1, source_target_pairs={{2,4},{4,2},{3,5},{5,3},{10,12},{12,10},{11,13},{13,11},{18,20},{2... | collective-permute-start | bytes 2654216 | tf_op jit(solution)/shard_map/ppermute | solution.py:644
  21.3 3.9 collective-permute-start.2
  26.3 5.2 collective-permute-start.3
  31.6 4.4 collective-permute-start.4
  37.4 15.9 %collective-permute-start.8 = (f32[1,2,2,6,384]{4,1,3,2,0:T(2,128)S(1)}, f32[1,2,2,6,384]{4,1,3,2,0:T(2,128)S(1)}, u32[]{:S(2)}, u32[]{:S(2)}) collective-permute-start(f32[1,2,2,6,384]{4,1,3,2,0:T(2,128)S(1)} %bitcast.213), channel_id=1, source_target_pairs={{0,1},{1,0},{2,3},{3,2},{4,5},{5,4},{6,7},{7,6},{8,9},{9,8},{10,11... | collective-permute-start | bytes 110600 | tf_op jit(solution)/shard_map/ppermute | solution.py:19
  53.3 5.3 collective-permute-start.9
  60.9 22.7 %collective-permute-start.11 = (bf16[384,1152]{1,0:T(8,128)(2,1)S(1)}, bf16[384,1152]{1,0:T(8,128)(2,1)S(1)}, u32[]{:S(2)}, u32[]{:S(2)}) collective-permute-start(bf16[384,1152]{1,0:T(8,128)(2,1)S(1)} %get-tuple-element.355), channel_id=1, source_target_pairs={{0,16},{16,0},{1,17},{17,1},{2,18},{18,2},{3,19},{19,3},{4,20},{20... | collective-permute-start | bytes 2654216 | tf_op jit(solution)/shard_map/ppermute | solution.py:19
  62.5 22.6 %collective-permute-start.10 = (bf16[384,1152]{1,0:T(8,128)(2,1)S(1)}, bf16[384,1152]{1,0:T(8,128)(2,1)S(1)}, u32[]{:S(2)}, u32[]{:S(2)}) collective-permute-start(bf16[384,1152]{1,0:T(8,128)(2,1)S(1)} %get-tuple-element.356), channel_id=1, source_target_pairs={{0,8},{8,0},{1,9},{9,1},{2,10},{10,2},{3,11},{11,3},{4,12},{12,4},... | collective-permute-start | bytes 2654216 | tf_op jit(solution)/shard_map/ppermute | solution.py:19
  64.2 38.2 %collective-permute-start.15 = (bf16[384,1152]{1,0:T(8,128)(2,1)S(1)}, bf16[384,1152]{1,0:T(8,128)(2,1)S(1)}, u32[]{:S(2)}, u32[]{:S(2)}) collective-permute-start(bf16[384,1152]{1,0:T(8,128)(2,1)S(1)} %get-tuple-element.356), channel_id=1, source_target_pairs={{0,16},{16,0},{1,17},{17,1},{2,18},{18,2},{3,19},{19,3},{4,20},{20... | collective-permute-start | bytes 2654216 | tf_op jit(solution)/shard_map/ppermute | solution.py:19
  71.1 53.6 %collective-permute-start.17 = (bf16[384,1152]{1,0:T(8,128)(2,1)S(1)}, bf16[384,1152]{1,0:T(8,128)(2,1)S(1)}, u32[]{:S(2)}, u32[]{:S(2)}) collective-permute-start(bf16[384,1152]{1,0:T(8,128)(2,1)S(1)} %get-tuple-element.355), channel_id=1, source_target_pairs={{0,8},{8,0},{1,9},{9,1},{2,10},{10,2},{3,11},{11,3},{4,12},{12,4},... | collective-permute-start | bytes 2654216 | tf_op jit(solution)/shard_map/ppermute | solution.py:19
  85.1 39.5 %collective-permute-start.13 = (bf16[592,1536]{1,0:T(8,128)(2,1)S(1)}, bf16[592,1536]{1,0:T(8,128)(2,1)S(1)}, u32[]{:S(2)}, u32[]{:S(2)}) collective-permute-start(bf16[592,1536]{1,0:T(8,128)(2,1)S(1)} %get-tuple-element.134.refs_0_), channel_id=1, source_target_pairs={{0,1},{1,0},{2,3},{3,2},{4,5},{5,4},{6,7},{7,6},{8,9},{9,8},{10,11... | collective-permute-start | bytes 5455880 | tf_op jit(solution)/shard_map/ppermute | solution.py:19
  88.5 37.3 %collective-permute-start.12 = (bf16[592,1536]{1,0:T(8,128)(2,1)S(1)}, bf16[592,1536]{1,0:T(8,128)(2,1)S(1)}, u32[]{:S(2)}, u32[]{:S(2)}) collective-permute-start(bf16[592,1536]{1,0:T(8,128)(2,1)S(1)} %get-tuple-element.134.refs_0_), channel_id=1, source_target_pairs={{0,4},{4,0},{1,5},{5,1},{2,6},{6,2},{3,7},{7,3},{8,12},{12,8},{9,1... | collective-permute-start | bytes 5455880 | tf_op jit(solution)/shard_map/ppermute | solution.py:19
  88.6 30.7 %collective-permute-start.16 = (bf16[384,1152]{1,0:T(8,128)(2,1)S(1)}, bf16[384,1152]{1,0:T(8,128)(2,1)S(1)}, u32[]{:S(2)}, u32[]{:S(2)}) collective-permute-start(bf16[384,1152]{1,0:T(8,128)(2,1)S(1)} %collective-permute-done.10), channel_id=1, source_target_pairs={{0,16},{16,0},{1,17},{17,1},{2,18},{18,2},{3,19},{19,3},{4,20},{20... | collective-permute-start | bytes 2654216 | tf_op jit(solution)/shard_map/ppermute | solution.py:19
  102.5 22.5 %collective-permute-start.18 = (bf16[384,1152]{1,0:T(8,128)(2,1)S(1)}, bf16[384,1152]{1,0:T(8,128)(2,1)S(1)}, u32[]{:S(2)}, u32[]{:S(2)}) collective-permute-start(bf16[384,1152]{1,0:T(8,128)(2,1)S(1)} %collective-permute-done.11), channel_id=1, source_target_pairs={{0,8},{8,0},{1,9},{9,1},{2,10},{10,2},{3,11},{11,3},{4,12},{12,4},... | collective-permute-start | bytes 2654216 | tf_op jit(solution)/shard_map/ppermute | solution.py:19
  124.6 3.8 collective-permute-start.14
  154.4 204.6 %all-gather.8.cloned.1.call-start = ((), (), s32[]{:S(2)}) async-start(), calls=%async_computation.4 | async-start | bytes 5898240 | tf_op jit(solution)/shard_map/all_gather | solution.py:674
  183.2 175.8 %all-gather.10.cloned.1.call-start = ((), (), s32[]{:S(2)}) async-start(), calls=%async_computation.5 | async-start | bytes 5898240 | tf_op jit(solution)/shard_map/all_gather | solution.py:674
  222.2 186.8 %all-gather.12.cloned.1.call-start = ((), (), s32[]{:S(2)}) async-start(), calls=%async_computation.6 | async-start | bytes 11796480 | tf_op jit(solution)/shard_map/all_gather | solution.py:674
  228.5 9.8 collective-permute-start.20
  228.5 26.7 %collective-permute-start.23 = (bf16[2,192,1536]{2,1,0:T(8,128)(2,1)S(1)}, bf16[2,192,1536]{2,1,0:T(8,128)(2,1)S(1)}, u32[]{:S(2)}, u32[]{:S(2)}) collective-permute-start(bf16[2,192,1536]{2,1,0:T(8,128)(2,1)S(1)} %bitcast.207), channel_id=1, source_target_pairs={{0,2},{6,4},{4,0},{2,6},{1,3},{7,5},{5,1},{3,7},{8,10},{14,12},{12... | collective-permute-start | bytes 3538952 | tf_op jit(solution)/shard_map/ppermute | solution.py:645
  230.7 24.5 %collective-permute-start.22 = (bf16[2,192,1536]{2,1,0:T(8,128)(2,1)S(1)}, bf16[2,192,1536]{2,1,0:T(8,128)(2,1)}, u32[]{:S(2)}, u32[]{:S(2)}) collective-permute-start(bf16[2,192,1536]{2,1,0:T(8,128)(2,1)S(1)} %bitcast.208), channel_id=1, source_target_pairs={{2,4},{4,2},{3,5},{5,3},{10,12},{12,10},{11,13},{13,11},{18,20},{2... | collective-permute-start | bytes 3538952 | tf_op jit(solution)/shard_map/ppermute | solution.py:644
  237.4 19.6 %collective-permute-start.19 = (bf16[592,1536]{1,0:T(8,128)(2,1)}, bf16[592,1536]{1,0:T(8,128)(2,1)}, u32[]{:S(2)}, u32[]{:S(2)}) collective-permute-start(bf16[592,1536]{1,0:T(8,128)(2,1)} %get-tuple-element.149), channel_id=1, source_target_pairs={{0,4},{4,0},{1,5},{5,1},{2,6},{6,2},{3,7},{7,3},{8,12},{12,8},{9,1... | collective-permute-start | bytes 5455880 | tf_op jit(solution)/shard_map/ppermute | solution.py:19
  240.1 66.4 %collective-permute-start.21 = (bf16[592,1536]{1,0:T(8,128)(2,1)}, bf16[592,1536]{1,0:T(8,128)(2,1)}, u32[]{:S(2)}, u32[]{:S(2)}) collective-permute-start(bf16[592,1536]{1,0:T(8,128)(2,1)} %add_convert_fusion.4), channel_id=1, source_target_pairs={{0,1},{1,0},{2,3},{3,2},{4,5},{5,4},{6,7},{7,6},{8,9},{9,8},{10,11... | collective-permute-start | bytes 5455880 | tf_op jit(solution)/shard_map/ppermute | solution.py:19
  315.1 293.4 %reduce-scatter.10.cloned.1.call-start = ((), (), s32[]{:S(2)}) async-start(), calls=%async_computation.7 | async-start | bytes 11796480
  315.2 41.1 %collective-permute-start.25 = (bf16[592,1536]{1,0:T(8,128)(2,1)}, bf16[592,1536]{1,0:T(8,128)(2,1)}, u32[]{:S(2)}, u32[]{:S(2)}) collective-permute-start(bf16[592,1536]{1,0:T(8,128)(2,1)} %add_convert_fusion.3.refs_0_), channel_id=1, source_target_pairs={{0,1},{1,0},{2,3},{3,2},{4,5},{5,4},{6,7},{7,6},{8,9},{9,8},{10,11... | collective-permute-start | bytes 5455880 | tf_op jit(solution)/shard_map/ppermute | solution.py:19
  315.2 43.8 %collective-permute-start.24 = (bf16[592,1536]{1,0:T(8,128)(2,1)}, bf16[592,1536]{1,0:T(8,128)(2,1)}, u32[]{:S(2)}, u32[]{:S(2)}) collective-permute-start(bf16[592,1536]{1,0:T(8,128)(2,1)} %add_convert_fusion.3.refs_0_), channel_id=1, source_target_pairs={{0,4},{4,0},{1,5},{5,1},{2,6},{6,2},{3,7},{7,3},{8,12},{12,8},{9,1... | collective-permute-start | bytes 5455880 | tf_op jit(solution)/shard_map/ppermute | solution.py:19
  356.3 4.1 collective-permute-start.26
  356.4 34.8 %collective-permute-start.27 = (bf16[592,1536]{1,0:T(8,128)(2,1)}, bf16[592,1536]{1,0:T(8,128)(2,1)}, u32[]{:S(2)}, u32[]{:S(2)}) collective-permute-start(bf16[592,1536]{1,0:T(8,128)(2,1)} %get-tuple-element.182.refs_6_.refs_7_.refs_0_), channel_id=1, source_target_pairs={{0,4},{4,0},{1,5},{5,1},{2,6},{6,2},{3,7},{7,3},{8,12},{12,8},{9,1... | collective-permute-start | bytes 5455880 | tf_op jit(solution)/shard_map/ppermute | solution.py:19
  391.2 3.9 collective-permute-start.28
  442.1 3.8 collective-permute-start.29
  468.6 4.0 collective-permute-start.30
  504.1 193.2 %reduce-scatter.12.cloned.1.call-start = ((), (), s32[]{:S(2)}) async-start(), calls=%async_computation.8 | async-start | bytes 11796480
  544.9 236.3 %reduce-scatter.14.cloned.1.call-start = ((), (), s32[]{:S(2)}) async-start(), calls=%async_computation.9 | async-start | bytes 2949120
  560.9 4.6 collective-permute-start.31
  560.9 33.5 %collective-permute-start.32 = (bf16[592,1536]{1,0:T(8,128)(2,1)}, bf16[592,1536]{1,0:T(8,128)(2,1)}, u32[]{:S(2)}, u32[]{:S(2)}) collective-permute-start(bf16[592,1536]{1,0:T(8,128)(2,1)} %get-tuple-element.216.refs_8_.refs_4_.refs_0_), channel_id=1, source_target_pairs={{0,4},{4,0},{1,5},{5,1},{2,6},{6,2},{3,7},{7,3},{8,12},{12,8},{9,1... | collective-permute-start | bytes 5455880 | tf_op jit(solution)/shard_map/ppermute | solution.py:19
  586.3 8.0 collective-permute-start.33
  589.1 16.1 %collective-permute-start.34 = (bf16[592,1536]{1,0:T(8,128)(2,1)}, bf16[592,1536]{1,0:T(8,128)(2,1)}, u32[]{:S(2)}, u32[]{:S(2)}) collective-permute-start(bf16[592,1536]{1,0:T(8,128)(2,1)} %get-tuple-element.208), channel_id=1, source_target_pairs={{0,4},{4,0},{1,5},{5,1},{2,6},{6,2},{3,7},{7,3},{8,12},{12,8},{9,1... | collective-permute-start | bytes 5455880 | tf_op jit(solution)/shard_map/ppermute | solution.py:19
  592.8 69.1 %collective-permute-start.53 = (f32[2,2,1536]{2,1,0:T(2,128)S(1)}, f32[2,2,1536]{2,1,0:T(2,128)S(1)}, u32[]{:S(2)}, u32[]{:S(2)}) collective-permute-start(f32[2,2,1536]{2,1,0:T(2,128)S(1)} %pad_maximum_fusion.13), channel_id=1, source_target_pairs={{0,1},{1,0},{2,3},{3,2},{4,5},{5,4},{6,7},{7,6},{8,9},{9,8},{10,11... | collective-permute-start | bytes 73736 | tf_op jit(solution)/shard_map/ppermute | solution.py:19
  661.9 103.3 %collective-permute-start.54 = (f32[2,2,1536]{2,1,0:T(2,128)S(1)}, f32[2,2,1536]{2,1,0:T(2,128)S(1)}, u32[]{:S(2)}, u32[]{:S(2)}) collective-permute-start(f32[2,2,1536]{2,1,0:T(2,128)S(1)} %fusion.56), channel_id=1, source_target_pairs={{0,4},{4,0},{1,5},{5,1},{2,6},{6,2},{3,7},{7,3},{8,12},{12,8},{9,1... | collective-permute-start | bytes 73736 | tf_op jit(solution)/shard_map/ppermute | solution.py:19
  753.5 24.2 %collective-permute-start.35 = (bf16[592,1536]{1,0:T(8,128)(2,1)}, bf16[592,1536]{1,0:T(8,128)(2,1)}, u32[]{:S(2)}, u32[]{:S(2)}) collective-permute-start(bf16[592,1536]{1,0:T(8,128)(2,1)} %get-tuple-element.226), channel_id=1, source_target_pairs={{0,4},{4,0},{1,5},{5,1},{2,6},{6,2},{3,7},{7,3},{8,12},{12,8},{9,1... | collective-permute-start | bytes 5455880 | tf_op jit(solution)/shard_map/ppermute | solution.py:19
  853.7 20.5 %collective-permute-start.38 = (bf16[384,1152]{1,0:T(8,128)(2,1)}, bf16[384,1152]{1,0:T(8,128)(2,1)}, u32[]{:S(2)}, u32[]{:S(2)}) collective-permute-start(bf16[384,1152]{1,0:T(8,128)(2,1)} %fusion.37), channel_id=1, source_target_pairs={{0,8},{8,0},{1,9},{9,1},{2,10},{10,2},{3,11},{11,3},{4,12},{12,4},... | collective-permute-start | bytes 2654216 | tf_op jit(solution)/shard_map/ppermute | solution.py:19
  858.6 20.7 %collective-permute-start.37 = (bf16[384,1152]{1,0:T(8,128)(2,1)}, bf16[384,1152]{1,0:T(8,128)(2,1)}, u32[]{:S(2)}, u32[]{:S(2)}) collective-permute-start(bf16[384,1152]{1,0:T(8,128)(2,1)} %fusion.36), channel_id=1, source_target_pairs={{0,16},{16,0},{1,17},{17,1},{2,18},{18,2},{3,19},{19,3},{4,20},{20... | collective-permute-start | bytes 2654216 | tf_op jit(solution)/shard_map/ppermute | solution.py:19
  860.1 22.6 %collective-permute-start.36 = (bf16[592,1536]{1,0:T(8,128)(2,1)}, bf16[592,1536]{1,0:T(8,128)(2,1)}, u32[]{:S(2)}, u32[]{:S(2)}) collective-permute-start(bf16[592,1536]{1,0:T(8,128)(2,1)} %get-tuple-element.231), channel_id=1, source_target_pairs={{0,4},{4,0},{1,5},{5,1},{2,6},{6,2},{3,7},{7,3},{8,12},{12,8},{9,1... | collective-permute-start | bytes 5455880 | tf_op jit(solution)/shard_map/ppermute | solution.py:19
  901.1 4.1 collective-permute-start.55
  905.2 7.7 collective-permute-start.56
  912.3 4.6 collective-permute-start.39
  913.0 5.9 collective-permute-start.57
  917.0 9.5 collective-permute-start.40
  922.6 9.2 collective-permute-start.59
  926.4 9.2 collective-permute-start.61
  927.4 6.4 collective-permute-start.41
  930.1 49.1 %collective-permute-start.48 = (bf16[2,192,1152]{2,1,0:T(8,128)(2,1)S(1)}, bf16[2,192,1152]{2,1,0:T(8,128)(2,1)}, u32[]{:S(2)}, u32[]{:S(2)}) collective-permute-start(bf16[2,192,1152]{2,1,0:T(8,128)(2,1)S(1)} %get-tuple-element.349), channel_id=1, source_target_pairs={{2,0},{4,6},{0,4},{6,2},{3,1},{5,7},{1,5},{7,3},{10,8},{12,14},{8,... | collective-permute-start | bytes 2654216 | tf_op jit(solution)/shard_map/ppermute | solution.py:733
  930.2 49.0 %collective-permute-start.47 = (bf16[2,192,1152]{2,1,0:T(8,128)(2,1)S(1)}, bf16[2,192,1152]{2,1,0:T(8,128)(2,1)}, u32[]{:S(2)}, u32[]{:S(2)}) collective-permute-start(bf16[2,192,1152]{2,1,0:T(8,128)(2,1)S(1)} %get-tuple-element.350), channel_id=1, source_target_pairs={{2,4},{4,2},{3,5},{5,3},{10,12},{12,10},{11,13},{13,11},{18,20},{2... | collective-permute-start | bytes 2654216 | tf_op jit(solution)/shard_map/ppermute | solution.py:732
  934.6 4.4 collective-permute-start.42
  939.2 5.2 collective-permute-start.43
  945.9 6.1 collective-permute-start.44
  952.0 20.6 %collective-permute-start.51 = (f32[1,2,6,384]{3,2,1,0:T(8,128)S(1)}, f32[1,2,6,384]{3,2,1,0:T(8,128)S(1)}, u32[]{:S(2)}, u32[]{:S(2)}) collective-permute-start(f32[1,2,6,384]{3,2,1,0:T(8,128)S(1)} %add_bitcast_fusion.4), channel_id=1, source_target_pairs={{0,1},{1,0},{2,3},{3,2},{4,5},{5,4},{6,7},{7,6},{8,9},{9,8},{10,11... | collective-permute-start | bytes 55304 | tf_op jit(solution)/shard_map/ppermute | solution.py:19
  952.0 20.7 %collective-permute-start.45 = (f32[2,16,192]{2,1,0:T(8,128)S(1)}, f32[2,16,192]{2,1,0:T(8,128)S(1)}, u32[]{:S(2)}, u32[]{:S(2)}) collective-permute-start(f32[2,16,192]{2,1,0:T(8,128)S(1)} %pad_maximum_fusion.11), channel_id=1, source_target_pairs={{0,8},{8,0},{1,9},{9,1},{2,10},{10,2},{3,11},{11,3},{4,12},{12,4},... | collective-permute-start | bytes 73736 | tf_op jit(solution)/shard_map/ppermute | solution.py:19
  972.6 5.1 collective-permute-start.52
  972.8 5.7 collective-permute-start.46
  979.2 3.9 collective-permute-start.49
  983.8 9.1 collective-permute-start.50
  (94 other events, 956.4 us)
Sparse Core Ops, SparseCore 0:
  154.5 36.0 all-gather.5
  192.5 57.0 all-gather.7
  251.4 57.0 all-gather.9
  315.2 93.7 all-gather.11
  504.2 95.0 reduce-scatter.9
  602.3 94.9 reduce-scatter.11
  700.9 37.3 reduce-scatter.13

commit v6 on v5

--- a/solution.py
+++ b/solution.py
@@ -911,12 +911,14 @@
     grad_inner, up_part = back_out[:4], back_out[4].reshape(2, up_n)
     far_two, unused = lay.sum_far(up_full, unflat(grad_inner), img)
     cut = rows * 15 // 37 // 16 * 16
-    near_two, rode = lay.sum_near(up_full, unflat(grad_inner), img, [ride(far_two, 0, cut)], 5)
     down_grads, rode_two = weight_grad(
-        after(grad_two_flat, near_two), activated, img, rides=[ride(far_two, cut, rows)], cid=4
+        grad_two_flat, activated, img, rides=[ride(far_two, cut, rows)], cid=4
     )
     if compact:
         down_plane = lay.sum_plane_async(down_grads)
+    near_two, rode = lay.sum_near(
+        up_full, after(unflat(grad_inner), down_grads), img, [ride(far_two, 0, cut)], 5
+    )
     grad_hidden_two = near_two + jnp.concatenate(rode + rode_two, axis=0).astype(F32)
     grad_middle = grad_out + norm_back(
         second_norm[0], second_norm[1], grad_hidden_two * (1.0 + scale_two)

time: 1010 us -> 985 us (0.975)
  waiting for transfers between devices: 290 us -> 270 us
    unnamed x10, waiting for transfers between devices: 21.7 us -> 1.78 us
    unnamed x184 -> x188, local copies, waits for them, and re-layouts: 38.5 us -> 37.4 us
  transfers between devices with their start and end apart: 69 -> 69, of which waited for: 35 -> 35; matrix products, arithmetic and copies ran while one was open for 12% -> 12% of each run, Pallas kernels for 26% -> 29%
where the time goes in v6:
time: 985 us; the launch traced here: 975 us
  Pallas kernels  432 us (44%)
  waiting for transfers between devices  270 us (27%)
  other arithmetic  102 us (10%)
  starting transfers between devices  83.8 us (9%)
  local copies, waits for them, and re-layouts  63.8 us (6%)
  between operations  16.7 us (2%)
    pallas_call x13, Pallas kernels, launch(): pl.pallas_call(body, in_specs=[anywhere] * (n_in + n_rides), out_specs=[a...  365 us
    ppermute x56, waiting for transfers between devices, swap(): return lax.ppermute(v, axis, [(0, 1), (1, 0)])  232 us
    ppermute x56, starting transfers between devices, swap(): return lax.ppermute(v, axis, [(0, 1), (1, 0)])  71.9 us
    pallas_call x7, Pallas kernels, launch(): pl.pallas_call(kernel, grid=grid, in_specs=in_specs, out_specs=out_specs,...  67.7 us
    unnamed x188, local copies, waits for them, and re-layouts  37.4 us
    all_gather x4, waiting for transfers between devices, spread_rows_async(): return lax.all_gather(own, (self.y, self.x), axis=0, tiled=False)  21.4 us
  transfers between devices with their start and end apart: 69, of which 35 were waited for; matrix products, arithmetic and copies ran while one was open for 12% of the time, Pallas kernels for 29%

profile of v6, /device:TPU:0, one launch (start us, length us, event | category | flops | bytes accessed | tf_op | source)
XLA Modules:
  0.0 974.7 jit_solution(16938345927539746058)
XLA Ops:
  9.6 4.0 collective-permute-start.7
  33.1 2.9 collective-permute-done.4
  40.3 12.9 %collective-permute-done.8 = f32[1,2,2,6,384]{4,1,3,2,0:T(2,128)S(1)} collective-permute-done((f32[1,2,2,6,384]{4,1,3,2,0:T(2,128)S(1)}, f32[1,2,2,6,384]{4,1,3,2,0:T(2,128)S(1)}, u32[]{:S(2)}, u32[]{:S(2)}) %collective-permute-start.8) | collective-permute-done | bytes 36896 | tf_op jit(solution)/shard_map/ppermute | solution.py:19
  53.3 2.8 collective-permute-start.9
  64.8 6.2 fusion.61
  71.6 11.9 %collective-permute-done.11 = bf16[384,1152]{1,0:T(8,128)(2,1)S(1)} collective-permute-done((bf16[384,1152]{1,0:T(8,128)(2,1)S(1)}, bf16[384,1152]{1,0:T(8,128)(2,1)S(1)}, u32[]{:S(2)}, u32[]{:S(2)}) %collective-permute-start.11) | collective-permute-done | bytes 884768 | tf_op jit(solution)/shard_map/ppermute | solution.py:19
  89.3 13.2 %collective-permute-done.15 = bf16[384,1152]{1,0:T(8,128)(2,1)S(1)} collective-permute-done((bf16[384,1152]{1,0:T(8,128)(2,1)S(1)}, bf16[384,1152]{1,0:T(8,128)(2,1)S(1)}, u32[]{:S(2)}, u32[]{:S(2)}) %collective-permute-start.15) | collective-permute-done | bytes 884768 | tf_op jit(solution)/shard_map/ppermute | solution.py:19
  104.1 15.1 %collective-permute-done.16 = bf16[384,1152]{1,0:T(8,128)(2,1)S(1)} collective-permute-done((bf16[384,1152]{1,0:T(8,128)(2,1)S(1)}, bf16[384,1152]{1,0:T(8,128)(2,1)S(1)}, u32[]{:S(2)}, u32[]{:S(2)}) %collective-permute-start.16) | collective-permute-done | bytes 884768 | tf_op jit(solution)/shard_map/ppermute | solution.py:19
  119.4 5.1 collective-permute-done.13.refs_2_
  125.8 2.5 collective-permute-done.14.refs_3_
  129.8 24.4 %rows_bias_1.1 = (bf16[592,1152]{1,0:T(8,128)(2,1)}, bf16[592,1152]{1,0:T(8,128)(2,1)}, bf16[592,1152]{1,0:T(8,128)(2,1)}, bf16[592,1152]{1,0:T(8,128)(2,1)}, bf16[2,2,192,384]{3,2,1,0:T(8,128)(2,1)}) custom-call(bf16[592,1536]{1,0:T(8,128)(2,1)} %copy-done.59, bf16[592,1536]{1,0:T(8,128)(2,1)} %copy-done.88, bf16[592,1536]{1,0:T(8,128)(2,1)} %copy-done.87, ...), custom_call_target="tpu_custom_call" | custom-call | flops 8380219392 | bytes 16367616 | tf_op jit(solution)/shard_map/rows_bias_1/pallas_call | solution.py:128
  155.6 27.4 %attend_1_2.1 = (bf16[592,384]{1,0:T(8,128)(2,1)S(1)}, bf16[592,384]{1,0:T(8,128)(2,1)S(1)}, f32[3,2,4,256]{3,2,1,0:T(4,128)S(1)}, f32[3,2,1,160]{3,2,1,0:T(1,128)S(1)}, bf16[1,2,192,1536]{3,2,1,0:T(8,128)(2,1)}) custom-call(bf16[592,1152]{1,0:T(8,128)(2,1)} %get-tuple-element.193.refs_0_.refs_1_.refs_2_, ...), custom_call_target="tpu_custom_call" | custom-call | flops 5383127040 | bytes 10513920 | tf_op jit(solution)/shard_map/attend_1_2/pallas_call | solution.py:128
  183.1 7.3 all-gather.6.cloned.1.call-done.refs_2_.refs_3_.refs_4_.refs_5_
  190.5 29.9 %attend_0_10.1 = (bf16[592,384]{1,0:T(8,128)(2,1)S(1)}, bf16[592,384]{1,0:T(8,128)(2,1)S(1)}, f32[3,2,4,256]{3,2,1,0:T(4,128)S(1)}, f32[3,2,1,160]{3,2,1,0:T(1,1...) custom-call(bf16[592,1152]{1,0:T(8,128)(2,1)} %get-tuple-element.143.refs_0_.refs_1_.refs_2_, ...), custom_call_target="tpu_custom_call" | custom-call | flops 5383127040 | bytes 10513920 | tf_op jit(solution)/shard_map/attend_0_10/pallas_call | solution.py:128
  223.2 5.1 rows_back.5
  232.3 5.0 rows_back.4
  240.1 15.0 %collective-permute-done.23 = bf16[2,192,1536]{2,1,0:T(8,128)(2,1)S(1)} collective-permute-done((bf16[2,192,1536]{2,1,0:T(8,128)(2,1)S(1)}, bf16[2,192,1536]{2,1,0:T(8,128)(2,1)S(1)}, u32[]{:S(2)}, u32[]{:S(2)}) %collective-permute-start.23) | collective-permute-done | bytes 1179680 | tf_op jit(solution)/shard_map/ppermute | solution.py:645
  256.9 49.5 %collective-permute-done.21 = bf16[592,1536]{1,0:T(8,128)(2,1)} collective-permute-done((bf16[592,1536]{1,0:T(8,128)(2,1)}, bf16[592,1536]{1,0:T(8,128)(2,1)}, u32[]{:S(2)}, u32[]{:S(2)}) %collective-permute-start.21) | collective-permute-done | bytes 1818656 | tf_op jit(solution)/shard_map/ppermute | solution.py:19
  306.4 4.4 fusion.65
  315.2 41.0 %collective-permute-done.25.refs_2_ = bf16[592,1536]{1,0:T(8,128)(2,1)} collective-permute-done((bf16[592,1536]{1,0:T(8,128)(2,1)}, bf16[592,1536]{1,0:T(8,128)(2,1)}, u32[]{:S(2)}, u32[]{:S(2)}) %collective-permute-start.25) | collective-permute-done | bytes 1818656 | tf_op jit(solution)/shard_map/ppermute | solution.py:19
  360.3 29.3 %rows_gelu_13.1 = (bf16[592,1536]{1,0:T(8,128)(2,1)}, bf16[592,1536]{1,0:T(8,128)(2,1)}, bf16[592,1536]{1,0:T(8,128)(2,1)}, bf16[592,1536]{1,0:T(8,128)(2,1)}, f...) custom-call(bf16[592,1536]{1,0:T(8,128)(2,1)} %add_convert_fusion.3., ...), custom_call_target="tpu_custom_call" | custom-call | flops 11173625856 | bytes 21823488 | tf_op jit(solution)/shard_map/rows_gelu_13/pallas_call | solution.py:128
  391.0 3.9 collective-permute-done.28.refs_3_
  394.9 14.0 %all-gather.12.cloned.1.call-done = bf16[8,384,1536]{2,1,0:T(8,128)(2,1)} async-done(((bf16[2,384,1536]{2,1,0:T(8,128)(2,1)}), bf16[8,384,1536]{2,1,0:T(8,128)(2,1)}) %all-gather.12.cloned.1.call-update) | async-done | bytes 9437200 | tf_op jit(solution)/shard_map/all_gather | solution.py:674
  408.9 20.0 %rows_slope.1 = (bf16[592,1536]{1,0:T(8,128)(2,1)S(1)}, bf16[592,1536]{1,0:T(8,128)(2,1)}, bf16[592,1536]{1,0:T(8,128)(2,1)}, bf16[592,1536]{1,0:T(8,128)(2,1)}, f32[2,1,1536]{2,1,0:T(1,128)S(1)}) custom-call(bf16[592,1536]{1,0:T(8,128)(2,1)} %get-tuple-element.327.refs_6_.refs_7_.refs_0_, bf16[592,1536]{1,0:T(8,128)(2,1)} %collective-permute-done.27.refs_1_, ...), custom_call_target="tpu_custom_call" | custom-call | flops 11173625856 | bytes 21823488 | tf_op jit(solution)/shard_map/rows_slope/pallas_call | solution.py:81
  430.2 12.0 %rows_back.6 = (bf16[592,1536]{1,0:T(8,128)(2,1)S(1)}, f32[592,1536]{1,0:T(8,128)}) custom-call(bf16[592,1536]{1,0:T(8,128)(2,1)} %get-tuple-element.174.refs_0_.refs_7_, bf16[592,1536]{1,0:T(8,128)(2,1)} %get-tuple-element.173.refs_1_.refs_6_, bf16[4,1,384,1536]{3,2,1,0:T(8,128)(2,1)} %all-gather.8.cloned.1.call-done.refs_4_.refs_2_, ...), custom_call_target="tpu_custom_call" | custom-call | flops 5586812928 | bytes 10911744 | tf_op jit(solution)/shard_map/rows_back/pallas_call | solution.py:81
  442.3 3.8 collective-permute-done.29
  446.0 3.8 add_convert_fusion.2.refs_8_.refs_4_
  449.8 26.2 %weight_grad_4.1 = (bf16[4,2,384,1536]{3,2,1,0:T(8,128)(2,1)}, bf16[352,1536]{1,0:T(8,128)(2,1)S(1)}) custom-call(bf16[592,1536]{1,0:T(8,128)(2,1)} %get-tuple-element.327.refs_6_.refs_7_.refs_0_, bf16[592,1536]{1,0:T(8,128)(2,1)} %collective-permute-done.27.refs_1_, bf16[592,1536]{1,0:T(8,128)(2,1)} %copy-done.64, ...), custom_call_target="tpu_custom_call" | custom-call | flops 11173625856 | bytes 21823488 | tf_op jit(solution)/shard_map/weight_grad_4/pallas_call | solution.py:128
  477.1 18.0 %rows_back_5.1 = (bf16[592,1536]{1,0:T(8,128)(2,1)}, f32[592,1536]{1,0:T(8,128)}, bf16[240,1536]{1,0:T(8,128)(2,1)S(1)}) custom-call(bf16[592,1536]{1,0:T(8,128)(2,1)} %get-tuple-element.178.refs_0_.refs_5_, bf16[592,1536]{1,0:T(8,128)(2,1)} %copy-done.26, bf16[4,1,384,1536]{3,2,1,0:T(8,128)(2,1)} %all-gather.8.cloned.1.call-done.refs_4_.refs_2_, ...), custom_call_target="tpu_custom_call" | custom-call | flops 5586812928 | bytes 10911744 | tf_op jit(solution)/shard_map/rows_back_5/pallas_call | solution.py:128
  495.2 4.0 collective-permute-done.30
  499.2 4.6 fusion.23
  506.5 6.3 fusion.59
  512.9 24.2 %weight_grad_6.1 = (bf16[4,2,384,1536]{3,2,1,0:T(8,128)(2,1)}, bf16[272,1536]{1,0:T(8,128)(2,1)S(1)}) custom-call(bf16[592,1536]{1,0:T(8,128)(2,1)} %add_convert_fusion.3.refs_0_, bf16[592,1536]{1,0:T(8,128)(2,1)} %collective-permute-done.24.refs_1_, bf16[592,1536]{1,0:T(8,128)(2,1)} %collective-permute-done.25.refs_2_, ...), custom_call_target="tpu_custom_call" | custom-call | flops 11173625856 | bytes 21823488 | tf_op jit(solution)/shard_map/weight_grad_6/pallas_call | solution.py:128
  538.1 15.7 %rows_back_7.1 = (bf16[592,1536]{1,0:T(8,128)(2,1)}, f32[592,1536]{1,0:T(8,128)}, bf16[160,1536]{1,0:T(8,128)(2,1)S(1)}) custom-call(bf16[592,1536]{1,0:T(8,128)(2,1)} %get-tuple-element.189.refs_5_.refs_0_, bf16[592,1536]{1,0:T(8,128)(2,1)} %get-tuple-element.190.refs_4_.refs_1_, bf16[4,2,384,1536]{3,2,1,0:T(8,128)(2,1)} %bitcast.195, ...), custom_call_target="tpu_custom_call" | custom-call | flops 5586812928 | bytes 10911744 | tf_op jit(solution)/shard_map/rows_back_7/pallas_call | solution.py:128
  559.2 5.2 convert_add_fusion.3
  564.4 15.3 %rows_back_3.1 = (bf16[592,1536]{1,0:T(8,128)(2,1)}, f32[592,1536]{1,0:T(8,128)}, bf16[160,1536]{1,0:T(8,128)(2,1)S(1)}) custom-call(bf16[592,1536]{1,0:T(8,128)(2,1)} %get-tuple-element.197.refs_7_.refs_0_, bf16[592,1536]{1,0:T(8,128)(2,1)} %get-tuple-element.198.refs_6_.refs_1_, bf16[4,2,384,1536]{3,2,1,0:T(8,128)(2,1)} %bitcast.197, ...), custom_call_target="tpu_custom_call" | custom-call | flops 5586812928 | bytes 10911744 | tf_op jit(solution)/shard_map/rows_back_3/pallas_call | solution.py:128
  587.4 8.0 rows_plain.1
  598.5 3.3 add_convert_fusion.1.refs_10_
  603.8 42.1 %attend_back_1_11.1 = (bf16[592,1152]{1,0:T(8,128)(2,1)}, bf16[592,1152]{1,0:T(8,128)(2,1)}, f32[3,4,128]{2,1,0:T(4,128)S(1)}, bf16[288,1536]{1,0:T(8,128)(2,1)S(1)}, bf16[2,2,192,1536]{3,2,1,0:T(8,128)(2,1)}) custom-call(bf16[592,1152]{1,0:T(8,128)(2,1)} %get-tuple-element.193.refs_0_.refs_1_.refs_2_, ...), custom_call_target="tpu_custom_call" | custom-call | flops 13457817600 | bytes 26284800 | tf_op jit(solution)/shard_map/attend_back_1_11/pallas_call | solution.py:128
  646.8 8.0 weight_grad.1
  654.9 13.7 %collective-permute-start.54 = (f32[2,2,1536]{2,1,0:T(2,128)S(1)}, f32[2,2,1536]{2,1,0:T(2,128)S(1)}, u32[]{:S(2)}, u32[]{:S(2)}) collective-permute-start(f32[2,2,1536]{2,1,0:T(2,128)S(1)} %fusion.56), channel_id=1, source_target_pairs={{0,4},{4,0},{1,5},{5,1},{2,6},{6,2},{3,7},{7,3},{8,12},{12,8},{9,1... | collective-permute-start | bytes 73736 | tf_op jit(solution)/shard_map/ppermute | solution.py:19
  672.3 44.7 %attend_back_0_12.1 = (bf16[592,1152]{1,0:T(8,128)(2,1)}, bf16[592,1152]{1,0:T(8,128)(2,1)}, f32[3,4,128]{2,1,0:T(4,128)S(1)}, bf16[304,1536]{1,0:T(8,128)(2,1)S(1)}, bf16[2,2,192,1536]{3,2,1,0:T(8,128)(2,1)}) custom-call(bf16[592,1152]{1,0:T(8,128)(2,1)} %get-tuple-element.143.refs_0_.refs_1_.refs_2_, ...), custom_call_target="tpu_custom_call" | custom-call | flops 13457817600 | bytes 26284800 | tf_op jit(solution)/shard_map/attend_back_0_12/pallas_call | solution.py:128
  717.0 9.6 rows_back.7
  726.6 11.7 %collective-permute-start.35 = (bf16[592,1536]{1,0:T(8,128)(2,1)}, bf16[592,1536]{1,0:T(8,128)(2,1)}, u32[]{:S(2)}, u32[]{:S(2)}) collective-permute-start(bf16[592,1536]{1,0:T(8,128)(2,1)} %get-tuple-element.222), channel_id=1, source_target_pairs={{0,4},{4,0},{1,5},{5,1},{2,6},{6,2},{3,7},{7,3},{8,12},{12,8},{9,1... | collective-permute-start | bytes 5455880 | tf_op jit(solution)/shard_map/ppermute | solution.py:19
  738.4 3.5 add_bitcast_fusion
  742.0 9.3 fusion.21
  751.3 3.4 add_convert_fusion.refs_8_.refs_4_
  755.8 26.8 %weight_grad_8.1 = (bf16[4,2,384,1152]{3,2,1,0:T(8,128)(2,1)}, bf16[256,1536]{1,0:T(8,128)(2,1)S(1)}, bf16[2,2,192,384]{3,2,1,0:T(8,128)(2,1)S(1)}) custom-call(bf16[592,1536]{1,0:T(8,128)(2,1)} %copy-done.59, bf16[592,1536]{1,0:T(8,128)(2,1)} %copy-done.88, bf16[592,1536]{1,0:T(8,128)(2,1)} %copy-done.87, bf16[592,1536]{1,0:T(8,128)(2,1)} %copy-done.89, ...), custom_call_target="tpu_custom_call" | custom-call | flops 8380219392 | bytes 16367616 | tf_op jit(solution)/shard_map/weight_grad_8/pallas_call | solution.py:128
  782.6 40.6 %rows_back_9.1 = (bf16[592,1536]{1,0:T(8,128)(2,1)}, f32[592,1536]{1,0:T(8,128)}, bf16[336,1536]{1,0:T(8,128)(2,1)S(1)}, bf16[2,384,1152]{2,1,0:T(8,128)(2,1)}, bf16[2,384,1152]{2,1,0:T(8,128)(2,1)}) custom-call(bf16[592,1152]{1,0:T(8,128)(2,1)} %get-tuple-element.224.refs_5_.refs_0_, bf16[592,1152]{1,0:T(8,128)(2,1)} %get-tuple-element.225.refs_4_.refs_1_, ...), custom_call_target="tpu_custom_call" | custom-call | flops 4190109696 | bytes 8183808 | tf_op jit(solution)/shard_map/rows_back_9/pallas_call | solution.py:128
  823.3 2.9 convert_add_fusion.6
  836.6 11.1 %collective-permute-done.38 = bf16[384,1152]{1,0:T(8,128)(2,1)} collective-permute-done((bf16[384,1152]{1,0:T(8,128)(2,1)}, bf16[384,1152]{1,0:T(8,128)(2,1)}, u32[]{:S(2)}, u32[]{:S(2)}) %collective-permute-start.38) | collective-permute-done | bytes 884768 | tf_op jit(solution)/shard_map/ppermute | solution.py:19
  849.6 3.2 collective-permute-done.37
  858.2 5.7 fusion.2
  867.4 6.9 fusion.42
  876.2 2.5 collective-permute-done.55
  882.1 3.8 slice.304
  886.5 2.7 collective-permute-start.57
  896.2 3.1 collective-permute-done.60
  909.9 2.6 collective-permute-done.42
  914.3 3.6 collective-permute-done.43
  921.3 4.2 convolution_bitcast_fusion
  926.8 19.4 %collective-permute-done.51 = f32[1,2,6,384]{3,2,1,0:T(8,128)S(1)} collective-permute-done((f32[1,2,6,384]{3,2,1,0:T(8,128)S(1)}, f32[1,2,6,384]{3,2,1,0:T(8,128)S(1)}, u32[]{:S(2)}, u32[]{:S(2)}) %collective-permute-start.51) | collective-permute-done | bytes 18464 | tf_op jit(solution)/shard_map/ppermute | solution.py:19
  947.7 3.6 collective-permute-done.52
  963.4 3.0 copy.128
  (476 shorter events, 163.0 us)
Async XLA Ops:
  7.2 183.3 %all-gather.6.cloned.1.call-start = ((), (), s32[]{:S(2)}) async-start(), calls=%async_computation.3 | async-start | bytes 2949120 | tf_op jit(solution)/shard_map/all_gather | solution.py:674
  9.6 49.4 %collective-permute-start.7 = (bf16[2,192,1152]{2,1,0:T(8,128)(2,1)}, bf16[2,192,1152]{2,1,0:T(8,128)(2,1)}, u32[]{:S(2)}, u32[]{:S(2)}) collective-permute-start(bf16[2,192,1152]{2,1,0:T(8,128)(2,1)} %bitcast.93), channel_id=1, source_target_pairs={{0,2},{6,4},{4,0},{2,6},{1,3},{7,5},{5,1},{3,7},{8,10},{14,12},{12... | collective-permute-start | bytes 2654216 | tf_op jit(solution)/shard_map/ppermute | solution.py:645
  13.6 45.3 %collective-permute-start.6 = (bf16[2,192,1152]{2,1,0:T(8,128)(2,1)}, bf16[2,192,1152]{2,1,0:T(8,128)(2,1)}, u32[]{:S(2)}, u32[]{:S(2)}) collective-permute-start(bf16[2,192,1152]{2,1,0:T(8,128)(2,1)} %bitcast.93), channel_id=1, source_target_pairs={{2,4},{4,2},{3,5},{5,3},{10,12},{12,10},{11,13},{13,11},{18,20},{2... | collective-permute-start | bytes 2654216 | tf_op jit(solution)/shard_map/ppermute | solution.py:644
  21.3 3.9 collective-permute-start.2
  26.3 5.2 collective-permute-start.3
  31.6 4.4 collective-permute-start.4
  37.4 15.9 %collective-permute-start.8 = (f32[1,2,2,6,384]{4,1,3,2,0:T(2,128)S(1)}, f32[1,2,2,6,384]{4,1,3,2,0:T(2,128)S(1)}, u32[]{:S(2)}, u32[]{:S(2)}) collective-permute-start(f32[1,2,2,6,384]{4,1,3,2,0:T(2,128)S(1)} %bitcast.213), channel_id=1, source_target_pairs={{0,1},{1,0},{2,3},{3,2},{4,5},{5,4},{6,7},{7,6},{8,9},{9,8},{10,11... | collective-permute-start | bytes 110600 | tf_op jit(solution)/shard_map/ppermute | solution.py:19
  53.3 5.3 collective-permute-start.9
  60.9 22.7 %collective-permute-start.11 = (bf16[384,1152]{1,0:T(8,128)(2,1)S(1)}, bf16[384,1152]{1,0:T(8,128)(2,1)S(1)}, u32[]{:S(2)}, u32[]{:S(2)}) collective-permute-start(bf16[384,1152]{1,0:T(8,128)(2,1)S(1)} %get-tuple-element.351), channel_id=1, source_target_pairs={{0,16},{16,0},{1,17},{17,1},{2,18},{18,2},{3,19},{19,3},{4,20},{20... | collective-permute-start | bytes 2654216 | tf_op jit(solution)/shard_map/ppermute | solution.py:19
  62.5 22.6 %collective-permute-start.10 = (bf16[384,1152]{1,0:T(8,128)(2,1)S(1)}, bf16[384,1152]{1,0:T(8,128)(2,1)S(1)}, u32[]{:S(2)}, u32[]{:S(2)}) collective-permute-start(bf16[384,1152]{1,0:T(8,128)(2,1)S(1)} %get-tuple-element.352), channel_id=1, source_target_pairs={{0,8},{8,0},{1,9},{9,1},{2,10},{10,2},{3,11},{11,3},{4,12},{12,4},... | collective-permute-start | bytes 2654216 | tf_op jit(solution)/shard_map/ppermute | solution.py:19
  64.2 38.2 %collective-permute-start.15 = (bf16[384,1152]{1,0:T(8,128)(2,1)S(1)}, bf16[384,1152]{1,0:T(8,128)(2,1)S(1)}, u32[]{:S(2)}, u32[]{:S(2)}) collective-permute-start(bf16[384,1152]{1,0:T(8,128)(2,1)S(1)} %get-tuple-element.352), channel_id=1, source_target_pairs={{0,16},{16,0},{1,17},{17,1},{2,18},{18,2},{3,19},{19,3},{4,20},{20... | collective-permute-start | bytes 2654216 | tf_op jit(solution)/shard_map/ppermute | solution.py:19
  71.1 53.6 %collective-permute-start.17 = (bf16[384,1152]{1,0:T(8,128)(2,1)S(1)}, bf16[384,1152]{1,0:T(8,128)(2,1)S(1)}, u32[]{:S(2)}, u32[]{:S(2)}) collective-permute-start(bf16[384,1152]{1,0:T(8,128)(2,1)S(1)} %get-tuple-element.351), channel_id=1, source_target_pairs={{0,8},{8,0},{1,9},{9,1},{2,10},{10,2},{3,11},{11,3},{4,12},{12,4},... | collective-permute-start | bytes 2654216 | tf_op jit(solution)/shard_map/ppermute | solution.py:19
  85.1 39.5 %collective-permute-start.13 = (bf16[592,1536]{1,0:T(8,128)(2,1)S(1)}, bf16[592,1536]{1,0:T(8,128)(2,1)S(1)}, u32[]{:S(2)}, u32[]{:S(2)}) collective-permute-start(bf16[592,1536]{1,0:T(8,128)(2,1)S(1)} %get-tuple-element.132.refs_0_), channel_id=1, source_target_pairs={{0,1},{1,0},{2,3},{3,2},{4,5},{5,4},{6,7},{7,6},{8,9},{9,8},{10,11... | collective-permute-start | bytes 5455880 | tf_op jit(solution)/shard_map/ppermute | solution.py:19
  88.5 37.3 %collective-permute-start.12 = (bf16[592,1536]{1,0:T(8,128)(2,1)S(1)}, bf16[592,1536]{1,0:T(8,128)(2,1)S(1)}, u32[]{:S(2)}, u32[]{:S(2)}) collective-permute-start(bf16[592,1536]{1,0:T(8,128)(2,1)S(1)} %get-tuple-element.132.refs_0_), channel_id=1, source_target_pairs={{0,4},{4,0},{1,5},{5,1},{2,6},{6,2},{3,7},{7,3},{8,12},{12,8},{9,1... | collective-permute-start | bytes 5455880 | tf_op jit(solution)/shard_map/ppermute | solution.py:19
  88.6 30.7 %collective-permute-start.16 = (bf16[384,1152]{1,0:T(8,128)(2,1)S(1)}, bf16[384,1152]{1,0:T(8,128)(2,1)S(1)}, u32[]{:S(2)}, u32[]{:S(2)}) collective-permute-start(bf16[384,1152]{1,0:T(8,128)(2,1)S(1)} %collective-permute-done.10), channel_id=1, source_target_pairs={{0,16},{16,0},{1,17},{17,1},{2,18},{18,2},{3,19},{19,3},{4,20},{20... | collective-permute-start | bytes 2654216 | tf_op jit(solution)/shard_map/ppermute | solution.py:19
  102.5 22.5 %collective-permute-start.18 = (bf16[384,1152]{1,0:T(8,128)(2,1)S(1)}, bf16[384,1152]{1,0:T(8,128)(2,1)S(1)}, u32[]{:S(2)}, u32[]{:S(2)}) collective-permute-start(bf16[384,1152]{1,0:T(8,128)(2,1)S(1)} %collective-permute-done.11), channel_id=1, source_target_pairs={{0,8},{8,0},{1,9},{9,1},{2,10},{10,2},{3,11},{11,3},{4,12},{12,4},... | collective-permute-start | bytes 2654216 | tf_op jit(solution)/shard_map/ppermute | solution.py:19
  124.6 3.8 collective-permute-start.14
  154.2 204.7 %all-gather.8.cloned.1.call-start = ((), (), s32[]{:S(2)}) async-start(), calls=%async_computation.4 | async-start | bytes 5898240 | tf_op jit(solution)/shard_map/all_gather | solution.py:674
  183.1 175.9 %all-gather.10.cloned.1.call-start = ((), (), s32[]{:S(2)}) async-start(), calls=%async_computation.5 | async-start | bytes 5898240 | tf_op jit(solution)/shard_map/all_gather | solution.py:674
  222.0 186.9 %all-gather.12.cloned.1.call-start = ((), (), s32[]{:S(2)}) async-start(), calls=%async_computation.6 | async-start | bytes 11796480 | tf_op jit(solution)/shard_map/all_gather | solution.py:674
  228.3 9.8 %collective-permute-start.20 = (bf16[592,1536]{1,0:T(8,128)(2,1)}, bf16[592,1536]{1,0:T(8,128)(2,1)S(1)}, u32[]{:S(2)}, u32[]{:S(2)}) collective-permute-start(bf16[592,1536]{1,0:T(8,128)(2,1)} %get-tuple-element.151), channel_id=1, source_target_pairs={{0,4},{4,0},{1,5},{5,1},{2,6},{6,2},{3,7},{7,3},{8,12},{12,8},{9,1... | collective-permute-start | bytes 5455880 | tf_op jit(solution)/shard_map/ppermute | solution.py:19
  228.4 26.7 %collective-permute-start.23 = (bf16[2,192,1536]{2,1,0:T(8,128)(2,1)S(1)}, bf16[2,192,1536]{2,1,0:T(8,128)(2,1)S(1)}, u32[]{:S(2)}, u32[]{:S(2)}) collective-permute-start(bf16[2,192,1536]{2,1,0:T(8,128)(2,1)S(1)} %bitcast.207), channel_id=1, source_target_pairs={{0,2},{6,4},{4,0},{2,6},{1,3},{7,5},{5,1},{3,7},{8,10},{14,12},{12... | collective-permute-start | bytes 3538952 | tf_op jit(solution)/shard_map/ppermute | solution.py:645
  230.6 24.5 %collective-permute-start.22 = (bf16[2,192,1536]{2,1,0:T(8,128)(2,1)S(1)}, bf16[2,192,1536]{2,1,0:T(8,128)(2,1)}, u32[]{:S(2)}, u32[]{:S(2)}) collective-permute-start(bf16[2,192,1536]{2,1,0:T(8,128)(2,1)S(1)} %bitcast.208), channel_id=1, source_target_pairs={{2,4},{4,2},{3,5},{5,3},{10,12},{12,10},{11,13},{13,11},{18,20},{2... | collective-permute-start | bytes 3538952 | tf_op jit(solution)/shard_map/ppermute | solution.py:644
  237.3 19.6 %collective-permute-start.19 = (bf16[592,1536]{1,0:T(8,128)(2,1)}, bf16[592,1536]{1,0:T(8,128)(2,1)}, u32[]{:S(2)}, u32[]{:S(2)}) collective-permute-start(bf16[592,1536]{1,0:T(8,128)(2,1)} %get-tuple-element.147), channel_id=1, source_target_pairs={{0,4},{4,0},{1,5},{5,1},{2,6},{6,2},{3,7},{7,3},{8,12},{12,8},{9,1... | collective-permute-start | bytes 5455880 | tf_op jit(solution)/shard_map/ppermute | solution.py:19
  239.9 66.4 %collective-permute-start.21 = (bf16[592,1536]{1,0:T(8,128)(2,1)}, bf16[592,1536]{1,0:T(8,128)(2,1)}, u32[]{:S(2)}, u32[]{:S(2)}) collective-permute-start(bf16[592,1536]{1,0:T(8,128)(2,1)} %add_convert_fusion.4), channel_id=1, source_target_pairs={{0,1},{1,0},{2,3},{3,2},{4,5},{5,4},{6,7},{7,6},{8,9},{9,8},{10,11... | collective-permute-start | bytes 5455880 | tf_op jit(solution)/shard_map/ppermute | solution.py:19
  315.0 286.7 %reduce-scatter.10.cloned.1.call-start = ((), (), s32[]{:S(2)}) async-start(), calls=%async_computation.7 | async-start | bytes 11796480
  315.1 41.1 %collective-permute-start.25 = (bf16[592,1536]{1,0:T(8,128)(2,1)}, bf16[592,1536]{1,0:T(8,128)(2,1)}, u32[]{:S(2)}, u32[]{:S(2)}) collective-permute-start(bf16[592,1536]{1,0:T(8,128)(2,1)} %add_convert_fusion.3.refs_0_), channel_id=1, source_target_pairs={{0,1},{1,0},{2,3},{3,2},{4,5},{5,4},{6,7},{7,6},{8,9},{9,8},{10,11... | collective-permute-start | bytes 5455880 | tf_op jit(solution)/shard_map/ppermute | solution.py:19
  315.2 43.8 %collective-permute-start.24 = (bf16[592,1536]{1,0:T(8,128)(2,1)}, bf16[592,1536]{1,0:T(8,128)(2,1)}, u32[]{:S(2)}, u32[]{:S(2)}) collective-permute-start(bf16[592,1536]{1,0:T(8,128)(2,1)} %add_convert_fusion.3.refs_0_), channel_id=1, source_target_pairs={{0,4},{4,0},{1,5},{5,1},{2,6},{6,2},{3,7},{7,3},{8,12},{12,8},{9,1... | collective-permute-start | bytes 5455880 | tf_op jit(solution)/shard_map/ppermute | solution.py:19
  356.2 4.1 collective-permute-start.26
  356.3 34.8 %collective-permute-start.27 = (bf16[592,1536]{1,0:T(8,128)(2,1)}, bf16[592,1536]{1,0:T(8,128)(2,1)}, u32[]{:S(2)}, u32[]{:S(2)}) collective-permute-start(bf16[592,1536]{1,0:T(8,128)(2,1)} %get-tuple-element.327.refs_6_.refs_7_.refs_0_), channel_id=1, source_target_pairs={{0,4},{4,0},{1,5},{5,1},{2,6},{6,2},{3,7},{7,3},{8,12},{12,8},{9,1... | collective-permute-start | bytes 5455880 | tf_op jit(solution)/shard_map/ppermute | solution.py:19
  391.0 3.9 collective-permute-start.28
  442.2 3.8 collective-permute-start.29
  477.0 193.2 %reduce-scatter.12.cloned.1.call-start = ((), (), s32[]{:S(2)}) async-start(), calls=%async_computation.8 | async-start | bytes 11796480
  495.1 4.0 collective-permute-start.30
  538.0 216.7 %reduce-scatter.14.cloned.1.call-start = ((), (), s32[]{:S(2)}) async-start(), calls=%async_computation.9 | async-start | bytes 2949120
  554.6 4.6 collective-permute-start.31
  554.7 32.7 %collective-permute-start.32 = (bf16[592,1536]{1,0:T(8,128)(2,1)}, bf16[592,1536]{1,0:T(8,128)(2,1)}, u32[]{:S(2)}, u32[]{:S(2)}) collective-permute-start(bf16[592,1536]{1,0:T(8,128)(2,1)} %get-tuple-element.212.refs_8_.refs_4_.refs_0_), channel_id=1, source_target_pairs={{0,4},{4,0},{1,5},{5,1},{2,6},{6,2},{3,7},{7,3},{8,12},{12,8},{9,1... | collective-permute-start | bytes 5455880 | tf_op jit(solution)/shard_map/ppermute | solution.py:19
  580.5 6.9 collective-permute-start.33
  580.7 17.8 %collective-permute-start.34 = (bf16[592,1536]{1,0:T(8,128)(2,1)}, bf16[592,1536]{1,0:T(8,128)(2,1)}, u32[]{:S(2)}, u32[]{:S(2)}) collective-permute-start(bf16[592,1536]{1,0:T(8,128)(2,1)} %get-tuple-element.205), channel_id=1, source_target_pairs={{0,4},{4,0},{1,5},{5,1},{2,6},{6,2},{3,7},{7,3},{8,12},{12,8},{9,1... | collective-permute-start | bytes 5455880 | tf_op jit(solution)/shard_map/ppermute | solution.py:19
  585.9 69.0 %collective-permute-start.53 = (f32[2,2,1536]{2,1,0:T(2,128)S(1)}, f32[2,2,1536]{2,1,0:T(2,128)S(1)}, u32[]{:S(2)}, u32[]{:S(2)}) collective-permute-start(f32[2,2,1536]{2,1,0:T(2,128)S(1)} %pad_maximum_fusion.13), channel_id=1, source_target_pairs={{0,1},{1,0},{2,3},{3,2},{4,5},{5,4},{6,7},{7,6},{8,9},{9,8},{10,11... | collective-permute-start | bytes 73736 | tf_op jit(solution)/shard_map/ppermute | solution.py:19
  654.9 83.5 %collective-permute-start.54 = (f32[2,2,1536]{2,1,0:T(2,128)S(1)}, f32[2,2,1536]{2,1,0:T(2,128)S(1)}, u32[]{:S(2)}, u32[]{:S(2)}) collective-permute-start(f32[2,2,1536]{2,1,0:T(2,128)S(1)} %fusion.56), channel_id=1, source_target_pairs={{0,4},{4,0},{1,5},{5,1},{2,6},{6,2},{3,7},{7,3},{8,12},{12,8},{9,1... | collective-permute-start | bytes 73736 | tf_op jit(solution)/shard_map/ppermute | solution.py:19
  726.6 24.7 %collective-permute-start.35 = (bf16[592,1536]{1,0:T(8,128)(2,1)}, bf16[592,1536]{1,0:T(8,128)(2,1)}, u32[]{:S(2)}, u32[]{:S(2)}) collective-permute-start(bf16[592,1536]{1,0:T(8,128)(2,1)} %get-tuple-element.222), channel_id=1, source_target_pairs={{0,4},{4,0},{1,5},{5,1},{2,6},{6,2},{3,7},{7,3},{8,12},{12,8},{9,1... | collective-permute-start | bytes 5455880 | tf_op jit(solution)/shard_map/ppermute | solution.py:19
  827.2 20.5 %collective-permute-start.38 = (bf16[384,1152]{1,0:T(8,128)(2,1)}, bf16[384,1152]{1,0:T(8,128)(2,1)}, u32[]{:S(2)}, u32[]{:S(2)}) collective-permute-start(bf16[384,1152]{1,0:T(8,128)(2,1)} %fusion.37), channel_id=1, source_target_pairs={{0,8},{8,0},{1,9},{9,1},{2,10},{10,2},{3,11},{11,3},{4,12},{12,4},... | collective-permute-start | bytes 2654216 | tf_op jit(solution)/shard_map/ppermute | solution.py:19
  832.1 20.7 %collective-permute-start.37 = (bf16[384,1152]{1,0:T(8,128)(2,1)}, bf16[384,1152]{1,0:T(8,128)(2,1)}, u32[]{:S(2)}, u32[]{:S(2)}) collective-permute-start(bf16[384,1152]{1,0:T(8,128)(2,1)} %fusion.36), channel_id=1, source_target_pairs={{0,16},{16,0},{1,17},{17,1},{2,18},{18,2},{3,19},{19,3},{4,20},{20... | collective-permute-start | bytes 2654216 | tf_op jit(solution)/shard_map/ppermute | solution.py:19
  833.6 22.6 %collective-permute-start.36 = (bf16[592,1536]{1,0:T(8,128)(2,1)}, bf16[592,1536]{1,0:T(8,128)(2,1)}, u32[]{:S(2)}, u32[]{:S(2)}) collective-permute-start(bf16[592,1536]{1,0:T(8,128)(2,1)} %get-tuple-element.227), channel_id=1, source_target_pairs={{0,4},{4,0},{1,5},{5,1},{2,6},{6,2},{3,7},{7,3},{8,12},{12,8},{9,1... | collective-permute-start | bytes 5455880 | tf_op jit(solution)/shard_map/ppermute | solution.py:19
  874.6 4.1 collective-permute-start.55
  878.7 7.7 collective-permute-start.56
  885.8 4.6 collective-permute-start.39
  886.5 5.9 collective-permute-start.57
  890.5 9.4 collective-permute-start.40
  896.1 9.2 collective-permute-start.59
  899.9 9.2 collective-permute-start.61
  900.9 6.4 collective-permute-start.41
  903.6 49.1 %collective-permute-start.48 = (bf16[2,192,1152]{2,1,0:T(8,128)(2,1)S(1)}, bf16[2,192,1152]{2,1,0:T(8,128)(2,1)}, u32[]{:S(2)}, u32[]{:S(2)}) collective-permute-start(bf16[2,192,1152]{2,1,0:T(8,128)(2,1)S(1)} %get-tuple-element.345), channel_id=1, source_target_pairs={{2,0},{4,6},{0,4},{6,2},{3,1},{5,7},{1,5},{7,3},{10,8},{12,14},{8,... | collective-permute-start | bytes 2654216 | tf_op jit(solution)/shard_map/ppermute | solution.py:733
  903.7 49.0 %collective-permute-start.47 = (bf16[2,192,1152]{2,1,0:T(8,128)(2,1)S(1)}, bf16[2,192,1152]{2,1,0:T(8,128)(2,1)}, u32[]{:S(2)}, u32[]{:S(2)}) collective-permute-start(bf16[2,192,1152]{2,1,0:T(8,128)(2,1)S(1)} %get-tuple-element.346), channel_id=1, source_target_pairs={{2,4},{4,2},{3,5},{5,3},{10,12},{12,10},{11,13},{13,11},{18,20},{2... | collective-permute-start | bytes 2654216 | tf_op jit(solution)/shard_map/ppermute | solution.py:732
  908.2 4.4 collective-permute-start.42
  912.7 5.2 collective-permute-start.43
  919.5 6.1 collective-permute-start.44
  925.5 20.6 %collective-permute-start.51 = (f32[1,2,6,384]{3,2,1,0:T(8,128)S(1)}, f32[1,2,6,384]{3,2,1,0:T(8,128)S(1)}, u32[]{:S(2)}, u32[]{:S(2)}) collective-permute-start(f32[1,2,6,384]{3,2,1,0:T(8,128)S(1)} %add_bitcast_fusion.4), channel_id=1, source_target_pairs={{0,1},{1,0},{2,3},{3,2},{4,5},{5,4},{6,7},{7,6},{8,9},{9,8},{10,11... | collective-permute-start | bytes 55304 | tf_op jit(solution)/shard_map/ppermute | solution.py:19
  925.6 20.7 %collective-permute-start.45 = (f32[2,16,192]{2,1,0:T(8,128)S(1)}, f32[2,16,192]{2,1,0:T(8,128)S(1)}, u32[]{:S(2)}, u32[]{:S(2)}) collective-permute-start(f32[2,16,192]{2,1,0:T(8,128)S(1)} %pad_maximum_fusion.11), channel_id=1, source_target_pairs={{0,8},{8,0},{1,9},{9,1},{2,10},{10,2},{3,11},{11,3},{4,12},{12,4},... | collective-permute-start | bytes 73736 | tf_op jit(solution)/shard_map/ppermute | solution.py:19
  946.2 5.1 collective-permute-start.52
  946.3 5.7 collective-permute-start.46
  952.7 3.9 collective-permute-start.49
  957.3 9.1 collective-permute-start.50
  (96 other events, 1006.5 us)
Sparse Core Ops, SparseCore 0:
  154.3 36.0 all-gather.5
  192.3 57.0 all-gather.7
  251.2 57.0 all-gather.9
  315.1 93.7 all-gather.11
  477.2 95.0 reduce-scatter.9
  575.2 95.0 reduce-scatter.11
  673.9 37.3 reduce-scatter.13
